TPU v7x, 32 devices: a whole 2x2x4 slice. The times are simulated.
32 devices in a mesh: ctx: 8 (over y, x, core), exp: 4 (over z).
Axes of the slice: x: 2, y: 2, z: 4, core: 2. Of those that a mesh axis runs over, the one named last changes fastest.
Arguments:
- queries: bfloat16 [1024, 8192], P('ctx', 'exp'), may hold values from -160 to 160, as said below
- keys: bfloat16 [1024, 512], P('ctx'), may hold values from -7 to 7
- values: bfloat16 [1024, 512], P('ctx'), may hold values from -6 to 6
- positions: int32 [1024], P('ctx'), may hold values from 0 to 1023, as said below
- bounds: int32 [1024], P('ctx'), may hold values from 0 to 1023, as said below
- w_out: bfloat16 [8192, 4096], P('exp'), may hold values from -0.0625 to 0.0625
- residual: bfloat16 [1024, 4096], P(('ctx', 'exp')), may hold values from -60 to 60
- norm_gain: float32 [4096], replicated, may hold values from 0.1 to 1.9
- routes: int32 [1024, 8], P(('ctx', 'exp')), may hold values from 0 to 127, as said below
- gates: float32 [1024, 8], P(('ctx', 'exp')), may hold values from 0.1 to 1
- w_in: bfloat16 [4, 384, 4096], P('exp'), may hold values from -0.09375 to 0.09375
- w_back: bfloat16 [4, 192, 4096], P('exp'), may hold values from -1.75 to 1.75
Outputs:
- middle: bfloat16 [1024, 4096], P(('ctx', 'exp'))
- expert_out: bfloat16 [1024, 4096], P(('ctx', 'exp'))
Inputs may be any that keep to these rules, and one draw needn't show every extreme that they name: `queries`: rows scaled at most as far as the range. Each of 0 to 1023 appears once; a device's 128 tokens hold consecutive positions in order. bounds[i] is positions[i] or the last position of its frame of 256 positions (frames start at multiples of 256). `routes`: each row names 8 different experts, exactly one of them below 1; among the rows of one device, each expert below 1 is chosen by at most 32 rows and some one by exactly 32; for some index of ctx, one expert below 1 is chosen by 32 rows on every device of that index.
All inputs are finite; a program needn't handle non-finite values.
Results may differ from a plain program's by a relative error of at most 0.022.
Values may be sent and summed in bfloat16 or wider, within the bound.
No kernel may reach another device: no remote copies, remote signals or barrier semaphores. Data moves between devices by JAX's collectives and lax.ppermute only.
A program may use at most 64 MiB of HBM per device.

v0:
```python
import jax
import jax.numpy as jnp
from jax import lax
from jax.sharding import PartitionSpec as P

D = 4096
HEADS = 64
KV_HEADS = 4
HEAD_DIM = 128
HID_SPLIT = 4


def largest_divisor(row_count):
    candidate = min(row_count, 1024)
    while row_count % candidate != 0:
        candidate = candidate - 1
    return candidate


def apply_slice(row_block, coefficient, w_in, w_back):
    hidden_here = w_back.shape[1]
    flat_in = w_in.reshape(2 * hidden_here, D)
    projected = lax.dot_general(
        row_block, flat_in, (((1,), (1,)), ((), ())), preferred_element_type=jnp.float32
    )
    activated = jax.nn.silu(projected[:, :hidden_here]) * projected[:, hidden_here:]
    blended = (coefficient.astype(jnp.float32) * activated).astype(jnp.bfloat16)
    flat_back = w_back.reshape(hidden_here, D)
    return jnp.dot(blended, flat_back, preferred_element_type=jnp.float32).astype(jnp.bfloat16)


def per_device(
    queries,
    keys,
    values,
    positions,
    bounds,
    w_out,
    residual,
    norm_gain,
    routes,
    gates,
    w_in,
    w_back,
):
    tok_rows = queries.shape[0]
    head_cols = queries.shape[1]
    heads_here = head_cols // HEAD_DIM
    exp_count = lax.axis_size("exp")
    exp_rank = lax.axis_index("exp")
    kv_number = exp_rank * heads_here // (HEADS // KV_HEADS)
    key_head = lax.dynamic_slice_in_dim(keys, kv_number * HEAD_DIM, HEAD_DIM, 1)
    value_head = lax.dynamic_slice_in_dim(values, kv_number * HEAD_DIM, HEAD_DIM, 1)
    query_heads = queries.reshape(tok_rows, heads_here, HEAD_DIM).transpose(1, 0, 2)
    scale = HEAD_DIM ** (-0.5)
    reach_max = jnp.max(bounds)
    all_keys, all_values, all_places = (
        lax.all_gather(key_head, "ctx", axis=0, tiled=True),
        lax.all_gather(value_head, "ctx", axis=0, tiled=True),
        lax.all_gather(positions, "ctx", axis=0, tiled=True),
    )
    total_rows = all_keys.shape[0]
    tile_len = largest_divisor(total_rows)
    tile_count = total_rows // tile_len

    def process(state_in, key_rows, value_rows, place_rows):
        row_max, row_sum, running = state_in
        scores = (
            jnp.einsum("htd,nd->htn", query_heads, key_rows, preferred_element_type=jnp.float32)
            * scale
        )
        visible = (place_rows[None, :] <= bounds[:, None])[None, :, :]
        masked = jnp.where(visible, scores, -1e30)
        new_max = jnp.maximum(row_max, jnp.max(masked, axis=2))
        weights = jnp.exp(masked - new_max[..., None])
        rescale = jnp.exp(row_max - new_max)
        row_sum = row_sum * rescale + jnp.sum(weights, axis=2)
        running = running * rescale[..., None] + jnp.einsum(
            "htn,nd->htd",
            weights.astype(jnp.bfloat16),
            value_rows,
            preferred_element_type=jnp.float32,
        )
        return (new_max, row_sum, running)

    def one_tile(tile_number, state_now):
        first = tile_number * tile_len
        key_rows = lax.dynamic_slice_in_dim(all_keys, first, tile_len, 0)
        value_rows = lax.dynamic_slice_in_dim(all_values, first, tile_len, 0)
        place_rows = lax.dynamic_slice_in_dim(all_places, first, tile_len, 0)
        return lax.cond(
            jnp.min(place_rows) <= reach_max,
            lambda state_in: process(state_in, key_rows, value_rows, place_rows),
            lambda state_in: state_in,
            state_now,
        )

    start_state = (
        jnp.full((heads_here, tok_rows), -1e30, jnp.float32),
        jnp.zeros((heads_here, tok_rows), jnp.float32),
        jnp.zeros((heads_here, tok_rows, HEAD_DIM), jnp.float32),
    )
    row_max, row_sum, running = lax.fori_loop(0, tile_count, one_tile, start_state)
    attended = (running / row_sum[..., None]).astype(jnp.bfloat16)
    attended = attended.transpose(1, 0, 2).reshape(tok_rows, head_cols)
    attention_rows = lax.psum_scatter(
        jnp.dot(attended, w_out, preferred_element_type=jnp.float32).astype(jnp.bfloat16),
        "exp",
        scatter_dimension=0,
        tiled=True,
    ).astype(jnp.float32)
    middle = (residual.astype(jnp.float32) + attention_rows).astype(jnp.bfloat16)
    wide = middle.astype(jnp.float32)
    mean_square = jnp.mean(wide * wide, axis=1, keepdims=True)
    normed = (wide * lax.rsqrt(mean_square + 1e-06) * norm_gain[None, :]).astype(jnp.bfloat16)
    local_rows = residual.shape[0]
    shares = gates / jnp.sum(gates, axis=1, keepdims=True)
    slice_expert = jnp.arange(exp_count, dtype=jnp.int32) // HID_SPLIT
    hits = routes[:, :, None] == slice_expert[None, None, :]
    coefficient = jnp.sum(jnp.where(hits, shares[:, :, None], 0.0), axis=1).astype(jnp.bfloat16)
    owner_weights = coefficient.transpose(1, 0)[:, :, None]
    copies = jnp.broadcast_to(normed[None, :, :], (exp_count, local_rows, D))
    row_block = lax.all_to_all(copies, "exp", split_axis=0, concat_axis=0, tiled=True)
    weight_block = lax.all_to_all(owner_weights, "exp", split_axis=0, concat_axis=0, tiled=True)
    slot_count = row_block.shape[1]
    produced = apply_slice(
        row_block.reshape(exp_count * slot_count, D),
        weight_block.reshape(exp_count * slot_count, 1),
        w_in,
        w_back,
    )
    produced = produced.reshape(exp_count, slot_count, D)
    arrived = lax.all_to_all(produced, "exp", split_axis=0, concat_axis=0, tiled=True)
    expert_out = jnp.sum(arrived.astype(jnp.float32), axis=0).astype(jnp.bfloat16)
    return (middle, expert_out)


def solution(mesh):
    in_specs = (
        P("ctx", "exp"),
        P("ctx", None),
        P("ctx", None),
        P("ctx"),
        P("ctx"),
        P("exp", None),
        P(("ctx", "exp"), None),
        P(),
        P(("ctx", "exp"), None),
        P(("ctx", "exp"), None),
        P("exp", None, None),
        P("exp", None, None),
    )
    out_specs = (P(("ctx", "exp"), None), P(("ctx", "exp"), None))
    return jax.shard_map(
        per_device, mesh=mesh, in_specs=in_specs, out_specs=out_specs, check_vma=False
    )
```

profile of v0, /device:TPU:0, one launch (start us, length us, event | category | flops | bytes accessed | tf_op | source)
XLA Modules:
  0.0 168.9 jit_solution(5024576009381085851)
XLA Ops:
  7.2 10.6 %all-gather = s32[8,1,128]{2,1,0:T(1,128)S(1)} all-gather(s32[1,1,128]{2,1,0:T(1,128)} %bitcast.38), channel_id=1, replica_groups=mesh['ctx'=8,'exp'=4] {'ctx'}, dimensions={0}, use_global_device_ids=true | all-gather | bytes 4608 | tf_op jit(solution)/shard_map/all_gather | solution.py:60
  18.4 1.3 reduce_max.20
  21.0 2.0 %copy.27 = bf16[128,2048]{0,1:T(8,128)(2,1)} copy(bf16[128,2048]{1,0:T(8,128)(2,1)} %param.14) | data formatting | bytes 1048576 | tf_op args[0]
  23.8 9.2 %all_gather.10 = bf16[1024,128]{1,0:T(8,128)(2,1)S(1)} all-gather(bf16[128,128]{1,0:T(8,128)(2,1)S(1)} %constant_dynamic-slice_fusion.1), channel_id=1, replica_groups=mesh['ctx'=8,'exp'=4] {'ctx'}, dimensions={0}, use_global_device_ids=true | all-gather | bytes 294912 | tf_op jit(solution)/shard_map/all_gather | solution.py:58
  33.8 9.4 %all_gather.11 = bf16[1024,128]{1,0:T(8,128)(2,1)} all-gather(bf16[128,128]{1,0:T(8,128)(2,1)S(1)} %constant_dynamic-slice_fusion), channel_id=1, replica_groups=mesh['ctx'=8,'exp'=4] {'ctx'}, dimensions={0}, use_global_device_ids=true | all-gather | bytes 294912 | tf_op jit(solution)/shard_map/all_gather | solution.py:59
  43.2 1.1 broadcast_in_dim.63
  44.3 11.5 %conditional.1 = (f32[16,128]{1,0:T(8,128)S(1)}, f32[16,128,128]{1,2,0:T(8,128)}) conditional(s32[]{:T(128)} %convert_element_type.57, (f32[16,128]{1,0:T(8,128)S(1)}, f32[16,128,128]{2,1,0:T(8,128)}) %tuple.25, (s32[1024]{0:T(1024)S(1)}, s32[128]{0:T(128)}, bf16[16,128,128]{1,2,0:T(8,128)(2,1)}, bf16[1024,128]{1,0:T(8,128)(2,1)S(1)}, ...), branch_computations={%region_2.3_spmd, %region_3.6_spmd} | conditional | flops 1097472000 | bytes 36278856 | solution.py:91
  44.3 0.8 broadcast_compare_fusion
  45.1 2.7 %fusion = (f32[16,128]{1,0:T(8,128)S(1)}, f32[16,128,1024]{2,1,0:T(8,128)S(1)}) fusion(pred[128,1024]{1,0:T(8,128)(4,1)S(1)} %broadcast_compare_fusion, bf16[16,128,128]{1,2,0:T(8,128)(2,1)} %get-tuple-element.113, bf16[1024,128]{1,0:T(8,128)(2,1)S(1)} %get-tuple-element.88), kind=kOutput, calls=%fused_computation.2 | convolution fusion | flops 543160320 | bytes 9314304 | tf_op jit(solution)/shard_map/while/body/eval_jaxpr/cond/branch_1_fun/htd,nd->htn/dot_general | solution.py:69
  47.8 2.2 %fusion.2 = f32[16,128]{1,0:T(8,128)S(1)} fusion(f32[16,128,1024]{2,1,0:T(8,128)S(1)} %get-tuple-element.126, f32[16,128]{1,0:T(8,128)S(1)} %broadcast_maximum_fusion, pred[128,1024]{1,0:T(8,128)(4,1)S(1)} %broadcast_compare_fusion), kind=kLoop, calls=%fused_computation.4 | loop fusion | flops 8386560 | bytes 8536064 | tf_op jit(solution)/shard_map/while/body/eval_jaxpr/cond/branch_1_fun/reduce_sum | solution.py:77
  50.1 3.1 %fusion.6 = f32[16,128,128]{2,1,0:T(8,128)} fusion(f32[16,128,1024]{2,1,0:T(8,128)S(1)} %get-tuple-element.126, f32[16,128]{1,0:T(8,128)S(1)} %broadcast_maximum_fusion, pred[128,1024]{1,0:T(8,128)(4,1)S(1)} %broadcast_compare_fusion, f32[16,128,128]{2,1,0:T(8,128)S(1)} %copy-done.1, f32[16,128]{1,0:T(8,128)S(1)} %get-tuple-element.123, ...), kind=kOutput, calls=%fused_computation.7 | convolution fusion | flops 545783808 | bytes 10895360 | tf_op jit(solution)/shard_map/while/body/eval_jaxpr/cond/branch_1_fun/htn,nd->htd/dot_general | solution.py:78
  53.2 2.5 %copy.33 = f32[16,128,128]{1,2,0:T(8,128)} copy(f32[16,128,128]{2,1,0:T(8,128)} %fusion.6) | data formatting | bytes 2097152 | tf_op jit(solution)/shard_map/while/body/eval_jaxpr/cond | solution.py:91
  55.8 1.3 divide_convert_fusion
  57.2 9.2 %convolution_convert_fusion = bf16[128,4096]{1,0:T(8,128)(2,1)} fusion(bf16[128,2048]{0,1:T(8,128)(2,1)S(1)} %bitcast.34, bf16[2048,4096]{1,0:T(8,128)(2,1)} %param.19), kind=kOutput, calls=%fused_computation.17 | convolution fusion | flops 2148007936 | bytes 18350080 | tf_op jit(solution)/shard_map/dot_general | solution.py:107
  67.1 4.9 %all-to-all-start = ((bf16[4,32,1]{1,2,0:T(2,128)(2,1)}), bf16[4,32,1]{1,2,0:T(2,128)(2,1)S(1)}, u32[]{:S(2)}, u32[]{:S(2)}) async-start(bf16[4,32,1]{1,2,0:T(2,128)(2,1)} %copy.30), calls=%async_computation.1 | async-start | bytes 4096 | tf_op jit(solution)/shard_map/all_to_all | solution.py:124
  72.0 22.0 %reduce-scatter.2.cloned.1.call-done = bf16[32,4096]{1,0:T(8,128)(2,1)} async-done(((bf16[128,4096]{1,0:T(8,128)(2,1)}), bf16[32,4096]{1,0:T(8,128)(2,1)}) %reduce-scatter.2.cloned.1.call-update) | async-done | bytes 262160 | tf_op jit(solution)/shard_map/reduce_scatter | solution.py:106
  94.0 1.2 fusion.17
  96.0 1.1 broadcast_in_dim.67
  97.1 4.2 %all-to-all-start.1 = ((bf16[4,32,4096]{2,1,0:T(8,128)(2,1)}), bf16[4,32,4096]{2,1,0:T(8,128)(2,1)}, u32[]{:S(2)}, u32[]{:S(2)}) async-start(bf16[4,32,4096]{2,1,0:T(8,128)(2,1)} %broadcast_in_dim.67), calls=%async_computation.2 | async-start | bytes 2097152 | tf_op jit(solution)/shard_map/all_to_all | solution.py:123
  101.5 25.8 %all-to-all-done.1 = bf16[4,32,4096]{2,1,0:T(8,128)(2,1)} async-done(((bf16[4,32,4096]{2,1,0:T(8,128)(2,1)}), bf16[4,32,4096]{2,1,0:T(8,128)(2,1)}, u32[]{:S(2)}, u32[]{:S(2)}) %all-to-all-start.1) | async-done | bytes 1048608 | tf_op jit(solution)/shard_map/all_to_all | solution.py:123
  127.3 2.3 %fusion.14 = f32[128,384]{1,0:T(8,128)S(1)} fusion(bf16[128,4096]{1,0:T(8,128)(2,1)} %bitcast.10, bf16[1,384,4096]{2,1,0:T(8,128)(2,1)S(1)} %copy-done), kind=kOutput, calls=%fused_computation.19 | convolution fusion | flops 402653184 | bytes 4390912 | tf_op jit(solution)/shard_map/dot_general | solution.py:23
  129.6 1.9 %convolution_convert_fusion.1 = bf16[128,4096]{1,0:T(8,128)(2,1)S(1)} fusion(bf16[1,192,4096]{2,1,0:T(8,128)(2,1)} %param.25, f32[128,384]{1,0:T(8,128)S(1)} %fusion.14, f32[128]{0:T(128)S(1)} %reshape.94), kind=kOutput, calls=%fused_computation.18 | convolution fusion | flops 202022912 | bytes 2884096 | tf_op jit(solution)/shard_map/dot_general | solution.py:29
  131.5 28.4 %all_to_all.15 = bf16[4,32,4096]{2,1,0:T(8,128)(2,1)} all-to-all(bf16[4,32,4096]{2,1,0:T(8,128)(2,1)S(1)} %bitcast.33), channel_id=1, replica_groups=mesh['ctx'=8,'exp'=4] {'exp'}, dimensions={0} | all-to-all | bytes 2097152 | tf_op jit(solution)/shard_map/all_to_all | solution.py:133
  159.9 2.2 %reduce_sum.53 = bf16[32,4096]{1,0:T(8,128)(2,1)} reduce(bf16[4,32,4096]{2,1,0:T(8,128)(2,1)} %all_to_all.15, bf16[]{:T(256)} %constant.86.clone.1), dimensions={0}, to_apply=%region_10.11 | reduce | flops 393216 | bytes 1310722 | tf_op jit(solution)/shard_map/reduce_sum | solution.py:134
  (34 shorter events, 3.9 us)
Async XLA Ops:
  7.2 120.1 %copy-start = (bf16[1,384,4096]{2,1,0:T(8,128)(2,1)S(1)}, bf16[1,384,4096]{2,1,0:T(8,128)(2,1)}, u32[]{:S(2)}) copy-start(bf16[1,384,4096]{2,1,0:T(8,128)(2,1)} %param.24) | copy-start | bytes 9437188
  7.2 86.8 %reduce-scatter.2.cloned.1.call-start = ((), (), s32[]{:S(2)}) async-start(), calls=%async_computation.4 | async-start | bytes 1310720 | tf_op jit(solution)/shard_map/reduce_scatter | solution.py:106
  45.1 5.0 %copy-start.1 = (f32[16,128,128]{2,1,0:T(8,128)S(1)}, f32[16,128,128]{2,1,0:T(8,128)}, u32[]{:S(2)}) copy-start(f32[16,128,128]{2,1,0:T(8,128)} %get-tuple-element.89) | copy-start | bytes 3145732 | tf_op jit(solution)/shard_map/while/body/eval_jaxpr/cond
  45.1 5.0 %copy-start.3 = (bf16[1024,128]{1,0:T(8,128)(2,1)S(1)}, bf16[1024,128]{1,0:T(8,128)(2,1)}, u32[]{:S(2)}) copy-start(bf16[1024,128]{1,0:T(8,128)(2,1)} %get-tuple-element.90) | copy-start | bytes 786436 | tf_op jit(solution)/shard_map/while/body/eval_jaxpr/cond
  57.1 9.3 %copy-start.6 = (f32[32,8]{0,1:T(8,128)S(1)}, f32[32,8]{0,1:T(8,128)}, u32[]{:S(2)}) copy-start(f32[32,8]{0,1:T(8,128)} %param.23) | copy-start | bytes 3076
  57.1 9.3 %copy-start.7 = (s32[32,8]{0,1:T(8,128)S(1)}, s32[32,8]{0,1:T(8,128)}, u32[]{:S(2)}) copy-start(s32[32,8]{0,1:T(8,128)} %param.22) | copy-start | bytes 3076
  57.1 36.8 %copy-start.4 = (bf16[32,4096]{1,0:T(8,128)(2,1)S(1)}, bf16[32,4096]{1,0:T(8,128)(2,1)}, u32[]{:S(2)}) copy-start(bf16[32,4096]{1,0:T(8,128)(2,1)} %param.20) | copy-start | bytes 786436
  57.1 38.7 %copy-start.5 = (f32[4096]{0:T(1024)S(1)}, f32[4096]{0:T(1024)}, u32[]{:S(2)}) copy-start(f32[4096]{0:T(1024)} %param.21) | copy-start | bytes 49156
  67.1 28.9 %all-to-all-start = ((bf16[4,32,1]{1,2,0:T(2,128)(2,1)}), bf16[4,32,1]{1,2,0:T(2,128)(2,1)S(1)}, u32[]{:S(2)}, u32[]{:S(2)}) async-start(bf16[4,32,1]{1,2,0:T(2,128)(2,1)} %copy.30), calls=%async_computation.1 | async-start | bytes 4096 | tf_op jit(solution)/shard_map/all_to_all | solution.py:124
  95.1 0.7 copy-start.2
  97.1 30.1 %all-to-all-start.1 = ((bf16[4,32,4096]{2,1,0:T(8,128)(2,1)}), bf16[4,32,4096]{2,1,0:T(8,128)(2,1)}, u32[]{:S(2)}, u32[]{:S(2)}) async-start(bf16[4,32,4096]{2,1,0:T(8,128)(2,1)} %broadcast_in_dim.67), calls=%async_computation.2 | async-start | bytes 2097152 | tf_op jit(solution)/shard_map/all_to_all | solution.py:123
Sparse Core Ops, SparseCore 0:
  66.5 27.4 reduce-scatter.1
where the time goes:
time: 170 us; the launch traced here: 169 us
  blocking collectives  57.5 us (34%)
  waiting for transfers between devices  47.8 us (28%)
  matrix products  19.3 us (11%)
  between operations  15.5 us (9%)
  other arithmetic  9.85 us (6%)
  local copies, waits for them, and re-layouts  9.74 us (6%)
  starting transfers between devices  9.14 us (5%)
    all_to_all x1, blocking collectives, per_device(): lax.all_to_all(produced, 'exp', split_axis=0, concat_axis=0, tiled=True)  28.4 us
    all_to_all x1, waiting for transfers between devices, per_device(): lax.all_to_all(copies, 'exp', split_axis=0, concat_axis=0, tiled=True)  25.8 us
    reduce_scatter x1, waiting for transfers between devices, per_device(): lax.psum_scatter(jnp.dot(attended, w_out, preferred_element_type=jnp.floa...  22 us
    all_gather x1, blocking collectives, per_device(): lax.all_gather(positions, 'ctx', axis=0, tiled=True)  10.6 us
    all_gather x1, blocking collectives, per_device(): lax.all_gather(value_head, 'ctx', axis=0, tiled=True)  9.4 us
    dot_general x1, matrix products, per_device(): jnp.dot(attended, w_out, preferred_element_type=jnp.float32)  9.19 us
    all_gather x1, blocking collectives, per_device(): lax.all_gather(key_head, 'ctx', axis=0, tiled=True)  9.17 us
    all_to_all x1, starting transfers between devices, per_device(): lax.all_to_all(owner_weights, 'exp', split_axis=0, concat_axis=0, tiled=T...  4.87 us
  transfers between devices with their start and end apart: 3, of which 2 were waited for; matrix products, arithmetic and copies ran while one was open for 1% of the time, Pallas kernels for 0%

commit v1 on v0

--- a/solution.py
+++ b/solution.py
@@ -1,6 +1,10 @@
+import functools
+
 import jax
 import jax.numpy as jnp
 from jax import lax
+from jax.experimental import pallas as pl
+from jax.experimental.pallas import tpu as pltpu
 from jax.sharding import PartitionSpec as P
 
 D = 4096
@@ -8,6 +12,197 @@
 KV_HEADS = 4
 HEAD_DIM = 128
 HID_SPLIT = 4
+STACK = 4
+COL_CHUNKS = 4
+PAD_ROWS = 16
+LOG2E = 1.4426950408889634
+VMEM = pl.BlockSpec(memory_space=pltpu.VMEM)
+
+
+def exchange(value, axis, offset, size):
+    return lax.ppermute(value, axis, [(i, i ^ offset) for i in range(size)])
+
+
+def attend_kernel(
+    block_count,
+    rank_ref,
+    q_ref,
+    bound_ref,
+    resid_ref,
+    *refs,
+):
+    payloads = refs[:block_count]
+    w_hbm = refs[block_count]
+    outs = refs[block_count + 1 : block_count + 1 + COL_CHUNKS]
+    w_buf, k_buf, v_buf, bias, attended, acc, sems = refs[block_count + 1 + COL_CHUNKS :]
+    tok = q_ref.shape[0]
+    heads = q_ref.shape[1] // HEAD_DIM
+    cols = D // COL_CHUNKS
+    copies = []
+    for chunk in range(COL_CHUNKS):
+        copy = pltpu.make_async_copy(
+            w_hbm.at[:, pl.ds(chunk * cols, cols)], w_buf.at[chunk], sems.at[chunk]
+        )
+        copy.start()
+        copies.append(copy)
+    bound = bound_ref[...]
+    lane = lax.broadcasted_iota(jnp.int32, (1, tok), 1).astype(jnp.float32)
+    ones = jnp.ones((tok, HEAD_DIM), jnp.bfloat16)
+    for b in range(block_count):
+        rows = slice(b * tok, (b + 1) * tok)
+        k_buf[rows, :] = payloads[b][:tok, :HEAD_DIM]
+        v_buf[rows, :HEAD_DIM] = payloads[b][:tok, HEAD_DIM:]
+        v_buf[rows, HEAD_DIM:] = ones
+        start = payloads[b][tok : tok + PAD_ROWS, :HEAD_DIM].astype(jnp.float32)[:1]
+        place = start * tok + lane
+        bias[:, rows] = jnp.where(place <= bound, 0.0, -1e30)
+    factor = HEAD_DIM ** (-0.5) * LOG2E
+
+    def some_heads(step, carry):
+        base = step * STACK * HEAD_DIM
+        parts = []
+        for j in range(STACK):
+            start = pl.multiple_of(base + j * HEAD_DIM, HEAD_DIM)
+            parts.append(q_ref[:, pl.ds(start, HEAD_DIM)])
+        stacked = jnp.concatenate(parts, axis=0)
+        scores = lax.dot_general(
+            stacked, k_buf[...], (((1,), (1,)), ((), ())), preferred_element_type=jnp.float32
+        )
+        scores = scores.reshape(STACK, tok, -1) * factor + bias[...][None]
+        row_max = jnp.max(scores, axis=2, keepdims=True)
+        weights = jnp.exp2(scores - row_max).astype(jnp.bfloat16)
+        summed = jnp.dot(
+            weights.reshape(STACK * tok, -1), v_buf[...], preferred_element_type=jnp.float32
+        )
+        result = (summed[:, :HEAD_DIM] / summed[:, HEAD_DIM:]).astype(jnp.bfloat16)
+        for j in range(STACK):
+            start = pl.multiple_of(base + j * HEAD_DIM, HEAD_DIM)
+            attended[:, pl.ds(start, HEAD_DIM)] = result[j * tok : (j + 1) * tok]
+        return carry
+
+    lax.fori_loop(0, heads // STACK, some_heads, 0)
+    home = resid_ref.shape[0]
+    first = pl.multiple_of(rank_ref[0] * home, home)
+    for chunk in range(COL_CHUNKS):
+        copies[chunk].wait()
+        acc[...] = jnp.dot(attended[...], w_buf[chunk], preferred_element_type=jnp.float32)
+        own = resid_ref[:, chunk * cols : (chunk + 1) * cols].astype(jnp.float32)
+        acc[pl.ds(first, home), :] += own
+        outs[chunk][...] = acc[...].astype(jnp.bfloat16)
+
+
+def attend_project(rank, queries, bounds, residual, payloads, w_out):
+    tok, width = queries.shape
+    count = len(payloads)
+    cols = D // COL_CHUNKS
+    keys_in_all = tok * count
+    return pl.pallas_call(
+        functools.partial(attend_kernel, count),
+        out_shape=[jax.ShapeDtypeStruct((tok, cols), jnp.bfloat16)] * COL_CHUNKS,
+        in_specs=[pl.BlockSpec(memory_space=pltpu.SMEM)]
+        + [VMEM] * (3 + count)
+        + [pl.BlockSpec(memory_space=pl.ANY)],
+        out_specs=[VMEM] * COL_CHUNKS,
+        scratch_shapes=[
+            pltpu.VMEM((COL_CHUNKS, width, cols), jnp.bfloat16),
+            pltpu.VMEM((keys_in_all, HEAD_DIM), jnp.bfloat16),
+            pltpu.VMEM((keys_in_all, 2 * HEAD_DIM), jnp.bfloat16),
+            pltpu.VMEM((tok, keys_in_all), jnp.float32),
+            pltpu.VMEM((tok, width), jnp.bfloat16),
+            pltpu.VMEM((tok, cols), jnp.float32),
+            pltpu.SemaphoreType.DMA((COL_CHUNKS,)),
+        ],
+        compiler_params=pltpu.CompilerParams(vmem_limit_bytes=44 * 1024 * 1024),
+        cost_estimate=pl.CostEstimate(
+            flops=2 * tok * width * (2 * keys_in_all + D),
+            bytes_accessed=2 * width * D,
+            transcendentals=tok * width // HEAD_DIM * keys_in_all,
+        ),
+        name="attend_project",
+    )(rank, queries, bounds, residual, *payloads, w_out)
+
+
+def own_heads(queries, keys, values):
+    heads_here = queries.shape[1] // HEAD_DIM
+    kv_number = lax.axis_index("exp") * heads_here // (HEADS // KV_HEADS)
+    key_head = lax.dynamic_slice_in_dim(keys, kv_number * HEAD_DIM, HEAD_DIM, 1)
+    value_head = lax.dynamic_slice_in_dim(values, kv_number * HEAD_DIM, HEAD_DIM, 1)
+    return key_head, value_head
+
+
+def line_device(
+    queries,
+    keys,
+    values,
+    positions,
+    bounds,
+    w_out,
+    residual,
+    norm_gain,
+    routes,
+    gates,
+    w_in,
+    w_back,
+):
+    tok = queries.shape[0]
+    home = residual.shape[0]
+    hidden = w_back.shape[1]
+    ctx_count = lax.axis_size("ctx")
+    exp_count = lax.axis_size("exp")
+    rank = lax.axis_index("exp")
+    key_head, value_head = own_heads(queries, keys, values)
+    block = (positions[0] // tok).astype(jnp.bfloat16)
+    pair = jnp.concatenate([key_head, value_head], axis=1)
+    payload = jnp.concatenate(
+        [pair, jnp.full((PAD_ROWS, 2 * HEAD_DIM), block, jnp.bfloat16)], axis=0
+    )
+    payloads = [payload] + [exchange(payload, "ctx", r, ctx_count) for r in range(1, ctx_count)]
+    parts = attend_project(
+        rank.astype(jnp.int32).reshape(1),
+        queries,
+        bounds.astype(jnp.float32).reshape(tok, 1),
+        residual,
+        payloads,
+        w_out,
+    )
+    at_end = (rank == 0) | (rank == exp_count - 1)
+    cols = D // COL_CHUNKS
+    flat_in = w_in.reshape(2 * hidden, D)
+    total_square = jnp.zeros((tok, 1), jnp.float32)
+    projected = jnp.zeros((tok, 2 * hidden), jnp.float32)
+    middles = []
+    for chunk in range(COL_CHUNKS):
+        inward = lax.ppermute(parts[chunk], "exp", [(0, 1), (3, 2)])
+        near = parts[chunk] + inward
+        across = lax.ppermute(near, "exp", [(1, 2), (2, 1)])
+        total = near + across
+        outward = lax.ppermute(total, "exp", [(1, 0), (2, 3)])
+        middle = jnp.where(at_end, outward, total)
+        wide = middle.astype(jnp.float32)
+        total_square = total_square + jnp.sum(wide * wide, axis=1, keepdims=True)
+        span = slice(chunk * cols, (chunk + 1) * cols)
+        gained = (wide * norm_gain[None, span]).astype(jnp.bfloat16)
+        projected = projected + lax.dot_general(
+            gained,
+            flat_in[:, span],
+            (((1,), (1,)), ((), ())),
+            preferred_element_type=jnp.float32,
+        )
+        middles.append(lax.dynamic_slice_in_dim(middle, rank * home, home, 0))
+    middle_out = jnp.concatenate(middles, axis=1)
+    projected = projected * lax.rsqrt(total_square / D + 1e-06)
+    activated = (jax.nn.silu(projected[:, :hidden]) * projected[:, hidden:]).astype(jnp.bfloat16)
+    share = jnp.dot(
+        activated, w_back.reshape(hidden, D), preferred_element_type=jnp.float32
+    ).astype(jnp.bfloat16)
+    gathered = lax.dynamic_slice_in_dim(share, rank * home, home, 0).astype(jnp.float32)
+    for offset in range(1, exp_count):
+        leaving = lax.dynamic_slice_in_dim(share, (rank ^ offset) * home, home, 0)
+        gathered = gathered + exchange(leaving, "exp", offset, exp_count).astype(jnp.float32)
+    shares = gates / jnp.sum(gates, axis=1, keepdims=True)
+    coefficient = jnp.sum(jnp.where(routes == 0, shares, 0.0), axis=1, keepdims=True)
+    coefficient = coefficient.astype(jnp.bfloat16).astype(jnp.float32)
+    return (middle_out, (gathered * coefficient).astype(jnp.bfloat16))
 
 
 def largest_divisor(row_count):
@@ -29,7 +224,7 @@
     return jnp.dot(blended, flat_back, preferred_element_type=jnp.float32).astype(jnp.bfloat16)
 
 
-def per_device(
+def wide_device(
     queries,
     keys,
     values,
@@ -47,10 +242,7 @@
     head_cols = queries.shape[1]
     heads_here = head_cols // HEAD_DIM
     exp_count = lax.axis_size("exp")
-    exp_rank = lax.axis_index("exp")
-    kv_number = exp_rank * heads_here // (HEADS // KV_HEADS)
-    key_head = lax.dynamic_slice_in_dim(keys, kv_number * HEAD_DIM, HEAD_DIM, 1)
-    value_head = lax.dynamic_slice_in_dim(values, kv_number * HEAD_DIM, HEAD_DIM, 1)
+    key_head, value_head = own_heads(queries, keys, values)
     query_heads = queries.reshape(tok_rows, heads_here, HEAD_DIM).transpose(1, 0, 2)
     scale = HEAD_DIM ** (-0.5)
     reach_max = jnp.max(bounds)
@@ -151,6 +343,11 @@
         P("exp", None, None),
     )
     out_specs = (P(("ctx", "exp"), None), P(("ctx", "exp"), None))
+    one_line = mesh.shape["exp"] == HID_SPLIT and mesh.shape["ctx"] == 8
     return jax.shard_map(
-        per_device, mesh=mesh, in_specs=in_specs, out_specs=out_specs, check_vma=False
-    )
+        line_device if one_line else wide_device,
+        mesh=mesh,
+        in_specs=in_specs,
+        out_specs=out_specs,
+        check_vma=False,
+    )

time: 170 us -> 112 us (0.66)
  blocking collectives: 57.5 us -> 0 us
  starting transfers between devices: 9.14 us -> 29.3 us
  matrix products: 19.3 us -> 1.97 us
  between operations: 15.5 us -> 3.71 us
  Pallas kernels: 0 us -> 8.87 us
  waiting for transfers between devices: 47.8 us -> 53.6 us
  local copies, waits for them, and re-layouts: 9.74 us -> 4.37 us
    ppermute x0 -> x22, waiting for transfers between devices: none -> 53.6 us  [the longest x10 21.8 us: exchange(): return lax.ppermute(value, axis, [(i, i ^ offset) for i in range(size)])]
    ppermute x0 -> x22, starting transfers between devices: none -> 29.3 us  [the longest x10 12.4 us: exchange(): return lax.ppermute(value, axis, [(i, i ^ offset) for i in range(size)])]
    all_gather x3 -> x0, blocking collectives: 29.1 us -> none  [the longest x1 10.6 us: per_device(): lax.all_gather(positions, 'ctx', axis=0, tiled=True)]
    all_to_all x1 -> x0, blocking collectives: 28.4 us -> none  [per_device(): lax.all_to_all(produced, 'exp', split_axis=0, concat_axis=0, tiled=True)]
    all_to_all x2 -> x0, waiting for transfers between devices: 25.8 us -> none  [the longest x1 25.8 us: per_device(): lax.all_to_all(copies, 'exp', split_axis=0, concat_axis=0, tiled=True)]
    reduce_scatter x1 -> x0, waiting for transfers between devices: 22 us -> none  [per_device(): lax.psum_scatter(jnp.dot(attended, w_out, preferred_element_type=jnp.floa...]
    dot_general x5, matrix products: 19.3 us -> 1.97 us  [the longest x4 1.49 us: line_device(): lax.dot_general(gained, flat_in[:, span], (((1,), (1,)), ((), ())), prefe...]
    all_to_all x2 -> x0, starting transfers between devices: 9.11 us -> none  [the longest x1 4.87 us: per_device(): lax.all_to_all(owner_weights, 'exp', split_axis=0, concat_axis=0, tiled=T...]
  transfers between devices with their start and end apart: 3 -> 22, of which waited for: 2 -> 12; matrix products, arithmetic and copies ran while one was open for 1% -> 9% of each run, Pallas kernels for 0% -> 0%
where the time goes in v1:
time: 112 us; the launch traced here: 111 us
  waiting for transfers between devices  53.6 us (48%)
  starting transfers between devices  29.3 us (26%)
  other arithmetic  9.12 us (8%)
  Pallas kernels  8.87 us (8%)
  local copies, waits for them, and re-layouts  4.37 us (4%)
  between operations  3.71 us (3%)
  matrix products  1.97 us (2%)
    ppermute x10, waiting for transfers between devices, exchange(): return lax.ppermute(value, axis, [(i, i ^ offset) for i in range(size)])  21.8 us
    ppermute x4, waiting for transfers between devices, line_device(): outward = lax.ppermute(total, 'exp', [(1, 0), (2, 3)])  17.2 us
    ppermute x4, waiting for transfers between devices, line_device(): inward = lax.ppermute(parts[chunk], 'exp', [(0, 1), (3, 2)])  14.5 us
    ppermute x10, starting transfers between devices, exchange(): return lax.ppermute(value, axis, [(i, i ^ offset) for i in range(size)])  12.4 us
    pallas_call x1, Pallas kernels, attend_project(): pl.pallas_call(functools.partial(attend_kernel, count), out_shape=[jax.Sh...  8.87 us
    ppermute x4, starting transfers between devices, line_device(): inward = lax.ppermute(parts[chunk], 'exp', [(0, 1), (3, 2)])  7.41 us
    ppermute x4, starting transfers between devices, line_device(): outward = lax.ppermute(total, 'exp', [(1, 0), (2, 3)])  5.43 us
    ppermute x4, starting transfers between devices, line_device(): across = lax.ppermute(near, 'exp', [(1, 2), (2, 1)])  4.08 us
  transfers between devices with their start and end apart: 22, of which 12 were waited for; matrix products, arithmetic and copies ran while one was open for 9% of the time, Pallas kernels for 0%

profile of v1, /device:TPU:0, one launch (start us, length us, event | category | flops | bytes accessed | tf_op | source)
XLA Modules:
  0.0 110.9 jit_solution(6923535760178711704)
XLA Ops:
  4.7 2.6 %collective-permute-start.1 = (bf16[144,256]{1,0:T(8,128)(2,1)S(1)}, bf16[144,256]{1,0:T(8,128)(2,1)S(1)}, u32[]{:S(2)}, u32[]{:S(2)}) collective-permute-start(bf16[144,256]{1,0:T(8,128)(2,1)S(1)} %fusion.26.refs_0_), channel_id=1, source_target_pairs={{0,8},{4,12},{8,0},{12,4},{16,24},{20,28},{24,16},{28,20},{1,9},{5... | collective-permute-start | bytes 221192 | tf_op jit(solution)/shard_map/ppermute | solution.py:23
  7.3 1.8 %collective-permute-start.3 = (bf16[144,256]{1,0:T(8,128)(2,1)S(1)}, bf16[144,256]{1,0:T(8,128)(2,1)S(1)}, u32[]{:S(2)}, u32[]{:S(2)}) collective-permute-start(bf16[144,256]{1,0:T(8,128)(2,1)S(1)} %fusion.26.refs_0_), channel_id=1, source_target_pairs={{0,16},{4,20},{8,24},{12,28},{16,0},{20,4},{24,8},{28,12},{1,17},{... | collective-permute-start | bytes 221192 | tf_op jit(solution)/shard_map/ppermute | solution.py:23
  9.1 2.6 %collective-permute-start.5 = (bf16[144,256]{1,0:T(8,128)(2,1)S(1)}, bf16[144,256]{1,0:T(8,128)(2,1)S(1)}, u32[]{:S(2)}, u32[]{:S(2)}) collective-permute-start(bf16[144,256]{1,0:T(8,128)(2,1)S(1)} %fusion.26.refs_0_), channel_id=1, source_target_pairs={{0,24},{4,28},{8,16},{12,20},{16,8},{20,12},{24,0},{28,4},{1,25},{... | collective-permute-start | bytes 221192 | tf_op jit(solution)/shard_map/ppermute | solution.py:23
  12.9 3.0 %collective-permute-done.4.refs_5_ = bf16[144,256]{1,0:T(8,128)(2,1)S(1)} collective-permute-done((bf16[144,256]{1,0:T(8,128)(2,1)S(1)}, bf16[144,256]{1,0:T(8,128)(2,1)S(1)}, u32[]{:S(2)}, u32[]{:S(2)}) %collective-permute-start.4) | collective-permute-done | bytes 73760 | tf_op jit(solution)/shard_map/ppermute | solution.py:23
  18.8 8.9 %attend_project.1 = (bf16[128,1024]{1,0:T(8,128)(2,1)S(1)}, bf16[128,1024]{1,0:T(8,128)(2,1)S(1)}, bf16[128,1024]{1,0:T(8,128)(2,1)S(1)}, bf16[128,1024]{1,0:T(8,128)(2,1)S(1)}) custom-call(s32[1]{0:T(128)} %bitcast.rank_ref, bf16[128,2048]{1,0:T(8,128)(2,1)S(1)} %copy-done.1, f32[128,1]{1,0:T(8,128)S(1)} %copy.14.bound_ref, bf16[32,4096]{1,0:T(8,128)(2,1)S(1)} %copy-done.2, ...), custom_call_target="tpu_custom_call" | custom-call | flops 3221225472 | bytes 16777216 | tf_op jit(solution)/shard_map/attend_project/pallas_call | solution.py:99
  27.7 3.5 %collective-permute-start.16 = (bf16[128,1024]{1,0:T(8,128)(2,1)S(1)}, bf16[128,1024]{1,0:T(8,128)(2,1)S(1)}, u32[]{:S(2)}, u32[]{:S(2)}) collective-permute-start(bf16[128,1024]{1,0:T(8,128)(2,1)S(1)} %get-tuple-element.9), channel_id=1, source_target_pairs={{0,1},{3,2},{4,5},{7,6},{8,9},{11,10},{12,13},{15,14},{16,17},{19,... | collective-permute-start | bytes 786440 | tf_op jit(solution)/shard_map/ppermute | solution.py:175
  31.2 1.3 %collective-permute-start.13 = (bf16[128,1024]{1,0:T(8,128)(2,1)S(1)}, bf16[128,1024]{1,0:T(8,128)(2,1)S(1)}, u32[]{:S(2)}, u32[]{:S(2)}) collective-permute-start(bf16[128,1024]{1,0:T(8,128)(2,1)S(1)} %get-tuple-element.8), channel_id=1, source_target_pairs={{0,1},{3,2},{4,5},{7,6},{8,9},{11,10},{12,13},{15,14},{16,17},{19,... | collective-permute-start | bytes 786440 | tf_op jit(solution)/shard_map/ppermute | solution.py:175
  32.5 1.3 %collective-permute-start.10 = (bf16[128,1024]{1,0:T(8,128)(2,1)S(1)}, bf16[128,1024]{1,0:T(8,128)(2,1)S(1)}, u32[]{:S(2)}, u32[]{:S(2)}) collective-permute-start(bf16[128,1024]{1,0:T(8,128)(2,1)S(1)} %get-tuple-element.7), channel_id=1, source_target_pairs={{0,1},{3,2},{4,5},{7,6},{8,9},{11,10},{12,13},{15,14},{16,17},{19,... | collective-permute-start | bytes 786440 | tf_op jit(solution)/shard_map/ppermute | solution.py:175
  35.2 2.7 %collective-permute-done.16 = bf16[128,1024]{1,0:T(8,128)(2,1)S(1)} collective-permute-done((bf16[128,1024]{1,0:T(8,128)(2,1)S(1)}, bf16[128,1024]{1,0:T(8,128)(2,1)S(1)}, u32[]{:S(2)}, u32[]{:S(2)}) %collective-permute-start.16) | collective-permute-done | bytes 262176 | tf_op jit(solution)/shard_map/ppermute | solution.py:175
  37.9 1.4 %collective-permute-start.17 = (bf16[128,1024]{1,0:T(8,128)(2,1)S(1)}, bf16[128,1024]{1,0:T(8,128)(2,1)}, u32[]{:S(2)}, u32[]{:S(2)}) collective-permute-start(bf16[128,1024]{1,0:T(8,128)(2,1)S(1)} %add.113), channel_id=1, source_target_pairs={{1,2},{2,1},{5,6},{6,5},{9,10},{10,9},{13,14},{14,13},{17,18},{18,... | collective-permute-start | bytes 786440 | tf_op jit(solution)/shard_map/ppermute | solution.py:177
  39.3 4.2 %collective-permute-done.13 = bf16[128,1024]{1,0:T(8,128)(2,1)S(1)} collective-permute-done((bf16[128,1024]{1,0:T(8,128)(2,1)S(1)}, bf16[128,1024]{1,0:T(8,128)(2,1)S(1)}, u32[]{:S(2)}, u32[]{:S(2)}) %collective-permute-start.13) | collective-permute-done | bytes 262176 | tf_op jit(solution)/shard_map/ppermute | solution.py:175
  43.6 1.4 %collective-permute-start.14 = (bf16[128,1024]{1,0:T(8,128)(2,1)S(1)}, bf16[128,1024]{1,0:T(8,128)(2,1)}, u32[]{:S(2)}, u32[]{:S(2)}) collective-permute-start(bf16[128,1024]{1,0:T(8,128)(2,1)S(1)} %add.111), channel_id=1, source_target_pairs={{1,2},{2,1},{5,6},{6,5},{9,10},{10,9},{13,14},{14,13},{17,18},{18,... | collective-permute-start | bytes 786440 | tf_op jit(solution)/shard_map/ppermute | solution.py:177
  45.5 3.6 %collective-permute-done.10 = bf16[128,1024]{1,0:T(8,128)(2,1)S(1)} collective-permute-done((bf16[128,1024]{1,0:T(8,128)(2,1)S(1)}, bf16[128,1024]{1,0:T(8,128)(2,1)S(1)}, u32[]{:S(2)}, u32[]{:S(2)}) %collective-permute-start.10) | collective-permute-done | bytes 262176 | tf_op jit(solution)/shard_map/ppermute | solution.py:175
  49.9 4.1 %collective-permute-done.7 = bf16[128,1024]{1,0:T(8,128)(2,1)S(1)} collective-permute-done((bf16[128,1024]{1,0:T(8,128)(2,1)S(1)}, bf16[128,1024]{1,0:T(8,128)(2,1)S(1)}, u32[]{:S(2)}, u32[]{:S(2)}) %collective-permute-start.7) | collective-permute-done | bytes 262176 | tf_op jit(solution)/shard_map/ppermute | solution.py:175
  57.0 1.3 %fusion.30 = (f32[1024]{0:T(1024)}, f32[1024]{0:T(1024)}, f32[1024]{0:T(1024)S(1)}, f32[1024]{0:T(1024)S(1)}) fusion(f32[4096]{0:T(1024)} %param.19), kind=kLoop, calls=%fused_computation.58 | loop fusion | bytes 32768 | tf_op jit(solution)/shard_map/slice | solution.py:184
  62.0 1.6 %collective-permute-start.12 = (bf16[128,1024]{1,0:T(8,128)(2,1)S(1)}, bf16[128,1024]{1,0:T(8,128)(2,1)S(1)}, u32[]{:S(2)}, u32[]{:S(2)}) collective-permute-start(bf16[128,1024]{1,0:T(8,128)(2,1)S(1)} %add.110), channel_id=1, source_target_pairs={{1,0},{2,3},{5,4},{6,7},{9,8},{10,11},{13,12},{14,15},{17,16},{18,... | collective-permute-start | bytes 786440 | tf_op jit(solution)/shard_map/ppermute | solution.py:179
  65.0 4.1 %collective-permute-done.18 = bf16[128,1024]{1,0:T(8,128)(2,1)} collective-permute-done((bf16[128,1024]{1,0:T(8,128)(2,1)S(1)}, bf16[128,1024]{1,0:T(8,128)(2,1)}, u32[]{:S(2)}, u32[]{:S(2)}) %collective-permute-start.18) | collective-permute-done | bytes 262176 | tf_op jit(solution)/shard_map/ppermute | solution.py:179
  70.2 4.5 %collective-permute-done.15 = bf16[128,1024]{1,0:T(8,128)(2,1)} collective-permute-done((bf16[128,1024]{1,0:T(8,128)(2,1)S(1)}, bf16[128,1024]{1,0:T(8,128)(2,1)}, u32[]{:S(2)}, u32[]{:S(2)}) %collective-permute-start.15) | collective-permute-done | bytes 262176 | tf_op jit(solution)/shard_map/ppermute | solution.py:179
  75.9 4.4 %collective-permute-done.12 = bf16[128,1024]{1,0:T(8,128)(2,1)S(1)} collective-permute-done((bf16[128,1024]{1,0:T(8,128)(2,1)S(1)}, bf16[128,1024]{1,0:T(8,128)(2,1)S(1)}, u32[]{:S(2)}, u32[]{:S(2)}) %collective-permute-start.12) | collective-permute-done | bytes 262176 | tf_op jit(solution)/shard_map/ppermute | solution.py:179
  80.5 4.2 %collective-permute-done.9 = bf16[128,1024]{1,0:T(8,128)(2,1)S(1)} collective-permute-done((bf16[128,1024]{1,0:T(8,128)(2,1)S(1)}, bf16[128,1024]{1,0:T(8,128)(2,1)S(1)}, u32[]{:S(2)}, u32[]{:S(2)}) %collective-permute-start.9) | collective-permute-done | bytes 262176 | tf_op jit(solution)/shard_map/ppermute | solution.py:179
  87.0 1.4 %collective-permute-start.21 = (bf16[32,4096]{1,0:T(8,128)(2,1)S(1)}, bf16[32,4096]{1,0:T(8,128)(2,1)S(1)}, u32[]{:S(2)}, u32[]{:S(2)}) collective-permute-start(bf16[32,4096]{1,0:T(8,128)(2,1)S(1)} %get-tuple-element.19), channel_id=1, source_target_pairs={{0,3},{1,2},{2,1},{3,0},{4,7},{5,6},{6,5},{7,4},{8,11},{9,10},{10,... | collective-permute-start | bytes 786440 | tf_op jit(solution)/shard_map/ppermute | solution.py:23
  88.4 3.0 %collective-permute-start.19 = (bf16[32,4096]{1,0:T(8,128)(2,1)S(1)}, bf16[32,4096]{1,0:T(8,128)(2,1)S(1)}, u32[]{:S(2)}, u32[]{:S(2)}) collective-permute-start(bf16[32,4096]{1,0:T(8,128)(2,1)S(1)} %get-tuple-element.18), channel_id=1, source_target_pairs={{0,1},{1,0},{2,3},{3,2},{4,5},{5,4},{6,7},{7,6},{8,9},{9,8},{10,11... | collective-permute-start | bytes 786440 | tf_op jit(solution)/shard_map/ppermute | solution.py:23
  92.2 6.0 %collective-permute-done.21 = bf16[32,4096]{1,0:T(8,128)(2,1)S(1)} collective-permute-done((bf16[32,4096]{1,0:T(8,128)(2,1)S(1)}, bf16[32,4096]{1,0:T(8,128)(2,1)S(1)}, u32[]{:S(2)}, u32[]{:S(2)}) %collective-permute-start.21) | collective-permute-done | bytes 262176 | tf_op jit(solution)/shard_map/ppermute | solution.py:23
  98.2 11.8 %collective-permute-done.20 = bf16[32,4096]{1,0:T(8,128)(2,1)S(1)} collective-permute-done((bf16[32,4096]{1,0:T(8,128)(2,1)S(1)}, bf16[32,4096]{1,0:T(8,128)(2,1)S(1)}, u32[]{:S(2)}, u32[]{:S(2)}) %collective-permute-start.20) | collective-permute-done | bytes 262176 | tf_op jit(solution)/shard_map/ppermute | solution.py:23
  (72 shorter events, 22.6 us)
Async XLA Ops:
  0.6 85.8 %copy-start = (bf16[1,192,4096]{2,1,0:T(8,128)(2,1)S(1)}, bf16[1,192,4096]{2,1,0:T(8,128)(2,1)}, u32[]{:S(2)}) copy-start(bf16[1,192,4096]{2,1,0:T(8,128)(2,1)} %param.23) | copy-start | bytes 4718596
  4.2 4.9 %collective-permute-start = (bf16[144,256]{1,0:T(8,128)(2,1)S(1)}, bf16[144,256]{1,0:T(8,128)(2,1)S(1)}, u32[]{:S(2)}, u32[]{:S(2)}) collective-permute-start(bf16[144,256]{1,0:T(8,128)(2,1)S(1)} %fusion.26.refs_0_), channel_id=1, source_target_pairs={{0,4},{4,0},{8,12},{12,8},{16,20},{20,16},{24,28},{28,24},{1,5},{5... | collective-permute-start | bytes 221192 | tf_op jit(solution)/shard_map/ppermute | solution.py:23
  4.7 7.0 %collective-permute-start.1 = (bf16[144,256]{1,0:T(8,128)(2,1)S(1)}, bf16[144,256]{1,0:T(8,128)(2,1)S(1)}, u32[]{:S(2)}, u32[]{:S(2)}) collective-permute-start(bf16[144,256]{1,0:T(8,128)(2,1)S(1)} %fusion.26.refs_0_), channel_id=1, source_target_pairs={{0,8},{4,12},{8,0},{12,4},{16,24},{20,28},{24,16},{28,20},{1,9},{5... | collective-permute-start | bytes 221192 | tf_op jit(solution)/shard_map/ppermute | solution.py:23
  7.3 5.6 %collective-permute-start.2 = (bf16[144,256]{1,0:T(8,128)(2,1)S(1)}, bf16[144,256]{1,0:T(8,128)(2,1)S(1)}, u32[]{:S(2)}, u32[]{:S(2)}) collective-permute-start(bf16[144,256]{1,0:T(8,128)(2,1)S(1)} %fusion.26.refs_0_), channel_id=1, source_target_pairs={{0,12},{4,8},{8,4},{12,0},{16,28},{20,24},{24,20},{28,16},{1,13},{... | collective-permute-start | bytes 221192 | tf_op jit(solution)/shard_map/ppermute | solution.py:23
  7.3 5.5 %collective-permute-start.3 = (bf16[144,256]{1,0:T(8,128)(2,1)S(1)}, bf16[144,256]{1,0:T(8,128)(2,1)S(1)}, u32[]{:S(2)}, u32[]{:S(2)}) collective-permute-start(bf16[144,256]{1,0:T(8,128)(2,1)S(1)} %fusion.26.refs_0_), channel_id=1, source_target_pairs={{0,16},{4,20},{8,24},{12,28},{16,0},{20,4},{24,8},{28,12},{1,17},{... | collective-permute-start | bytes 221192 | tf_op jit(solution)/shard_map/ppermute | solution.py:23
  9.1 6.8 %collective-permute-start.4 = (bf16[144,256]{1,0:T(8,128)(2,1)S(1)}, bf16[144,256]{1,0:T(8,128)(2,1)S(1)}, u32[]{:S(2)}, u32[]{:S(2)}) collective-permute-start(bf16[144,256]{1,0:T(8,128)(2,1)S(1)} %fusion.26.refs_0_), channel_id=1, source_target_pairs={{0,20},{4,16},{8,28},{12,24},{16,4},{20,0},{24,12},{28,8},{1,21},{... | collective-permute-start | bytes 221192 | tf_op jit(solution)/shard_map/ppermute | solution.py:23
  9.1 6.8 %collective-permute-start.5 = (bf16[144,256]{1,0:T(8,128)(2,1)S(1)}, bf16[144,256]{1,0:T(8,128)(2,1)S(1)}, u32[]{:S(2)}, u32[]{:S(2)}) collective-permute-start(bf16[144,256]{1,0:T(8,128)(2,1)S(1)} %fusion.26.refs_0_), channel_id=1, source_target_pairs={{0,24},{4,28},{8,16},{12,20},{16,8},{20,12},{24,0},{28,4},{1,25},{... | collective-permute-start | bytes 221192 | tf_op jit(solution)/shard_map/ppermute | solution.py:23
  11.7 5.1 %collective-permute-start.6 = (bf16[144,256]{1,0:T(8,128)(2,1)S(1)}, bf16[144,256]{1,0:T(8,128)(2,1)S(1)}, u32[]{:S(2)}, u32[]{:S(2)}) collective-permute-start(bf16[144,256]{1,0:T(8,128)(2,1)S(1)} %fusion.26.refs_0_), channel_id=1, source_target_pairs={{0,28},{4,24},{8,20},{12,16},{16,12},{20,8},{24,4},{28,0},{1,29},{... | collective-permute-start | bytes 221192 | tf_op jit(solution)/shard_map/ppermute | solution.py:23
  18.8 26.1 %copy-start.4 = (f32[32,8]{0,1:T(8,128)S(1)}, f32[32,8]{0,1:T(8,128)}, u32[]{:S(2)}) copy-start(f32[32,8]{0,1:T(8,128)} %param.21) | copy-start | bytes 3076
  27.7 10.1 %collective-permute-start.16 = (bf16[128,1024]{1,0:T(8,128)(2,1)S(1)}, bf16[128,1024]{1,0:T(8,128)(2,1)S(1)}, u32[]{:S(2)}, u32[]{:S(2)}) collective-permute-start(bf16[128,1024]{1,0:T(8,128)(2,1)S(1)} %get-tuple-element.9), channel_id=1, source_target_pairs={{0,1},{3,2},{4,5},{7,6},{8,9},{11,10},{12,13},{15,14},{16,17},{19,... | collective-permute-start | bytes 786440 | tf_op jit(solution)/shard_map/ppermute | solution.py:175
  31.2 12.3 %collective-permute-start.13 = (bf16[128,1024]{1,0:T(8,128)(2,1)S(1)}, bf16[128,1024]{1,0:T(8,128)(2,1)S(1)}, u32[]{:S(2)}, u32[]{:S(2)}) collective-permute-start(bf16[128,1024]{1,0:T(8,128)(2,1)S(1)} %get-tuple-element.8), channel_id=1, source_target_pairs={{0,1},{3,2},{4,5},{7,6},{8,9},{11,10},{12,13},{15,14},{16,17},{19,... | collective-permute-start | bytes 786440 | tf_op jit(solution)/shard_map/ppermute | solution.py:175
  32.5 16.6 %collective-permute-start.10 = (bf16[128,1024]{1,0:T(8,128)(2,1)S(1)}, bf16[128,1024]{1,0:T(8,128)(2,1)S(1)}, u32[]{:S(2)}, u32[]{:S(2)}) collective-permute-start(bf16[128,1024]{1,0:T(8,128)(2,1)S(1)} %get-tuple-element.7), channel_id=1, source_target_pairs={{0,1},{3,2},{4,5},{7,6},{8,9},{11,10},{12,13},{15,14},{16,17},{19,... | collective-permute-start | bytes 786440 | tf_op jit(solution)/shard_map/ppermute | solution.py:175
  33.8 20.1 %collective-permute-start.7 = (bf16[128,1024]{1,0:T(8,128)(2,1)S(1)}, bf16[128,1024]{1,0:T(8,128)(2,1)S(1)}, u32[]{:S(2)}, u32[]{:S(2)}) collective-permute-start(bf16[128,1024]{1,0:T(8,128)(2,1)S(1)} %get-tuple-element.6), channel_id=1, source_target_pairs={{0,1},{3,2},{4,5},{7,6},{8,9},{11,10},{12,13},{15,14},{16,17},{19,... | collective-permute-start | bytes 786440 | tf_op jit(solution)/shard_map/ppermute | solution.py:175
  37.9 16.8 %collective-permute-start.17 = (bf16[128,1024]{1,0:T(8,128)(2,1)S(1)}, bf16[128,1024]{1,0:T(8,128)(2,1)}, u32[]{:S(2)}, u32[]{:S(2)}) collective-permute-start(bf16[128,1024]{1,0:T(8,128)(2,1)S(1)} %add.113), channel_id=1, source_target_pairs={{1,2},{2,1},{5,6},{6,5},{9,10},{10,9},{13,14},{14,13},{17,18},{18,... | collective-permute-start | bytes 786440 | tf_op jit(solution)/shard_map/ppermute | solution.py:177
  43.6 14.8 %collective-permute-start.14 = (bf16[128,1024]{1,0:T(8,128)(2,1)S(1)}, bf16[128,1024]{1,0:T(8,128)(2,1)}, u32[]{:S(2)}, u32[]{:S(2)}) collective-permute-start(bf16[128,1024]{1,0:T(8,128)(2,1)S(1)} %add.111), channel_id=1, source_target_pairs={{1,2},{2,1},{5,6},{6,5},{9,10},{10,9},{13,14},{14,13},{17,18},{18,... | collective-permute-start | bytes 786440 | tf_op jit(solution)/shard_map/ppermute | solution.py:177
  49.2 12.8 %collective-permute-start.11 = (bf16[128,1024]{1,0:T(8,128)(2,1)S(1)}, bf16[128,1024]{1,0:T(8,128)(2,1)S(1)}, u32[]{:S(2)}, u32[]{:S(2)}) collective-permute-start(bf16[128,1024]{1,0:T(8,128)(2,1)S(1)} %add.109), channel_id=1, source_target_pairs={{1,2},{2,1},{5,6},{6,5},{9,10},{10,9},{13,14},{14,13},{17,18},{18,... | collective-permute-start | bytes 786440 | tf_op jit(solution)/shard_map/ppermute | solution.py:177
  54.0 9.6 %collective-permute-start.8 = (bf16[128,1024]{1,0:T(8,128)(2,1)S(1)}, bf16[128,1024]{1,0:T(8,128)(2,1)S(1)}, u32[]{:S(2)}, u32[]{:S(2)}) collective-permute-start(bf16[128,1024]{1,0:T(8,128)(2,1)S(1)} %add.106), channel_id=1, source_target_pairs={{1,2},{2,1},{5,6},{6,5},{9,10},{10,9},{13,14},{14,13},{17,18},{18,... | collective-permute-start | bytes 786440 | tf_op jit(solution)/shard_map/ppermute | solution.py:177
  55.7 13.4 %collective-permute-start.18 = (bf16[128,1024]{1,0:T(8,128)(2,1)S(1)}, bf16[128,1024]{1,0:T(8,128)(2,1)}, u32[]{:S(2)}, u32[]{:S(2)}) collective-permute-start(bf16[128,1024]{1,0:T(8,128)(2,1)S(1)} %add.114), channel_id=1, source_target_pairs={{1,0},{2,3},{5,4},{6,7},{9,8},{10,11},{13,12},{14,15},{17,16},{18,... | collective-permute-start | bytes 786440 | tf_op jit(solution)/shard_map/ppermute | solution.py:179
  59.4 15.3 %collective-permute-start.15 = (bf16[128,1024]{1,0:T(8,128)(2,1)S(1)}, bf16[128,1024]{1,0:T(8,128)(2,1)}, u32[]{:S(2)}, u32[]{:S(2)}) collective-permute-start(bf16[128,1024]{1,0:T(8,128)(2,1)S(1)} %add.112), channel_id=1, source_target_pairs={{1,0},{2,3},{5,4},{6,7},{9,8},{10,11},{13,12},{14,15},{17,16},{18,... | collective-permute-start | bytes 786440 | tf_op jit(solution)/shard_map/ppermute | solution.py:179
  62.0 18.2 %collective-permute-start.12 = (bf16[128,1024]{1,0:T(8,128)(2,1)S(1)}, bf16[128,1024]{1,0:T(8,128)(2,1)S(1)}, u32[]{:S(2)}, u32[]{:S(2)}) collective-permute-start(bf16[128,1024]{1,0:T(8,128)(2,1)S(1)} %add.110), channel_id=1, source_target_pairs={{1,0},{2,3},{5,4},{6,7},{9,8},{10,11},{13,12},{14,15},{17,16},{18,... | collective-permute-start | bytes 786440 | tf_op jit(solution)/shard_map/ppermute | solution.py:179
  63.7 21.0 %collective-permute-start.9 = (bf16[128,1024]{1,0:T(8,128)(2,1)S(1)}, bf16[128,1024]{1,0:T(8,128)(2,1)S(1)}, u32[]{:S(2)}, u32[]{:S(2)}) collective-permute-start(bf16[128,1024]{1,0:T(8,128)(2,1)S(1)} %add.107), channel_id=1, source_target_pairs={{1,0},{2,3},{5,4},{6,7},{9,8},{10,11},{13,12},{14,15},{17,16},{18,... | collective-permute-start | bytes 786440 | tf_op jit(solution)/shard_map/ppermute | solution.py:179
  87.0 11.2 %collective-permute-start.21 = (bf16[32,4096]{1,0:T(8,128)(2,1)S(1)}, bf16[32,4096]{1,0:T(8,128)(2,1)S(1)}, u32[]{:S(2)}, u32[]{:S(2)}) collective-permute-start(bf16[32,4096]{1,0:T(8,128)(2,1)S(1)} %get-tuple-element.19), channel_id=1, source_target_pairs={{0,3},{1,2},{2,1},{3,0},{4,7},{5,6},{6,5},{7,4},{8,11},{9,10},{10,... | collective-permute-start | bytes 786440 | tf_op jit(solution)/shard_map/ppermute | solution.py:23
  88.4 21.6 %collective-permute-start.20 = (bf16[32,4096]{1,0:T(8,128)(2,1)S(1)}, bf16[32,4096]{1,0:T(8,128)(2,1)S(1)}, u32[]{:S(2)}, u32[]{:S(2)}) collective-permute-start(bf16[32,4096]{1,0:T(8,128)(2,1)S(1)} %get-tuple-element.20), channel_id=1, source_target_pairs={{0,2},{1,3},{2,0},{3,1},{4,6},{5,7},{6,4},{7,5},{8,10},{9,11},{10,... | collective-permute-start | bytes 786440 | tf_op jit(solution)/shard_map/ppermute | solution.py:23
  88.4 21.6 %collective-permute-start.19 = (bf16[32,4096]{1,0:T(8,128)(2,1)S(1)}, bf16[32,4096]{1,0:T(8,128)(2,1)S(1)}, u32[]{:S(2)}, u32[]{:S(2)}) collective-permute-start(bf16[32,4096]{1,0:T(8,128)(2,1)S(1)} %get-tuple-element.18), channel_id=1, source_target_pairs={{0,1},{1,0},{2,3},{3,2},{4,5},{5,4},{6,7},{7,6},{8,9},{9,8},{10,11... | collective-permute-start | bytes 786440 | tf_op jit(solution)/shard_map/ppermute | solution.py:23
  (7 other events, 97.2 us)

commit v2 on v1

--- a/solution.py
+++ b/solution.py
@@ -13,50 +13,66 @@
 HEAD_DIM = 128
 HID_SPLIT = 4
 STACK = 4
-COL_CHUNKS = 4
+WIDTHS = (1024, 1024, 1024, 512, 512)
+SPANS = tuple((sum(WIDTHS[:i]), width) for i, width in enumerate(WIDTHS))
 PAD_ROWS = 16
+ORDER = (
+    ("near", 0),
+    ("near", 1),
+    ("total", 0),
+    ("near", 2),
+    ("total", 1),
+    ("near", 3),
+    ("absorb", 0),
+    ("near", 4),
+    ("total", 2),
+    ("absorb", 1),
+    ("total", 3),
+    ("total", 4),
+    ("absorb", 2),
+    ("absorb", 3),
+    ("absorb", 4),
+)
 LOG2E = 1.4426950408889634
 VMEM = pl.BlockSpec(memory_space=pltpu.VMEM)
+ANY = pl.BlockSpec(memory_space=pl.ANY)
+LIGHT = pl.CostEstimate(flops=1024, bytes_accessed=1024, transcendentals=0)
 
 
 def exchange(value, axis, offset, size):
     return lax.ppermute(value, axis, [(i, i ^ offset) for i in range(size)])
 
 
-def attend_kernel(
-    block_count,
-    rank_ref,
-    q_ref,
-    bound_ref,
-    resid_ref,
-    *refs,
-):
-    payloads = refs[:block_count]
-    w_hbm = refs[block_count]
-    outs = refs[block_count + 1 : block_count + 1 + COL_CHUNKS]
-    w_buf, k_buf, v_buf, bias, attended, acc, sems = refs[block_count + 1 + COL_CHUNKS :]
+def attend_kernel(rank_ref, bound_ref, same_ref, other_ref, q_hbm, resid_hbm, w_hbm, after_ref, *refs):
+    outs = refs[: len(WIDTHS)]
+    q_ref, resid_ref, w_buf, k_buf, v_buf, bias, attended, acc, sems, side = refs[len(WIDTHS) :]
     tok = q_ref.shape[0]
     heads = q_ref.shape[1] // HEAD_DIM
-    cols = D // COL_CHUNKS
+    q_copy = pltpu.make_async_copy(q_hbm, q_ref, side.at[0])
+    q_copy.start()
+    resid_copy = pltpu.make_async_copy(resid_hbm, resid_ref, side.at[1])
+    resid_copy.start()
     copies = []
-    for chunk in range(COL_CHUNKS):
-        copy = pltpu.make_async_copy(
-            w_hbm.at[:, pl.ds(chunk * cols, cols)], w_buf.at[chunk], sems.at[chunk]
-        )
+    for chunk, (first, width) in enumerate(SPANS):
+        span = pl.ds(first, width)
+        copy = pltpu.make_async_copy(w_hbm.at[:, span], w_buf.at[:, span], sems.at[chunk])
         copy.start()
         copies.append(copy)
     bound = bound_ref[...]
     lane = lax.broadcasted_iota(jnp.int32, (1, tok), 1).astype(jnp.float32)
     ones = jnp.ones((tok, HEAD_DIM), jnp.bfloat16)
-    for b in range(block_count):
+    half_count = same_ref.shape[0]
+    for b in range(2 * half_count):
         rows = slice(b * tok, (b + 1) * tok)
-        k_buf[rows, :] = payloads[b][:tok, :HEAD_DIM]
-        v_buf[rows, :HEAD_DIM] = payloads[b][:tok, HEAD_DIM:]
+        group, row = (same_ref, b) if b < half_count else (other_ref, b - half_count)
+        k_buf[rows, :] = group[row, :tok, :HEAD_DIM]
+        v_buf[rows, :HEAD_DIM] = group[row, :tok, HEAD_DIM:]
         v_buf[rows, HEAD_DIM:] = ones
-        start = payloads[b][tok : tok + PAD_ROWS, :HEAD_DIM].astype(jnp.float32)[:1]
+        start = group[row, tok : tok + PAD_ROWS, :HEAD_DIM].astype(jnp.float32)[:1]
         place = start * tok + lane
         bias[:, rows] = jnp.where(place <= bound, 0.0, -1e30)
     factor = HEAD_DIM ** (-0.5) * LOG2E
+    q_copy.wait()
 
     def some_heads(step, carry):
         base = step * STACK * HEAD_DIM
@@ -81,45 +97,217 @@
         return carry
 
     lax.fori_loop(0, heads // STACK, some_heads, 0)
+    resid_copy.wait()
     home = resid_ref.shape[0]
-    first = pl.multiple_of(rank_ref[0] * home, home)
-    for chunk in range(COL_CHUNKS):
+    top = pl.multiple_of(rank_ref[0] * home, home)
+    for chunk, (first, width) in enumerate(SPANS):
         copies[chunk].wait()
-        acc[...] = jnp.dot(attended[...], w_buf[chunk], preferred_element_type=jnp.float32)
-        own = resid_ref[:, chunk * cols : (chunk + 1) * cols].astype(jnp.float32)
-        acc[pl.ds(first, home), :] += own
-        outs[chunk][...] = acc[...].astype(jnp.bfloat16)
-
-
-def attend_project(rank, queries, bounds, residual, payloads, w_out):
+        span = slice(first, first + width)
+        acc[:, span] = jnp.dot(
+            attended[...], w_buf[:, span], preferred_element_type=jnp.float32
+        )
+        acc[pl.ds(top, home), span] += resid_ref[:, span].astype(jnp.float32)
+        outs[chunk][...] = acc[:, span].astype(jnp.bfloat16)
+
+
+def attend_project(rank, bounds, same, other, queries, residual, w_out, after):
     tok, width = queries.shape
-    count = len(payloads)
-    cols = D // COL_CHUNKS
-    keys_in_all = tok * count
-    return pl.pallas_call(
-        functools.partial(attend_kernel, count),
-        out_shape=[jax.ShapeDtypeStruct((tok, cols), jnp.bfloat16)] * COL_CHUNKS,
-        in_specs=[pl.BlockSpec(memory_space=pltpu.SMEM)]
-        + [VMEM] * (3 + count)
-        + [pl.BlockSpec(memory_space=pl.ANY)],
-        out_specs=[VMEM] * COL_CHUNKS,
+    keys_in_all = 2 * same.shape[0] * tok
+    return pl.pallas_call(
+        attend_kernel,
+        out_shape=[jax.ShapeDtypeStruct((tok, w), jnp.bfloat16) for w in WIDTHS],
+        in_specs=[pl.BlockSpec(memory_space=pltpu.SMEM)] + [VMEM] * 3 + [ANY] * 4,
+        out_specs=[VMEM] * len(WIDTHS),
         scratch_shapes=[
-            pltpu.VMEM((COL_CHUNKS, width, cols), jnp.bfloat16),
+            pltpu.VMEM(queries.shape, jnp.bfloat16),
+            pltpu.VMEM(residual.shape, jnp.bfloat16),
+            pltpu.VMEM((width, D), jnp.bfloat16),
             pltpu.VMEM((keys_in_all, HEAD_DIM), jnp.bfloat16),
             pltpu.VMEM((keys_in_all, 2 * HEAD_DIM), jnp.bfloat16),
             pltpu.VMEM((tok, keys_in_all), jnp.float32),
             pltpu.VMEM((tok, width), jnp.bfloat16),
-            pltpu.VMEM((tok, cols), jnp.float32),
-            pltpu.SemaphoreType.DMA((COL_CHUNKS,)),
+            pltpu.VMEM((tok, D), jnp.float32),
+            pltpu.SemaphoreType.DMA((len(WIDTHS),)),
+            pltpu.SemaphoreType.DMA((2,)),
         ],
-        compiler_params=pltpu.CompilerParams(vmem_limit_bytes=44 * 1024 * 1024),
-        cost_estimate=pl.CostEstimate(
-            flops=2 * tok * width * (2 * keys_in_all + D),
-            bytes_accessed=2 * width * D,
-            transcendentals=tok * width // HEAD_DIM * keys_in_all,
-        ),
+        compiler_params=pltpu.CompilerParams(vmem_limit_bytes=36 * 1024 * 1024),
+        cost_estimate=LIGHT,
         name="attend_project",
-    )(rank, queries, bounds, residual, *payloads, w_out)
+    )(rank, bounds, same, other, queries, residual, w_out, after)
+
+
+def down_kernel(place_ref, coef_ref, a0, a1, a2, a3, own_ref, same_ref, other_ref, out_ref):
+    coef = coef_ref[...]
+    blended = [(a[...].astype(jnp.float32) * coef).astype(jnp.bfloat16) for a in (a0, a1, a2, a3)]
+    hidden = own_ref.shape[0]
+    count, _, width = same_ref.shape
+    for group, buf in enumerate((same_ref, other_ref)):
+        for j in range(count):
+            block = place_ref[0] ^ (2 * j + group)
+            span = pl.ds(pl.multiple_of(block * width, width), width)
+            total = jnp.dot(blended[0], own_ref[:, span], preferred_element_type=jnp.float32)
+            for s in range(1, len(blended)):
+                rows = slice((s - 1) * hidden, s * hidden)
+                total += jnp.dot(
+                    blended[s], buf[j, rows, :], preferred_element_type=jnp.float32
+                )
+            out_ref[:, span] = total.astype(jnp.bfloat16)
+
+
+def down(place, coefficient, acts, own, same, other):
+    rows = acts[0].shape[0]
+    return pl.pallas_call(
+        down_kernel,
+        out_shape=jax.ShapeDtypeStruct((rows, D), jnp.bfloat16),
+        in_specs=[pl.BlockSpec(memory_space=pltpu.SMEM)] + [VMEM] * 8,
+        out_specs=VMEM,
+        compiler_params=pltpu.CompilerParams(vmem_limit_bytes=24 * 1024 * 1024),
+        cost_estimate=LIGHT,
+        name="down",
+    )(place, coefficient, *acts, own, same, other)
+
+
+def half_kernel(first, after_ref, piece_ref, out_ref):
+    out_ref[...] = piece_ref[first : first + out_ref.shape[0], :]
+
+
+def half_after(piece, first, after):
+    shape = (piece.shape[0] // 2, piece.shape[1])
+    return pl.pallas_call(
+        functools.partial(half_kernel, first),
+        out_shape=jax.ShapeDtypeStruct(shape, jnp.bfloat16),
+        in_specs=[ANY, VMEM],
+        out_specs=VMEM,
+        compiler_params=pltpu.CompilerParams(vmem_limit_bytes=4 * 1024 * 1024),
+        cost_estimate=LIGHT,
+        name="half_after",
+    )(after, piece)
+
+
+def join_kernel(*refs):
+    out_ref = refs[-1]
+    first = 0
+    for piece in refs[1:-1]:
+        rows = piece.shape[0]
+        out_ref[first : first + rows, :] = piece[...]
+        first += rows
+
+
+def join_after(pieces, after):
+    rows = sum(piece.shape[0] for piece in pieces)
+    width = pieces[0].shape[1]
+    return pl.pallas_call(
+        join_kernel,
+        out_shape=jax.ShapeDtypeStruct((rows, width), jnp.bfloat16),
+        in_specs=[ANY] + [VMEM] * len(pieces),
+        out_specs=VMEM,
+        compiler_params=pltpu.CompilerParams(vmem_limit_bytes=8 * 1024 * 1024),
+        cost_estimate=LIGHT,
+        name="join_after",
+    )(after, *pieces)
+
+
+def shard_kernel(place_ref, whole_hbm, after_ref, out_ref, sem):
+    width = out_ref.shape[1]
+    first = pl.multiple_of(place_ref[0] * width, width)
+    copy = pltpu.make_async_copy(whole_hbm.at[:, pl.ds(first, width)], out_ref, sem)
+    copy.start()
+    copy.wait()
+
+
+def shard_after(place, whole, width, after):
+    return pl.pallas_call(
+        shard_kernel,
+        out_shape=jax.ShapeDtypeStruct((whole.shape[0], width), jnp.bfloat16),
+        in_specs=[pl.BlockSpec(memory_space=pltpu.SMEM), ANY, ANY],
+        out_specs=VMEM,
+        scratch_shapes=[pltpu.SemaphoreType.DMA],
+        compiler_params=pltpu.CompilerParams(vmem_limit_bytes=4 * 1024 * 1024),
+        cost_estimate=LIGHT,
+        name="shard_after",
+    )(place, whole, after)
+
+
+def add_kernel(a_ref, b_ref, after_ref, out_ref):
+    out_ref[...] = (a_ref[...].astype(jnp.float32) + b_ref[...].astype(jnp.float32)).astype(
+        jnp.bfloat16
+    )
+
+
+def add_after(left, right, after):
+    return pl.pallas_call(
+        add_kernel,
+        out_shape=jax.ShapeDtypeStruct(left.shape, jnp.bfloat16),
+        in_specs=[VMEM, VMEM, ANY],
+        out_specs=VMEM,
+        compiler_params=pltpu.CompilerParams(vmem_limit_bytes=4 * 1024 * 1024),
+        cost_estimate=LIGHT,
+        name="add_after",
+    )(left, right, after)
+
+
+def absorb_kernel(chunk, flag_ref, total_ref, outward_ref, gain_ref, w_ref, *refs):
+    last = chunk == len(WIDTHS) - 1
+    states = refs[1 : 1 if chunk == 0 else 3]
+    outs = refs[1 + len(states) : -1]
+    scratch = refs[-1]
+    first, width = SPANS[chunk]
+    span = slice(first, first + width)
+    middle = jnp.where(flag_ref[1] == 1, outward_ref[...], total_ref[...])
+    scratch[...] = middle
+    home_ref = outs[0]
+    home = home_ref.shape[0]
+    top = pl.multiple_of(flag_ref[0] * home, home)
+    home_ref[...] = scratch[pl.ds(top, home), :]
+    wide = middle.astype(jnp.float32)
+    gained = (wide * gain_ref[:, span]).astype(jnp.bfloat16)
+    product = lax.dot_general(
+        gained, w_ref[:, span], (((1,), (1,)), ((), ())), preferred_element_type=jnp.float32
+    )
+    square = sum(
+        wide[:, i * 128 : (i + 1) * 128] * wide[:, i * 128 : (i + 1) * 128]
+        for i in range(width // 128)
+    )
+    if chunk > 0:
+        product += states[0][...]
+        square += states[1][...]
+    if last:
+        hidden = product.shape[1] // 2
+        mean_square = jnp.sum(square, axis=1, keepdims=True) / D
+        product = product * lax.rsqrt(mean_square + 1e-06)
+        gate = product[:, :hidden]
+        act = gate / (1.0 + jnp.exp(-gate)) * product[:, hidden:]
+        outs[1][...] = act.astype(jnp.bfloat16)
+    else:
+        outs[1][...] = product
+        outs[2][...] = square
+
+
+def absorb(chunk, flags, total, outward, gain, w_in, after, states):
+    tok, width = total.shape
+    rows = w_in.shape[0]
+    home = jax.ShapeDtypeStruct((tok // lax.axis_size("exp"), width), jnp.bfloat16)
+    if chunk == len(WIDTHS) - 1:
+        out_shape = [home, jax.ShapeDtypeStruct((tok, rows // 2), jnp.bfloat16)]
+    else:
+        out_shape = [
+            home,
+            jax.ShapeDtypeStruct((tok, rows), jnp.float32),
+            jax.ShapeDtypeStruct((tok, 128), jnp.float32),
+        ]
+    return pl.pallas_call(
+        functools.partial(absorb_kernel, chunk),
+        out_shape=out_shape,
+        in_specs=[pl.BlockSpec(memory_space=pltpu.SMEM)]
+        + [VMEM] * 4
+        + [ANY]
+        + [VMEM] * len(states),
+        out_specs=[VMEM] * len(out_shape),
+        scratch_shapes=[pltpu.VMEM((tok, width), jnp.bfloat16)],
+        compiler_params=pltpu.CompilerParams(vmem_limit_bytes=12 * 1024 * 1024),
+        cost_estimate=LIGHT,
+        name="absorb",
+    )(flags, total, outward, gain, w_in, after, *states)
 
 
 def own_heads(queries, keys, values):
@@ -150,59 +338,74 @@
     ctx_count = lax.axis_size("ctx")
     exp_count = lax.axis_size("exp")
     rank = lax.axis_index("exp")
+    place = lax.axis_index("ctx")
     key_head, value_head = own_heads(queries, keys, values)
     block = (positions[0] // tok).astype(jnp.bfloat16)
     pair = jnp.concatenate([key_head, value_head], axis=1)
     payload = jnp.concatenate(
         [pair, jnp.full((PAD_ROWS, 2 * HEAD_DIM), block, jnp.bfloat16)], axis=0
     )
-    payloads = [payload] + [exchange(payload, "ctx", r, ctx_count) for r in range(1, ctx_count)]
+    same_rows = join_after(
+        [payload] + [exchange(payload, "ctx", r, ctx_count) for r in range(2, ctx_count, 2)],
+        payload,
+    )
+    same_keys = same_rows.reshape(ctx_count // 2, tok + PAD_ROWS, 2 * HEAD_DIM)
+    other_keys = exchange(same_rows, "ctx", 1, ctx_count).reshape(same_keys.shape)
+    places = place.astype(jnp.int32).reshape(1)
+    flat_back = w_back.reshape(hidden, D)
+    mine = shard_after(places, flat_back, D // ctx_count, same_rows)
+    planes = [exchange(mine, "exp", s, exp_count) for s in range(1, exp_count)]
+
     parts = attend_project(
         rank.astype(jnp.int32).reshape(1),
+        bounds.astype(jnp.float32).reshape(tok, 1),
+        same_keys,
+        other_keys,
         queries,
-        bounds.astype(jnp.float32).reshape(tok, 1),
         residual,
-        payloads,
         w_out,
+        mine,
     )
     at_end = (rank == 0) | (rank == exp_count - 1)
-    cols = D // COL_CHUNKS
+    flags = jnp.stack([rank, at_end]).astype(jnp.int32)
+    gain = norm_gain.reshape(1, D)
     flat_in = w_in.reshape(2 * hidden, D)
-    total_square = jnp.zeros((tok, 1), jnp.float32)
-    projected = jnp.zeros((tok, 2 * hidden), jnp.float32)
-    middles = []
-    for chunk in range(COL_CHUNKS):
-        inward = lax.ppermute(parts[chunk], "exp", [(0, 1), (3, 2)])
-        near = parts[chunk] + inward
-        across = lax.ppermute(near, "exp", [(1, 2), (2, 1)])
-        total = near + across
-        outward = lax.ppermute(total, "exp", [(1, 0), (2, 3)])
-        middle = jnp.where(at_end, outward, total)
-        wide = middle.astype(jnp.float32)
-        total_square = total_square + jnp.sum(wide * wide, axis=1, keepdims=True)
-        span = slice(chunk * cols, (chunk + 1) * cols)
-        gained = (wide * norm_gain[None, span]).astype(jnp.bfloat16)
-        projected = projected + lax.dot_general(
-            gained,
-            flat_in[:, span],
-            (((1,), (1,)), ((), ())),
-            preferred_element_type=jnp.float32,
-        )
-        middles.append(lax.dynamic_slice_in_dim(middle, rank * home, home, 0))
-    middle_out = jnp.concatenate(middles, axis=1)
-    projected = projected * lax.rsqrt(total_square / D + 1e-06)
-    activated = (jax.nn.silu(projected[:, :hidden]) * projected[:, hidden:]).astype(jnp.bfloat16)
-    share = jnp.dot(
-        activated, w_back.reshape(hidden, D), preferred_element_type=jnp.float32
-    ).astype(jnp.bfloat16)
-    gathered = lax.dynamic_slice_in_dim(share, rank * home, home, 0).astype(jnp.float32)
+    count = len(parts)
+    inward = [lax.ppermute(part, "exp", [(0, 1), (3, 2)]) for part in parts]
+    near, across, total, outward = {}, {}, {}, {}
+    homes, states, after = [], [], parts[0]
+    for step, chunk in ORDER:
+        if step == "near":
+            after = near[chunk] = add_after(parts[chunk], inward[chunk], after)
+            across[chunk] = lax.ppermute(near[chunk], "exp", [(1, 2), (2, 1)])
+        elif step == "total":
+            after = total[chunk] = add_after(near[chunk], across[chunk], after)
+            outward[chunk] = lax.ppermute(total[chunk], "exp", [(1, 0), (2, 3)])
+        else:
+            own, *states = absorb(
+                chunk, flags, total[chunk], outward[chunk], gain, flat_in, after, states
+            )
+            homes.append(own)
+            after = states[0]
+    planes = join_after(planes, near[0])
+    from_x = exchange(planes, "ctx", 2, ctx_count)
+    from_y = exchange(planes, "ctx", 4, ctx_count)
+    upper = exchange(half_after(from_x, 0, homes[0]), "ctx", 4, ctx_count)
+    lower = exchange(half_after(from_y, planes.shape[0] // 2, homes[0]), "ctx", 2, ctx_count)
+    same_rows = join_after([planes, from_x, from_y, upper, lower], homes[2])
+    same_back = same_rows.reshape(ctx_count // 2, planes.shape[0], planes.shape[1])
+    other_back = exchange(same_rows, "ctx", 1, ctx_count).reshape(same_back.shape)
+    middle_out = jnp.concatenate(homes, axis=1)
+    activated = states[0]
+    acts = [lax.dynamic_slice_in_dim(activated, rank * home, home, 0)]
     for offset in range(1, exp_count):
-        leaving = lax.dynamic_slice_in_dim(share, (rank ^ offset) * home, home, 0)
-        gathered = gathered + exchange(leaving, "exp", offset, exp_count).astype(jnp.float32)
+        leaving = lax.dynamic_slice_in_dim(activated, (rank ^ offset) * home, home, 0)
+        acts.append(exchange(leaving, "exp", offset, exp_count))
     shares = gates / jnp.sum(gates, axis=1, keepdims=True)
     coefficient = jnp.sum(jnp.where(routes == 0, shares, 0.0), axis=1, keepdims=True)
     coefficient = coefficient.astype(jnp.bfloat16).astype(jnp.float32)
-    return (middle_out, (gathered * coefficient).astype(jnp.bfloat16))
+    expert_out = down(places, coefficient, acts, flat_back, same_back, other_back)
+    return (middle_out, expert_out)
 
 
 def largest_divisor(row_count):

time: 112 us -> 127 us (1.13)
  waiting for transfers between devices: 53.6 us -> 32.7 us
  Pallas kernels: 8.87 us -> 28 us
  starting transfers between devices: 29.3 us -> 47.7 us
  local copies, waits for them, and re-layouts: 4.37 us -> 10.2 us
  other arithmetic: 9.12 us -> 3.35 us
  matrix products: 1.97 us -> 0 us
    pallas_call x1 -> x23, Pallas kernels: 8.87 us -> 28 us  [the longest x1 9.31 us: attend_project(): pl.pallas_call(attend_kernel, out_shape=[jax.ShapeDtypeStruct((tok, w), j...]
    ppermute x12 -> x15, waiting for transfers between devices: 31.8 us -> 13.5 us  [the longest x5 11.8 us: line_device(): outward[chunk] = lax.ppermute(total[chunk], 'exp', [(1, 0), (2, 3)])]
    ppermute x12 -> x15, starting transfers between devices: 16.9 us -> 29.9 us  [the longest x5 19.4 us: line_device(): inward = [lax.ppermute(part, 'exp', [(0, 1), (3, 2)]) for part in parts]]
    unnamed x18 -> x46, local copies, waits for them, and re-layouts: 2.02 us -> 7.94 us
    ppermute x10 -> x15, starting transfers between devices: 12.4 us -> 17.8 us  [exchange(): return lax.ppermute(value, axis, [(i, i ^ offset) for i in range(size)])]
    reduce_sum x4 -> x0, other arithmetic: 2.61 us -> none  [line_device(): total_square = total_square + jnp.sum(wide * wide, axis=1, keepdims=True)]
    ppermute x10 -> x15, waiting for transfers between devices: 21.8 us -> 19.3 us  [exchange(): return lax.ppermute(value, axis, [(i, i ^ offset) for i in range(size)])]
    add x8 -> x0, other arithmetic: 2.43 us -> none  [the longest x4 2.17 us: line_device(): total = near + across]
  transfers between devices with their start and end apart: 22 -> 30, of which waited for: 12 -> 11; matrix products, arithmetic and copies ran while one was open for 9% -> 5% of each run, Pallas kernels for 0% -> 9%
where the time goes in v2:
time: 127 us; the launch traced here: 126 us
  starting transfers between devices  47.7 us (38%)
  waiting for transfers between devices  32.7 us (26%)
  Pallas kernels  28 us (22%)
  local copies, waits for them, and re-layouts  10.2 us (8%)
  between operations  3.89 us (3%)
  other arithmetic  3.35 us (3%)
    ppermute x5, starting transfers between devices, line_device(): inward = [lax.ppermute(part, 'exp', [(0, 1), (3, 2)]) for part in parts]  19.4 us
    ppermute x15, waiting for transfers between devices, exchange(): return lax.ppermute(value, axis, [(i, i ^ offset) for i in range(size)])  19.3 us
    ppermute x15, starting transfers between devices, exchange(): return lax.ppermute(value, axis, [(i, i ^ offset) for i in range(size)])  17.8 us
    ppermute x5, waiting for transfers between devices, line_device(): outward[chunk] = lax.ppermute(total[chunk], 'exp', [(1, 0), (2, 3)])  11.8 us
    pallas_call x1, Pallas kernels, attend_project(): pl.pallas_call(attend_kernel, out_shape=[jax.ShapeDtypeStruct((tok, w), j...  9.31 us
    unnamed x46, local copies, waits for them, and re-layouts  7.94 us
    ppermute x5, starting transfers between devices, line_device(): outward[chunk] = lax.ppermute(total[chunk], 'exp', [(1, 0), (2, 3)])  6.44 us
    pallas_call x5, Pallas kernels, absorb(): pl.pallas_call(functools.partial(absorb_kernel, chunk), out_shape=out_sha...  5.05 us
  transfers between devices with their start and end apart: 30, of which 11 were waited for; matrix products, arithmetic and copies ran while one was open for 5% of the time, Pallas kernels for 9%

profile of v2, /device:TPU:0, one launch (start us, length us, event | category | flops | bytes accessed | tf_op | source)
XLA Modules:
  0.0 125.9 jit_solution(16439956610420032439)
XLA Ops:
  4.1 4.0 %collective-permute-start.2 = (bf16[144,256]{1,0:T(8,128)(2,1)S(1)}, bf16[144,256]{1,0:T(8,128)(2,1)S(1)}, u32[]{:S(2)}, u32[]{:S(2)}) collective-permute-start(bf16[144,256]{1,0:T(8,128)(2,1)S(1)} %fusion.2.refs_0_.refs_1_), channel_id=1, source_target_pairs={{0,24},{4,28},{8,16},{12,20},{16,8},{20,12},{24,0},{28,4},{1,25},{... | collective-permute-start | bytes 221192 | tf_op jit(solution)/shard_map/ppermute | solution.py:43
  8.7 1.7 %collective-permute-done.2.refs_4_ = bf16[144,256]{1,0:T(8,128)(2,1)S(1)} collective-permute-done((bf16[144,256]{1,0:T(8,128)(2,1)S(1)}, bf16[144,256]{1,0:T(8,128)(2,1)S(1)}, u32[]{:S(2)}, u32[]{:S(2)}) %collective-permute-start.2) | collective-permute-done | bytes 73760 | tf_op jit(solution)/shard_map/ppermute | solution.py:43
  10.5 2.0 %collective-permute-done.1.refs_3_ = bf16[144,256]{1,0:T(8,128)(2,1)S(1)} collective-permute-done((bf16[144,256]{1,0:T(8,128)(2,1)S(1)}, bf16[144,256]{1,0:T(8,128)(2,1)S(1)}, u32[]{:S(2)}, u32[]{:S(2)}) %collective-permute-start.1) | collective-permute-done | bytes 73760 | tf_op jit(solution)/shard_map/ppermute | solution.py:43
  13.9 1.4 %copy-done.1 = bf16[1,192,4096]{2,1,0:T(8,128)(2,1)S(1)} copy-done((bf16[1,192,4096]{2,1,0:T(8,128)(2,1)S(1)}, bf16[1,192,4096]{2,1,0:T(8,128)(2,1)}, u32[]{:S(2)}) %copy-start.1) | copy-done | bytes 1572888
  15.3 9.3 %attend_project.1 = (bf16[128,1024]{1,0:T(8,128)(2,1)S(1)}, bf16[128,1024]{1,0:T(8,128)(2,1)S(1)}, bf16[128,1024]{1,0:T(8,128)(2,1)S(1)}, bf16[128,512]{1,0:T(8,128)(2,1)}, bf16[128,512]{1,0:T(8,128)(2,1)S(1)}) custom-call(s32[1]{0:T(128)} %bitcast.rank_ref, f32[128,1]{1,0:T(8,128)S(1)} %copy.14.bound_ref, bf16[4,144,256]{2,1,0:T(8,128)(2,1)S(1)} %bitcast.24, ...), custom_call_target="tpu_custom_call" | custom-call | flops 1024 | bytes 1024 | tf_op jit(solution)/shard_map/attend_project/pallas_call | solution.py:116
  25.3 3.5 %collective-permute-start.4 = (bf16[128,1024]{1,0:T(8,128)(2,1)S(1)}, bf16[128,1024]{1,0:T(8,128)(2,1)S(1)}, u32[]{:S(2)}, u32[]{:S(2)}) collective-permute-start(bf16[128,1024]{1,0:T(8,128)(2,1)S(1)} %get-tuple-element.21.a_ref.after_ref), channel_id=1, source_target_pairs={{0,1},{3,2},{4,5},{7,6},{8,9},{11,10},{12,13},{15,14},{16,17},{19,... | collective-permute-start | bytes 786440 | tf_op jit(solution)/shard_map/ppermute | solution.py:374
  28.8 2.5 %collective-permute-start.24 = (bf16[192,512]{1,0:T(8,128)(2,1)S(1)}, bf16[192,512]{1,0:T(8,128)(2,1)S(1)}, u32[]{:S(2)}, u32[]{:S(2)}) collective-permute-start(bf16[192,512]{1,0:T(8,128)(2,1)S(1)} %shard_after.1.after_ref), channel_id=1, source_target_pairs={{0,3},{1,2},{2,1},{3,0},{4,7},{5,6},{6,5},{7,4},{8,11},{9,10},{10,... | collective-permute-start | bytes 589832 | tf_op jit(solution)/shard_map/ppermute | solution.py:43
  31.3 1.9 %collective-permute-start.22 = (bf16[192,512]{1,0:T(8,128)(2,1)S(1)}, bf16[192,512]{1,0:T(8,128)(2,1)S(1)}, u32[]{:S(2)}, u32[]{:S(2)}) collective-permute-start(bf16[192,512]{1,0:T(8,128)(2,1)S(1)} %shard_after.1.after_ref), channel_id=1, source_target_pairs={{0,1},{1,0},{2,3},{3,2},{4,5},{5,4},{6,7},{7,6},{8,9},{9,8},{10,11... | collective-permute-start | bytes 589832 | tf_op jit(solution)/shard_map/ppermute | solution.py:43
  33.2 2.0 %collective-permute-start.6 = (bf16[128,1024]{1,0:T(8,128)(2,1)S(1)}, bf16[128,1024]{1,0:T(8,128)(2,1)S(1)}, u32[]{:S(2)}, u32[]{:S(2)}) collective-permute-start(bf16[128,1024]{1,0:T(8,128)(2,1)S(1)} %get-tuple-element.22.a_ref), channel_id=1, source_target_pairs={{0,1},{3,2},{4,5},{7,6},{8,9},{11,10},{12,13},{15,14},{16,17},{19,... | collective-permute-start | bytes 786440 | tf_op jit(solution)/shard_map/ppermute | solution.py:374
  36.1 6.5 %collective-permute-done.24.refs_3_ = bf16[192,512]{1,0:T(8,128)(2,1)S(1)} collective-permute-done((bf16[192,512]{1,0:T(8,128)(2,1)S(1)}, bf16[192,512]{1,0:T(8,128)(2,1)S(1)}, u32[]{:S(2)}, u32[]{:S(2)}) %collective-permute-start.24) | collective-permute-done | bytes 196640 | tf_op jit(solution)/shard_map/ppermute | solution.py:43
  42.6 5.9 %collective-permute-done.23.refs_2_ = bf16[192,512]{1,0:T(8,128)(2,1)S(1)} collective-permute-done((bf16[192,512]{1,0:T(8,128)(2,1)S(1)}, bf16[192,512]{1,0:T(8,128)(2,1)S(1)}, u32[]{:S(2)}, u32[]{:S(2)}) %collective-permute-start.23) | collective-permute-done | bytes 196640 | tf_op jit(solution)/shard_map/ppermute | solution.py:43
  49.3 1.5 %collective-permute-start.26 = (bf16[576,512]{1,0:T(8,128)(2,1)}, bf16[576,512]{1,0:T(8,128)(2,1)}, u32[]{:S(2)}, u32[]{:S(2)}) collective-permute-start(bf16[576,512]{1,0:T(8,128)(2,1)} %join_after.4.refs_1_), channel_id=1, source_target_pairs={{0,16},{4,20},{8,24},{12,28},{16,0},{20,4},{24,8},{28,12},{1,17},{... | collective-permute-start | bytes 1769480 | tf_op jit(solution)/shard_map/ppermute | solution.py:43
  51.4 4.2 %collective-permute-start.10 = (bf16[128,1024]{1,0:T(8,128)(2,1)S(1)}, bf16[128,1024]{1,0:T(8,128)(2,1)S(1)}, u32[]{:S(2)}, u32[]{:S(2)}) collective-permute-start(bf16[128,1024]{1,0:T(8,128)(2,1)S(1)} %get-tuple-element.24.a_ref), channel_id=1, source_target_pairs={{0,1},{3,2},{4,5},{7,6},{8,9},{11,10},{12,13},{15,14},{16,17},{19,... | collective-permute-start | bytes 786440 | tf_op jit(solution)/shard_map/ppermute | solution.py:374
  58.5 1.6 %collective-permute-done.10.b_ref = bf16[128,1024]{1,0:T(8,128)(2,1)S(1)} collective-permute-done((bf16[128,1024]{1,0:T(8,128)(2,1)S(1)}, bf16[128,1024]{1,0:T(8,128)(2,1)S(1)}, u32[]{:S(2)}, u32[]{:S(2)}) %collective-permute-start.10) | collective-permute-done | bytes 262176 | tf_op jit(solution)/shard_map/ppermute | solution.py:374
  60.1 5.0 %collective-permute-start.8 = (bf16[128,512]{1,0:T(8,128)(2,1)}, bf16[128,512]{1,0:T(8,128)(2,1)}, u32[]{:S(2)}, u32[]{:S(2)}) collective-permute-start(bf16[128,512]{1,0:T(8,128)(2,1)} %get-tuple-element.23.a_ref), channel_id=1, source_target_pairs={{0,1},{3,2},{4,5},{7,6},{8,9},{11,10},{12,13},{15,14},{16,17},{19,... | collective-permute-start | bytes 393224 | tf_op jit(solution)/shard_map/ppermute | solution.py:374
  69.2 4.6 %collective-permute-start.13 = (bf16[128,512]{1,0:T(8,128)(2,1)}, bf16[128,512]{1,0:T(8,128)(2,1)S(1)}, u32[]{:S(2)}, u32[]{:S(2)}) collective-permute-start(bf16[128,512]{1,0:T(8,128)(2,1)} %copy-done.12), channel_id=1, source_target_pairs={{0,1},{3,2},{4,5},{7,6},{8,9},{11,10},{12,13},{15,14},{16,17},{19,... | collective-permute-start | bytes 393224 | tf_op jit(solution)/shard_map/ppermute | solution.py:374
  76.3 1.5 %absorb.5 = (bf16[32,1024]{1,0:T(8,128)(2,1)S(1)}, f32[128,384]{1,0:T(8,128)S(1)}, f32[128,128]{1,0:T(8,128)S(1)}) custom-call(s32[2]{0:T(128)S(1)} %pad_add_fusion.flag_ref, bf16[128,1024]{1,0:T(8,128)(2,1)} %add_after.12.after_ref.total_ref, bf16[128,1024]{1,0:T(8,128)(2,1)} %collective-permute-done.7.outward_ref, f32[1,4096]{1,0:T(1,128)S(1)} %bitcast.25, ...), custom_call_target="tpu_custom_call" | custom-call | flops 1024 | bytes 1024 | tf_op jit(solution)/shard_map/absorb/pallas_call | solution.py:298
  86.9 4.6 %collective-permute-done.14.outward_ref = bf16[128,1024]{1,0:T(8,128)(2,1)S(1)} collective-permute-done((bf16[128,1024]{1,0:T(8,128)(2,1)S(1)}, bf16[128,1024]{1,0:T(8,128)(2,1)S(1)}, u32[]{:S(2)}, u32[]{:S(2)}) %collective-permute-start.14) | collective-permute-done | bytes 262176 | tf_op jit(solution)/shard_map/ppermute | solution.py:383
  92.4 3.1 %join_after.5 = bf16[2304,512]{1,0:T(8,128)(2,1)} custom-call(bf16[32,1024]{1,0:T(8,128)(2,1)S(1)} %get-tuple-element.32.refs_0_, bf16[576,512]{1,0:T(8,128)(2,1)} %join_after.4.refs_1_, bf16[576,512]{1,0:T(8,128)(2,1)} %collective-permute-done.25.piece_ref.refs_2_, bf16[576,512]{1,0:T(8,128)(2,1)} %collective-permute-done.26.piece_ref.refs_3_, ...), custom_call_target="tpu_custom_call" | custom-call | flops 1024 | bytes 1024 | tf_op jit(solution)/shard_map/join_after/pallas_call | solution.py:199
  102.9 7.2 %collective-permute-done.17.outward_ref = bf16[128,512]{1,0:T(8,128)(2,1)S(1)} collective-permute-done((bf16[128,512]{1,0:T(8,128)(2,1)S(1)}, bf16[128,512]{1,0:T(8,128)(2,1)S(1)}, u32[]{:S(2)}, u32[]{:S(2)}) %collective-permute-start.17) | collective-permute-done | bytes 131104 | tf_op jit(solution)/shard_map/ppermute | solution.py:383
  114.3 2.5 %collective-permute-start.21 = (bf16[32,192]{1,0:T(8,128)(2,1)S(1)}, bf16[32,192]{1,0:T(8,128)(2,1)S(1)}, u32[]{:S(2)}, u32[]{:S(2)}) collective-permute-start(bf16[32,192]{1,0:T(8,128)(2,1)S(1)} %get-tuple-element.40), channel_id=1, source_target_pairs={{0,3},{1,2},{2,1},{3,0},{4,7},{5,6},{6,5},{7,4},{8,11},{9,10},{10,... | collective-permute-start | bytes 36872 | tf_op jit(solution)/shard_map/ppermute | solution.py:43
  116.8 1.9 %collective-permute-start.19 = (bf16[32,192]{1,0:T(8,128)(2,1)S(1)}, bf16[32,192]{1,0:T(8,128)(2,1)S(1)}, u32[]{:S(2)}, u32[]{:S(2)}) collective-permute-start(bf16[32,192]{1,0:T(8,128)(2,1)S(1)} %get-tuple-element.42), channel_id=1, source_target_pairs={{0,1},{1,0},{2,3},{3,2},{4,5},{5,4},{6,7},{7,6},{8,9},{9,8},{10,11... | collective-permute-start | bytes 36872 | tf_op jit(solution)/shard_map/ppermute | solution.py:43
  119.9 1.5 %collective-permute-done.20.a2 = bf16[32,192]{1,0:T(8,128)(2,1)S(1)} collective-permute-done((bf16[32,192]{1,0:T(8,128)(2,1)S(1)}, bf16[32,192]{1,0:T(8,128)(2,1)S(1)}, u32[]{:S(2)}, u32[]{:S(2)}) %collective-permute-start.20) | collective-permute-done | bytes 12320 | tf_op jit(solution)/shard_map/ppermute | solution.py:43
  121.5 4.4 %down.1 = bf16[32,4096]{1,0:T(8,128)(2,1)} custom-call(s32[1]{0:T(128)} %bitcast.6.place_ref, f32[32,1]{1,0:T(8,128)S(1)} %copy-done.16, bf16[32,192]{1,0:T(8,128)(2,1)S(1)} %get-tuple-element.43.a0, bf16[32,192]{1,0:T(8,128)(2,1)S(1)} %collective-permute-done.19.a1, bf16[32,192]{1,0:T(8,128)(2,1)S(1)} %collective-permute-done.20.a2, ...), custom_call_target="tpu_custom_call" | custom-call | flops 1024 | bytes 1024 | tf_op jit(solution)/shard_map/down/pallas_call | solution.py:159
  (116 shorter events, 37.6 us)
Async XLA Ops:
  4.1 6.3 %collective-permute-start.2 = (bf16[144,256]{1,0:T(8,128)(2,1)S(1)}, bf16[144,256]{1,0:T(8,128)(2,1)S(1)}, u32[]{:S(2)}, u32[]{:S(2)}) collective-permute-start(bf16[144,256]{1,0:T(8,128)(2,1)S(1)} %fusion.2.refs_0_.refs_1_), channel_id=1, source_target_pairs={{0,24},{4,28},{8,16},{12,20},{16,8},{20,12},{24,0},{28,4},{1,25},{... | collective-permute-start | bytes 221192 | tf_op jit(solution)/shard_map/ppermute | solution.py:43
  25.3 10.1 %collective-permute-start.4 = (bf16[128,1024]{1,0:T(8,128)(2,1)S(1)}, bf16[128,1024]{1,0:T(8,128)(2,1)S(1)}, u32[]{:S(2)}, u32[]{:S(2)}) collective-permute-start(bf16[128,1024]{1,0:T(8,128)(2,1)S(1)} %get-tuple-element.21.a_ref.after_ref), channel_id=1, source_target_pairs={{0,1},{3,2},{4,5},{7,6},{8,9},{11,10},{12,13},{15,14},{16,17},{19,... | collective-permute-start | bytes 786440 | tf_op jit(solution)/shard_map/ppermute | solution.py:374
  28.8 13.8 %collective-permute-start.24 = (bf16[192,512]{1,0:T(8,128)(2,1)S(1)}, bf16[192,512]{1,0:T(8,128)(2,1)S(1)}, u32[]{:S(2)}, u32[]{:S(2)}) collective-permute-start(bf16[192,512]{1,0:T(8,128)(2,1)S(1)} %shard_after.1.after_ref), channel_id=1, source_target_pairs={{0,3},{1,2},{2,1},{3,0},{4,7},{5,6},{6,5},{7,4},{8,11},{9,10},{10,... | collective-permute-start | bytes 589832 | tf_op jit(solution)/shard_map/ppermute | solution.py:43
  31.3 17.1 %collective-permute-start.23 = (bf16[192,512]{1,0:T(8,128)(2,1)S(1)}, bf16[192,512]{1,0:T(8,128)(2,1)S(1)}, u32[]{:S(2)}, u32[]{:S(2)}) collective-permute-start(bf16[192,512]{1,0:T(8,128)(2,1)S(1)} %shard_after.1.after_ref), channel_id=1, source_target_pairs={{0,2},{1,3},{2,0},{3,1},{4,6},{5,7},{6,4},{7,5},{8,10},{9,11},{10,... | collective-permute-start | bytes 589832 | tf_op jit(solution)/shard_map/ppermute | solution.py:43
  31.3 17.1 %collective-permute-start.22 = (bf16[192,512]{1,0:T(8,128)(2,1)S(1)}, bf16[192,512]{1,0:T(8,128)(2,1)S(1)}, u32[]{:S(2)}, u32[]{:S(2)}) collective-permute-start(bf16[192,512]{1,0:T(8,128)(2,1)S(1)} %shard_after.1.after_ref), channel_id=1, source_target_pairs={{0,1},{1,0},{2,3},{3,2},{4,5},{5,4},{6,7},{7,6},{8,9},{9,8},{10,11... | collective-permute-start | bytes 589832 | tf_op jit(solution)/shard_map/ppermute | solution.py:43
  33.2 22.4 %collective-permute-start.6 = (bf16[128,1024]{1,0:T(8,128)(2,1)S(1)}, bf16[128,1024]{1,0:T(8,128)(2,1)S(1)}, u32[]{:S(2)}, u32[]{:S(2)}) collective-permute-start(bf16[128,1024]{1,0:T(8,128)(2,1)S(1)} %get-tuple-element.22.a_ref), channel_id=1, source_target_pairs={{0,1},{3,2},{4,5},{7,6},{8,9},{11,10},{12,13},{15,14},{16,17},{19,... | collective-permute-start | bytes 786440 | tf_op jit(solution)/shard_map/ppermute | solution.py:374
  35.4 21.0 %collective-permute-start.5 = (bf16[128,1024]{1,0:T(8,128)(2,1)S(1)}, bf16[128,1024]{1,0:T(8,128)(2,1)S(1)}, u32[]{:S(2)}, u32[]{:S(2)}) collective-permute-start(bf16[128,1024]{1,0:T(8,128)(2,1)S(1)} %add_after.10.after_ref.a_ref.refs_0_), channel_id=1, source_target_pairs={{1,2},{2,1},{5,6},{6,5},{9,10},{10,9},{13,14},{14,13},{17,18},{18,... | collective-permute-start | bytes 786440 | tf_op jit(solution)/shard_map/ppermute | solution.py:380
  49.3 28.4 %collective-permute-start.26 = (bf16[576,512]{1,0:T(8,128)(2,1)}, bf16[576,512]{1,0:T(8,128)(2,1)}, u32[]{:S(2)}, u32[]{:S(2)}) collective-permute-start(bf16[576,512]{1,0:T(8,128)(2,1)} %join_after.4.refs_1_), channel_id=1, source_target_pairs={{0,16},{4,20},{8,24},{12,28},{16,0},{20,4},{24,8},{28,12},{1,17},{... | collective-permute-start | bytes 1769480 | tf_op jit(solution)/shard_map/ppermute | solution.py:43
  50.9 28.8 %collective-permute-start.25 = (bf16[576,512]{1,0:T(8,128)(2,1)}, bf16[576,512]{1,0:T(8,128)(2,1)}, u32[]{:S(2)}, u32[]{:S(2)}) collective-permute-start(bf16[576,512]{1,0:T(8,128)(2,1)} %join_after.4.refs_1_), channel_id=1, source_target_pairs={{0,8},{4,12},{8,0},{12,4},{16,24},{20,28},{24,16},{28,20},{1,9},{5... | collective-permute-start | bytes 1769480 | tf_op jit(solution)/shard_map/ppermute | solution.py:43
  51.4 8.7 %collective-permute-start.10 = (bf16[128,1024]{1,0:T(8,128)(2,1)S(1)}, bf16[128,1024]{1,0:T(8,128)(2,1)S(1)}, u32[]{:S(2)}, u32[]{:S(2)}) collective-permute-start(bf16[128,1024]{1,0:T(8,128)(2,1)S(1)} %get-tuple-element.24.a_ref), channel_id=1, source_target_pairs={{0,1},{3,2},{4,5},{7,6},{8,9},{11,10},{12,13},{15,14},{16,17},{19,... | collective-permute-start | bytes 786440 | tf_op jit(solution)/shard_map/ppermute | solution.py:374
  55.7 9.5 %collective-permute-start.9 = (bf16[128,1024]{1,0:T(8,128)(2,1)S(1)}, bf16[128,1024]{1,0:T(8,128)(2,1)S(1)}, u32[]{:S(2)}, u32[]{:S(2)}) collective-permute-start(bf16[128,1024]{1,0:T(8,128)(2,1)S(1)} %add_after.11.after_ref.a_ref), channel_id=1, source_target_pairs={{1,2},{2,1},{5,6},{6,5},{9,10},{10,9},{13,14},{14,13},{17,18},{18,... | collective-permute-start | bytes 786440 | tf_op jit(solution)/shard_map/ppermute | solution.py:380
  57.2 16.7 %collective-permute-start.7 = (bf16[128,1024]{1,0:T(8,128)(2,1)}, bf16[128,1024]{1,0:T(8,128)(2,1)}, u32[]{:S(2)}, u32[]{:S(2)}) collective-permute-start(bf16[128,1024]{1,0:T(8,128)(2,1)} %add_after.12.after_ref.total_ref), channel_id=1, source_target_pairs={{1,0},{2,3},{5,4},{6,7},{9,8},{10,11},{13,12},{14,15},{17,16},{18,... | collective-permute-start | bytes 786440 | tf_op jit(solution)/shard_map/ppermute | solution.py:383
  60.1 9.1 %collective-permute-start.8 = (bf16[128,512]{1,0:T(8,128)(2,1)}, bf16[128,512]{1,0:T(8,128)(2,1)}, u32[]{:S(2)}, u32[]{:S(2)}) collective-permute-start(bf16[128,512]{1,0:T(8,128)(2,1)} %get-tuple-element.23.a_ref), channel_id=1, source_target_pairs={{0,1},{3,2},{4,5},{7,6},{8,9},{11,10},{12,13},{15,14},{16,17},{19,... | collective-permute-start | bytes 393224 | tf_op jit(solution)/shard_map/ppermute | solution.py:374
  65.9 16.2 %collective-permute-start.12 = (bf16[128,1024]{1,0:T(8,128)(2,1)S(1)}, bf16[128,1024]{1,0:T(8,128)(2,1)}, u32[]{:S(2)}, u32[]{:S(2)}) collective-permute-start(bf16[128,1024]{1,0:T(8,128)(2,1)S(1)} %add_after.13.after_ref.a_ref), channel_id=1, source_target_pairs={{1,2},{2,1},{5,6},{6,5},{9,10},{10,9},{13,14},{14,13},{17,18},{18,... | collective-permute-start | bytes 786440 | tf_op jit(solution)/shard_map/ppermute | solution.py:380
  69.2 12.9 %collective-permute-start.13 = (bf16[128,512]{1,0:T(8,128)(2,1)}, bf16[128,512]{1,0:T(8,128)(2,1)S(1)}, u32[]{:S(2)}, u32[]{:S(2)}) collective-permute-start(bf16[128,512]{1,0:T(8,128)(2,1)} %copy-done.12), channel_id=1, source_target_pairs={{0,1},{3,2},{4,5},{7,6},{8,9},{11,10},{12,13},{15,14},{16,17},{19,... | collective-permute-start | bytes 393224 | tf_op jit(solution)/shard_map/ppermute | solution.py:374
  73.9 11.3 %collective-permute-start.11 = (bf16[128,1024]{1,0:T(8,128)(2,1)S(1)}, bf16[128,1024]{1,0:T(8,128)(2,1)S(1)}, u32[]{:S(2)}, u32[]{:S(2)}) collective-permute-start(bf16[128,1024]{1,0:T(8,128)(2,1)S(1)} %add_after.14.after_ref.total_ref), channel_id=1, source_target_pairs={{1,0},{2,3},{5,4},{6,7},{9,8},{10,11},{13,12},{14,15},{17,16},{18,... | collective-permute-start | bytes 786440 | tf_op jit(solution)/shard_map/ppermute | solution.py:383
  78.8 13.6 %collective-permute-start.28 = (bf16[288,512]{1,0:T(8,128)(2,1)S(1)}, bf16[288,512]{1,0:T(8,128)(2,1)S(1)}, u32[]{:S(2)}, u32[]{:S(2)}) collective-permute-start(bf16[288,512]{1,0:T(8,128)(2,1)S(1)} %half_after.3), channel_id=1, source_target_pairs={{0,8},{4,12},{8,0},{12,4},{16,24},{20,28},{24,16},{28,20},{1,9},{5... | collective-permute-start | bytes 884744 | tf_op jit(solution)/shard_map/ppermute | solution.py:43
  80.7 11.7 %collective-permute-start.27 = (bf16[288,512]{1,0:T(8,128)(2,1)S(1)}, bf16[288,512]{1,0:T(8,128)(2,1)S(1)}, u32[]{:S(2)}, u32[]{:S(2)}) collective-permute-start(bf16[288,512]{1,0:T(8,128)(2,1)S(1)} %half_after.2), channel_id=1, source_target_pairs={{0,16},{4,20},{8,24},{12,28},{16,0},{20,4},{24,8},{28,12},{1,17},{... | collective-permute-start | bytes 884744 | tf_op jit(solution)/shard_map/ppermute | solution.py:43
  83.2 8.3 %collective-permute-start.14 = (bf16[128,1024]{1,0:T(8,128)(2,1)S(1)}, bf16[128,1024]{1,0:T(8,128)(2,1)S(1)}, u32[]{:S(2)}, u32[]{:S(2)}) collective-permute-start(bf16[128,1024]{1,0:T(8,128)(2,1)S(1)} %add_after.17.refs_0_.total_ref), channel_id=1, source_target_pairs={{1,0},{2,3},{5,4},{6,7},{9,8},{10,11},{13,12},{14,15},{17,16},{18,... | collective-permute-start | bytes 786440 | tf_op jit(solution)/shard_map/ppermute | solution.py:383
  95.5 26.0 %collective-permute-start.29 = (bf16[2304,512]{1,0:T(8,128)(2,1)}, bf16[2304,512]{1,0:T(8,128)(2,1)}, u32[]{:S(2)}, u32[]{:S(2)}) collective-permute-start(bf16[2304,512]{1,0:T(8,128)(2,1)} %join_after.5), channel_id=1, source_target_pairs={{0,4},{4,0},{8,12},{12,8},{16,20},{20,16},{24,28},{28,24},{1,5},{5... | collective-permute-start | bytes 7077896 | tf_op jit(solution)/shard_map/ppermute | solution.py:43
  99.5 10.6 %collective-permute-start.17 = (bf16[128,512]{1,0:T(8,128)(2,1)S(1)}, bf16[128,512]{1,0:T(8,128)(2,1)S(1)}, u32[]{:S(2)}, u32[]{:S(2)}) collective-permute-start(bf16[128,512]{1,0:T(8,128)(2,1)S(1)} %add_after.18.after_ref.total_ref), channel_id=1, source_target_pairs={{1,0},{2,3},{5,4},{6,7},{9,8},{10,11},{13,12},{14,15},{17,16},{18,... | collective-permute-start | bytes 393224 | tf_op jit(solution)/shard_map/ppermute | solution.py:383
  100.8 12.6 %collective-permute-start.18 = (bf16[128,512]{1,0:T(8,128)(2,1)S(1)}, bf16[128,512]{1,0:T(8,128)(2,1)S(1)}, u32[]{:S(2)}, u32[]{:S(2)}) collective-permute-start(bf16[128,512]{1,0:T(8,128)(2,1)S(1)} %add_after.19.refs_0_.total_ref), channel_id=1, source_target_pairs={{1,0},{2,3},{5,4},{6,7},{9,8},{10,11},{13,12},{14,15},{17,16},{18,... | collective-permute-start | bytes 393224 | tf_op jit(solution)/shard_map/ppermute | solution.py:383
  114.3 5.6 %collective-permute-start.21 = (bf16[32,192]{1,0:T(8,128)(2,1)S(1)}, bf16[32,192]{1,0:T(8,128)(2,1)S(1)}, u32[]{:S(2)}, u32[]{:S(2)}) collective-permute-start(bf16[32,192]{1,0:T(8,128)(2,1)S(1)} %get-tuple-element.40), channel_id=1, source_target_pairs={{0,3},{1,2},{2,1},{3,0},{4,7},{5,6},{6,5},{7,4},{8,11},{9,10},{10,... | collective-permute-start | bytes 36872 | tf_op jit(solution)/shard_map/ppermute | solution.py:43
  116.8 4.6 %collective-permute-start.20 = (bf16[32,192]{1,0:T(8,128)(2,1)S(1)}, bf16[32,192]{1,0:T(8,128)(2,1)S(1)}, u32[]{:S(2)}, u32[]{:S(2)}) collective-permute-start(bf16[32,192]{1,0:T(8,128)(2,1)S(1)} %get-tuple-element.41), channel_id=1, source_target_pairs={{0,2},{1,3},{2,0},{3,1},{4,6},{5,7},{6,4},{7,5},{8,10},{9,11},{10,... | collective-permute-start | bytes 36872 | tf_op jit(solution)/shard_map/ppermute | solution.py:43
  (27 other events, 174.5 us)

commit v3 on v2

--- a/solution.py
+++ b/solution.py
@@ -13,7 +13,7 @@
 HEAD_DIM = 128
 HID_SPLIT = 4
 STACK = 4
-WIDTHS = (1024, 1024, 1024, 512, 512)
+WIDTHS = (896, 896, 768, 768, 768)
 SPANS = tuple((sum(WIDTHS[:i]), width) for i, width in enumerate(WIDTHS))
 PAD_ROWS = 16
 ORDER = (
@@ -43,7 +43,7 @@
     return lax.ppermute(value, axis, [(i, i ^ offset) for i in range(size)])
 
 
-def attend_kernel(rank_ref, bound_ref, same_ref, other_ref, q_hbm, resid_hbm, w_hbm, after_ref, *refs):
+def attend_kernel(rank_ref, bound_ref, same_ref, other_ref, q_hbm, resid_hbm, w_hbm, *refs):
     outs = refs[: len(WIDTHS)]
     q_ref, resid_ref, w_buf, k_buf, v_buf, bias, attended, acc, sems, side = refs[len(WIDTHS) :]
     tok = q_ref.shape[0]
@@ -110,13 +110,13 @@
         outs[chunk][...] = acc[:, span].astype(jnp.bfloat16)
 
 
-def attend_project(rank, bounds, same, other, queries, residual, w_out, after):
+def attend_project(rank, bounds, same, other, queries, residual, w_out):
     tok, width = queries.shape
     keys_in_all = 2 * same.shape[0] * tok
     return pl.pallas_call(
         attend_kernel,
         out_shape=[jax.ShapeDtypeStruct((tok, w), jnp.bfloat16) for w in WIDTHS],
-        in_specs=[pl.BlockSpec(memory_space=pltpu.SMEM)] + [VMEM] * 3 + [ANY] * 4,
+        in_specs=[pl.BlockSpec(memory_space=pltpu.SMEM)] + [VMEM] * 3 + [ANY] * 3,
         out_specs=[VMEM] * len(WIDTHS),
         scratch_shapes=[
             pltpu.VMEM(queries.shape, jnp.bfloat16),
@@ -130,58 +130,39 @@
             pltpu.SemaphoreType.DMA((len(WIDTHS),)),
             pltpu.SemaphoreType.DMA((2,)),
         ],
-        compiler_params=pltpu.CompilerParams(vmem_limit_bytes=36 * 1024 * 1024),
+        compiler_params=pltpu.CompilerParams(vmem_limit_bytes=40 * 1024 * 1024),
         cost_estimate=LIGHT,
         name="attend_project",
-    )(rank, bounds, same, other, queries, residual, w_out, after)
-
-
-def down_kernel(place_ref, coef_ref, a0, a1, a2, a3, own_ref, same_ref, other_ref, out_ref):
+    )(rank, bounds, same, other, queries, residual, w_out)
+
+
+def down_kernel(rank_ref, coef_ref, a0, a1, a2, a3, back_ref, out_ref):
+    count, _, width = back_ref.shape
     coef = coef_ref[...]
     blended = [(a[...].astype(jnp.float32) * coef).astype(jnp.bfloat16) for a in (a0, a1, a2, a3)]
-    hidden = own_ref.shape[0]
-    count, _, width = same_ref.shape
-    for group, buf in enumerate((same_ref, other_ref)):
-        for j in range(count):
-            block = place_ref[0] ^ (2 * j + group)
-            span = pl.ds(pl.multiple_of(block * width, width), width)
-            total = jnp.dot(blended[0], own_ref[:, span], preferred_element_type=jnp.float32)
-            for s in range(1, len(blended)):
-                rows = slice((s - 1) * hidden, s * hidden)
-                total += jnp.dot(
-                    blended[s], buf[j, rows, :], preferred_element_type=jnp.float32
-                )
-            out_ref[:, span] = total.astype(jnp.bfloat16)
-
-
-def down(place, coefficient, acts, own, same, other):
+    hidden = blended[0].shape[1]
+    for block in range(count):
+        total = None
+        for s in range(len(blended)):
+            rows = pl.ds(pl.multiple_of((rank_ref[0] ^ s) * hidden, hidden), hidden)
+            term = jnp.dot(
+                blended[s], back_ref[block, rows, :], preferred_element_type=jnp.float32
+            )
+            total = term if total is None else total + term
+        out_ref[:, block * width : (block + 1) * width] = total.astype(jnp.bfloat16)
+
+
+def down(rank, coefficient, acts, back):
     rows = acts[0].shape[0]
     return pl.pallas_call(
         down_kernel,
         out_shape=jax.ShapeDtypeStruct((rows, D), jnp.bfloat16),
-        in_specs=[pl.BlockSpec(memory_space=pltpu.SMEM)] + [VMEM] * 8,
+        in_specs=[pl.BlockSpec(memory_space=pltpu.SMEM)] + [VMEM] * 6,
         out_specs=VMEM,
-        compiler_params=pltpu.CompilerParams(vmem_limit_bytes=24 * 1024 * 1024),
+        compiler_params=pltpu.CompilerParams(vmem_limit_bytes=12 * 1024 * 1024),
         cost_estimate=LIGHT,
         name="down",
-    )(place, coefficient, *acts, own, same, other)
-
-
-def half_kernel(first, after_ref, piece_ref, out_ref):
-    out_ref[...] = piece_ref[first : first + out_ref.shape[0], :]
-
-
-def half_after(piece, first, after):
-    shape = (piece.shape[0] // 2, piece.shape[1])
-    return pl.pallas_call(
-        functools.partial(half_kernel, first),
-        out_shape=jax.ShapeDtypeStruct(shape, jnp.bfloat16),
-        in_specs=[ANY, VMEM],
-        out_specs=VMEM,
-        compiler_params=pltpu.CompilerParams(vmem_limit_bytes=4 * 1024 * 1024),
-        cost_estimate=LIGHT,
-        name="half_after",
-    )(after, piece)
+    )(rank, coefficient, *acts, back)
 
 
 def join_kernel(*refs):
@@ -205,27 +186,6 @@
         cost_estimate=LIGHT,
         name="join_after",
     )(after, *pieces)
-
-
-def shard_kernel(place_ref, whole_hbm, after_ref, out_ref, sem):
-    width = out_ref.shape[1]
-    first = pl.multiple_of(place_ref[0] * width, width)
-    copy = pltpu.make_async_copy(whole_hbm.at[:, pl.ds(first, width)], out_ref, sem)
-    copy.start()
-    copy.wait()
-
-
-def shard_after(place, whole, width, after):
-    return pl.pallas_call(
-        shard_kernel,
-        out_shape=jax.ShapeDtypeStruct((whole.shape[0], width), jnp.bfloat16),
-        in_specs=[pl.BlockSpec(memory_space=pltpu.SMEM), ANY, ANY],
-        out_specs=VMEM,
-        scratch_shapes=[pltpu.SemaphoreType.DMA],
-        compiler_params=pltpu.CompilerParams(vmem_limit_bytes=4 * 1024 * 1024),
-        cost_estimate=LIGHT,
-        name="shard_after",
-    )(place, whole, after)
 
 
 def add_kernel(a_ref, b_ref, after_ref, out_ref):
@@ -351,10 +311,10 @@
     )
     same_keys = same_rows.reshape(ctx_count // 2, tok + PAD_ROWS, 2 * HEAD_DIM)
     other_keys = exchange(same_rows, "ctx", 1, ctx_count).reshape(same_keys.shape)
-    places = place.astype(jnp.int32).reshape(1)
     flat_back = w_back.reshape(hidden, D)
-    mine = shard_after(places, flat_back, D // ctx_count, same_rows)
-    planes = [exchange(mine, "exp", s, exp_count) for s in range(1, exp_count)]
+    mine = lax.dynamic_slice_in_dim(flat_back, place * (D // ctx_count), D // ctx_count, 1)
+    all_back = lax.all_gather(mine, ("ctx", "exp"), axis=0, tiled=True)
+    all_back = all_back.reshape(ctx_count, exp_count * hidden, D // ctx_count)
 
     parts = attend_project(
         rank.astype(jnp.int32).reshape(1),
@@ -364,7 +324,6 @@
         queries,
         residual,
         w_out,
-        mine,
     )
     at_end = (rank == 0) | (rank == exp_count - 1)
     flags = jnp.stack([rank, at_end]).astype(jnp.int32)
@@ -387,14 +346,6 @@
             )
             homes.append(own)
             after = states[0]
-    planes = join_after(planes, near[0])
-    from_x = exchange(planes, "ctx", 2, ctx_count)
-    from_y = exchange(planes, "ctx", 4, ctx_count)
-    upper = exchange(half_after(from_x, 0, homes[0]), "ctx", 4, ctx_count)
-    lower = exchange(half_after(from_y, planes.shape[0] // 2, homes[0]), "ctx", 2, ctx_count)
-    same_rows = join_after([planes, from_x, from_y, upper, lower], homes[2])
-    same_back = same_rows.reshape(ctx_count // 2, planes.shape[0], planes.shape[1])
-    other_back = exchange(same_rows, "ctx", 1, ctx_count).reshape(same_back.shape)
     middle_out = jnp.concatenate(homes, axis=1)
     activated = states[0]
     acts = [lax.dynamic_slice_in_dim(activated, rank * home, home, 0)]
@@ -404,7 +355,7 @@
     shares = gates / jnp.sum(gates, axis=1, keepdims=True)
     coefficient = jnp.sum(jnp.where(routes == 0, shares, 0.0), axis=1, keepdims=True)
     coefficient = coefficient.astype(jnp.bfloat16).astype(jnp.float32)
-    expert_out = down(places, coefficient, acts, flat_back, same_back, other_back)
+    expert_out = down(flags, coefficient, acts, all_back)
     return (middle_out, expert_out)
 
 

time: 127 us -> 134 us (1.055)
  waiting for transfers between devices: 32.7 us -> 47.7 us
  between operations: 3.89 us -> 17 us
  starting transfers between devices: 47.7 us -> 36.2 us
  Pallas kernels: 28 us -> 20.3 us
  other arithmetic: 3.35 us -> 0.79 us
    ppermute x5, waiting for transfers between devices: 1.71 us -> 26.9 us  [line_device(): inward = [lax.ppermute(part, 'exp', [(0, 1), (3, 2)]) for part in parts]]
    ppermute x15 -> x7, waiting for transfers between devices: 19.3 us -> 10.3 us  [exchange(): return lax.ppermute(value, axis, [(i, i ^ offset) for i in range(size)])]
    ppermute x15 -> x7, starting transfers between devices: 17.8 us -> 9.06 us  [exchange(): return lax.ppermute(value, axis, [(i, i ^ offset) for i in range(size)])]
    pallas_call x3 -> x1, Pallas kernels: 3.94 us -> 0.02 us  [join_after(): pl.pallas_call(join_kernel, out_shape=jax.ShapeDtypeStruct((rows, width),...]
    ppermute x5, starting transfers between devices: 19.4 us -> 16.6 us  [line_device(): inward = [lax.ppermute(part, 'exp', [(0, 1), (3, 2)]) for part in parts]]
    pallas_call x3 -> x0, Pallas kernels: 2.21 us -> none  [the longest x2 2.17 us: half_after(): pl.pallas_call(functools.partial(half_kernel, first), out_shape=jax.Shape...]
    pallas_call x1, Pallas kernels: 4.4 us -> 2.56 us  [down(): pl.pallas_call(down_kernel, out_shape=jax.ShapeDtypeStruct((rows, D), jnp...]
    unnamed x46 -> x28, local copies, waits for them, and re-layouts: 7.94 us -> 9.02 us
  transfers between devices with their start and end apart: 30 -> 23, of which waited for: 11 -> 14; matrix products, arithmetic and copies ran while one was open for 5% -> 1% of each run, Pallas kernels for 9% -> 13%
where the time goes in v3:
time: 134 us; the launch traced here: 133 us
  waiting for transfers between devices  47.7 us (36%)
  starting transfers between devices  36.2 us (27%)
  Pallas kernels  20.3 us (15%)
  between operations  17 us (13%)
  local copies, waits for them, and re-layouts  10.7 us (8%)
    ppermute x5, waiting for transfers between devices, line_device(): inward = [lax.ppermute(part, 'exp', [(0, 1), (3, 2)]) for part in parts]  26.9 us
    ppermute x5, starting transfers between devices, line_device(): inward = [lax.ppermute(part, 'exp', [(0, 1), (3, 2)]) for part in parts]  16.6 us
    ppermute x5, waiting for transfers between devices, line_device(): outward[chunk] = lax.ppermute(total[chunk], 'exp', [(1, 0), (2, 3)])  10.5 us
    ppermute x7, waiting for transfers between devices, exchange(): return lax.ppermute(value, axis, [(i, i ^ offset) for i in range(size)])  10.3 us
    pallas_call x1, Pallas kernels, attend_project(): pl.pallas_call(attend_kernel, out_shape=[jax.ShapeDtypeStruct((tok, w), j...  9.81 us
    ppermute x7, starting transfers between devices, exchange(): return lax.ppermute(value, axis, [(i, i ^ offset) for i in range(size)])  9.06 us
    unnamed x28, local copies, waits for them, and re-layouts  9.02 us
    ppermute x5, starting transfers between devices, line_device(): outward[chunk] = lax.ppermute(total[chunk], 'exp', [(1, 0), (2, 3)])  6.46 us
  transfers between devices with their start and end apart: 23, of which 14 were waited for; matrix products, arithmetic and copies ran while one was open for 1% of the time, Pallas kernels for 13%

profile of v3, /device:TPU:0, one launch (start us, length us, event | category | flops | bytes accessed | tf_op | source)
XLA Modules:
  0.0 132.8 jit_solution(6215634854984715055)
XLA Ops:
  7.2 1.3 %copy-done = bf16[1,192,4096]{2,1,0:T(8,128)(2,1)S(1)} copy-done((bf16[1,192,4096]{2,1,0:T(8,128)(2,1)S(1)}, bf16[1,192,4096]{2,1,0:T(8,128)(2,1)}, u32[]{:S(2)}) %copy-start) | copy-done | bytes 1572888
  12.7 3.0 %collective-permute-start = (bf16[144,256]{1,0:T(8,128)(2,1)S(1)}, bf16[144,256]{1,0:T(8,128)(2,1)S(1)}, u32[]{:S(2)}, u32[]{:S(2)}) collective-permute-start(bf16[144,256]{1,0:T(8,128)(2,1)S(1)} %fusion.2.refs_0_.refs_1_), channel_id=1, source_target_pairs={{0,8},{4,12},{8,0},{12,4},{16,24},{20,28},{24,16},{28,20},{1,9},{5... | collective-permute-start | bytes 221192 | tf_op jit(solution)/shard_map/ppermute | solution.py:43
  15.7 1.5 %collective-permute-start.1 = (bf16[144,256]{1,0:T(8,128)(2,1)S(1)}, bf16[144,256]{1,0:T(8,128)(2,1)S(1)}, u32[]{:S(2)}, u32[]{:S(2)}) collective-permute-start(bf16[144,256]{1,0:T(8,128)(2,1)S(1)} %fusion.2.refs_0_.refs_1_), channel_id=1, source_target_pairs={{0,16},{4,20},{8,24},{12,28},{16,0},{20,4},{24,8},{28,12},{1,17},{... | collective-permute-start | bytes 221192 | tf_op jit(solution)/shard_map/ppermute | solution.py:43
  18.2 1.8 %collective-permute-done.1.refs_3_ = bf16[144,256]{1,0:T(8,128)(2,1)S(1)} collective-permute-done((bf16[144,256]{1,0:T(8,128)(2,1)S(1)}, bf16[144,256]{1,0:T(8,128)(2,1)S(1)}, u32[]{:S(2)}, u32[]{:S(2)}) %collective-permute-start.1) | collective-permute-done | bytes 73760 | tf_op jit(solution)/shard_map/ppermute | solution.py:43
  20.1 2.4 %collective-permute-done.2.refs_4_ = bf16[144,256]{1,0:T(8,128)(2,1)S(1)} collective-permute-done((bf16[144,256]{1,0:T(8,128)(2,1)S(1)}, bf16[144,256]{1,0:T(8,128)(2,1)S(1)}, u32[]{:S(2)}, u32[]{:S(2)}) %collective-permute-start.2) | collective-permute-done | bytes 73760 | tf_op jit(solution)/shard_map/ppermute | solution.py:43
  26.2 9.8 %attend_project.1 = (bf16[128,896]{1,0:T(8,128)(2,1)S(1)}, bf16[128,896]{1,0:T(8,128)(2,1)S(1)}, bf16[128,768]{1,0:T(8,128)(2,1)S(1)}, bf16[128,768]{1,0:T(8,128)(2,1)}, bf16[128,768]{1,0:T(8,128)(2,1)S(1)}) custom-call(s32[1]{0:T(128)} %bitcast.rank_ref, f32[128,1]{1,0:T(8,128)S(1)} %copy.14.bound_ref, bf16[4,144,256]{2,1,0:T(8,128)(2,1)S(1)} %bitcast.20, ...), custom_call_target="tpu_custom_call" | custom-call | flops 1024 | bytes 1024 | tf_op jit(solution)/shard_map/attend_project/pallas_call | solution.py:116
  36.0 3.6 %collective-permute-start.4 = (bf16[128,896]{1,0:T(8,128)(2,1)S(1)}, bf16[128,896]{1,0:T(8,128)(2,1)S(1)}, u32[]{:S(2)}, u32[]{:S(2)}) collective-permute-start(bf16[128,896]{1,0:T(8,128)(2,1)S(1)} %get-tuple-element.21.a_ref.after_ref), channel_id=1, source_target_pairs={{0,1},{3,2},{4,5},{7,6},{8,9},{11,10},{12,13},{15,14},{16,17},{19,... | collective-permute-start | bytes 688136 | tf_op jit(solution)/shard_map/ppermute | solution.py:333
  39.6 1.3 collective-permute-start.6
  40.9 9.3 %collective-permute-done.4.b_ref = bf16[128,896]{1,0:T(8,128)(2,1)S(1)} collective-permute-done((bf16[128,896]{1,0:T(8,128)(2,1)S(1)}, bf16[128,896]{1,0:T(8,128)(2,1)S(1)}, u32[]{:S(2)}, u32[]{:S(2)}) %collective-permute-start.4) | collective-permute-done | bytes 229408 | tf_op jit(solution)/shard_map/ppermute | solution.py:333
  51.0 6.6 %collective-permute-done.6.b_ref = bf16[128,896]{1,0:T(8,128)(2,1)S(1)} collective-permute-done((bf16[128,896]{1,0:T(8,128)(2,1)S(1)}, bf16[128,896]{1,0:T(8,128)(2,1)S(1)}, u32[]{:S(2)}, u32[]{:S(2)}) %collective-permute-start.6) | collective-permute-done | bytes 229408 | tf_op jit(solution)/shard_map/ppermute | solution.py:333
  58.4 8.4 %collective-permute-start.10 = (bf16[128,768]{1,0:T(8,128)(2,1)S(1)}, bf16[128,768]{1,0:T(8,128)(2,1)}, u32[]{:S(2)}, u32[]{:S(2)}) collective-permute-start(bf16[128,768]{1,0:T(8,128)(2,1)S(1)} %get-tuple-element.24.a_ref), channel_id=1, source_target_pairs={{0,1},{3,2},{4,5},{7,6},{8,9},{11,10},{12,13},{15,14},{16,17},{19,... | collective-permute-start | bytes 589832 | tf_op jit(solution)/shard_map/ppermute | solution.py:333
  66.7 2.0 %collective-permute-start.8 = (bf16[128,768]{1,0:T(8,128)(2,1)}, bf16[128,768]{1,0:T(8,128)(2,1)}, u32[]{:S(2)}, u32[]{:S(2)}) collective-permute-start(bf16[128,768]{1,0:T(8,128)(2,1)} %get-tuple-element.23.a_ref), channel_id=1, source_target_pairs={{0,1},{3,2},{4,5},{7,6},{8,9},{11,10},{12,13},{15,14},{16,17},{19,... | collective-permute-start | bytes 589832 | tf_op jit(solution)/shard_map/ppermute | solution.py:333
  68.8 1.3 collective-permute-start.13
  71.5 4.1 %collective-permute-done.10.b_ref = bf16[128,768]{1,0:T(8,128)(2,1)} collective-permute-done((bf16[128,768]{1,0:T(8,128)(2,1)S(1)}, bf16[128,768]{1,0:T(8,128)(2,1)}, u32[]{:S(2)}, u32[]{:S(2)}) %collective-permute-start.10) | collective-permute-done | bytes 196640 | tf_op jit(solution)/shard_map/ppermute | solution.py:333
  77.4 1.4 %collective-permute-start.12 = (bf16[128,768]{1,0:T(8,128)(2,1)S(1)}, bf16[128,768]{1,0:T(8,128)(2,1)}, u32[]{:S(2)}, u32[]{:S(2)}) collective-permute-start(bf16[128,768]{1,0:T(8,128)(2,1)S(1)} %add_after.13.after_ref.a_ref), channel_id=1, source_target_pairs={{1,2},{2,1},{5,6},{6,5},{9,10},{10,9},{13,14},{14,13},{17,18},{18,... | collective-permute-start | bytes 589832 | tf_op jit(solution)/shard_map/ppermute | solution.py:339
  80.1 3.9 %collective-permute-done.8.b_ref = bf16[128,768]{1,0:T(8,128)(2,1)} collective-permute-done((bf16[128,768]{1,0:T(8,128)(2,1)}, bf16[128,768]{1,0:T(8,128)(2,1)}, u32[]{:S(2)}, u32[]{:S(2)}) %collective-permute-start.8) | collective-permute-done | bytes 196640 | tf_op jit(solution)/shard_map/ppermute | solution.py:333
  86.0 1.9 %copy-done.1 = bf16[1,384,4096]{2,1,0:T(8,128)(2,1)S(1)} copy-done((bf16[1,384,4096]{2,1,0:T(8,128)(2,1)S(1)}, bf16[1,384,4096]{2,1,0:T(8,128)(2,1)}, u32[]{:S(2)}) %copy-start.1) | copy-done | bytes 3145752
  88.8 3.0 %collective-permute-done.13.b_ref = bf16[128,768]{1,0:T(8,128)(2,1)S(1)} collective-permute-done((bf16[128,768]{1,0:T(8,128)(2,1)S(1)}, bf16[128,768]{1,0:T(8,128)(2,1)S(1)}, u32[]{:S(2)}, u32[]{:S(2)}) %collective-permute-start.13) | collective-permute-done | bytes 196640 | tf_op jit(solution)/shard_map/ppermute | solution.py:333
  98.5 6.1 %collective-permute-done.14.outward_ref = bf16[128,768]{1,0:T(8,128)(2,1)S(1)} collective-permute-done((bf16[128,768]{1,0:T(8,128)(2,1)S(1)}, bf16[128,768]{1,0:T(8,128)(2,1)S(1)}, u32[]{:S(2)}, u32[]{:S(2)}) %collective-permute-start.14) | collective-permute-done | bytes 196640 | tf_op jit(solution)/shard_map/ppermute | solution.py:342
  105.5 3.1 %collective-permute-done.17.outward_ref = bf16[128,768]{1,0:T(8,128)(2,1)S(1)} collective-permute-done((bf16[128,768]{1,0:T(8,128)(2,1)S(1)}, bf16[128,768]{1,0:T(8,128)(2,1)S(1)}, u32[]{:S(2)}, u32[]{:S(2)}) %collective-permute-start.17) | collective-permute-done | bytes 196640 | tf_op jit(solution)/shard_map/ppermute | solution.py:342
  111.9 3.2 %collective-permute-start.20 = (bf16[32,192]{1,0:T(8,128)(2,1)S(1)}, bf16[32,192]{1,0:T(8,128)(2,1)S(1)}, u32[]{:S(2)}, u32[]{:S(2)}) collective-permute-start(bf16[32,192]{1,0:T(8,128)(2,1)S(1)} %get-tuple-element.41), channel_id=1, source_target_pairs={{0,2},{1,3},{2,0},{3,1},{4,6},{5,7},{6,4},{7,5},{8,10},{9,11},{10,... | collective-permute-start | bytes 36872 | tf_op jit(solution)/shard_map/ppermute | solution.py:43
  116.7 3.8 %collective-permute-done.21.a3 = bf16[32,192]{1,0:T(8,128)(2,1)S(1)} collective-permute-done((bf16[32,192]{1,0:T(8,128)(2,1)S(1)}, bf16[32,192]{1,0:T(8,128)(2,1)S(1)}, u32[]{:S(2)}, u32[]{:S(2)}) %collective-permute-start.21) | collective-permute-done | bytes 12320 | tf_op jit(solution)/shard_map/ppermute | solution.py:43
  120.6 2.8 %copy-done.3 = bf16[1,6144,512]{2,1,0:T(8,128)(2,1)S(1)} copy-done((bf16[1,6144,512]{2,1,0:T(8,128)(2,1)S(1)}, bf16[1,6144,512]{2,1,0:T(8,128)(2,1)}, u32[]{:S(2)}) %copy-start.3) | copy-done | bytes 6291480
  123.3 2.6 %down.1 = bf16[32,4096]{1,0:T(8,128)(2,1)} custom-call(s32[2]{0:T(128)S(1)} %pad_add_fusion.flag_ref.rank_ref, f32[32,1]{1,0:T(8,128)S(1)} %copy.15.coef_ref, bf16[32,192]{1,0:T(8,128)(2,1)S(1)} %get-tuple-element.43.a0, bf16[32,192]{1,0:T(8,128)(2,1)S(1)} %collective-permute-done.19.a1, bf16[32,192]{1,0:T(8,128)(2,1)S(1)} %collective-permute-done.20.a2, ...), custom_call_target="tpu_custom_call" | custom-call | flops 1024 | bytes 1024 | tf_op jit(solution)/shard_map/down/pallas_call | solution.py:157
  (81 shorter events, 27.5 us)
Async XLA Ops:
  7.2 113.4 %all-gather.3.cloned.1.call-start = ((), (), s32[]{:S(2)}) async-start(), calls=%async_computation | async-start | bytes 6488064 | tf_op jit(solution)/shard_map/all_gather | solution.py:316
  12.7 5.5 %collective-permute-start = (bf16[144,256]{1,0:T(8,128)(2,1)S(1)}, bf16[144,256]{1,0:T(8,128)(2,1)S(1)}, u32[]{:S(2)}, u32[]{:S(2)}) collective-permute-start(bf16[144,256]{1,0:T(8,128)(2,1)S(1)} %fusion.2.refs_0_.refs_1_), channel_id=1, source_target_pairs={{0,8},{4,12},{8,0},{12,4},{16,24},{20,28},{24,16},{28,20},{1,9},{5... | collective-permute-start | bytes 221192 | tf_op jit(solution)/shard_map/ppermute | solution.py:43
  15.7 4.4 %collective-permute-start.1 = (bf16[144,256]{1,0:T(8,128)(2,1)S(1)}, bf16[144,256]{1,0:T(8,128)(2,1)S(1)}, u32[]{:S(2)}, u32[]{:S(2)}) collective-permute-start(bf16[144,256]{1,0:T(8,128)(2,1)S(1)} %fusion.2.refs_0_.refs_1_), channel_id=1, source_target_pairs={{0,16},{4,20},{8,24},{12,28},{16,0},{20,4},{24,8},{28,12},{1,17},{... | collective-permute-start | bytes 221192 | tf_op jit(solution)/shard_map/ppermute | solution.py:43
  17.2 5.3 %collective-permute-start.2 = (bf16[144,256]{1,0:T(8,128)(2,1)S(1)}, bf16[144,256]{1,0:T(8,128)(2,1)S(1)}, u32[]{:S(2)}, u32[]{:S(2)}) collective-permute-start(bf16[144,256]{1,0:T(8,128)(2,1)S(1)} %fusion.2.refs_0_.refs_1_), channel_id=1, source_target_pairs={{0,24},{4,28},{8,16},{12,20},{16,8},{20,12},{24,0},{28,4},{1,25},{... | collective-permute-start | bytes 221192 | tf_op jit(solution)/shard_map/ppermute | solution.py:43
  22.5 1.6 %collective-permute-start.3 = (bf16[576,256]{1,0:T(8,128)(2,1)S(1)}, bf16[576,256]{1,0:T(8,128)(2,1)S(1)}, u32[]{:S(2)}, u32[]{:S(2)}) collective-permute-start(bf16[576,256]{1,0:T(8,128)(2,1)S(1)} %join_after.1), channel_id=1, source_target_pairs={{0,4},{4,0},{8,12},{12,8},{16,20},{20,16},{24,28},{28,24},{1,5},{5... | collective-permute-start | bytes 884744 | tf_op jit(solution)/shard_map/ppermute | solution.py:43
  36.0 50.0 %copy-start.5 = (f32[4096]{0:T(1024)S(1)}, f32[4096]{0:T(1024)}, u32[]{:S(2)}) copy-start(f32[4096]{0:T(1024)} %param.19) | copy-start | bytes 49156
  36.0 14.2 %collective-permute-start.4 = (bf16[128,896]{1,0:T(8,128)(2,1)S(1)}, bf16[128,896]{1,0:T(8,128)(2,1)S(1)}, u32[]{:S(2)}, u32[]{:S(2)}) collective-permute-start(bf16[128,896]{1,0:T(8,128)(2,1)S(1)} %get-tuple-element.21.a_ref.after_ref), channel_id=1, source_target_pairs={{0,1},{3,2},{4,5},{7,6},{8,9},{11,10},{12,13},{15,14},{16,17},{19,... | collective-permute-start | bytes 688136 | tf_op jit(solution)/shard_map/ppermute | solution.py:333
  39.6 18.0 %collective-permute-start.6 = (bf16[128,896]{1,0:T(8,128)(2,1)S(1)}, bf16[128,896]{1,0:T(8,128)(2,1)S(1)}, u32[]{:S(2)}, u32[]{:S(2)}) collective-permute-start(bf16[128,896]{1,0:T(8,128)(2,1)S(1)} %get-tuple-element.22.a_ref), channel_id=1, source_target_pairs={{0,1},{3,2},{4,5},{7,6},{8,9},{11,10},{12,13},{15,14},{16,17},{19,... | collective-permute-start | bytes 688136 | tf_op jit(solution)/shard_map/ppermute | solution.py:333
  50.3 19.8 %collective-permute-start.5 = (bf16[128,896]{1,0:T(8,128)(2,1)S(1)}, bf16[128,896]{1,0:T(8,128)(2,1)S(1)}, u32[]{:S(2)}, u32[]{:S(2)}) collective-permute-start(bf16[128,896]{1,0:T(8,128)(2,1)S(1)} %add_after.10.after_ref.a_ref), channel_id=1, source_target_pairs={{1,2},{2,1},{5,6},{6,5},{9,10},{10,9},{13,14},{14,13},{17,18},{18,... | collective-permute-start | bytes 688136 | tf_op jit(solution)/shard_map/ppermute | solution.py:339
  57.7 21.1 %collective-permute-start.9 = (bf16[128,896]{1,0:T(8,128)(2,1)S(1)}, bf16[128,896]{1,0:T(8,128)(2,1)S(1)}, u32[]{:S(2)}, u32[]{:S(2)}) collective-permute-start(bf16[128,896]{1,0:T(8,128)(2,1)S(1)} %add_after.11.after_ref.a_ref), channel_id=1, source_target_pairs={{1,2},{2,1},{5,6},{6,5},{9,10},{10,9},{13,14},{14,13},{17,18},{18,... | collective-permute-start | bytes 688136 | tf_op jit(solution)/shard_map/ppermute | solution.py:339
  58.4 17.1 %collective-permute-start.10 = (bf16[128,768]{1,0:T(8,128)(2,1)S(1)}, bf16[128,768]{1,0:T(8,128)(2,1)}, u32[]{:S(2)}, u32[]{:S(2)}) collective-permute-start(bf16[128,768]{1,0:T(8,128)(2,1)S(1)} %get-tuple-element.24.a_ref), channel_id=1, source_target_pairs={{0,1},{3,2},{4,5},{7,6},{8,9},{11,10},{12,13},{15,14},{16,17},{19,... | collective-permute-start | bytes 589832 | tf_op jit(solution)/shard_map/ppermute | solution.py:333
  66.7 17.3 %collective-permute-start.8 = (bf16[128,768]{1,0:T(8,128)(2,1)}, bf16[128,768]{1,0:T(8,128)(2,1)}, u32[]{:S(2)}, u32[]{:S(2)}) collective-permute-start(bf16[128,768]{1,0:T(8,128)(2,1)} %get-tuple-element.23.a_ref), channel_id=1, source_target_pairs={{0,1},{3,2},{4,5},{7,6},{8,9},{11,10},{12,13},{15,14},{16,17},{19,... | collective-permute-start | bytes 589832 | tf_op jit(solution)/shard_map/ppermute | solution.py:333
  68.8 23.0 %collective-permute-start.13 = (bf16[128,768]{1,0:T(8,128)(2,1)S(1)}, bf16[128,768]{1,0:T(8,128)(2,1)S(1)}, u32[]{:S(2)}, u32[]{:S(2)}) collective-permute-start(bf16[128,768]{1,0:T(8,128)(2,1)S(1)} %get-tuple-element.26.a_ref), channel_id=1, source_target_pairs={{0,1},{3,2},{4,5},{7,6},{8,9},{11,10},{12,13},{15,14},{16,17},{19,... | collective-permute-start | bytes 589832 | tf_op jit(solution)/shard_map/ppermute | solution.py:333
  70.1 15.8 %collective-permute-start.7 = (bf16[128,896]{1,0:T(8,128)(2,1)S(1)}, bf16[128,896]{1,0:T(8,128)(2,1)S(1)}, u32[]{:S(2)}, u32[]{:S(2)}) collective-permute-start(bf16[128,896]{1,0:T(8,128)(2,1)S(1)} %add_after.12.after_ref.total_ref), channel_id=1, source_target_pairs={{1,0},{2,3},{5,4},{6,7},{9,8},{10,11},{13,12},{14,15},{17,16},{18,... | collective-permute-start | bytes 688136 | tf_op jit(solution)/shard_map/ppermute | solution.py:342
  77.4 15.1 %collective-permute-start.12 = (bf16[128,768]{1,0:T(8,128)(2,1)S(1)}, bf16[128,768]{1,0:T(8,128)(2,1)}, u32[]{:S(2)}, u32[]{:S(2)}) collective-permute-start(bf16[128,768]{1,0:T(8,128)(2,1)S(1)} %add_after.13.after_ref.a_ref), channel_id=1, source_target_pairs={{1,2},{2,1},{5,6},{6,5},{9,10},{10,9},{13,14},{14,13},{17,18},{18,... | collective-permute-start | bytes 589832 | tf_op jit(solution)/shard_map/ppermute | solution.py:339
  78.8 16.0 %collective-permute-start.11 = (bf16[128,896]{1,0:T(8,128)(2,1)S(1)}, bf16[128,896]{1,0:T(8,128)(2,1)S(1)}, u32[]{:S(2)}, u32[]{:S(2)}) collective-permute-start(bf16[128,896]{1,0:T(8,128)(2,1)S(1)} %add_after.14.after_ref.total_ref), channel_id=1, source_target_pairs={{1,0},{2,3},{5,4},{6,7},{9,8},{10,11},{13,12},{14,15},{17,16},{18,... | collective-permute-start | bytes 688136 | tf_op jit(solution)/shard_map/ppermute | solution.py:342
  85.1 10.6 %collective-permute-start.16 = (bf16[128,768]{1,0:T(8,128)(2,1)S(1)}, bf16[128,768]{1,0:T(8,128)(2,1)S(1)}, u32[]{:S(2)}, u32[]{:S(2)}) collective-permute-start(bf16[128,768]{1,0:T(8,128)(2,1)S(1)} %add_after.15.refs_0_.a_ref), channel_id=1, source_target_pairs={{1,2},{2,1},{5,6},{6,5},{9,10},{10,9},{13,14},{14,13},{17,18},{18,... | collective-permute-start | bytes 589832 | tf_op jit(solution)/shard_map/ppermute | solution.py:339
  91.9 5.3 %collective-permute-start.15 = (bf16[128,768]{1,0:T(8,128)(2,1)S(1)}, bf16[128,768]{1,0:T(8,128)(2,1)S(1)}, u32[]{:S(2)}, u32[]{:S(2)}) collective-permute-start(bf16[128,768]{1,0:T(8,128)(2,1)S(1)} %add_after.16.after_ref.a_ref), channel_id=1, source_target_pairs={{1,2},{2,1},{5,6},{6,5},{9,10},{10,9},{13,14},{14,13},{17,18},{18,... | collective-permute-start | bytes 589832 | tf_op jit(solution)/shard_map/ppermute | solution.py:339
  93.5 11.1 %collective-permute-start.14 = (bf16[128,768]{1,0:T(8,128)(2,1)S(1)}, bf16[128,768]{1,0:T(8,128)(2,1)S(1)}, u32[]{:S(2)}, u32[]{:S(2)}) collective-permute-start(bf16[128,768]{1,0:T(8,128)(2,1)S(1)} %add_after.17.refs_0_.total_ref), channel_id=1, source_target_pairs={{1,0},{2,3},{5,4},{6,7},{9,8},{10,11},{13,12},{14,15},{17,16},{18,... | collective-permute-start | bytes 589832 | tf_op jit(solution)/shard_map/ppermute | solution.py:342
  95.8 12.9 %collective-permute-start.17 = (bf16[128,768]{1,0:T(8,128)(2,1)S(1)}, bf16[128,768]{1,0:T(8,128)(2,1)S(1)}, u32[]{:S(2)}, u32[]{:S(2)}) collective-permute-start(bf16[128,768]{1,0:T(8,128)(2,1)S(1)} %add_after.18.after_ref.total_ref), channel_id=1, source_target_pairs={{1,0},{2,3},{5,4},{6,7},{9,8},{10,11},{13,12},{14,15},{17,16},{18,... | collective-permute-start | bytes 589832 | tf_op jit(solution)/shard_map/ppermute | solution.py:342
  97.2 13.6 %collective-permute-start.18 = (bf16[128,768]{1,0:T(8,128)(2,1)S(1)}, bf16[128,768]{1,0:T(8,128)(2,1)S(1)}, u32[]{:S(2)}, u32[]{:S(2)}) collective-permute-start(bf16[128,768]{1,0:T(8,128)(2,1)S(1)} %add_after.19.refs_0_.total_ref), channel_id=1, source_target_pairs={{1,0},{2,3},{5,4},{6,7},{9,8},{10,11},{13,12},{14,15},{17,16},{18,... | collective-permute-start | bytes 589832 | tf_op jit(solution)/shard_map/ppermute | solution.py:342
  111.8 4.5 %collective-permute-start.19 = (bf16[32,192]{1,0:T(8,128)(2,1)S(1)}, bf16[32,192]{1,0:T(8,128)(2,1)S(1)}, u32[]{:S(2)}, u32[]{:S(2)}) collective-permute-start(bf16[32,192]{1,0:T(8,128)(2,1)S(1)} %get-tuple-element.42), channel_id=1, source_target_pairs={{0,1},{1,0},{2,3},{3,2},{4,5},{5,4},{6,7},{7,6},{8,9},{9,8},{10,11... | collective-permute-start | bytes 36872 | tf_op jit(solution)/shard_map/ppermute | solution.py:43
  111.9 4.9 %collective-permute-start.20 = (bf16[32,192]{1,0:T(8,128)(2,1)S(1)}, bf16[32,192]{1,0:T(8,128)(2,1)S(1)}, u32[]{:S(2)}, u32[]{:S(2)}) collective-permute-start(bf16[32,192]{1,0:T(8,128)(2,1)S(1)} %get-tuple-element.41), channel_id=1, source_target_pairs={{0,2},{1,3},{2,0},{3,1},{4,6},{5,7},{6,4},{7,5},{8,10},{9,11},{10,... | collective-permute-start | bytes 36872 | tf_op jit(solution)/shard_map/ppermute | solution.py:43
  115.0 5.5 %collective-permute-start.21 = (bf16[32,192]{1,0:T(8,128)(2,1)S(1)}, bf16[32,192]{1,0:T(8,128)(2,1)S(1)}, u32[]{:S(2)}, u32[]{:S(2)}) collective-permute-start(bf16[32,192]{1,0:T(8,128)(2,1)S(1)} %get-tuple-element.40), channel_id=1, source_target_pairs={{0,3},{1,2},{2,1},{3,0},{4,7},{5,6},{6,5},{7,4},{8,11},{9,10},{10,... | collective-permute-start | bytes 36872 | tf_op jit(solution)/shard_map/ppermute | solution.py:43
  (11 other events, 146.2 us)
Sparse Core Ops, SparseCore 0:
  10.9 84.3 all-gather.2

commit v4 on v3

--- a/solution.py
+++ b/solution.py
@@ -16,6 +16,8 @@
 WIDTHS = (896, 896, 768, 768, 768)
 SPANS = tuple((sum(WIDTHS[:i]), width) for i, width in enumerate(WIDTHS))
 PAD_ROWS = 16
+ROW_ORDER = (0, 2, 1, 3)
+SHARE_WIDTHS = (1792, 2304)
 ORDER = (
     ("near", 0),
     ("near", 1),
@@ -58,7 +60,7 @@
         copy = pltpu.make_async_copy(w_hbm.at[:, span], w_buf.at[:, span], sems.at[chunk])
         copy.start()
         copies.append(copy)
-    bound = bound_ref[...]
+    bound = jnp.broadcast_to(bound_ref[...].astype(jnp.float32), (tok, tok)).T
     lane = lax.broadcasted_iota(jnp.int32, (1, tok), 1).astype(jnp.float32)
     ones = jnp.ones((tok, HEAD_DIM), jnp.bfloat16)
     half_count = same_ref.shape[0]
@@ -96,7 +98,7 @@
             attended[:, pl.ds(start, HEAD_DIM)] = result[j * tok : (j + 1) * tok]
         return carry
 
-    lax.fori_loop(0, heads // STACK, some_heads, 0)
+    lax.fori_loop(0, heads // STACK, some_heads, 0, unroll=True)
     resid_copy.wait()
     home = resid_ref.shape[0]
     top = pl.multiple_of(rank_ref[0] * home, home)
@@ -130,39 +132,86 @@
             pltpu.SemaphoreType.DMA((len(WIDTHS),)),
             pltpu.SemaphoreType.DMA((2,)),
         ],
-        compiler_params=pltpu.CompilerParams(vmem_limit_bytes=40 * 1024 * 1024),
+        compiler_params=pltpu.CompilerParams(vmem_limit_bytes=52 * 1024 * 1024),
         cost_estimate=LIGHT,
         name="attend_project",
     )(rank, bounds, same, other, queries, residual, w_out)
 
 
-def down_kernel(rank_ref, coef_ref, a0, a1, a2, a3, back_ref, out_ref):
-    count, _, width = back_ref.shape
-    coef = coef_ref[...]
-    blended = [(a[...].astype(jnp.float32) * coef).astype(jnp.bfloat16) for a in (a0, a1, a2, a3)]
-    hidden = blended[0].shape[1]
-    for block in range(count):
-        total = None
-        for s in range(len(blended)):
-            rows = pl.ds(pl.multiple_of((rank_ref[0] ^ s) * hidden, hidden), hidden)
-            term = jnp.dot(
-                blended[s], back_ref[block, rows, :], preferred_element_type=jnp.float32
-            )
-            total = term if total is None else total + term
-        out_ref[:, block * width : (block + 1) * width] = total.astype(jnp.bfloat16)
-
-
-def down(rank, coefficient, acts, back):
-    rows = acts[0].shape[0]
-    return pl.pallas_call(
-        down_kernel,
-        out_shape=jax.ShapeDtypeStruct((rows, D), jnp.bfloat16),
-        in_specs=[pl.BlockSpec(memory_space=pltpu.SMEM)] + [VMEM] * 6,
+def share_kernel(act_ref, back_ref, *outs):
+    half = act_ref.shape[0] // 2
+    first = 0
+    for i, width in enumerate(SHARE_WIDTHS):
+        product = jnp.dot(
+            act_ref[...], back_ref[:, first : first + width], preferred_element_type=jnp.float32
+        )
+        outs[2 * i][...] = product[:half].astype(jnp.bfloat16)
+        outs[2 * i + 1][...] = product[half:].astype(jnp.bfloat16)
+        first += width
+
+
+def make_shares(act, back):
+    shapes = [
+        jax.ShapeDtypeStruct((act.shape[0] // 2, width), jnp.bfloat16)
+        for width in SHARE_WIDTHS
+        for _ in range(2)
+    ]
+    return pl.pallas_call(
+        share_kernel,
+        out_shape=shapes,
+        in_specs=[VMEM, VMEM],
+        out_specs=[VMEM] * len(shapes),
+        compiler_params=pltpu.CompilerParams(vmem_limit_bytes=12 * 1024 * 1024),
+        cost_estimate=LIGHT,
+        name="make_shares",
+    )(act, back)
+
+
+def pair_kernel(kept_ref, arrived_ref, after_ref, own_ref, leaving_ref):
+    rows = own_ref.shape[0]
+    total = kept_ref[...].astype(jnp.float32) + arrived_ref[...].astype(jnp.float32)
+    own_ref[...] = total[:rows]
+    leaving_ref[...] = total[rows:].astype(jnp.bfloat16)
+
+
+def pair_sum(kept, arrived, after):
+    shape = (kept.shape[0] // 2, kept.shape[1])
+    return pl.pallas_call(
+        pair_kernel,
+        out_shape=[
+            jax.ShapeDtypeStruct(shape, jnp.float32),
+            jax.ShapeDtypeStruct(shape, jnp.bfloat16),
+        ],
+        in_specs=[VMEM, VMEM, ANY],
+        out_specs=[VMEM, VMEM],
+        compiler_params=pltpu.CompilerParams(vmem_limit_bytes=4 * 1024 * 1024),
+        cost_estimate=LIGHT,
+        name="pair_sum",
+    )(kept, arrived, after)
+
+
+def last_kernel(coef_ref, own_ref, arrived_ref, *refs):
+    out_ref = refs[-1]
+    first = 0
+    if len(refs) > 1:
+        first = refs[0].shape[1]
+        out_ref[:, :first] = refs[0][...]
+    total = own_ref[...] + arrived_ref[...].astype(jnp.float32)
+    out_ref[:, first:] = (total * coef_ref[...]).astype(jnp.bfloat16)
+
+
+def last_sum(coefficient, own, arrived, earlier):
+    rows, width = own.shape
+    width += sum(piece.shape[1] for piece in earlier)
+    return pl.pallas_call(
+        last_kernel,
+        out_shape=jax.ShapeDtypeStruct((rows, width), jnp.bfloat16),
+        in_specs=[VMEM] * (3 + len(earlier)),
         out_specs=VMEM,
-        compiler_params=pltpu.CompilerParams(vmem_limit_bytes=12 * 1024 * 1024),
-        cost_estimate=LIGHT,
-        name="down",
-    )(rank, coefficient, *acts, back)
+        compiler_params=pltpu.CompilerParams(vmem_limit_bytes=4 * 1024 * 1024),
+        cost_estimate=LIGHT,
+        name="last_sum",
+    )(coefficient, own, arrived, *earlier)
 
 
 def join_kernel(*refs):
@@ -209,8 +258,8 @@
 def absorb_kernel(chunk, flag_ref, total_ref, outward_ref, gain_ref, w_ref, *refs):
     last = chunk == len(WIDTHS) - 1
     states = refs[1 : 1 if chunk == 0 else 3]
-    outs = refs[1 + len(states) : -1]
-    scratch = refs[-1]
+    outs = refs[1 + len(states) : -2]
+    scratch, order_buf = refs[-2:]
     first, width = SPANS[chunk]
     span = slice(first, first + width)
     middle = jnp.where(flag_ref[1] == 1, outward_ref[...], total_ref[...])
@@ -237,7 +286,13 @@
         product = product * lax.rsqrt(mean_square + 1e-06)
         gate = product[:, :hidden]
         act = gate / (1.0 + jnp.exp(-gate)) * product[:, hidden:]
-        outs[1][...] = act.astype(jnp.bfloat16)
+        rows = home_ref.shape[0]
+        order_buf[...] = act
+        for i, offset in enumerate(ROW_ORDER):
+            source = pl.multiple_of((flag_ref[0] ^ offset) * rows, rows)
+            outs[1][i * rows : (i + 1) * rows, :] = order_buf[pl.ds(source, rows), :].astype(
+                jnp.bfloat16
+            )
     else:
         outs[1][...] = product
         outs[2][...] = square
@@ -263,7 +318,10 @@
         + [ANY]
         + [VMEM] * len(states),
         out_specs=[VMEM] * len(out_shape),
-        scratch_shapes=[pltpu.VMEM((tok, width), jnp.bfloat16)],
+        scratch_shapes=[
+            pltpu.VMEM((tok, width), jnp.bfloat16),
+            pltpu.VMEM((tok, rows // 2), jnp.float32),
+        ],
         compiler_params=pltpu.CompilerParams(vmem_limit_bytes=12 * 1024 * 1024),
         cost_estimate=LIGHT,
         name="absorb",
@@ -298,7 +356,6 @@
     ctx_count = lax.axis_size("ctx")
     exp_count = lax.axis_size("exp")
     rank = lax.axis_index("exp")
-    place = lax.axis_index("ctx")
     key_head, value_head = own_heads(queries, keys, values)
     block = (positions[0] // tok).astype(jnp.bfloat16)
     pair = jnp.concatenate([key_head, value_head], axis=1)
@@ -311,14 +368,9 @@
     )
     same_keys = same_rows.reshape(ctx_count // 2, tok + PAD_ROWS, 2 * HEAD_DIM)
     other_keys = exchange(same_rows, "ctx", 1, ctx_count).reshape(same_keys.shape)
-    flat_back = w_back.reshape(hidden, D)
-    mine = lax.dynamic_slice_in_dim(flat_back, place * (D // ctx_count), D // ctx_count, 1)
-    all_back = lax.all_gather(mine, ("ctx", "exp"), axis=0, tiled=True)
-    all_back = all_back.reshape(ctx_count, exp_count * hidden, D // ctx_count)
-
     parts = attend_project(
         rank.astype(jnp.int32).reshape(1),
-        bounds.astype(jnp.float32).reshape(tok, 1),
+        bounds.reshape(1, tok),
         same_keys,
         other_keys,
         queries,
@@ -348,15 +400,19 @@
             after = states[0]
     middle_out = jnp.concatenate(homes, axis=1)
     activated = states[0]
-    acts = [lax.dynamic_slice_in_dim(activated, rank * home, home, 0)]
-    for offset in range(1, exp_count):
-        leaving = lax.dynamic_slice_in_dim(activated, (rank ^ offset) * home, home, 0)
-        acts.append(exchange(leaving, "exp", offset, exp_count))
     shares = gates / jnp.sum(gates, axis=1, keepdims=True)
     coefficient = jnp.sum(jnp.where(routes == 0, shares, 0.0), axis=1, keepdims=True)
     coefficient = coefficient.astype(jnp.bfloat16).astype(jnp.float32)
-    expert_out = down(flags, coefficient, acts, all_back)
-    return (middle_out, expert_out)
+    share_parts = make_shares(activated, w_back.reshape(hidden, D))
+    parts_count = len(SHARE_WIDTHS)
+    arrivals = [exchange(share_parts[2 * i + 1], "exp", 1, exp_count) for i in range(parts_count)]
+    earlier, after = [], activated
+    for i in range(parts_count):
+        own, leaving = pair_sum(share_parts[2 * i], arrivals[i], after)
+        arrived = exchange(leaving, "exp", 2, exp_count)
+        after = last_sum(coefficient, own, arrived, earlier)
+        earlier = [after]
+    return (middle_out, after)
 
 
 def largest_divisor(row_count):

time: 134 us -> 121 us (0.903)
  between operations: 17 us -> 3.71 us
  waiting for transfers between devices: 47.7 us -> 42.2 us
  starting transfers between devices: 36.2 us -> 40.2 us
  Pallas kernels: 20.3 us -> 22.9 us
  local copies, waits for them, and re-layouts: 10.7 us -> 8.64 us
    ppermute x5, waiting for transfers between devices: 26.9 us -> 7.98 us  [line_device(): inward = [lax.ppermute(part, 'exp', [(0, 1), (3, 2)]) for part in parts]]
    ppermute x7 -> x8, waiting for transfers between devices: 10.3 us -> 26 us  [exchange(): return lax.ppermute(value, axis, [(i, i ^ offset) for i in range(size)])]
    ppermute x5, starting transfers between devices: 16.6 us -> 20.1 us  [line_device(): inward = [lax.ppermute(part, 'exp', [(0, 1), (3, 2)]) for part in parts]]
    pallas_call x10, Pallas kernels: 3.39 us -> 5.92 us  [add_after(): pl.pallas_call(add_kernel, out_shape=jax.ShapeDtypeStruct(left.shape, jnp...]
    ppermute x5, waiting for transfers between devices: 10.5 us -> 8.21 us  [line_device(): outward[chunk] = lax.ppermute(total[chunk], 'exp', [(1, 0), (2, 3)])]
    unnamed x28 -> x44, local copies, waits for them, and re-layouts: 9.02 us -> 6.96 us
    pallas_call x5, Pallas kernels: 4.5 us -> 6.38 us  [absorb(): pl.pallas_call(functools.partial(absorb_kernel, chunk), out_shape=out_sha...]
    ppermute x7 -> x8, starting transfers between devices: 9.06 us -> 9.58 us  [exchange(): return lax.ppermute(value, axis, [(i, i ^ offset) for i in range(size)])]
  transfers between devices with their start and end apart: 23 -> 23, of which waited for: 14 -> 11; matrix products, arithmetic and copies ran while one was open for 1% -> 4% of each run, Pallas kernels for 13% -> 9%
where the time goes in v4:
time: 121 us; the launch traced here: 120 us
  waiting for transfers between devices  42.2 us (35%)
  starting transfers between devices  40.2 us (33%)
  Pallas kernels  22.9 us (19%)
  local copies, waits for them, and re-layouts  8.64 us (7%)
  between operations  3.71 us (3%)
  other arithmetic  2.06 us (2%)
    ppermute x8, waiting for transfers between devices, exchange(): return lax.ppermute(value, axis, [(i, i ^ offset) for i in range(size)])  26 us
    ppermute x5, starting transfers between devices, line_device(): inward = [lax.ppermute(part, 'exp', [(0, 1), (3, 2)]) for part in parts]  20.1 us
    ppermute x8, starting transfers between devices, exchange(): return lax.ppermute(value, axis, [(i, i ^ offset) for i in range(size)])  9.58 us
    pallas_call x1, Pallas kernels, attend_project(): pl.pallas_call(attend_kernel, out_shape=[jax.ShapeDtypeStruct((tok, w), j...  9.11 us
    ppermute x5, waiting for transfers between devices, line_device(): outward[chunk] = lax.ppermute(total[chunk], 'exp', [(1, 0), (2, 3)])  8.21 us
    ppermute x5, waiting for transfers between devices, line_device(): inward = [lax.ppermute(part, 'exp', [(0, 1), (3, 2)]) for part in parts]  7.98 us
    unnamed x44, local copies, waits for them, and re-layouts  6.96 us
    ppermute x5, starting transfers between devices, line_device(): outward[chunk] = lax.ppermute(total[chunk], 'exp', [(1, 0), (2, 3)])  6.44 us
  transfers between devices with their start and end apart: 23, of which 11 were waited for; matrix products, arithmetic and copies ran while one was open for 4% of the time, Pallas kernels for 9%

profile of v4, /device:TPU:0, one launch (start us, length us, event | category | flops | bytes accessed | tf_op | source)
XLA Modules:
  0.0 119.6 jit_solution(1677505734215081068)
XLA Ops:
  4.1 3.0 %collective-permute-start = (bf16[144,256]{1,0:T(8,128)(2,1)S(1)}, bf16[144,256]{1,0:T(8,128)(2,1)S(1)}, u32[]{:S(2)}, u32[]{:S(2)}) collective-permute-start(bf16[144,256]{1,0:T(8,128)(2,1)S(1)} %fusion.2.refs_0_.refs_1_), channel_id=1, source_target_pairs={{0,8},{4,12},{8,0},{12,4},{16,24},{20,28},{24,16},{28,20},{1,9},{5... | collective-permute-start | bytes 221192 | tf_op jit(solution)/shard_map/ppermute | solution.py:45
  7.1 1.5 %collective-permute-start.1 = (bf16[144,256]{1,0:T(8,128)(2,1)S(1)}, bf16[144,256]{1,0:T(8,128)(2,1)S(1)}, u32[]{:S(2)}, u32[]{:S(2)}) collective-permute-start(bf16[144,256]{1,0:T(8,128)(2,1)S(1)} %fusion.2.refs_0_.refs_1_), channel_id=1, source_target_pairs={{0,16},{4,20},{8,24},{12,28},{16,0},{20,4},{24,8},{28,12},{1,17},{... | collective-permute-start | bytes 221192 | tf_op jit(solution)/shard_map/ppermute | solution.py:45
  9.6 1.8 %collective-permute-done.1.refs_3_ = bf16[144,256]{1,0:T(8,128)(2,1)S(1)} collective-permute-done((bf16[144,256]{1,0:T(8,128)(2,1)S(1)}, bf16[144,256]{1,0:T(8,128)(2,1)S(1)}, u32[]{:S(2)}, u32[]{:S(2)}) %collective-permute-start.1) | collective-permute-done | bytes 73760 | tf_op jit(solution)/shard_map/ppermute | solution.py:45
  11.4 2.4 %collective-permute-done.2.refs_4_ = bf16[144,256]{1,0:T(8,128)(2,1)S(1)} collective-permute-done((bf16[144,256]{1,0:T(8,128)(2,1)S(1)}, bf16[144,256]{1,0:T(8,128)(2,1)S(1)}, u32[]{:S(2)}, u32[]{:S(2)}) %collective-permute-start.2) | collective-permute-done | bytes 73760 | tf_op jit(solution)/shard_map/ppermute | solution.py:45
  13.9 1.6 %collective-permute-done.3 = bf16[576,256]{1,0:T(8,128)(2,1)S(1)} collective-permute-done((bf16[576,256]{1,0:T(8,128)(2,1)S(1)}, bf16[576,256]{1,0:T(8,128)(2,1)S(1)}, u32[]{:S(2)}, u32[]{:S(2)}) %collective-permute-start.3) | collective-permute-done | bytes 294944 | tf_op jit(solution)/shard_map/ppermute | solution.py:45
  17.1 9.1 %attend_project.1 = (bf16[128,896]{1,0:T(8,128)(2,1)S(1)}, bf16[128,896]{1,0:T(8,128)(2,1)S(1)}, bf16[128,768]{1,0:T(8,128)(2,1)}, bf16[128,768]{1,0:T(8,128)(2,1)}, bf16[128,768]{1,0:T(8,128)(2,1)}) custom-call(s32[1]{0:T(128)} %bitcast.rank_ref, s32[1,128]{1,0:T(1,128)S(1)} %bitcast.26, bf16[4,144,256]{2,1,0:T(8,128)(2,1)S(1)} %bitcast.19, ...), custom_call_target="tpu_custom_call" | custom-call | flops 1024 | bytes 1024 | tf_op jit(solution)/shard_map/attend_project/pallas_call | solution.py:118
  26.3 3.7 %collective-permute-start.4 = (bf16[128,896]{1,0:T(8,128)(2,1)S(1)}, bf16[128,896]{1,0:T(8,128)(2,1)S(1)}, u32[]{:S(2)}, u32[]{:S(2)}) collective-permute-start(bf16[128,896]{1,0:T(8,128)(2,1)S(1)} %get-tuple-element.29.a_ref.after_ref), channel_id=1, source_target_pairs={{0,1},{3,2},{4,5},{7,6},{8,9},{11,10},{12,13},{15,14},{16,17},{19,... | collective-permute-start | bytes 688136 | tf_op jit(solution)/shard_map/ppermute | solution.py:385
  30.0 1.3 %collective-permute-start.6 = (bf16[128,896]{1,0:T(8,128)(2,1)S(1)}, bf16[128,896]{1,0:T(8,128)(2,1)S(1)}, u32[]{:S(2)}, u32[]{:S(2)}) collective-permute-start(bf16[128,896]{1,0:T(8,128)(2,1)S(1)} %get-tuple-element.30.a_ref), channel_id=1, source_target_pairs={{0,1},{3,2},{4,5},{7,6},{8,9},{11,10},{12,13},{15,14},{16,17},{19,... | collective-permute-start | bytes 688136 | tf_op jit(solution)/shard_map/ppermute | solution.py:385
  31.3 4.6 %collective-permute-done.4.b_ref = bf16[128,896]{1,0:T(8,128)(2,1)S(1)} collective-permute-done((bf16[128,896]{1,0:T(8,128)(2,1)S(1)}, bf16[128,896]{1,0:T(8,128)(2,1)S(1)}, u32[]{:S(2)}, u32[]{:S(2)}) %collective-permute-start.4) | collective-permute-done | bytes 229408 | tf_op jit(solution)/shard_map/ppermute | solution.py:385
  36.7 3.3 %collective-permute-done.6.b_ref = bf16[128,896]{1,0:T(8,128)(2,1)S(1)} collective-permute-done((bf16[128,896]{1,0:T(8,128)(2,1)S(1)}, bf16[128,896]{1,0:T(8,128)(2,1)S(1)}, u32[]{:S(2)}, u32[]{:S(2)}) %collective-permute-start.6) | collective-permute-done | bytes 229408 | tf_op jit(solution)/shard_map/ppermute | solution.py:385
  40.1 1.4 %collective-permute-start.9 = (bf16[128,896]{1,0:T(8,128)(2,1)S(1)}, bf16[128,896]{1,0:T(8,128)(2,1)}, u32[]{:S(2)}, u32[]{:S(2)}) collective-permute-start(bf16[128,896]{1,0:T(8,128)(2,1)S(1)} %add_after.11.after_ref.a_ref), channel_id=1, source_target_pairs={{1,2},{2,1},{5,6},{6,5},{9,10},{10,9},{13,14},{14,13},{17,18},{18,... | collective-permute-start | bytes 688136 | tf_op jit(solution)/shard_map/ppermute | solution.py:391
  41.5 7.2 %collective-permute-start.10 = (bf16[128,768]{1,0:T(8,128)(2,1)}, bf16[128,768]{1,0:T(8,128)(2,1)}, u32[]{:S(2)}, u32[]{:S(2)}) collective-permute-start(bf16[128,768]{1,0:T(8,128)(2,1)} %get-tuple-element.32.a_ref), channel_id=1, source_target_pairs={{0,1},{3,2},{4,5},{7,6},{8,9},{11,10},{12,13},{15,14},{16,17},{19,... | collective-permute-start | bytes 589832 | tf_op jit(solution)/shard_map/ppermute | solution.py:385
  50.7 5.9 %collective-permute-start.8 = (bf16[128,768]{1,0:T(8,128)(2,1)}, bf16[128,768]{1,0:T(8,128)(2,1)}, u32[]{:S(2)}, u32[]{:S(2)}) collective-permute-start(bf16[128,768]{1,0:T(8,128)(2,1)} %get-tuple-element.31.a_ref), channel_id=1, source_target_pairs={{0,1},{3,2},{4,5},{7,6},{8,9},{11,10},{12,13},{15,14},{16,17},{19,... | collective-permute-start | bytes 589832 | tf_op jit(solution)/shard_map/ppermute | solution.py:385
  56.6 2.0 %collective-permute-start.13 = (bf16[128,768]{1,0:T(8,128)(2,1)}, bf16[128,768]{1,0:T(8,128)(2,1)}, u32[]{:S(2)}, u32[]{:S(2)}) collective-permute-start(bf16[128,768]{1,0:T(8,128)(2,1)} %get-tuple-element.34.a_ref), channel_id=1, source_target_pairs={{0,1},{3,2},{4,5},{7,6},{8,9},{11,10},{12,13},{15,14},{16,17},{19,... | collective-permute-start | bytes 589832 | tf_op jit(solution)/shard_map/ppermute | solution.py:385
  64.5 1.4 %absorb.5 = (bf16[32,896]{1,0:T(8,128)(2,1)S(1)}, f32[128,384]{1,0:T(8,128)S(1)}, f32[128,128]{1,0:T(8,128)S(1)}) custom-call(s32[2]{0:T(128)S(1)} %pad_add_fusion.flag_ref, bf16[128,896]{1,0:T(8,128)(2,1)} %add_after.12.after_ref.total_ref, bf16[128,896]{1,0:T(8,128)(2,1)} %collective-permute-done.7.outward_ref, f32[1,4096]{1,0:T(1,128)S(1)} %bitcast.20, ...), custom_call_target="tpu_custom_call" | custom-call | flops 1024 | bytes 1024 | tf_op jit(solution)/shard_map/absorb/pallas_call | solution.py:313
  72.2 1.3 %collective-permute-start.18 = (bf16[128,768]{1,0:T(8,128)(2,1)S(1)}, bf16[128,768]{1,0:T(8,128)(2,1)}, u32[]{:S(2)}, u32[]{:S(2)}) collective-permute-start(bf16[128,768]{1,0:T(8,128)(2,1)S(1)} %add_after.19.refs_0_.total_ref), channel_id=1, source_target_pairs={{1,0},{2,3},{5,4},{6,7},{9,8},{10,11},{13,12},{14,15},{17,16},{18,... | collective-permute-start | bytes 589832 | tf_op jit(solution)/shard_map/ppermute | solution.py:394
  75.4 8.1 %collective-permute-done.14.outward_ref = bf16[128,768]{1,0:T(8,128)(2,1)} collective-permute-done((bf16[128,768]{1,0:T(8,128)(2,1)S(1)}, bf16[128,768]{1,0:T(8,128)(2,1)}, u32[]{:S(2)}, u32[]{:S(2)}) %collective-permute-start.14) | collective-permute-done | bytes 196640 | tf_op jit(solution)/shard_map/ppermute | solution.py:394
  87.9 1.5 %absorb.8 = (bf16[32,768]{1,0:T(8,128)(2,1)S(1)}, f32[128,384]{1,0:T(8,128)S(1)}, f32[128,128]{1,0:T(8,128)S(1)}) custom-call(s32[2]{0:T(128)S(1)} %copy-done.17, bf16[128,768]{1,0:T(8,128)(2,1)} %add_after.18.after_ref.total_ref, bf16[128,768]{1,0:T(8,128)(2,1)} %collective-permute-done.17.outward_ref, f32[1,4096]{1,0:T(1,128)S(1)} %bitcast.23, ...), custom_call_target="tpu_custom_call" | custom-call | flops 1024 | bytes 1024 | tf_op jit(solution)/shard_map/absorb/pallas_call | solution.py:313
  90.1 1.4 %absorb.9 = (bf16[32,768]{1,0:T(8,128)(2,1)S(1)}, bf16[128,192]{1,0:T(8,128)(2,1)S(1)}) custom-call(s32[2]{0:T(128)S(1)} %copy-done.17, bf16[128,768]{1,0:T(8,128)(2,1)S(1)} %add_after.19.refs_0_.total_ref, bf16[128,768]{1,0:T(8,128)(2,1)} %collective-permute-done.18.outward_ref, f32[1,4096]{1,0:T(1,128)S(1)} %bitcast.24, bf16[384,4096]{1,0:T(8,128)(2,1)S(1)} %bitcast.17, ...), custom_call_target="tpu_custom_call" | custom-call | flops 1024 | bytes 1024 | tf_op jit(solution)/shard_map/absorb/pallas_call | solution.py:313
  91.9 2.7 %collective-permute-start.20 = (bf16[64,1792]{1,0:T(8,128)(2,1)S(1)}, bf16[64,1792]{1,0:T(8,128)(2,1)S(1)}, u32[]{:S(2)}, u32[]{:S(2)}) collective-permute-start(bf16[64,1792]{1,0:T(8,128)(2,1)S(1)} %get-tuple-element.51), channel_id=1, source_target_pairs={{0,1},{1,0},{2,3},{3,2},{4,5},{5,4},{6,7},{7,6},{8,9},{9,8},{10,11... | collective-permute-start | bytes 688136 | tf_op jit(solution)/shard_map/ppermute | solution.py:45
  94.8 7.3 %collective-permute-done.20.arrived_ref = bf16[64,1792]{1,0:T(8,128)(2,1)S(1)} collective-permute-done((bf16[64,1792]{1,0:T(8,128)(2,1)S(1)}, bf16[64,1792]{1,0:T(8,128)(2,1)S(1)}, u32[]{:S(2)}, u32[]{:S(2)}) %collective-permute-start.20) | collective-permute-done | bytes 229408 | tf_op jit(solution)/shard_map/ppermute | solution.py:45
  102.1 2.1 %collective-permute-start.21 = (bf16[32,1792]{1,0:T(8,128)(2,1)S(1)}, bf16[32,1792]{1,0:T(8,128)(2,1)S(1)}, u32[]{:S(2)}, u32[]{:S(2)}) collective-permute-start(bf16[32,1792]{1,0:T(8,128)(2,1)S(1)} %get-tuple-element.53), channel_id=1, source_target_pairs={{0,2},{1,3},{2,0},{3,1},{4,6},{5,7},{6,4},{7,5},{8,10},{9,11},{10,... | collective-permute-start | bytes 344072 | tf_op jit(solution)/shard_map/ppermute | solution.py:45
  105.9 5.4 %collective-permute-done.21.arrived_ref = bf16[32,1792]{1,0:T(8,128)(2,1)S(1)} collective-permute-done((bf16[32,1792]{1,0:T(8,128)(2,1)S(1)}, bf16[32,1792]{1,0:T(8,128)(2,1)S(1)}, u32[]{:S(2)}, u32[]{:S(2)}) %collective-permute-start.21) | collective-permute-done | bytes 114720 | tf_op jit(solution)/shard_map/ppermute | solution.py:45
  112.4 6.4 %collective-permute-done.22.arrived_ref = bf16[32,2304]{1,0:T(8,128)(2,1)S(1)} collective-permute-done((bf16[32,2304]{1,0:T(8,128)(2,1)S(1)}, bf16[32,2304]{1,0:T(8,128)(2,1)S(1)}, u32[]{:S(2)}, u32[]{:S(2)}) %collective-permute-start.22) | collective-permute-done | bytes 147488 | tf_op jit(solution)/shard_map/ppermute | solution.py:45
  (96 shorter events, 29.4 us)
Async XLA Ops:
  4.1 5.5 %collective-permute-start = (bf16[144,256]{1,0:T(8,128)(2,1)S(1)}, bf16[144,256]{1,0:T(8,128)(2,1)S(1)}, u32[]{:S(2)}, u32[]{:S(2)}) collective-permute-start(bf16[144,256]{1,0:T(8,128)(2,1)S(1)} %fusion.2.refs_0_.refs_1_), channel_id=1, source_target_pairs={{0,8},{4,12},{8,0},{12,4},{16,24},{20,28},{24,16},{28,20},{1,9},{5... | collective-permute-start | bytes 221192 | tf_op jit(solution)/shard_map/ppermute | solution.py:45
  7.1 4.4 %collective-permute-start.1 = (bf16[144,256]{1,0:T(8,128)(2,1)S(1)}, bf16[144,256]{1,0:T(8,128)(2,1)S(1)}, u32[]{:S(2)}, u32[]{:S(2)}) collective-permute-start(bf16[144,256]{1,0:T(8,128)(2,1)S(1)} %fusion.2.refs_0_.refs_1_), channel_id=1, source_target_pairs={{0,16},{4,20},{8,24},{12,28},{16,0},{20,4},{24,8},{28,12},{1,17},{... | collective-permute-start | bytes 221192 | tf_op jit(solution)/shard_map/ppermute | solution.py:45
  8.6 5.3 %collective-permute-start.2 = (bf16[144,256]{1,0:T(8,128)(2,1)S(1)}, bf16[144,256]{1,0:T(8,128)(2,1)S(1)}, u32[]{:S(2)}, u32[]{:S(2)}) collective-permute-start(bf16[144,256]{1,0:T(8,128)(2,1)S(1)} %fusion.2.refs_0_.refs_1_), channel_id=1, source_target_pairs={{0,24},{4,28},{8,16},{12,20},{16,8},{20,12},{24,0},{28,4},{1,25},{... | collective-permute-start | bytes 221192 | tf_op jit(solution)/shard_map/ppermute | solution.py:45
  13.9 1.6 %collective-permute-start.3 = (bf16[576,256]{1,0:T(8,128)(2,1)S(1)}, bf16[576,256]{1,0:T(8,128)(2,1)S(1)}, u32[]{:S(2)}, u32[]{:S(2)}) collective-permute-start(bf16[576,256]{1,0:T(8,128)(2,1)S(1)} %join_after.1), channel_id=1, source_target_pairs={{0,4},{4,0},{8,12},{12,8},{16,20},{20,16},{24,28},{28,24},{1,5},{5... | collective-permute-start | bytes 884744 | tf_op jit(solution)/shard_map/ppermute | solution.py:45
  26.2 38.3 %copy-start = (bf16[1,384,4096]{2,1,0:T(8,128)(2,1)S(1)}, bf16[1,384,4096]{2,1,0:T(8,128)(2,1)}, u32[]{:S(2)}) copy-start(bf16[1,384,4096]{2,1,0:T(8,128)(2,1)} %param.22) | copy-start | bytes 9437188
  26.3 9.7 %collective-permute-start.4 = (bf16[128,896]{1,0:T(8,128)(2,1)S(1)}, bf16[128,896]{1,0:T(8,128)(2,1)S(1)}, u32[]{:S(2)}, u32[]{:S(2)}) collective-permute-start(bf16[128,896]{1,0:T(8,128)(2,1)S(1)} %get-tuple-element.29.a_ref.after_ref), channel_id=1, source_target_pairs={{0,1},{3,2},{4,5},{7,6},{8,9},{11,10},{12,13},{15,14},{16,17},{19,... | collective-permute-start | bytes 688136 | tf_op jit(solution)/shard_map/ppermute | solution.py:385
  30.0 10.0 %collective-permute-start.6 = (bf16[128,896]{1,0:T(8,128)(2,1)S(1)}, bf16[128,896]{1,0:T(8,128)(2,1)S(1)}, u32[]{:S(2)}, u32[]{:S(2)}) collective-permute-start(bf16[128,896]{1,0:T(8,128)(2,1)S(1)} %get-tuple-element.30.a_ref), channel_id=1, source_target_pairs={{0,1},{3,2},{4,5},{7,6},{8,9},{11,10},{12,13},{15,14},{16,17},{19,... | collective-permute-start | bytes 688136 | tf_op jit(solution)/shard_map/ppermute | solution.py:385
  36.0 12.7 %collective-permute-start.5 = (bf16[128,896]{1,0:T(8,128)(2,1)S(1)}, bf16[128,896]{1,0:T(8,128)(2,1)S(1)}, u32[]{:S(2)}, u32[]{:S(2)}) collective-permute-start(bf16[128,896]{1,0:T(8,128)(2,1)S(1)} %add_after.10.after_ref.a_ref), channel_id=1, source_target_pairs={{1,2},{2,1},{5,6},{6,5},{9,10},{10,9},{13,14},{14,13},{17,18},{18,... | collective-permute-start | bytes 688136 | tf_op jit(solution)/shard_map/ppermute | solution.py:391
  40.1 19.6 %collective-permute-start.9 = (bf16[128,896]{1,0:T(8,128)(2,1)S(1)}, bf16[128,896]{1,0:T(8,128)(2,1)}, u32[]{:S(2)}, u32[]{:S(2)}) collective-permute-start(bf16[128,896]{1,0:T(8,128)(2,1)S(1)} %add_after.11.after_ref.a_ref), channel_id=1, source_target_pairs={{1,2},{2,1},{5,6},{6,5},{9,10},{10,9},{13,14},{14,13},{17,18},{18,... | collective-permute-start | bytes 688136 | tf_op jit(solution)/shard_map/ppermute | solution.py:391
  41.5 17.1 %collective-permute-start.10 = (bf16[128,768]{1,0:T(8,128)(2,1)}, bf16[128,768]{1,0:T(8,128)(2,1)}, u32[]{:S(2)}, u32[]{:S(2)}) collective-permute-start(bf16[128,768]{1,0:T(8,128)(2,1)} %get-tuple-element.32.a_ref), channel_id=1, source_target_pairs={{0,1},{3,2},{4,5},{7,6},{8,9},{11,10},{12,13},{15,14},{16,17},{19,... | collective-permute-start | bytes 589832 | tf_op jit(solution)/shard_map/ppermute | solution.py:385
  49.4 15.1 %collective-permute-start.7 = (bf16[128,896]{1,0:T(8,128)(2,1)}, bf16[128,896]{1,0:T(8,128)(2,1)}, u32[]{:S(2)}, u32[]{:S(2)}) collective-permute-start(bf16[128,896]{1,0:T(8,128)(2,1)} %add_after.12.after_ref.total_ref), channel_id=1, source_target_pairs={{1,0},{2,3},{5,4},{6,7},{9,8},{10,11},{13,12},{14,15},{17,16},{18,... | collective-permute-start | bytes 688136 | tf_op jit(solution)/shard_map/ppermute | solution.py:394
  50.7 12.0 %collective-permute-start.8 = (bf16[128,768]{1,0:T(8,128)(2,1)}, bf16[128,768]{1,0:T(8,128)(2,1)}, u32[]{:S(2)}, u32[]{:S(2)}) collective-permute-start(bf16[128,768]{1,0:T(8,128)(2,1)} %get-tuple-element.31.a_ref), channel_id=1, source_target_pairs={{0,1},{3,2},{4,5},{7,6},{8,9},{11,10},{12,13},{15,14},{16,17},{19,... | collective-permute-start | bytes 589832 | tf_op jit(solution)/shard_map/ppermute | solution.py:385
  56.6 9.3 %collective-permute-start.13 = (bf16[128,768]{1,0:T(8,128)(2,1)}, bf16[128,768]{1,0:T(8,128)(2,1)}, u32[]{:S(2)}, u32[]{:S(2)}) collective-permute-start(bf16[128,768]{1,0:T(8,128)(2,1)} %get-tuple-element.34.a_ref), channel_id=1, source_target_pairs={{0,1},{3,2},{4,5},{7,6},{8,9},{11,10},{12,13},{15,14},{16,17},{19,... | collective-permute-start | bytes 589832 | tf_op jit(solution)/shard_map/ppermute | solution.py:385
  60.7 8.4 %collective-permute-start.11 = (bf16[128,896]{1,0:T(8,128)(2,1)S(1)}, bf16[128,896]{1,0:T(8,128)(2,1)S(1)}, u32[]{:S(2)}, u32[]{:S(2)}) collective-permute-start(bf16[128,896]{1,0:T(8,128)(2,1)S(1)} %add_after.14.after_ref.total_ref), channel_id=1, source_target_pairs={{1,0},{2,3},{5,4},{6,7},{9,8},{10,11},{13,12},{14,15},{17,16},{18,... | collective-permute-start | bytes 688136 | tf_op jit(solution)/shard_map/ppermute | solution.py:394
  62.0 5.7 %collective-permute-start.12 = (bf16[128,768]{1,0:T(8,128)(2,1)S(1)}, bf16[128,768]{1,0:T(8,128)(2,1)S(1)}, u32[]{:S(2)}, u32[]{:S(2)}) collective-permute-start(bf16[128,768]{1,0:T(8,128)(2,1)S(1)} %add_after.13.after_ref.a_ref), channel_id=1, source_target_pairs={{1,2},{2,1},{5,6},{6,5},{9,10},{10,9},{13,14},{14,13},{17,18},{18,... | collective-permute-start | bytes 589832 | tf_op jit(solution)/shard_map/ppermute | solution.py:391
  63.8 6.2 %collective-permute-start.16 = (bf16[128,768]{1,0:T(8,128)(2,1)S(1)}, bf16[128,768]{1,0:T(8,128)(2,1)S(1)}, u32[]{:S(2)}, u32[]{:S(2)}) collective-permute-start(bf16[128,768]{1,0:T(8,128)(2,1)S(1)} %add_after.15.refs_0_.a_ref), channel_id=1, source_target_pairs={{1,2},{2,1},{5,6},{6,5},{9,10},{10,9},{13,14},{14,13},{17,18},{18,... | collective-permute-start | bytes 589832 | tf_op jit(solution)/shard_map/ppermute | solution.py:391
  67.0 5.1 %collective-permute-start.15 = (bf16[128,768]{1,0:T(8,128)(2,1)S(1)}, bf16[128,768]{1,0:T(8,128)(2,1)S(1)}, u32[]{:S(2)}, u32[]{:S(2)}) collective-permute-start(bf16[128,768]{1,0:T(8,128)(2,1)S(1)} %add_after.16.after_ref.a_ref), channel_id=1, source_target_pairs={{1,2},{2,1},{5,6},{6,5},{9,10},{10,9},{13,14},{14,13},{17,18},{18,... | collective-permute-start | bytes 589832 | tf_op jit(solution)/shard_map/ppermute | solution.py:391
  67.8 15.7 %collective-permute-start.14 = (bf16[128,768]{1,0:T(8,128)(2,1)S(1)}, bf16[128,768]{1,0:T(8,128)(2,1)}, u32[]{:S(2)}, u32[]{:S(2)}) collective-permute-start(bf16[128,768]{1,0:T(8,128)(2,1)S(1)} %add_after.17.refs_0_.total_ref), channel_id=1, source_target_pairs={{1,0},{2,3},{5,4},{6,7},{9,8},{10,11},{13,12},{14,15},{17,16},{18,... | collective-permute-start | bytes 589832 | tf_op jit(solution)/shard_map/ppermute | solution.py:394
  70.8 17.1 %collective-permute-start.17 = (bf16[128,768]{1,0:T(8,128)(2,1)}, bf16[128,768]{1,0:T(8,128)(2,1)}, u32[]{:S(2)}, u32[]{:S(2)}) collective-permute-start(bf16[128,768]{1,0:T(8,128)(2,1)} %add_after.18.after_ref.total_ref), channel_id=1, source_target_pairs={{1,0},{2,3},{5,4},{6,7},{9,8},{10,11},{13,12},{14,15},{17,16},{18,... | collective-permute-start | bytes 589832 | tf_op jit(solution)/shard_map/ppermute | solution.py:394
  72.2 17.9 %collective-permute-start.18 = (bf16[128,768]{1,0:T(8,128)(2,1)S(1)}, bf16[128,768]{1,0:T(8,128)(2,1)}, u32[]{:S(2)}, u32[]{:S(2)}) collective-permute-start(bf16[128,768]{1,0:T(8,128)(2,1)S(1)} %add_after.19.refs_0_.total_ref), channel_id=1, source_target_pairs={{1,0},{2,3},{5,4},{6,7},{9,8},{10,11},{13,12},{14,15},{17,16},{18,... | collective-permute-start | bytes 589832 | tf_op jit(solution)/shard_map/ppermute | solution.py:394
  91.9 10.2 %collective-permute-start.20 = (bf16[64,1792]{1,0:T(8,128)(2,1)S(1)}, bf16[64,1792]{1,0:T(8,128)(2,1)S(1)}, u32[]{:S(2)}, u32[]{:S(2)}) collective-permute-start(bf16[64,1792]{1,0:T(8,128)(2,1)S(1)} %get-tuple-element.51), channel_id=1, source_target_pairs={{0,1},{1,0},{2,3},{3,2},{4,5},{5,4},{6,7},{7,6},{8,9},{9,8},{10,11... | collective-permute-start | bytes 688136 | tf_op jit(solution)/shard_map/ppermute | solution.py:45
  94.7 16.8 %collective-permute-start.19 = (bf16[64,2304]{1,0:T(8,128)(2,1)S(1)}, bf16[64,2304]{1,0:T(8,128)(2,1)S(1)}, u32[]{:S(2)}, u32[]{:S(2)}) collective-permute-start(bf16[64,2304]{1,0:T(8,128)(2,1)S(1)} %get-tuple-element.49), channel_id=1, source_target_pairs={{0,1},{1,0},{2,3},{3,2},{4,5},{5,4},{6,7},{7,6},{8,9},{9,8},{10,11... | collective-permute-start | bytes 884744 | tf_op jit(solution)/shard_map/ppermute | solution.py:45
  102.1 9.2 %collective-permute-start.21 = (bf16[32,1792]{1,0:T(8,128)(2,1)S(1)}, bf16[32,1792]{1,0:T(8,128)(2,1)S(1)}, u32[]{:S(2)}, u32[]{:S(2)}) collective-permute-start(bf16[32,1792]{1,0:T(8,128)(2,1)S(1)} %get-tuple-element.53), channel_id=1, source_target_pairs={{0,2},{1,3},{2,0},{3,1},{4,6},{5,7},{6,4},{7,5},{8,10},{9,11},{10,... | collective-permute-start | bytes 344072 | tf_op jit(solution)/shard_map/ppermute | solution.py:45
  111.5 7.3 %collective-permute-start.22 = (bf16[32,2304]{1,0:T(8,128)(2,1)S(1)}, bf16[32,2304]{1,0:T(8,128)(2,1)S(1)}, u32[]{:S(2)}, u32[]{:S(2)}) collective-permute-start(bf16[32,2304]{1,0:T(8,128)(2,1)S(1)} %get-tuple-element.55), channel_id=1, source_target_pairs={{0,2},{1,3},{2,0},{3,1},{4,6},{5,7},{6,4},{7,5},{8,10},{9,11},{10,... | collective-permute-start | bytes 442376 | tf_op jit(solution)/shard_map/ppermute | solution.py:45
  (19 other events, 111.6 us)

commit v5 on v3

--- a/solution.py
+++ b/solution.py
@@ -13,26 +13,10 @@
 HEAD_DIM = 128
 HID_SPLIT = 4
 STACK = 4
-WIDTHS = (896, 896, 768, 768, 768)
+WIDTHS = (2048, 2048)
 SPANS = tuple((sum(WIDTHS[:i]), width) for i, width in enumerate(WIDTHS))
 PAD_ROWS = 16
-ORDER = (
-    ("near", 0),
-    ("near", 1),
-    ("total", 0),
-    ("near", 2),
-    ("total", 1),
-    ("near", 3),
-    ("absorb", 0),
-    ("near", 4),
-    ("total", 2),
-    ("absorb", 1),
-    ("total", 3),
-    ("total", 4),
-    ("absorb", 2),
-    ("absorb", 3),
-    ("absorb", 4),
-)
+BASE = 64
 LOG2E = 1.4426950408889634
 VMEM = pl.BlockSpec(memory_space=pltpu.VMEM)
 ANY = pl.BlockSpec(memory_space=pl.ANY)
@@ -43,22 +27,20 @@
     return lax.ppermute(value, axis, [(i, i ^ offset) for i in range(size)])
 
 
-def attend_kernel(rank_ref, bound_ref, same_ref, other_ref, q_hbm, resid_hbm, w_hbm, *refs):
-    outs = refs[: len(WIDTHS)]
-    q_ref, resid_ref, w_buf, k_buf, v_buf, bias, attended, acc, sems, side = refs[len(WIDTHS) :]
+def attend_kernel(rank_ref, same_ref, other_ref, q_ref, resid_ref, w_hbm, *refs):
+    outs = refs[: 2 * len(WIDTHS)]
+    w_buf, k_buf, v_buf, bias, attended, acc, sems = refs[2 * len(WIDTHS) :]
     tok = q_ref.shape[0]
     heads = q_ref.shape[1] // HEAD_DIM
-    q_copy = pltpu.make_async_copy(q_hbm, q_ref, side.at[0])
-    q_copy.start()
-    resid_copy = pltpu.make_async_copy(resid_hbm, resid_ref, side.at[1])
-    resid_copy.start()
     copies = []
     for chunk, (first, width) in enumerate(SPANS):
         span = pl.ds(first, width)
         copy = pltpu.make_async_copy(w_hbm.at[:, span], w_buf.at[:, span], sems.at[chunk])
         copy.start()
         copies.append(copy)
-    bound = bound_ref[...]
+    extra = same_ref[0, tok : tok + PAD_ROWS, :].astype(jnp.float32)
+    bound = extra[1:2, :tok] * BASE + extra[1:2, tok:]
+    bound = jnp.broadcast_to(bound, (tok, tok)).T
     lane = lax.broadcasted_iota(jnp.int32, (1, tok), 1).astype(jnp.float32)
     ones = jnp.ones((tok, HEAD_DIM), jnp.bfloat16)
     half_count = same_ref.shape[0]
@@ -72,7 +54,6 @@
         place = start * tok + lane
         bias[:, rows] = jnp.where(place <= bound, 0.0, -1e30)
     factor = HEAD_DIM ** (-0.5) * LOG2E
-    q_copy.wait()
 
     def some_heads(step, carry):
         base = step * STACK * HEAD_DIM
@@ -96,10 +77,13 @@
             attended[:, pl.ds(start, HEAD_DIM)] = result[j * tok : (j + 1) * tok]
         return carry
 
-    lax.fori_loop(0, heads // STACK, some_heads, 0)
-    resid_copy.wait()
+    lax.fori_loop(0, heads // STACK, some_heads, 0, unroll=True)
     home = resid_ref.shape[0]
-    top = pl.multiple_of(rank_ref[0] * home, home)
+    rank = rank_ref[0]
+    side = rank % 2
+    kept = [pl.multiple_of((side + 2 * i) * home, home) for i in range(2)]
+    leaving = [pl.multiple_of((1 - side + 2 * i) * home, home) for i in range(2)]
+    top = pl.multiple_of(rank * home, home)
     for chunk, (first, width) in enumerate(SPANS):
         copies[chunk].wait()
         span = slice(first, first + width)
@@ -107,20 +91,25 @@
             attended[...], w_buf[:, span], preferred_element_type=jnp.float32
         )
         acc[pl.ds(top, home), span] += resid_ref[:, span].astype(jnp.float32)
-        outs[chunk][...] = acc[:, span].astype(jnp.bfloat16)
-
-
-def attend_project(rank, bounds, same, other, queries, residual, w_out):
+        for i in range(2):
+            rows = slice(i * home, (i + 1) * home)
+            outs[2 * chunk][rows, :] = acc[pl.ds(kept[i], home), span].astype(jnp.bfloat16)
+            outs[2 * chunk + 1][rows, :] = acc[pl.ds(leaving[i], home), span].astype(
+                jnp.bfloat16
+            )
+
+
+def attend_project(rank, same, other, queries, residual, w_out):
     tok, width = queries.shape
     keys_in_all = 2 * same.shape[0] * tok
     return pl.pallas_call(
         attend_kernel,
-        out_shape=[jax.ShapeDtypeStruct((tok, w), jnp.bfloat16) for w in WIDTHS],
-        in_specs=[pl.BlockSpec(memory_space=pltpu.SMEM)] + [VMEM] * 3 + [ANY] * 3,
-        out_specs=[VMEM] * len(WIDTHS),
+        out_shape=[
+            jax.ShapeDtypeStruct((tok // 2, w), jnp.bfloat16) for w in WIDTHS for _ in range(2)
+        ],
+        in_specs=[pl.BlockSpec(memory_space=pltpu.SMEM)] + [VMEM] * 4 + [ANY],
+        out_specs=[VMEM] * (2 * len(WIDTHS)),
         scratch_shapes=[
-            pltpu.VMEM(queries.shape, jnp.bfloat16),
-            pltpu.VMEM(residual.shape, jnp.bfloat16),
             pltpu.VMEM((width, D), jnp.bfloat16),
             pltpu.VMEM((keys_in_all, HEAD_DIM), jnp.bfloat16),
             pltpu.VMEM((keys_in_all, 2 * HEAD_DIM), jnp.bfloat16),
@@ -128,41 +117,40 @@
             pltpu.VMEM((tok, width), jnp.bfloat16),
             pltpu.VMEM((tok, D), jnp.float32),
             pltpu.SemaphoreType.DMA((len(WIDTHS),)),
-            pltpu.SemaphoreType.DMA((2,)),
         ],
-        compiler_params=pltpu.CompilerParams(vmem_limit_bytes=40 * 1024 * 1024),
+        compiler_params=pltpu.CompilerParams(vmem_limit_bytes=44 * 1024 * 1024),
+        cost_estimate=pl.CostEstimate(
+            flops=2 * tok * width * (2 * keys_in_all + D),
+            bytes_accessed=2 * width * D,
+            transcendentals=tok * width // HEAD_DIM * keys_in_all,
+        ),
+        name="attend_project",
+    )(rank, same, other, queries, residual, w_out)
+
+
+def stage_kernel(q_hbm, resid_hbm, q_ref, resid_ref, sems):
+    copies = [
+        pltpu.make_async_copy(q_hbm, q_ref, sems.at[0]),
+        pltpu.make_async_copy(resid_hbm, resid_ref, sems.at[1]),
+    ]
+    for copy in copies:
+        copy.start()
+    for copy in copies:
+        copy.wait()
+
+
+def stage(queries, residual):
+    arrays = (queries, residual)
+    return pl.pallas_call(
+        stage_kernel,
+        out_shape=[jax.ShapeDtypeStruct(array.shape, array.dtype) for array in arrays],
+        in_specs=[ANY, ANY],
+        out_specs=[VMEM, VMEM],
+        scratch_shapes=[pltpu.SemaphoreType.DMA((2,))],
+        compiler_params=pltpu.CompilerParams(vmem_limit_bytes=4 * 1024 * 1024),
         cost_estimate=LIGHT,
-        name="attend_project",
-    )(rank, bounds, same, other, queries, residual, w_out)
-
-
-def down_kernel(rank_ref, coef_ref, a0, a1, a2, a3, back_ref, out_ref):
-    count, _, width = back_ref.shape
-    coef = coef_ref[...]
-    blended = [(a[...].astype(jnp.float32) * coef).astype(jnp.bfloat16) for a in (a0, a1, a2, a3)]
-    hidden = blended[0].shape[1]
-    for block in range(count):
-        total = None
-        for s in range(len(blended)):
-            rows = pl.ds(pl.multiple_of((rank_ref[0] ^ s) * hidden, hidden), hidden)
-            term = jnp.dot(
-                blended[s], back_ref[block, rows, :], preferred_element_type=jnp.float32
-            )
-            total = term if total is None else total + term
-        out_ref[:, block * width : (block + 1) * width] = total.astype(jnp.bfloat16)
-
-
-def down(rank, coefficient, acts, back):
-    rows = acts[0].shape[0]
-    return pl.pallas_call(
-        down_kernel,
-        out_shape=jax.ShapeDtypeStruct((rows, D), jnp.bfloat16),
-        in_specs=[pl.BlockSpec(memory_space=pltpu.SMEM)] + [VMEM] * 6,
-        out_specs=VMEM,
-        compiler_params=pltpu.CompilerParams(vmem_limit_bytes=12 * 1024 * 1024),
-        cost_estimate=LIGHT,
-        name="down",
-    )(rank, coefficient, *acts, back)
+        name="stage",
+    )(*arrays)
 
 
 def join_kernel(*refs):
@@ -188,38 +176,18 @@
     )(after, *pieces)
 
 
-def add_kernel(a_ref, b_ref, after_ref, out_ref):
-    out_ref[...] = (a_ref[...].astype(jnp.float32) + b_ref[...].astype(jnp.float32)).astype(
-        jnp.bfloat16
-    )
-
-
-def add_after(left, right, after):
-    return pl.pallas_call(
-        add_kernel,
-        out_shape=jax.ShapeDtypeStruct(left.shape, jnp.bfloat16),
-        in_specs=[VMEM, VMEM, ANY],
-        out_specs=VMEM,
-        compiler_params=pltpu.CompilerParams(vmem_limit_bytes=4 * 1024 * 1024),
-        cost_estimate=LIGHT,
-        name="add_after",
-    )(left, right, after)
-
-
-def absorb_kernel(chunk, flag_ref, total_ref, outward_ref, gain_ref, w_ref, *refs):
+def absorb_kernel(chunk, rank_ref, mine_ref, theirs_ref, gain_ref, w_ref, *refs):
     last = chunk == len(WIDTHS) - 1
-    states = refs[1 : 1 if chunk == 0 else 3]
-    outs = refs[1 + len(states) : -1]
-    scratch = refs[-1]
+    state_count = 0 if chunk == 0 else 2
+    states = refs[:state_count]
+    home_ref = refs[state_count + int(last)]
+    outs = refs[state_count + int(last) + 1 :]
     first, width = SPANS[chunk]
     span = slice(first, first + width)
-    middle = jnp.where(flag_ref[1] == 1, outward_ref[...], total_ref[...])
-    scratch[...] = middle
-    home_ref = outs[0]
     home = home_ref.shape[0]
-    top = pl.multiple_of(flag_ref[0] * home, home)
-    home_ref[...] = scratch[pl.ds(top, home), :]
-    wide = middle.astype(jnp.float32)
+    place = rank_ref[0] // 2
+    home_ref[...] = mine_ref[pl.ds(pl.multiple_of(place * home, home), home), :]
+    wide = jnp.concatenate([mine_ref[...], theirs_ref[...]], axis=0).astype(jnp.float32)
     gained = (wide * gain_ref[:, span]).astype(jnp.bfloat16)
     product = lax.dot_general(
         gained, w_ref[:, span], (((1,), (1,)), ((), ())), preferred_element_type=jnp.float32
@@ -231,43 +199,56 @@
     if chunk > 0:
         product += states[0][...]
         square += states[1][...]
-    if last:
-        hidden = product.shape[1] // 2
-        mean_square = jnp.sum(square, axis=1, keepdims=True) / D
-        product = product * lax.rsqrt(mean_square + 1e-06)
-        gate = product[:, :hidden]
-        act = gate / (1.0 + jnp.exp(-gate)) * product[:, hidden:]
-        outs[1][...] = act.astype(jnp.bfloat16)
+    if not last:
+        outs[0][...] = product
+        outs[1][...] = square
+        return
+    back_ref = refs[state_count]
+    shares, act_buf = outs[:-1], outs[-1]
+    hidden = product.shape[1] // 2
+    mean_square = jnp.sum(square, axis=1, keepdims=True) / D
+    product = product * lax.rsqrt(mean_square + 1e-06)
+    gate = product[:, :hidden]
+    act_buf[...] = gate / (1.0 + jnp.exp(-gate)) * product[:, hidden:]
+    ordered = []
+    for offset in range(len(shares)):
+        row = (offset % 2) * 2 * home + (place ^ (offset // 2)) * home
+        ordered.append(act_buf[pl.ds(pl.multiple_of(row, home), home), :])
+    ordered = jnp.concatenate(ordered, axis=0).astype(jnp.bfloat16)
+    for part_first, part_width in SPANS:
+        part = slice(part_first, part_first + part_width)
+        result = jnp.dot(ordered, back_ref[:, part], preferred_element_type=jnp.float32)
+        for i, share in enumerate(shares):
+            share[:, part] = result[i * home : (i + 1) * home].astype(jnp.bfloat16)
+
+
+def absorb(chunk, rank, mine, theirs, gain, w_in, states, back):
+    half, width = mine.shape
+    rows = w_in.shape[0]
+    count = lax.axis_size("exp")
+    home = 2 * half // count
+    out_shape = [jax.ShapeDtypeStruct((home, width), jnp.bfloat16)]
+    scratch = []
+    operands = [rank, mine, theirs, gain, w_in, *states]
+    if chunk == len(WIDTHS) - 1:
+        operands.append(back)
+        out_shape += [jax.ShapeDtypeStruct((home, D), jnp.bfloat16)] * count
+        scratch = [pltpu.VMEM((2 * half, rows // 2), jnp.float32)]
     else:
-        outs[1][...] = product
-        outs[2][...] = square
-
-
-def absorb(chunk, flags, total, outward, gain, w_in, after, states):
-    tok, width = total.shape
-    rows = w_in.shape[0]
-    home = jax.ShapeDtypeStruct((tok // lax.axis_size("exp"), width), jnp.bfloat16)
-    if chunk == len(WIDTHS) - 1:
-        out_shape = [home, jax.ShapeDtypeStruct((tok, rows // 2), jnp.bfloat16)]
-    else:
-        out_shape = [
-            home,
-            jax.ShapeDtypeStruct((tok, rows), jnp.float32),
-            jax.ShapeDtypeStruct((tok, 128), jnp.float32),
+        out_shape += [
+            jax.ShapeDtypeStruct((2 * half, rows), jnp.float32),
+            jax.ShapeDtypeStruct((2 * half, 128), jnp.float32),
         ]
     return pl.pallas_call(
         functools.partial(absorb_kernel, chunk),
         out_shape=out_shape,
-        in_specs=[pl.BlockSpec(memory_space=pltpu.SMEM)]
-        + [VMEM] * 4
-        + [ANY]
-        + [VMEM] * len(states),
+        in_specs=[pl.BlockSpec(memory_space=pltpu.SMEM)] + [VMEM] * (len(operands) - 1),
         out_specs=[VMEM] * len(out_shape),
-        scratch_shapes=[pltpu.VMEM((tok, width), jnp.bfloat16)],
-        compiler_params=pltpu.CompilerParams(vmem_limit_bytes=12 * 1024 * 1024),
+        scratch_shapes=scratch,
+        compiler_params=pltpu.CompilerParams(vmem_limit_bytes=16 * 1024 * 1024),
         cost_estimate=LIGHT,
         name="absorb",
-    )(flags, total, outward, gain, w_in, after, *states)
+    )(*operands)
 
 
 def own_heads(queries, keys, values):
@@ -298,12 +279,19 @@
     ctx_count = lax.axis_size("ctx")
     exp_count = lax.axis_size("exp")
     rank = lax.axis_index("exp")
-    place = lax.axis_index("ctx")
     key_head, value_head = own_heads(queries, keys, values)
+    staged_queries, staged_residual = stage(queries, residual)
     block = (positions[0] // tok).astype(jnp.bfloat16)
-    pair = jnp.concatenate([key_head, value_head], axis=1)
+    limits = jnp.concatenate([bounds // BASE, bounds % BASE]).astype(jnp.bfloat16)
+    width = 2 * HEAD_DIM
     payload = jnp.concatenate(
-        [pair, jnp.full((PAD_ROWS, 2 * HEAD_DIM), block, jnp.bfloat16)], axis=0
+        [
+            jnp.concatenate([key_head, value_head], axis=1),
+            jnp.full((1, width), block, jnp.bfloat16),
+            limits.reshape(1, width),
+            jnp.zeros((PAD_ROWS - 2, width), jnp.bfloat16),
+        ],
+        axis=0,
     )
     same_rows = join_after(
         [payload] + [exchange(payload, "ctx", r, ctx_count) for r in range(2, ctx_count, 2)],
@@ -311,52 +299,33 @@
     )
     same_keys = same_rows.reshape(ctx_count // 2, tok + PAD_ROWS, 2 * HEAD_DIM)
     other_keys = exchange(same_rows, "ctx", 1, ctx_count).reshape(same_keys.shape)
-    flat_back = w_back.reshape(hidden, D)
-    mine = lax.dynamic_slice_in_dim(flat_back, place * (D // ctx_count), D // ctx_count, 1)
-    all_back = lax.all_gather(mine, ("ctx", "exp"), axis=0, tiled=True)
-    all_back = all_back.reshape(ctx_count, exp_count * hidden, D // ctx_count)
-
+    ranks = rank.astype(jnp.int32).reshape(1)
     parts = attend_project(
-        rank.astype(jnp.int32).reshape(1),
-        bounds.astype(jnp.float32).reshape(tok, 1),
-        same_keys,
-        other_keys,
-        queries,
-        residual,
-        w_out,
-    )
-    at_end = (rank == 0) | (rank == exp_count - 1)
-    flags = jnp.stack([rank, at_end]).astype(jnp.int32)
+        ranks, same_keys, other_keys, staged_queries, staged_residual, w_out
+    )
     gain = norm_gain.reshape(1, D)
     flat_in = w_in.reshape(2 * hidden, D)
-    count = len(parts)
-    inward = [lax.ppermute(part, "exp", [(0, 1), (3, 2)]) for part in parts]
-    near, across, total, outward = {}, {}, {}, {}
-    homes, states, after = [], [], parts[0]
-    for step, chunk in ORDER:
-        if step == "near":
-            after = near[chunk] = add_after(parts[chunk], inward[chunk], after)
-            across[chunk] = lax.ppermute(near[chunk], "exp", [(1, 2), (2, 1)])
-        elif step == "total":
-            after = total[chunk] = add_after(near[chunk], across[chunk], after)
-            outward[chunk] = lax.ppermute(total[chunk], "exp", [(1, 0), (2, 3)])
-        else:
-            own, *states = absorb(
-                chunk, flags, total[chunk], outward[chunk], gain, flat_in, after, states
-            )
-            homes.append(own)
-            after = states[0]
+    flat_back = w_back.reshape(hidden, D)
+    count = len(WIDTHS)
+    arrived = [exchange(parts[2 * i + 1], "exp", 1, exp_count) for i in range(count)]
+    near = [parts[2 * i] + arrived[i] for i in range(count)]
+    across = [exchange(near[i], "exp", 2, exp_count) for i in range(count)]
+    mine = [near[i] + across[i] for i in range(count)]
+    theirs = [exchange(mine[i], "exp", 1, exp_count) for i in range(count)]
+    homes, states = [], []
+    for chunk in range(count):
+        own, *states = absorb(
+            chunk, ranks, mine[chunk], theirs[chunk], gain, flat_in, states, flat_back
+        )
+        homes.append(own)
     middle_out = jnp.concatenate(homes, axis=1)
-    activated = states[0]
-    acts = [lax.dynamic_slice_in_dim(activated, rank * home, home, 0)]
+    expert = states[0].astype(jnp.float32)
     for offset in range(1, exp_count):
-        leaving = lax.dynamic_slice_in_dim(activated, (rank ^ offset) * home, home, 0)
-        acts.append(exchange(leaving, "exp", offset, exp_count))
+        expert = expert + exchange(states[offset], "exp", offset, exp_count).astype(jnp.float32)
     shares = gates / jnp.sum(gates, axis=1, keepdims=True)
     coefficient = jnp.sum(jnp.where(routes == 0, shares, 0.0), axis=1, keepdims=True)
     coefficient = coefficient.astype(jnp.bfloat16).astype(jnp.float32)
-    expert_out = down(flags, coefficient, acts, all_back)
-    return (middle_out, expert_out)
+    return (middle_out, (expert * coefficient).astype(jnp.bfloat16))
 
 
 def largest_divisor(row_count):

time: 134 us -> 99.9 us (0.75)
  starting transfers between devices: 36.2 us -> 15.9 us
  between operations: 17 us -> 3.41 us
  waiting for transfers between devices: 47.7 us -> 59.1 us
  local copies, waits for them, and re-layouts: 10.7 us -> 2.88 us
  Pallas kernels: 20.3 us -> 13.2 us
  other arithmetic: 0.79 us -> 3.36 us
    ppermute x7 -> x13, waiting for transfers between devices: 10.3 us -> 59.1 us  [exchange(): return lax.ppermute(value, axis, [(i, i ^ offset) for i in range(size)])]
    ppermute x15 -> x0, waiting for transfers between devices: 37.4 us -> none  [the longest x5 26.9 us: line_device(): inward = [lax.ppermute(part, 'exp', [(0, 1), (3, 2)]) for part in parts]]
    ppermute x15 -> x0, starting transfers between devices: 27.1 us -> none  [the longest x5 16.6 us: line_device(): inward = [lax.ppermute(part, 'exp', [(0, 1), (3, 2)]) for part in parts]]
    unnamed x28 -> x14, local copies, waits for them, and re-layouts: 9.02 us -> 2.02 us
    ppermute x7 -> x13, starting transfers between devices: 9.06 us -> 15.9 us  [exchange(): return lax.ppermute(value, axis, [(i, i ^ offset) for i in range(size)])]
    pallas_call x12 -> x2, Pallas kernels: 15.8 us -> 9.26 us  [the longest x1 9.18 us: attend_project(): pl.pallas_call(attend_kernel, out_shape=[jax.ShapeDtypeStruct((tok // 2,...]
    concatenate x1 -> x3, other arithmetic: 0.01 us -> 1.49 us  [the longest x1 0.72 us: line_device(): middle_out = jnp.concatenate(homes, axis=1)]
    pallas_call x5 -> x2, Pallas kernels: 4.5 us -> 3.93 us  [absorb(): pl.pallas_call(functools.partial(absorb_kernel, chunk), out_shape=out_sha...]
  transfers between devices with their start and end apart: 23 -> 13, of which waited for: 14 -> 11; matrix products, arithmetic and copies ran while one was open for 1% -> 2% of each run, Pallas kernels for 13% -> 2%
where the time goes in v5:
time: 99.9 us; the launch traced here: 98 us
  waiting for transfers between devices  59.1 us (59%)
  starting transfers between devices  15.9 us (16%)
  Pallas kernels  13.2 us (13%)
  between operations  3.41 us (3%)
  other arithmetic  3.36 us (3%)
  local copies, waits for them, and re-layouts  2.88 us (3%)
    ppermute x13, waiting for transfers between devices, exchange(): return lax.ppermute(value, axis, [(i, i ^ offset) for i in range(size)])  59.1 us
    ppermute x13, starting transfers between devices, exchange(): return lax.ppermute(value, axis, [(i, i ^ offset) for i in range(size)])  15.9 us
    pallas_call x1, Pallas kernels, attend_project(): pl.pallas_call(attend_kernel, out_shape=[jax.ShapeDtypeStruct((tok // 2,...  9.18 us
    pallas_call x2, Pallas kernels, absorb(): pl.pallas_call(functools.partial(absorb_kernel, chunk), out_shape=out_sha...  3.93 us
    unnamed x14, local copies, waits for them, and re-layouts  2.02 us
  transfers between devices with their start and end apart: 13, of which 11 were waited for; matrix products, arithmetic and copies ran while one was open for 2% of the time, Pallas kernels for 2%

profile of v5, /device:TPU:0, one launch (start us, length us, event | category | flops | bytes accessed | tf_op | source)
XLA Modules:
  0.0 98.0 jit_solution(9583598816506941716)
XLA Ops:
  4.9 3.0 %collective-permute-start = (bf16[144,256]{1,0:T(8,128)(2,1)S(1)}, bf16[144,256]{1,0:T(8,128)(2,1)S(1)}, u32[]{:S(2)}, u32[]{:S(2)}) collective-permute-start(bf16[144,256]{1,0:T(8,128)(2,1)S(1)} %maximum_maximum_fusion.refs_0_.refs_1_), channel_id=1, source_target_pairs={{0,8},{4,12},{8,0},{12,4},{16,24},{20,28},{24,16},{28,20},{1,9},{5... | collective-permute-start | bytes 221192 | tf_op jit(solution)/shard_map/ppermute | solution.py:27
  7.9 1.5 %collective-permute-start.1 = (bf16[144,256]{1,0:T(8,128)(2,1)S(1)}, bf16[144,256]{1,0:T(8,128)(2,1)S(1)}, u32[]{:S(2)}, u32[]{:S(2)}) collective-permute-start(bf16[144,256]{1,0:T(8,128)(2,1)S(1)} %maximum_maximum_fusion.refs_0_.refs_1_), channel_id=1, source_target_pairs={{0,16},{4,20},{8,24},{12,28},{16,0},{20,4},{24,8},{28,12},{1,17},{... | collective-permute-start | bytes 221192 | tf_op jit(solution)/shard_map/ppermute | solution.py:27
  9.5 1.0 %collective-permute-done.refs_2_ = bf16[144,256]{1,0:T(8,128)(2,1)S(1)} collective-permute-done((bf16[144,256]{1,0:T(8,128)(2,1)S(1)}, bf16[144,256]{1,0:T(8,128)(2,1)S(1)}, u32[]{:S(2)}, u32[]{:S(2)}) %collective-permute-start) | collective-permute-done | bytes 73760 | tf_op jit(solution)/shard_map/ppermute | solution.py:27
  10.4 1.8 %collective-permute-done.1.refs_3_ = bf16[144,256]{1,0:T(8,128)(2,1)S(1)} collective-permute-done((bf16[144,256]{1,0:T(8,128)(2,1)S(1)}, bf16[144,256]{1,0:T(8,128)(2,1)S(1)}, u32[]{:S(2)}, u32[]{:S(2)}) %collective-permute-start.1) | collective-permute-done | bytes 73760 | tf_op jit(solution)/shard_map/ppermute | solution.py:27
  12.3 2.4 %collective-permute-done.2.refs_4_ = bf16[144,256]{1,0:T(8,128)(2,1)S(1)} collective-permute-done((bf16[144,256]{1,0:T(8,128)(2,1)S(1)}, bf16[144,256]{1,0:T(8,128)(2,1)S(1)}, u32[]{:S(2)}, u32[]{:S(2)}) %collective-permute-start.2) | collective-permute-done | bytes 73760 | tf_op jit(solution)/shard_map/ppermute | solution.py:27
  14.8 1.0 %copy-done.2 = bf16[128,2048]{1,0:T(8,128)(2,1)S(1)} copy-done((bf16[128,2048]{1,0:T(8,128)(2,1)S(1)}, bf16[128,2048]{1,0:T(8,128)(2,1)}, u32[]{:S(2)}) %copy-start.2) | copy-done | bytes 524312
  15.8 0.9 copy-done.3
  16.9 9.2 %attend_project.1 = (bf16[64,2048]{1,0:T(8,128)(2,1)S(1)}, bf16[64,2048]{1,0:T(8,128)(2,1)S(1)}, bf16[64,2048]{1,0:T(8,128)(2,1)S(1)}, bf16[64,2048]{1,0:T(8,128)(2,1)S(1)}) custom-call(s32[1]{0:T(128)} %bitcast.rank_ref, bf16[4,144,256]{2,1,0:T(8,128)(2,1)S(1)} %bitcast.16, bf16[4,144,256]{2,1,0:T(8,128)(2,1)S(1)} %bitcast.17, ...), custom_call_target="tpu_custom_call" | custom-call | flops 3221225472 | bytes 16777216 | tf_op jit(solution)/shard_map/attend_project/pallas_call | solution.py:105
  26.1 1.6 %collective-permute-start.4 = (bf16[64,2048]{1,0:T(8,128)(2,1)S(1)}, bf16[64,2048]{1,0:T(8,128)(2,1)S(1)}, u32[]{:S(2)}, u32[]{:S(2)}) collective-permute-start(bf16[64,2048]{1,0:T(8,128)(2,1)S(1)} %get-tuple-element.19), channel_id=1, source_target_pairs={{0,1},{1,0},{2,3},{3,2},{4,5},{5,4},{6,7},{7,6},{8,9},{9,8},{10,11... | collective-permute-start | bytes 786440 | tf_op jit(solution)/shard_map/ppermute | solution.py:27
  28.2 7.1 %collective-permute-done.4 = bf16[64,2048]{1,0:T(8,128)(2,1)S(1)} collective-permute-done((bf16[64,2048]{1,0:T(8,128)(2,1)S(1)}, bf16[64,2048]{1,0:T(8,128)(2,1)S(1)}, u32[]{:S(2)}, u32[]{:S(2)}) %collective-permute-start.4) | collective-permute-done | bytes 262176 | tf_op jit(solution)/shard_map/ppermute | solution.py:27
  35.3 2.7 %collective-permute-start.5 = (bf16[64,2048]{1,0:T(8,128)(2,1)S(1)}, bf16[64,2048]{1,0:T(8,128)(2,1)S(1)}, u32[]{:S(2)}, u32[]{:S(2)}) collective-permute-start(bf16[64,2048]{1,0:T(8,128)(2,1)S(1)} %add.36), channel_id=1, source_target_pairs={{0,2},{1,3},{2,0},{3,1},{4,6},{5,7},{6,4},{7,5},{8,10},{9,11},{10,... | collective-permute-start | bytes 786440 | tf_op jit(solution)/shard_map/ppermute | solution.py:27
  38.0 6.9 %collective-permute-done.7 = bf16[64,2048]{1,0:T(8,128)(2,1)S(1)} collective-permute-done((bf16[64,2048]{1,0:T(8,128)(2,1)S(1)}, bf16[64,2048]{1,0:T(8,128)(2,1)S(1)}, u32[]{:S(2)}, u32[]{:S(2)}) %collective-permute-start.7) | collective-permute-done | bytes 262176 | tf_op jit(solution)/shard_map/ppermute | solution.py:27
  45.0 11.3 %collective-permute-done.5 = bf16[64,2048]{1,0:T(8,128)(2,1)S(1)} collective-permute-done((bf16[64,2048]{1,0:T(8,128)(2,1)S(1)}, bf16[64,2048]{1,0:T(8,128)(2,1)S(1)}, u32[]{:S(2)}, u32[]{:S(2)}) %collective-permute-start.5) | collective-permute-done | bytes 262176 | tf_op jit(solution)/shard_map/ppermute | solution.py:27
  57.1 1.3 %collective-permute-start.6 = (bf16[64,2048]{1,0:T(8,128)(2,1)}, bf16[64,2048]{1,0:T(8,128)(2,1)}, u32[]{:S(2)}, u32[]{:S(2)}) collective-permute-start(bf16[64,2048]{1,0:T(8,128)(2,1)} %add.37.mine_ref), channel_id=1, source_target_pairs={{0,1},{1,0},{2,3},{3,2},{4,5},{5,4},{6,7},{7,6},{8,9},{9,8},{10,11... | collective-permute-start | bytes 786440 | tf_op jit(solution)/shard_map/ppermute | solution.py:27
  58.3 2.5 %collective-permute-done.8 = bf16[64,2048]{1,0:T(8,128)(2,1)S(1)} collective-permute-done((bf16[64,2048]{1,0:T(8,128)(2,1)S(1)}, bf16[64,2048]{1,0:T(8,128)(2,1)S(1)}, u32[]{:S(2)}, u32[]{:S(2)}) %collective-permute-start.8) | collective-permute-done | bytes 262176 | tf_op jit(solution)/shard_map/ppermute | solution.py:27
  60.9 0.8 collective-permute-start.9
  61.8 4.8 %collective-permute-done.6.theirs_ref = bf16[64,2048]{1,0:T(8,128)(2,1)} collective-permute-done((bf16[64,2048]{1,0:T(8,128)(2,1)}, bf16[64,2048]{1,0:T(8,128)(2,1)}, u32[]{:S(2)}, u32[]{:S(2)}) %collective-permute-start.6) | collective-permute-done | bytes 262176 | tf_op jit(solution)/shard_map/ppermute | solution.py:27
  66.6 1.6 %absorb.2 = (bf16[32,2048]{1,0:T(8,128)(2,1)S(1)}, f32[128,384]{1,0:T(8,128)S(1)}, f32[128,128]{1,0:T(8,128)S(1)}) custom-call(s32[1]{0:T(128)} %bitcast.rank_ref, bf16[64,2048]{1,0:T(8,128)(2,1)} %add.37.mine_ref, bf16[64,2048]{1,0:T(8,128)(2,1)} %collective-permute-done.6.theirs_ref, f32[1,4096]{1,0:T(1,128)S(1)} %bitcast.18, bf16[384,4096]{1,0:T(8,128)(2,1)S(1)} %bitcast.13), custom_call_target="tpu_custom_call" | custom-call | flops 1024 | bytes 1024 | tf_op jit(solution)/shard_map/absorb/pallas_call | solution.py:242
  68.2 3.9 %collective-permute-done.9.theirs_ref = bf16[64,2048]{1,0:T(8,128)(2,1)} collective-permute-done((bf16[64,2048]{1,0:T(8,128)(2,1)S(1)}, bf16[64,2048]{1,0:T(8,128)(2,1)}, u32[]{:S(2)}, u32[]{:S(2)}) %collective-permute-start.9) | collective-permute-done | bytes 262176 | tf_op jit(solution)/shard_map/ppermute | solution.py:27
  72.1 2.3 %absorb.3 = (bf16[32,2048]{1,0:T(8,128)(2,1)S(1)}, bf16[32,4096]{1,0:T(8,128)(2,1)S(1)}, bf16[32,4096]{1,0:T(8,128)(2,1)S(1)}, bf16[32,4096]{1,0:T(8,128)(2,1)S(1)}, bf16[32,4096]{1,0:T(8,128)(2,1)S(1)}) custom-call(s32[1]{0:T(128)} %bitcast.rank_ref, bf16[64,2048]{1,0:T(8,128)(2,1)S(1)} %add.39.mine_ref, ...), custom_call_target="tpu_custom_call" | custom-call | flops 1024 | bytes 1024 | tf_op jit(solution)/shard_map/absorb/pallas_call | solution.py:242
  74.5 4.2 %collective-permute-start.11 = (bf16[32,4096]{1,0:T(8,128)(2,1)S(1)}, bf16[32,4096]{1,0:T(8,128)(2,1)S(1)}, u32[]{:S(2)}, u32[]{:S(2)}) collective-permute-start(bf16[32,4096]{1,0:T(8,128)(2,1)S(1)} %get-tuple-element.28), channel_id=1, source_target_pairs={{0,2},{1,3},{2,0},{3,1},{4,6},{5,7},{6,4},{7,5},{8,10},{9,11},{10,... | collective-permute-start | bytes 786440 | tf_op jit(solution)/shard_map/ppermute | solution.py:27
  79.6 7.8 %collective-permute-done.10 = bf16[32,4096]{1,0:T(8,128)(2,1)S(1)} collective-permute-done((bf16[32,4096]{1,0:T(8,128)(2,1)S(1)}, bf16[32,4096]{1,0:T(8,128)(2,1)S(1)}, u32[]{:S(2)}, u32[]{:S(2)}) %collective-permute-start.10) | collective-permute-done | bytes 262176 | tf_op jit(solution)/shard_map/ppermute | solution.py:27
  87.4 9.7 %collective-permute-done.11 = bf16[32,4096]{1,0:T(8,128)(2,1)S(1)} collective-permute-done((bf16[32,4096]{1,0:T(8,128)(2,1)S(1)}, bf16[32,4096]{1,0:T(8,128)(2,1)S(1)}, u32[]{:S(2)}, u32[]{:S(2)}) %collective-permute-start.11) | collective-permute-done | bytes 262176 | tf_op jit(solution)/shard_map/ppermute | solution.py:27
  97.1 0.9 multiply_convert_fusion
  (36 shorter events, 4.4 us)
Async XLA Ops:
  4.9 5.5 %collective-permute-start = (bf16[144,256]{1,0:T(8,128)(2,1)S(1)}, bf16[144,256]{1,0:T(8,128)(2,1)S(1)}, u32[]{:S(2)}, u32[]{:S(2)}) collective-permute-start(bf16[144,256]{1,0:T(8,128)(2,1)S(1)} %maximum_maximum_fusion.refs_0_.refs_1_), channel_id=1, source_target_pairs={{0,8},{4,12},{8,0},{12,4},{16,24},{20,28},{24,16},{28,20},{1,9},{5... | collective-permute-start | bytes 221192 | tf_op jit(solution)/shard_map/ppermute | solution.py:27
  7.9 4.4 %collective-permute-start.1 = (bf16[144,256]{1,0:T(8,128)(2,1)S(1)}, bf16[144,256]{1,0:T(8,128)(2,1)S(1)}, u32[]{:S(2)}, u32[]{:S(2)}) collective-permute-start(bf16[144,256]{1,0:T(8,128)(2,1)S(1)} %maximum_maximum_fusion.refs_0_.refs_1_), channel_id=1, source_target_pairs={{0,16},{4,20},{8,24},{12,28},{16,0},{20,4},{24,8},{28,12},{1,17},{... | collective-permute-start | bytes 221192 | tf_op jit(solution)/shard_map/ppermute | solution.py:27
  9.4 5.3 %collective-permute-start.2 = (bf16[144,256]{1,0:T(8,128)(2,1)S(1)}, bf16[144,256]{1,0:T(8,128)(2,1)S(1)}, u32[]{:S(2)}, u32[]{:S(2)}) collective-permute-start(bf16[144,256]{1,0:T(8,128)(2,1)S(1)} %maximum_maximum_fusion.refs_0_.refs_1_), channel_id=1, source_target_pairs={{0,24},{4,28},{8,16},{12,20},{16,8},{20,12},{24,0},{28,4},{1,25},{... | collective-permute-start | bytes 221192 | tf_op jit(solution)/shard_map/ppermute | solution.py:27
  14.7 2.2 %collective-permute-start.3 = (bf16[576,256]{1,0:T(8,128)(2,1)S(1)}, bf16[576,256]{1,0:T(8,128)(2,1)S(1)}, u32[]{:S(2)}, u32[]{:S(2)}) collective-permute-start(bf16[576,256]{1,0:T(8,128)(2,1)S(1)} %join_after.1), channel_id=1, source_target_pairs={{0,4},{4,0},{8,12},{12,8},{16,20},{20,16},{24,28},{28,24},{1,5},{5... | collective-permute-start | bytes 884744 | tf_op jit(solution)/shard_map/ppermute | solution.py:27
  14.8 1.0 %copy-start.2 = (bf16[128,2048]{1,0:T(8,128)(2,1)S(1)}, bf16[128,2048]{1,0:T(8,128)(2,1)}, u32[]{:S(2)}) copy-start(bf16[128,2048]{1,0:T(8,128)(2,1)} %q_hbm.1) | copy-start | bytes 1572868
  15.8 0.9 copy-start.3
  16.9 44.8 %copy-start.5 = (f32[32,8]{0,1:T(8,128)S(1)}, f32[32,8]{0,1:T(8,128)}, u32[]{:S(2)}) copy-start(f32[32,8]{0,1:T(8,128)} %param.21) | copy-start | bytes 3076
  16.9 44.8 %copy-start.6 = (s32[32,8]{0,1:T(8,128)S(1)}, s32[32,8]{0,1:T(8,128)}, u32[]{:S(2)}) copy-start(s32[32,8]{0,1:T(8,128)} %param.20) | copy-start | bytes 3076
  26.1 40.5 %copy-start = (bf16[1,384,4096]{2,1,0:T(8,128)(2,1)S(1)}, bf16[1,384,4096]{2,1,0:T(8,128)(2,1)}, u32[]{:S(2)}) copy-start(bf16[1,384,4096]{2,1,0:T(8,128)(2,1)} %param.22) | copy-start | bytes 9437188
  26.1 40.5 %copy-start.4 = (f32[4096]{0:T(1024)S(1)}, f32[4096]{0:T(1024)}, u32[]{:S(2)}) copy-start(f32[4096]{0:T(1024)} %param.19) | copy-start | bytes 49156
  26.1 9.2 %collective-permute-start.4 = (bf16[64,2048]{1,0:T(8,128)(2,1)S(1)}, bf16[64,2048]{1,0:T(8,128)(2,1)S(1)}, u32[]{:S(2)}, u32[]{:S(2)}) collective-permute-start(bf16[64,2048]{1,0:T(8,128)(2,1)S(1)} %get-tuple-element.19), channel_id=1, source_target_pairs={{0,1},{1,0},{2,3},{3,2},{4,5},{5,4},{6,7},{7,6},{8,9},{9,8},{10,11... | collective-permute-start | bytes 786440 | tf_op jit(solution)/shard_map/ppermute | solution.py:27
  27.8 17.1 %collective-permute-start.7 = (bf16[64,2048]{1,0:T(8,128)(2,1)S(1)}, bf16[64,2048]{1,0:T(8,128)(2,1)S(1)}, u32[]{:S(2)}, u32[]{:S(2)}) collective-permute-start(bf16[64,2048]{1,0:T(8,128)(2,1)S(1)} %get-tuple-element.22), channel_id=1, source_target_pairs={{0,1},{1,0},{2,3},{3,2},{4,5},{5,4},{6,7},{7,6},{8,9},{9,8},{10,11... | collective-permute-start | bytes 786440 | tf_op jit(solution)/shard_map/ppermute | solution.py:27
  35.3 21.0 %collective-permute-start.5 = (bf16[64,2048]{1,0:T(8,128)(2,1)S(1)}, bf16[64,2048]{1,0:T(8,128)(2,1)S(1)}, u32[]{:S(2)}, u32[]{:S(2)}) collective-permute-start(bf16[64,2048]{1,0:T(8,128)(2,1)S(1)} %add.36), channel_id=1, source_target_pairs={{0,2},{1,3},{2,0},{3,1},{4,6},{5,7},{6,4},{7,5},{8,10},{9,11},{10,... | collective-permute-start | bytes 786440 | tf_op jit(solution)/shard_map/ppermute | solution.py:27
  44.9 15.9 %collective-permute-start.8 = (bf16[64,2048]{1,0:T(8,128)(2,1)S(1)}, bf16[64,2048]{1,0:T(8,128)(2,1)S(1)}, u32[]{:S(2)}, u32[]{:S(2)}) collective-permute-start(bf16[64,2048]{1,0:T(8,128)(2,1)S(1)} %add.38), channel_id=1, source_target_pairs={{0,2},{1,3},{2,0},{3,1},{4,6},{5,7},{6,4},{7,5},{8,10},{9,11},{10,... | collective-permute-start | bytes 786440 | tf_op jit(solution)/shard_map/ppermute | solution.py:27
  57.1 9.5 %collective-permute-start.6 = (bf16[64,2048]{1,0:T(8,128)(2,1)}, bf16[64,2048]{1,0:T(8,128)(2,1)}, u32[]{:S(2)}, u32[]{:S(2)}) collective-permute-start(bf16[64,2048]{1,0:T(8,128)(2,1)} %add.37.mine_ref), channel_id=1, source_target_pairs={{0,1},{1,0},{2,3},{3,2},{4,5},{5,4},{6,7},{7,6},{8,9},{9,8},{10,11... | collective-permute-start | bytes 786440 | tf_op jit(solution)/shard_map/ppermute | solution.py:27
  60.9 11.2 %collective-permute-start.9 = (bf16[64,2048]{1,0:T(8,128)(2,1)S(1)}, bf16[64,2048]{1,0:T(8,128)(2,1)}, u32[]{:S(2)}, u32[]{:S(2)}) collective-permute-start(bf16[64,2048]{1,0:T(8,128)(2,1)S(1)} %add.39.mine_ref), channel_id=1, source_target_pairs={{0,1},{1,0},{2,3},{3,2},{4,5},{5,4},{6,7},{7,6},{8,9},{9,8},{10,11... | collective-permute-start | bytes 786440 | tf_op jit(solution)/shard_map/ppermute | solution.py:27
  61.7 10.3 %copy-start.1 = (bf16[1,192,4096]{2,1,0:T(8,128)(2,1)S(1)}, bf16[1,192,4096]{2,1,0:T(8,128)(2,1)}, u32[]{:S(2)}) copy-start(bf16[1,192,4096]{2,1,0:T(8,128)(2,1)} %param.23) | copy-start | bytes 4718596
  74.4 13.0 %collective-permute-start.10 = (bf16[32,4096]{1,0:T(8,128)(2,1)S(1)}, bf16[32,4096]{1,0:T(8,128)(2,1)S(1)}, u32[]{:S(2)}, u32[]{:S(2)}) collective-permute-start(bf16[32,4096]{1,0:T(8,128)(2,1)S(1)} %get-tuple-element.27), channel_id=1, source_target_pairs={{0,1},{1,0},{2,3},{3,2},{4,5},{5,4},{6,7},{7,6},{8,9},{9,8},{10,11... | collective-permute-start | bytes 786440 | tf_op jit(solution)/shard_map/ppermute | solution.py:27
  74.5 22.6 %collective-permute-start.11 = (bf16[32,4096]{1,0:T(8,128)(2,1)S(1)}, bf16[32,4096]{1,0:T(8,128)(2,1)S(1)}, u32[]{:S(2)}, u32[]{:S(2)}) collective-permute-start(bf16[32,4096]{1,0:T(8,128)(2,1)S(1)} %get-tuple-element.28), channel_id=1, source_target_pairs={{0,2},{1,3},{2,0},{3,1},{4,6},{5,7},{6,4},{7,5},{8,10},{9,11},{10,... | collective-permute-start | bytes 786440 | tf_op jit(solution)/shard_map/ppermute | solution.py:27
  78.6 18.5 %collective-permute-start.12 = (bf16[32,4096]{1,0:T(8,128)(2,1)S(1)}, bf16[32,4096]{1,0:T(8,128)(2,1)S(1)}, u32[]{:S(2)}, u32[]{:S(2)}) collective-permute-start(bf16[32,4096]{1,0:T(8,128)(2,1)S(1)} %get-tuple-element.29), channel_id=1, source_target_pairs={{0,3},{1,2},{2,1},{3,0},{4,7},{5,6},{6,5},{7,4},{8,11},{9,10},{10,... | collective-permute-start | bytes 786440 | tf_op jit(solution)/shard_map/ppermute | solution.py:27

commit v6 on v5

--- a/solution.py
+++ b/solution.py
@@ -13,10 +13,11 @@
 HEAD_DIM = 128
 HID_SPLIT = 4
 STACK = 4
-WIDTHS = (2048, 2048)
+WIDTHS = (1024, 1024, 1024, 1024)
 SPANS = tuple((sum(WIDTHS[:i]), width) for i, width in enumerate(WIDTHS))
 PAD_ROWS = 16
 BASE = 64
+IN_FLIGHT = 2
 LOG2E = 1.4426950408889634
 VMEM = pl.BlockSpec(memory_space=pltpu.VMEM)
 ANY = pl.BlockSpec(memory_space=pl.ANY)
@@ -307,11 +308,20 @@
     flat_in = w_in.reshape(2 * hidden, D)
     flat_back = w_back.reshape(hidden, D)
     count = len(WIDTHS)
-    arrived = [exchange(parts[2 * i + 1], "exp", 1, exp_count) for i in range(count)]
-    near = [parts[2 * i] + arrived[i] for i in range(count)]
-    across = [exchange(near[i], "exp", 2, exp_count) for i in range(count)]
-    mine = [near[i] + across[i] for i in range(count)]
-    theirs = [exchange(mine[i], "exp", 1, exp_count) for i in range(count)]
+
+    def swap(values, offset):
+        results = []
+        for i, value in enumerate(values):
+            if i >= IN_FLIGHT:
+                value, _ = lax.optimization_barrier((value, results[i - IN_FLIGHT]))
+            results.append(exchange(value, "exp", offset, exp_count))
+        return results
+
+    arrived = swap(parts[1::2], 1)
+    near = [kept + other for kept, other in zip(parts[::2], arrived)]
+    across = swap(near, 2)
+    mine = [own + other for own, other in zip(near, across)]
+    theirs = swap(mine, 1)
     homes, states = [], []
     for chunk in range(count):
         own, *states = absorb(

time: 99.9 us -> 92.1 us (0.922)
  waiting for transfers between devices: 59.1 us -> 41.8 us
  starting transfers between devices: 15.9 us -> 21.8 us
  local copies, waits for them, and re-layouts: 2.88 us -> 5.6 us
  other arithmetic: 3.36 us -> 4.66 us
    ppermute x13 -> x19, waiting for transfers between devices: 59.1 us -> 41.8 us  [exchange(): return lax.ppermute(value, axis, [(i, i ^ offset) for i in range(size)])]
    ppermute x13 -> x19, starting transfers between devices: 15.9 us -> 21.8 us  [exchange(): return lax.ppermute(value, axis, [(i, i ^ offset) for i in range(size)])]
    unnamed x14 -> x22, local copies, waits for them, and re-layouts: 2.02 us -> 4.74 us
    reduce_sum x1, other arithmetic: 0.02 us -> 1.27 us  [line_device(): shares = gates / jnp.sum(gates, axis=1, keepdims=True)]
    pallas_call x2 -> x4, Pallas kernels: 3.93 us -> 4.01 us  [absorb(): pl.pallas_call(functools.partial(absorb_kernel, chunk), out_shape=out_sha...]
  transfers between devices with their start and end apart: 13 -> 19, of which waited for: 11 -> 12; matrix products, arithmetic and copies ran while one was open for 2% -> 3% of each run, Pallas kernels for 2% -> 2%
where the time goes in v6:
time: 92.1 us; the launch traced here: 90.2 us
  waiting for transfers between devices  41.8 us (45%)
  starting transfers between devices  21.8 us (24%)
  Pallas kernels  12.9 us (14%)
  local copies, waits for them, and re-layouts  5.6 us (6%)
  other arithmetic  4.66 us (5%)
  between operations  3.51 us (4%)
    ppermute x19, waiting for transfers between devices, exchange(): return lax.ppermute(value, axis, [(i, i ^ offset) for i in range(size)])  41.8 us
    ppermute x19, starting transfers between devices, exchange(): return lax.ppermute(value, axis, [(i, i ^ offset) for i in range(size)])  21.8 us
    pallas_call x1, Pallas kernels, attend_project(): pl.pallas_call(attend_kernel, out_shape=[jax.ShapeDtypeStruct((tok // 2,...  8.75 us
    unnamed x22, local copies, waits for them, and re-layouts  4.74 us
    pallas_call x4, Pallas kernels, absorb(): pl.pallas_call(functools.partial(absorb_kernel, chunk), out_shape=out_sha...  4.01 us
  transfers between devices with their start and end apart: 19, of which 12 were waited for; matrix products, arithmetic and copies ran while one was open for 3% of the time, Pallas kernels for 2%

profile of v6, /device:TPU:0, one launch (start us, length us, event | category | flops | bytes accessed | tf_op | source)
XLA Modules:
  0.0 90.2 jit_solution(11622390577322781540)
XLA Ops:
  4.9 3.0 %collective-permute-start = (bf16[144,256]{1,0:T(8,128)(2,1)S(1)}, bf16[144,256]{1,0:T(8,128)(2,1)S(1)}, u32[]{:S(2)}, u32[]{:S(2)}) collective-permute-start(bf16[144,256]{1,0:T(8,128)(2,1)S(1)} %maximum_maximum_fusion.refs_0_.refs_1_), channel_id=1, source_target_pairs={{0,8},{4,12},{8,0},{12,4},{16,24},{20,28},{24,16},{28,20},{1,9},{5... | collective-permute-start | bytes 221192 | tf_op jit(solution)/shard_map/ppermute | solution.py:28
  7.9 1.5 %collective-permute-start.1 = (bf16[144,256]{1,0:T(8,128)(2,1)S(1)}, bf16[144,256]{1,0:T(8,128)(2,1)S(1)}, u32[]{:S(2)}, u32[]{:S(2)}) collective-permute-start(bf16[144,256]{1,0:T(8,128)(2,1)S(1)} %maximum_maximum_fusion.refs_0_.refs_1_), channel_id=1, source_target_pairs={{0,16},{4,20},{8,24},{12,28},{16,0},{20,4},{24,8},{28,12},{1,17},{... | collective-permute-start | bytes 221192 | tf_op jit(solution)/shard_map/ppermute | solution.py:28
  10.4 1.8 %collective-permute-done.1.refs_3_ = bf16[144,256]{1,0:T(8,128)(2,1)S(1)} collective-permute-done((bf16[144,256]{1,0:T(8,128)(2,1)S(1)}, bf16[144,256]{1,0:T(8,128)(2,1)S(1)}, u32[]{:S(2)}, u32[]{:S(2)}) %collective-permute-start.1) | collective-permute-done | bytes 73760 | tf_op jit(solution)/shard_map/ppermute | solution.py:28
  12.3 2.4 %collective-permute-done.2.refs_4_ = bf16[144,256]{1,0:T(8,128)(2,1)S(1)} collective-permute-done((bf16[144,256]{1,0:T(8,128)(2,1)S(1)}, bf16[144,256]{1,0:T(8,128)(2,1)S(1)}, u32[]{:S(2)}, u32[]{:S(2)}) %collective-permute-start.2) | collective-permute-done | bytes 73760 | tf_op jit(solution)/shard_map/ppermute | solution.py:28
  16.9 8.8 %attend_project.1 = (bf16[64,1024]{1,0:T(8,128)(2,1)S(1)}, bf16[64,1024]{1,0:T(8,128)(2,1)S(1)}, bf16[64,1024]{1,0:T(8,128)(2,1)S(1)}, bf16[64,1024]{1,0:T(8,128...) custom-call(s32[1]{0:T(128)} %bitcast.rank_ref, ...), custom_call_target="tpu_custom_call" | custom-call | flops 3221225472 | bytes 16777216 | tf_op jit(solution)/shard_map/attend_project/pallas_call | solution.py:106
  25.7 1.6 %collective-permute-start.4 = (bf16[64,1024]{1,0:T(8,128)(2,1)S(1)}, bf16[64,1024]{1,0:T(8,128)(2,1)S(1)}, u32[]{:S(2)}, u32[]{:S(2)}) collective-permute-start(bf16[64,1024]{1,0:T(8,128)(2,1)S(1)} %get-tuple-element.35), channel_id=1, source_target_pairs={{0,1},{1,0},{2,3},{3,2},{4,5},{5,4},{6,7},{7,6},{8,9},{9,8},{10,11... | collective-permute-start | bytes 393224 | tf_op jit(solution)/shard_map/ppermute | solution.py:28
  27.7 4.3 %collective-permute-done.4 = bf16[64,1024]{1,0:T(8,128)(2,1)S(1)} collective-permute-done((bf16[64,1024]{1,0:T(8,128)(2,1)S(1)}, bf16[64,1024]{1,0:T(8,128)(2,1)S(1)}, u32[]{:S(2)}, u32[]{:S(2)}) %collective-permute-start.4) | collective-permute-done | bytes 131104 | tf_op jit(solution)/shard_map/ppermute | solution.py:28
  32.1 2.6 %collective-permute-start.5 = (bf16[64,1024]{1,0:T(8,128)(2,1)S(1)}, bf16[64,1024]{1,0:T(8,128)(2,1)S(1)}, u32[]{:S(2)}, u32[]{:S(2)}) collective-permute-start(bf16[64,1024]{1,0:T(8,128)(2,1)S(1)} %add.48), channel_id=1, source_target_pairs={{0,2},{1,3},{2,0},{3,1},{4,6},{5,7},{6,4},{7,5},{8,10},{9,11},{10,... | collective-permute-start | bytes 393224 | tf_op jit(solution)/shard_map/ppermute | solution.py:28
  34.7 1.6 %collective-permute-start.10 = (bf16[64,1024]{1,0:T(8,128)(2,1)S(1)}, bf16[64,1024]{1,0:T(8,128)(2,1)S(1)}, u32[]{:S(2)}, u32[]{:S(2)}) collective-permute-start(bf16[64,1024]{1,0:T(8,128)(2,1)S(1)} %get-tuple-element.44), channel_id=1, source_target_pairs={{0,1},{1,0},{2,3},{3,2},{4,5},{5,4},{6,7},{7,6},{8,9},{9,8},{10,11... | collective-permute-start | bytes 393224 | tf_op jit(solution)/shard_map/ppermute | solution.py:28
  36.8 2.2 %collective-permute-start.8 = (bf16[64,1024]{1,0:T(8,128)(2,1)S(1)}, bf16[64,1024]{1,0:T(8,128)(2,1)S(1)}, u32[]{:S(2)}, u32[]{:S(2)}) collective-permute-start(bf16[64,1024]{1,0:T(8,128)(2,1)S(1)} %add.50), channel_id=1, source_target_pairs={{0,2},{1,3},{2,0},{3,1},{4,6},{5,7},{6,4},{7,5},{8,10},{9,11},{10,... | collective-permute-start | bytes 393224 | tf_op jit(solution)/shard_map/ppermute | solution.py:28
  38.9 2.4 %collective-permute-done.5 = bf16[64,1024]{1,0:T(8,128)(2,1)S(1)} collective-permute-done((bf16[64,1024]{1,0:T(8,128)(2,1)S(1)}, bf16[64,1024]{1,0:T(8,128)(2,1)S(1)}, u32[]{:S(2)}, u32[]{:S(2)}) %collective-permute-start.5) | collective-permute-done | bytes 131104 | tf_op jit(solution)/shard_map/ppermute | solution.py:28
  41.6 3.4 %collective-permute-done.10 = bf16[64,1024]{1,0:T(8,128)(2,1)S(1)} collective-permute-done((bf16[64,1024]{1,0:T(8,128)(2,1)S(1)}, bf16[64,1024]{1,0:T(8,128)(2,1)S(1)}, u32[]{:S(2)}, u32[]{:S(2)}) %collective-permute-start.10) | collective-permute-done | bytes 131104 | tf_op jit(solution)/shard_map/ppermute | solution.py:28
  45.2 5.0 %collective-permute-done.13 = bf16[64,1024]{1,0:T(8,128)(2,1)S(1)} collective-permute-done((bf16[64,1024]{1,0:T(8,128)(2,1)S(1)}, bf16[64,1024]{1,0:T(8,128)(2,1)S(1)}, u32[]{:S(2)}, u32[]{:S(2)}) %collective-permute-start.13) | collective-permute-done | bytes 131104 | tf_op jit(solution)/shard_map/ppermute | solution.py:28
  50.5 2.5 %collective-permute-start.9 = (bf16[64,1024]{1,0:T(8,128)(2,1)S(1)}, bf16[64,1024]{1,0:T(8,128)(2,1)S(1)}, u32[]{:S(2)}, u32[]{:S(2)}) collective-permute-start(bf16[64,1024]{1,0:T(8,128)(2,1)S(1)} %add.51.mine_ref), channel_id=1, source_target_pairs={{0,1},{1,0},{2,3},{3,2},{4,5},{5,4},{6,7},{7,6},{8,9},{9,8},{10,11... | collective-permute-start | bytes 393224 | tf_op jit(solution)/shard_map/ppermute | solution.py:28
  53.0 3.8 %collective-permute-done.11 = bf16[64,1024]{1,0:T(8,128)(2,1)S(1)} collective-permute-done((bf16[64,1024]{1,0:T(8,128)(2,1)S(1)}, bf16[64,1024]{1,0:T(8,128)(2,1)S(1)}, u32[]{:S(2)}, u32[]{:S(2)}) %collective-permute-start.11) | collective-permute-done | bytes 131104 | tf_op jit(solution)/shard_map/ppermute | solution.py:28
  57.6 1.1 %collective-permute-done.14 = bf16[64,1024]{1,0:T(8,128)(2,1)S(1)} collective-permute-done((bf16[64,1024]{1,0:T(8,128)(2,1)S(1)}, bf16[64,1024]{1,0:T(8,128)(2,1)S(1)}, u32[]{:S(2)}, u32[]{:S(2)}) %collective-permute-start.14) | collective-permute-done | bytes 131104 | tf_op jit(solution)/shard_map/ppermute | solution.py:28
  61.1 1.3 %reduce_sum.18 = f32[32]{0:T(128)} reduce(f32[32,8]{0,1:T(8,128)} %param.21, f32[]{:T(128)} %constant.65.clone.1), dimensions={1}, to_apply=%region_0.1 | reduce | flops 224 | bytes 1156 | tf_op jit(solution)/shard_map/reduce_sum | solution.py:335
  65.4 1.4 %absorb.6 = (bf16[32,1024]{1,0:T(8,128)(2,1)S(1)}, f32[128,384]{1,0:T(8,128)S(1)}, f32[128,128]{1,0:T(8,128)S(1)}) custom-call(s32[1]{0:T(128)} %bitcast.rank_ref, bf16[64,1024]{1,0:T(8,128)(2,1)S(1)} %add.53.mine_ref, bf16[64,1024]{1,0:T(8,128)(2,1)} %collective-permute-done.12.theirs_ref, f32[1,4096]{1,0:T(1,128)S(1)} %bitcast.22, ...), custom_call_target="tpu_custom_call" | custom-call | flops 1024 | bytes 1024 | tf_op jit(solution)/shard_map/absorb/pallas_call | solution.py:243
  66.8 1.9 %absorb.7 = (bf16[32,1024]{1,0:T(8,128)(2,1)S(1)}, bf16[32,4096]{1,0:T(8,128)(2,1)S(1)}, bf16[32,4096]{1,0:T(8,128)(2,1)S(1)}, bf16[32,4096]{1,0:T(8,128)(2,1)S(1)}, bf16[32,4096]{1,0:T(8,128)(2,1)S(1)}) custom-call(s32[1]{0:T(128)} %bitcast.rank_ref, bf16[64,1024]{1,0:T(8,128)(2,1)S(1)} %add.55.mine_ref, ...), custom_call_target="tpu_custom_call" | custom-call | flops 1024 | bytes 1024 | tf_op jit(solution)/shard_map/absorb/pallas_call | solution.py:243
  68.7 1.3 %collective-permute-start.16 = (bf16[32,4096]{1,0:T(8,128)(2,1)S(1)}, bf16[32,4096]{1,0:T(8,128)(2,1)S(1)}, u32[]{:S(2)}, u32[]{:S(2)}) collective-permute-start(bf16[32,4096]{1,0:T(8,128)(2,1)S(1)} %get-tuple-element.59), channel_id=1, source_target_pairs={{0,1},{1,0},{2,3},{3,2},{4,5},{5,4},{6,7},{7,6},{8,9},{9,8},{10,11... | collective-permute-start | bytes 786440 | tf_op jit(solution)/shard_map/ppermute | solution.py:28
  70.0 1.0 %collective-permute-start.17 = (bf16[32,4096]{1,0:T(8,128)(2,1)S(1)}, bf16[32,4096]{1,0:T(8,128)(2,1)S(1)}, u32[]{:S(2)}, u32[]{:S(2)}) collective-permute-start(bf16[32,4096]{1,0:T(8,128)(2,1)S(1)} %get-tuple-element.60), channel_id=1, source_target_pairs={{0,2},{1,3},{2,0},{3,1},{4,6},{5,7},{6,4},{7,5},{8,10},{9,11},{10,... | collective-permute-start | bytes 786440 | tf_op jit(solution)/shard_map/ppermute | solution.py:28
  71.0 2.1 %collective-permute-start.18 = (bf16[32,4096]{1,0:T(8,128)(2,1)S(1)}, bf16[32,4096]{1,0:T(8,128)(2,1)S(1)}, u32[]{:S(2)}, u32[]{:S(2)}) collective-permute-start(bf16[32,4096]{1,0:T(8,128)(2,1)S(1)} %get-tuple-element.61), channel_id=1, source_target_pairs={{0,3},{1,2},{2,1},{3,0},{4,7},{5,6},{6,5},{7,4},{8,11},{9,10},{10,... | collective-permute-start | bytes 786440 | tf_op jit(solution)/shard_map/ppermute | solution.py:28
  73.9 3.3 %collective-permute-done.16 = bf16[32,4096]{1,0:T(8,128)(2,1)S(1)} collective-permute-done((bf16[32,4096]{1,0:T(8,128)(2,1)S(1)}, bf16[32,4096]{1,0:T(8,128)(2,1)S(1)}, u32[]{:S(2)}, u32[]{:S(2)}) %collective-permute-start.16) | collective-permute-done | bytes 262176 | tf_op jit(solution)/shard_map/ppermute | solution.py:28
  77.2 12.2 %collective-permute-done.17 = bf16[32,4096]{1,0:T(8,128)(2,1)S(1)} collective-permute-done((bf16[32,4096]{1,0:T(8,128)(2,1)S(1)}, bf16[32,4096]{1,0:T(8,128)(2,1)S(1)}, u32[]{:S(2)}, u32[]{:S(2)}) %collective-permute-start.17) | collective-permute-done | bytes 262176 | tf_op jit(solution)/shard_map/ppermute | solution.py:28
  (62 shorter events, 14.2 us)
Async XLA Ops:
  4.9 5.5 %collective-permute-start = (bf16[144,256]{1,0:T(8,128)(2,1)S(1)}, bf16[144,256]{1,0:T(8,128)(2,1)S(1)}, u32[]{:S(2)}, u32[]{:S(2)}) collective-permute-start(bf16[144,256]{1,0:T(8,128)(2,1)S(1)} %maximum_maximum_fusion.refs_0_.refs_1_), channel_id=1, source_target_pairs={{0,8},{4,12},{8,0},{12,4},{16,24},{20,28},{24,16},{28,20},{1,9},{5... | collective-permute-start | bytes 221192 | tf_op jit(solution)/shard_map/ppermute | solution.py:28
  7.9 4.4 %collective-permute-start.1 = (bf16[144,256]{1,0:T(8,128)(2,1)S(1)}, bf16[144,256]{1,0:T(8,128)(2,1)S(1)}, u32[]{:S(2)}, u32[]{:S(2)}) collective-permute-start(bf16[144,256]{1,0:T(8,128)(2,1)S(1)} %maximum_maximum_fusion.refs_0_.refs_1_), channel_id=1, source_target_pairs={{0,16},{4,20},{8,24},{12,28},{16,0},{20,4},{24,8},{28,12},{1,17},{... | collective-permute-start | bytes 221192 | tf_op jit(solution)/shard_map/ppermute | solution.py:28
  9.4 5.3 %collective-permute-start.2 = (bf16[144,256]{1,0:T(8,128)(2,1)S(1)}, bf16[144,256]{1,0:T(8,128)(2,1)S(1)}, u32[]{:S(2)}, u32[]{:S(2)}) collective-permute-start(bf16[144,256]{1,0:T(8,128)(2,1)S(1)} %maximum_maximum_fusion.refs_0_.refs_1_), channel_id=1, source_target_pairs={{0,24},{4,28},{8,16},{12,20},{16,8},{20,12},{24,0},{28,4},{1,25},{... | collective-permute-start | bytes 221192 | tf_op jit(solution)/shard_map/ppermute | solution.py:28
  14.7 2.2 %collective-permute-start.3 = (bf16[576,256]{1,0:T(8,128)(2,1)S(1)}, bf16[576,256]{1,0:T(8,128)(2,1)S(1)}, u32[]{:S(2)}, u32[]{:S(2)}) collective-permute-start(bf16[576,256]{1,0:T(8,128)(2,1)S(1)} %join_after.1), channel_id=1, source_target_pairs={{0,4},{4,0},{8,12},{12,8},{16,20},{20,16},{24,28},{28,24},{1,5},{5... | collective-permute-start | bytes 884744 | tf_op jit(solution)/shard_map/ppermute | solution.py:28
  25.6 37.6 %copy-start = (bf16[1,384,4096]{2,1,0:T(8,128)(2,1)S(1)}, bf16[1,384,4096]{2,1,0:T(8,128)(2,1)}, u32[]{:S(2)}) copy-start(bf16[1,384,4096]{2,1,0:T(8,128)(2,1)} %param.22) | copy-start | bytes 9437188
  25.6 37.6 %copy-start.5 = (f32[4096]{0:T(1024)S(1)}, f32[4096]{0:T(1024)}, u32[]{:S(2)}) copy-start(f32[4096]{0:T(1024)} %param.19) | copy-start | bytes 49156
  25.7 6.4 %collective-permute-start.4 = (bf16[64,1024]{1,0:T(8,128)(2,1)S(1)}, bf16[64,1024]{1,0:T(8,128)(2,1)S(1)}, u32[]{:S(2)}, u32[]{:S(2)}) collective-permute-start(bf16[64,1024]{1,0:T(8,128)(2,1)S(1)} %get-tuple-element.35), channel_id=1, source_target_pairs={{0,1},{1,0},{2,3},{3,2},{4,5},{5,4},{6,7},{7,6},{8,9},{9,8},{10,11... | collective-permute-start | bytes 393224 | tf_op jit(solution)/shard_map/ppermute | solution.py:28
  27.3 9.0 %collective-permute-start.7 = (bf16[64,1024]{1,0:T(8,128)(2,1)S(1)}, bf16[64,1024]{1,0:T(8,128)(2,1)S(1)}, u32[]{:S(2)}, u32[]{:S(2)}) collective-permute-start(bf16[64,1024]{1,0:T(8,128)(2,1)S(1)} %get-tuple-element.38), channel_id=1, source_target_pairs={{0,1},{1,0},{2,3},{3,2},{4,5},{5,4},{6,7},{7,6},{8,9},{9,8},{10,11... | collective-permute-start | bytes 393224 | tf_op jit(solution)/shard_map/ppermute | solution.py:28
  32.1 9.3 %collective-permute-start.5 = (bf16[64,1024]{1,0:T(8,128)(2,1)S(1)}, bf16[64,1024]{1,0:T(8,128)(2,1)S(1)}, u32[]{:S(2)}, u32[]{:S(2)}) collective-permute-start(bf16[64,1024]{1,0:T(8,128)(2,1)S(1)} %add.48), channel_id=1, source_target_pairs={{0,2},{1,3},{2,0},{3,1},{4,6},{5,7},{6,4},{7,5},{8,10},{9,11},{10,... | collective-permute-start | bytes 393224 | tf_op jit(solution)/shard_map/ppermute | solution.py:28
  34.7 10.4 %collective-permute-start.10 = (bf16[64,1024]{1,0:T(8,128)(2,1)S(1)}, bf16[64,1024]{1,0:T(8,128)(2,1)S(1)}, u32[]{:S(2)}, u32[]{:S(2)}) collective-permute-start(bf16[64,1024]{1,0:T(8,128)(2,1)S(1)} %get-tuple-element.44), channel_id=1, source_target_pairs={{0,1},{1,0},{2,3},{3,2},{4,5},{5,4},{6,7},{7,6},{8,9},{9,8},{10,11... | collective-permute-start | bytes 393224 | tf_op jit(solution)/shard_map/ppermute | solution.py:28
  36.3 13.9 %collective-permute-start.13 = (bf16[64,1024]{1,0:T(8,128)(2,1)S(1)}, bf16[64,1024]{1,0:T(8,128)(2,1)S(1)}, u32[]{:S(2)}, u32[]{:S(2)}) collective-permute-start(bf16[64,1024]{1,0:T(8,128)(2,1)S(1)} %get-tuple-element.52), channel_id=1, source_target_pairs={{0,1},{1,0},{2,3},{3,2},{4,5},{5,4},{6,7},{7,6},{8,9},{9,8},{10,11... | collective-permute-start | bytes 393224 | tf_op jit(solution)/shard_map/ppermute | solution.py:28
  36.8 13.5 %collective-permute-start.8 = (bf16[64,1024]{1,0:T(8,128)(2,1)S(1)}, bf16[64,1024]{1,0:T(8,128)(2,1)S(1)}, u32[]{:S(2)}, u32[]{:S(2)}) collective-permute-start(bf16[64,1024]{1,0:T(8,128)(2,1)S(1)} %add.50), channel_id=1, source_target_pairs={{0,2},{1,3},{2,0},{3,1},{4,6},{5,7},{6,4},{7,5},{8,10},{9,11},{10,... | collective-permute-start | bytes 393224 | tf_op jit(solution)/shard_map/ppermute | solution.py:28
  41.4 15.5 %collective-permute-start.6 = (bf16[64,1024]{1,0:T(8,128)(2,1)S(1)}, bf16[64,1024]{1,0:T(8,128)(2,1)S(1)}, u32[]{:S(2)}, u32[]{:S(2)}) collective-permute-start(bf16[64,1024]{1,0:T(8,128)(2,1)S(1)} %add.49.mine_ref), channel_id=1, source_target_pairs={{0,1},{1,0},{2,3},{3,2},{4,5},{5,4},{6,7},{7,6},{8,9},{9,8},{10,11... | collective-permute-start | bytes 393224 | tf_op jit(solution)/shard_map/ppermute | solution.py:28
  45.1 11.7 %collective-permute-start.11 = (bf16[64,1024]{1,0:T(8,128)(2,1)S(1)}, bf16[64,1024]{1,0:T(8,128)(2,1)S(1)}, u32[]{:S(2)}, u32[]{:S(2)}) collective-permute-start(bf16[64,1024]{1,0:T(8,128)(2,1)S(1)} %add.52), channel_id=1, source_target_pairs={{0,2},{1,3},{2,0},{3,1},{4,6},{5,7},{6,4},{7,5},{8,10},{9,11},{10,... | collective-permute-start | bytes 393224 | tf_op jit(solution)/shard_map/ppermute | solution.py:28
  50.3 8.4 %collective-permute-start.14 = (bf16[64,1024]{1,0:T(8,128)(2,1)S(1)}, bf16[64,1024]{1,0:T(8,128)(2,1)S(1)}, u32[]{:S(2)}, u32[]{:S(2)}) collective-permute-start(bf16[64,1024]{1,0:T(8,128)(2,1)S(1)} %add.54), channel_id=1, source_target_pairs={{0,2},{1,3},{2,0},{3,1},{4,6},{5,7},{6,4},{7,5},{8,10},{9,11},{10,... | collective-permute-start | bytes 393224 | tf_op jit(solution)/shard_map/ppermute | solution.py:28
  50.5 8.1 %copy-start.2 = (bf16[64,1024]{1,0:T(8,128)(2,1)}, bf16[64,1024]{1,0:T(8,128)(2,1)S(1)}, u32[]{:S(2)}) copy-start(bf16[64,1024]{1,0:T(8,128)(2,1)S(1)} %add.51.mine_ref) | copy-start | bytes 393220
  50.5 9.1 %collective-permute-start.9 = (bf16[64,1024]{1,0:T(8,128)(2,1)S(1)}, bf16[64,1024]{1,0:T(8,128)(2,1)S(1)}, u32[]{:S(2)}, u32[]{:S(2)}) collective-permute-start(bf16[64,1024]{1,0:T(8,128)(2,1)S(1)} %add.51.mine_ref), channel_id=1, source_target_pairs={{0,1},{1,0},{2,3},{3,2},{4,5},{5,4},{6,7},{7,6},{8,9},{9,8},{10,11... | collective-permute-start | bytes 393224 | tf_op jit(solution)/shard_map/ppermute | solution.py:28
  57.5 7.9 %collective-permute-start.12 = (bf16[64,1024]{1,0:T(8,128)(2,1)S(1)}, bf16[64,1024]{1,0:T(8,128)(2,1)}, u32[]{:S(2)}, u32[]{:S(2)}) collective-permute-start(bf16[64,1024]{1,0:T(8,128)(2,1)S(1)} %add.53.mine_ref), channel_id=1, source_target_pairs={{0,1},{1,0},{2,3},{3,2},{4,5},{5,4},{6,7},{7,6},{8,9},{9,8},{10,11... | collective-permute-start | bytes 393224 | tf_op jit(solution)/shard_map/ppermute | solution.py:28
  60.3 6.4 %collective-permute-start.15 = (bf16[64,1024]{1,0:T(8,128)(2,1)S(1)}, bf16[64,1024]{1,0:T(8,128)(2,1)}, u32[]{:S(2)}, u32[]{:S(2)}) collective-permute-start(bf16[64,1024]{1,0:T(8,128)(2,1)S(1)} %add.55.mine_ref), channel_id=1, source_target_pairs={{0,1},{1,0},{2,3},{3,2},{4,5},{5,4},{6,7},{7,6},{8,9},{9,8},{10,11... | collective-permute-start | bytes 393224 | tf_op jit(solution)/shard_map/ppermute | solution.py:28
  62.4 2.1 %copy-start.3 = (bf16[64,1024]{1,0:T(8,128)(2,1)S(1)}, bf16[64,1024]{1,0:T(8,128)(2,1)}, u32[]{:S(2)}) copy-start(bf16[64,1024]{1,0:T(8,128)(2,1)} %copy-done.2) | copy-start | bytes 393220
  65.0 1.8 %copy-start.1 = (bf16[1,192,4096]{2,1,0:T(8,128)(2,1)S(1)}, bf16[1,192,4096]{2,1,0:T(8,128)(2,1)}, u32[]{:S(2)}) copy-start(bf16[1,192,4096]{2,1,0:T(8,128)(2,1)} %param.23) | copy-start | bytes 4718596
  68.7 8.4 %collective-permute-start.16 = (bf16[32,4096]{1,0:T(8,128)(2,1)S(1)}, bf16[32,4096]{1,0:T(8,128)(2,1)S(1)}, u32[]{:S(2)}, u32[]{:S(2)}) collective-permute-start(bf16[32,4096]{1,0:T(8,128)(2,1)S(1)} %get-tuple-element.59), channel_id=1, source_target_pairs={{0,1},{1,0},{2,3},{3,2},{4,5},{5,4},{6,7},{7,6},{8,9},{9,8},{10,11... | collective-permute-start | bytes 786440 | tf_op jit(solution)/shard_map/ppermute | solution.py:28
  70.0 19.4 %collective-permute-start.17 = (bf16[32,4096]{1,0:T(8,128)(2,1)S(1)}, bf16[32,4096]{1,0:T(8,128)(2,1)S(1)}, u32[]{:S(2)}, u32[]{:S(2)}) collective-permute-start(bf16[32,4096]{1,0:T(8,128)(2,1)S(1)} %get-tuple-element.60), channel_id=1, source_target_pairs={{0,2},{1,3},{2,0},{3,1},{4,6},{5,7},{6,4},{7,5},{8,10},{9,11},{10,... | collective-permute-start | bytes 786440 | tf_op jit(solution)/shard_map/ppermute | solution.py:28
  71.0 18.4 %collective-permute-start.18 = (bf16[32,4096]{1,0:T(8,128)(2,1)S(1)}, bf16[32,4096]{1,0:T(8,128)(2,1)S(1)}, u32[]{:S(2)}, u32[]{:S(2)}) collective-permute-start(bf16[32,4096]{1,0:T(8,128)(2,1)S(1)} %get-tuple-element.61), channel_id=1, source_target_pairs={{0,3},{1,2},{2,1},{3,0},{4,7},{5,6},{6,5},{7,4},{8,11},{9,10},{10,... | collective-permute-start | bytes 786440 | tf_op jit(solution)/shard_map/ppermute | solution.py:28
  (6 other events, 5.1 us)

commit v7 on v6

--- a/solution.py
+++ b/solution.py
@@ -18,6 +18,7 @@
 PAD_ROWS = 16
 BASE = 64
 IN_FLIGHT = 2
+EARLY = 2
 LOG2E = 1.4426950408889634
 VMEM = pl.BlockSpec(memory_space=pltpu.VMEM)
 ANY = pl.BlockSpec(memory_space=pl.ANY)
@@ -28,30 +29,40 @@
     return lax.ppermute(value, axis, [(i, i ^ offset) for i in range(size)])
 
 
-def attend_kernel(rank_ref, same_ref, other_ref, q_ref, resid_ref, w_hbm, *refs):
-    outs = refs[: 2 * len(WIDTHS)]
-    w_buf, k_buf, v_buf, bias, attended, acc, sems = refs[2 * len(WIDTHS) :]
+def start_weights(w_hbm, w_buf, sems, spans):
+    copies = []
+    for i, (first, width) in enumerate(spans):
+        target = pl.ds(first - spans[0][0], width)
+        copy = pltpu.make_async_copy(
+            w_hbm.at[:, pl.ds(first, width)], w_buf.at[:, target], sems.at[i]
+        )
+        copy.start()
+        copies.append(copy)
+    return copies
+
+
+def attend_kernel(rank_ref, limit_ref, same_ref, other_ref, q_ref, resid_ref, w_hbm, *refs):
+    spans = SPANS[:EARLY]
+    outs = refs[: 2 * EARLY]
+    attended, w_buf, k_buf, v_buf, bias, acc, sems = refs[2 * EARLY :]
     tok = q_ref.shape[0]
     heads = q_ref.shape[1] // HEAD_DIM
-    copies = []
-    for chunk, (first, width) in enumerate(SPANS):
-        span = pl.ds(first, width)
-        copy = pltpu.make_async_copy(w_hbm.at[:, span], w_buf.at[:, span], sems.at[chunk])
-        copy.start()
-        copies.append(copy)
-    extra = same_ref[0, tok : tok + PAD_ROWS, :].astype(jnp.float32)
-    bound = extra[1:2, :tok] * BASE + extra[1:2, tok:]
+    copies = start_weights(w_hbm, w_buf, sems, spans)
+    extra = limit_ref[...].astype(jnp.float32)
+    bound = extra[:1, :tok] * BASE + extra[:1, tok:]
     bound = jnp.broadcast_to(bound, (tok, tok)).T
     lane = lax.broadcasted_iota(jnp.int32, (1, tok), 1).astype(jnp.float32)
     ones = jnp.ones((tok, HEAD_DIM), jnp.bfloat16)
-    half_count = same_ref.shape[0]
+    block_rows = tok + PAD_ROWS
+    half_count = same_ref.shape[0] // block_rows
     for b in range(2 * half_count):
         rows = slice(b * tok, (b + 1) * tok)
         group, row = (same_ref, b) if b < half_count else (other_ref, b - half_count)
-        k_buf[rows, :] = group[row, :tok, :HEAD_DIM]
-        v_buf[rows, :HEAD_DIM] = group[row, :tok, HEAD_DIM:]
+        top = row * block_rows
+        k_buf[rows, :] = group[top : top + tok, :HEAD_DIM]
+        v_buf[rows, :HEAD_DIM] = group[top : top + tok, HEAD_DIM:]
         v_buf[rows, HEAD_DIM:] = ones
-        start = group[row, tok : tok + PAD_ROWS, :HEAD_DIM].astype(jnp.float32)[:1]
+        start = group[top + tok : top + block_rows, :HEAD_DIM].astype(jnp.float32)[:1]
         place = start * tok + lane
         bias[:, rows] = jnp.where(place <= bound, 0.0, -1e30)
     factor = HEAD_DIM ** (-0.5) * LOG2E
@@ -79,19 +90,22 @@
         return carry
 
     lax.fori_loop(0, heads // STACK, some_heads, 0, unroll=True)
+    project_spans(spans, copies, rank_ref[0], attended, w_buf, resid_ref, acc, outs)
+
+
+def project_spans(spans, copies, rank, attended, w_buf, resid_ref, acc, outs):
     home = resid_ref.shape[0]
-    rank = rank_ref[0]
     side = rank % 2
     kept = [pl.multiple_of((side + 2 * i) * home, home) for i in range(2)]
     leaving = [pl.multiple_of((1 - side + 2 * i) * home, home) for i in range(2)]
     top = pl.multiple_of(rank * home, home)
-    for chunk, (first, width) in enumerate(SPANS):
+    for chunk, (first, width) in enumerate(spans):
         copies[chunk].wait()
-        span = slice(first, first + width)
+        span = slice(first - spans[0][0], first - spans[0][0] + width)
         acc[:, span] = jnp.dot(
             attended[...], w_buf[:, span], preferred_element_type=jnp.float32
         )
-        acc[pl.ds(top, home), span] += resid_ref[:, span].astype(jnp.float32)
+        acc[pl.ds(top, home), span] += resid_ref[:, first : first + width].astype(jnp.float32)
         for i in range(2):
             rows = slice(i * home, (i + 1) * home)
             outs[2 * chunk][rows, :] = acc[pl.ds(kept[i], home), span].astype(jnp.bfloat16)
@@ -100,33 +114,70 @@
             )
 
 
-def attend_project(rank, same, other, queries, residual, w_out):
+def part_shapes(tok, spans):
+    return [
+        jax.ShapeDtypeStruct((tok // 2, width), jnp.bfloat16) for _, width in spans for _ in range(2)
+    ]
+
+
+def attend_project(rank, limits, same, other, queries, residual, w_out):
     tok, width = queries.shape
-    keys_in_all = 2 * same.shape[0] * tok
+    keys_in_all = 2 * same.shape[0] // (tok + PAD_ROWS) * tok
+    spans = SPANS[:EARLY]
+    columns = sum(w for _, w in spans)
     return pl.pallas_call(
         attend_kernel,
-        out_shape=[
-            jax.ShapeDtypeStruct((tok // 2, w), jnp.bfloat16) for w in WIDTHS for _ in range(2)
-        ],
-        in_specs=[pl.BlockSpec(memory_space=pltpu.SMEM)] + [VMEM] * 4 + [ANY],
-        out_specs=[VMEM] * (2 * len(WIDTHS)),
+        out_shape=part_shapes(tok, spans) + [jax.ShapeDtypeStruct((tok, width), jnp.bfloat16)],
+        in_specs=[pl.BlockSpec(memory_space=pltpu.SMEM)] + [VMEM] * 5 + [ANY],
+        out_specs=[VMEM] * (2 * len(spans) + 1),
         scratch_shapes=[
-            pltpu.VMEM((width, D), jnp.bfloat16),
+            pltpu.VMEM((width, columns), jnp.bfloat16),
             pltpu.VMEM((keys_in_all, HEAD_DIM), jnp.bfloat16),
             pltpu.VMEM((keys_in_all, 2 * HEAD_DIM), jnp.bfloat16),
             pltpu.VMEM((tok, keys_in_all), jnp.float32),
-            pltpu.VMEM((tok, width), jnp.bfloat16),
-            pltpu.VMEM((tok, D), jnp.float32),
-            pltpu.SemaphoreType.DMA((len(WIDTHS),)),
+            pltpu.VMEM((tok, columns), jnp.float32),
+            pltpu.SemaphoreType.DMA((len(spans),)),
         ],
-        compiler_params=pltpu.CompilerParams(vmem_limit_bytes=44 * 1024 * 1024),
+        compiler_params=pltpu.CompilerParams(vmem_limit_bytes=48 * 1024 * 1024),
         cost_estimate=pl.CostEstimate(
-            flops=2 * tok * width * (2 * keys_in_all + D),
-            bytes_accessed=2 * width * D,
+            flops=2 * tok * width * (2 * keys_in_all + columns),
+            bytes_accessed=2 * width * columns,
             transcendentals=tok * width // HEAD_DIM * keys_in_all,
         ),
         name="attend_project",
-    )(rank, same, other, queries, residual, w_out)
+    )(rank, limits, same, other, queries, residual, w_out)
+
+
+def project_kernel(rank_ref, attended, resid_ref, w_hbm, *refs):
+    spans = SPANS[EARLY:]
+    outs = refs[: 2 * len(spans)]
+    w_buf, acc, sems = refs[2 * len(spans) :]
+    copies = start_weights(w_hbm, w_buf, sems, spans)
+    project_spans(spans, copies, rank_ref[0], attended, w_buf, resid_ref, acc, outs)
+
+
+def project(rank, attended, residual, w_out):
+    tok, width = attended.shape
+    spans = SPANS[EARLY:]
+    columns = sum(w for _, w in spans)
+    return pl.pallas_call(
+        project_kernel,
+        out_shape=part_shapes(tok, spans),
+        in_specs=[pl.BlockSpec(memory_space=pltpu.SMEM)] + [VMEM] * 2 + [ANY],
+        out_specs=[VMEM] * (2 * len(spans)),
+        scratch_shapes=[
+            pltpu.VMEM((width, columns), jnp.bfloat16),
+            pltpu.VMEM((tok, columns), jnp.float32),
+            pltpu.SemaphoreType.DMA((len(spans),)),
+        ],
+        compiler_params=pltpu.CompilerParams(vmem_limit_bytes=48 * 1024 * 1024),
+        cost_estimate=pl.CostEstimate(
+            flops=2 * tok * width * columns,
+            bytes_accessed=2 * width * columns,
+            transcendentals=0,
+        ),
+        name="project",
+    )(rank, attended, residual, w_out)
 
 
 def stage_kernel(q_hbm, resid_hbm, q_ref, resid_ref, sems):
@@ -283,27 +334,30 @@
     key_head, value_head = own_heads(queries, keys, values)
     staged_queries, staged_residual = stage(queries, residual)
     block = (positions[0] // tok).astype(jnp.bfloat16)
-    limits = jnp.concatenate([bounds // BASE, bounds % BASE]).astype(jnp.bfloat16)
     width = 2 * HEAD_DIM
     payload = jnp.concatenate(
         [
             jnp.concatenate([key_head, value_head], axis=1),
-            jnp.full((1, width), block, jnp.bfloat16),
-            limits.reshape(1, width),
-            jnp.zeros((PAD_ROWS - 2, width), jnp.bfloat16),
+            jnp.full((PAD_ROWS, width), block, jnp.bfloat16),
         ],
         axis=0,
     )
-    same_rows = join_after(
+    limits = jnp.concatenate([bounds // BASE, bounds % BASE]).astype(jnp.bfloat16)
+    limits = jnp.broadcast_to(limits.reshape(1, width), (PAD_ROWS, width))
+    same_keys = join_after(
         [payload] + [exchange(payload, "ctx", r, ctx_count) for r in range(2, ctx_count, 2)],
         payload,
     )
-    same_keys = same_rows.reshape(ctx_count // 2, tok + PAD_ROWS, 2 * HEAD_DIM)
-    other_keys = exchange(same_rows, "ctx", 1, ctx_count).reshape(same_keys.shape)
+    other_keys = exchange(same_keys, "ctx", 1, ctx_count)
+
     ranks = rank.astype(jnp.int32).reshape(1)
-    parts = attend_project(
-        ranks, same_keys, other_keys, staged_queries, staged_residual, w_out
-    )
+    *parts, attended = attend_project(
+        ranks, limits, same_keys, other_keys, staged_queries, staged_residual, w_out
+    )
+    parts += project(ranks, attended, staged_residual, w_out)
+    shares = gates / jnp.sum(gates, axis=1, keepdims=True)
+    coefficient = jnp.sum(jnp.where(routes == 0, shares, 0.0), axis=1, keepdims=True)
+    coefficient = coefficient.astype(jnp.bfloat16).astype(jnp.float32)
     gain = norm_gain.reshape(1, D)
     flat_in = w_in.reshape(2 * hidden, D)
     flat_back = w_back.reshape(hidden, D)
@@ -321,9 +375,30 @@
     near = [kept + other for kept, other in zip(parts[::2], arrived)]
     across = swap(near, 2)
     mine = [own + other for own, other in zip(near, across)]
-    theirs = swap(mine, 1)
-    homes, states = [], []
+    homes, states, theirs, done = [], [], [], [coefficient]
     for chunk in range(count):
+        value = mine[chunk]
+        if chunk >= IN_FLIGHT:
+            own, *states = absorb(
+                chunk - IN_FLIGHT,
+                ranks,
+                mine[chunk - IN_FLIGHT],
+                theirs[chunk - IN_FLIGHT],
+                gain,
+                flat_in,
+                states,
+                flat_back,
+            )
+            homes.append(own)
+            done = [states[0]]
+        if chunk >= IN_FLIGHT or chunk == 1:
+            value, *done = lax.optimization_barrier((value, *done))
+            if chunk == 1:
+                coefficient = done[0]
+            else:
+                states[0] = done[0]
+        theirs.append(exchange(value, "exp", 1, exp_count))
+    for chunk in range(count - IN_FLIGHT, count):
         own, *states = absorb(
             chunk, ranks, mine[chunk], theirs[chunk], gain, flat_in, states, flat_back
         )
@@ -332,9 +407,6 @@
     expert = states[0].astype(jnp.float32)
     for offset in range(1, exp_count):
         expert = expert + exchange(states[offset], "exp", offset, exp_count).astype(jnp.float32)
-    shares = gates / jnp.sum(gates, axis=1, keepdims=True)
-    coefficient = jnp.sum(jnp.where(routes == 0, shares, 0.0), axis=1, keepdims=True)
-    coefficient = coefficient.astype(jnp.bfloat16).astype(jnp.float32)
     return (middle_out, (expert * coefficient).astype(jnp.bfloat16))
 
 

time: 92.1 us -> 85.4 us (0.927); the launches traced: 90.2 us -> 84.7 us
  local copies, waits for them, and re-layouts: 5.6 us -> 2.8 us
  other arithmetic: 4.66 us -> 3.29 us
    unnamed x22 -> x14, local copies, waits for them, and re-layouts: 4.74 us -> 2.01 us
    pallas_call x1 -> x2, Pallas kernels: 8.75 us -> 10.8 us  [the longest x1 6.36 us: attend_project(): pl.pallas_call(attend_kernel, out_shape=part_shapes(tok, spans) + [jax.Sh...]
    pallas_call x4, Pallas kernels: 4.01 us -> 2.12 us  [absorb(): pl.pallas_call(functools.partial(absorb_kernel, chunk), out_shape=out_sha...]
  transfers between devices with their start and end apart: 19 -> 19, of which waited for: 12 -> 13; matrix products, arithmetic and copies ran while one was open for 3% -> 3% of each run, Pallas kernels for 2% -> 7%
where the time goes in v7:
time: 85.4 us; the launch traced here: 84.7 us
  waiting for transfers between devices  40.9 us (48%)
  starting transfers between devices  21.3 us (25%)
  Pallas kernels  13 us (15%)
  between operations  3.43 us (4%)
  other arithmetic  3.29 us (4%)
  local copies, waits for them, and re-layouts  2.8 us (3%)
    ppermute x19, waiting for transfers between devices, exchange(): return lax.ppermute(value, axis, [(i, i ^ offset) for i in range(size)])  40.9 us
    ppermute x19, starting transfers between devices, exchange(): return lax.ppermute(value, axis, [(i, i ^ offset) for i in range(size)])  21.3 us
    pallas_call x1, Pallas kernels, attend_project(): pl.pallas_call(attend_kernel, out_shape=part_shapes(tok, spans) + [jax.Sh...  6.36 us
    pallas_call x1, Pallas kernels, project(): pl.pallas_call(project_kernel, out_shape=part_shapes(tok, spans), in_spec...  4.41 us
    pallas_call x4, Pallas kernels, absorb(): pl.pallas_call(functools.partial(absorb_kernel, chunk), out_shape=out_sha...  2.12 us
    unnamed x14, local copies, waits for them, and re-layouts  2.01 us
  transfers between devices with their start and end apart: 19, of which 13 were waited for; matrix products, arithmetic and copies ran while one was open for 3% of the time, Pallas kernels for 7%

profile of v7, /device:TPU:0, one launch (start us, length us, event | category | flops | bytes accessed | tf_op | source)
XLA Modules:
  0.0 84.7 jit_solution(14521385146388441933)
XLA Ops:
  4.1 3.0 %collective-permute-start = (bf16[144,256]{1,0:T(8,128)(2,1)S(1)}, bf16[144,256]{1,0:T(8,128)(2,1)S(1)}, u32[]{:S(2)}, u32[]{:S(2)}) collective-permute-start(bf16[144,256]{1,0:T(8,128)(2,1)S(1)} %fusion.2.refs_0_.refs_1_), channel_id=1, source_target_pairs={{0,8},{4,12},{8,0},{12,4},{16,24},{20,28},{24,16},{28,20},{1,9},{5... | collective-permute-start | bytes 221192 | tf_op jit(solution)/shard_map/ppermute | solution.py:29
  7.1 1.5 %collective-permute-start.1 = (bf16[144,256]{1,0:T(8,128)(2,1)S(1)}, bf16[144,256]{1,0:T(8,128)(2,1)S(1)}, u32[]{:S(2)}, u32[]{:S(2)}) collective-permute-start(bf16[144,256]{1,0:T(8,128)(2,1)S(1)} %fusion.2.refs_0_.refs_1_), channel_id=1, source_target_pairs={{0,16},{4,20},{8,24},{12,28},{16,0},{20,4},{24,8},{28,12},{1,17},{... | collective-permute-start | bytes 221192 | tf_op jit(solution)/shard_map/ppermute | solution.py:29
  8.6 1.0 %copy-done.2 = bf16[128,2048]{1,0:T(8,128)(2,1)S(1)} copy-done((bf16[128,2048]{1,0:T(8,128)(2,1)S(1)}, bf16[128,2048]{1,0:T(8,128)(2,1)}, u32[]{:S(2)}) %copy-start.2) | copy-done | bytes 524312
  11.4 2.4 %collective-permute-done.2.refs_4_ = bf16[144,256]{1,0:T(8,128)(2,1)S(1)} collective-permute-done((bf16[144,256]{1,0:T(8,128)(2,1)S(1)}, bf16[144,256]{1,0:T(8,128)(2,1)S(1)}, u32[]{:S(2)}, u32[]{:S(2)}) %collective-permute-start.2) | collective-permute-done | bytes 73760 | tf_op jit(solution)/shard_map/ppermute | solution.py:29
  15.5 6.4 %attend_project.1 = (bf16[64,1024]{1,0:T(8,128)(2,1)S(1)}, bf16[64,1024]{1,0:T(8,128)(2,1)S(1)}, bf16[64,1024]{1,0:T(8,128)(2,1)S(1)}, bf16[64,1024]{1,0:T(8,128)(2,1)S(1)}, bf16[128,2048]{1,0:T(8,128)(2,1)S(1)}) custom-call(s32[1]{0:T(128)} %bitcast.rank_ref, bf16[16,256]{1,0:T(8,128)(2,1)S(1)} %broadcast_in_dim.5.limit_ref, ...), custom_call_target="tpu_custom_call" | custom-call | flops 2147483648 | bytes 8388608 | tf_op jit(solution)/shard_map/attend_project/pallas_call | solution.py:128
  21.9 1.6 %collective-permute-start.4 = (bf16[64,1024]{1,0:T(8,128)(2,1)S(1)}, bf16[64,1024]{1,0:T(8,128)(2,1)S(1)}, u32[]{:S(2)}, u32[]{:S(2)}) collective-permute-start(bf16[64,1024]{1,0:T(8,128)(2,1)S(1)} %get-tuple-element.40), channel_id=1, source_target_pairs={{0,1},{1,0},{2,3},{3,2},{4,5},{5,4},{6,7},{7,6},{8,9},{9,8},{10,11... | collective-permute-start | bytes 393224 | tf_op jit(solution)/shard_map/ppermute | solution.py:29
  24.0 4.4 %project.1 = (bf16[64,1024]{1,0:T(8,128)(2,1)S(1)}, bf16[64,1024]{1,0:T(8,128)(2,1)S(1)}, bf16[64,1024]{1,0:T(8,128)(2,1)S(1)}, bf16[64,1024]{1,0:T(8,128)(2,1)S(1)}) custom-call(s32[1]{0:T(128)} %bitcast.rank_ref, bf16[128,2048]{1,0:T(8,128)(2,1)S(1)} %get-tuple-element.45.attended, bf16[32,4096]{1,0:T(8,128)(2,1)S(1)} %get-tuple-element.38.resid_ref, ...), custom_call_target="tpu_custom_call" | custom-call | flops 1073741824 | bytes 8388608 | tf_op jit(solution)/shard_map/project/pallas_call | solution.py:163
  28.5 2.7 %collective-permute-start.5 = (bf16[64,1024]{1,0:T(8,128)(2,1)S(1)}, bf16[64,1024]{1,0:T(8,128)(2,1)S(1)}, u32[]{:S(2)}, u32[]{:S(2)}) collective-permute-start(bf16[64,1024]{1,0:T(8,128)(2,1)S(1)} %add.50), channel_id=1, source_target_pairs={{0,2},{1,3},{2,0},{3,1},{4,6},{5,7},{6,4},{7,5},{8,10},{9,11},{10,... | collective-permute-start | bytes 393224 | tf_op jit(solution)/shard_map/ppermute | solution.py:29
  31.1 1.6 %collective-permute-start.10 = (bf16[64,1024]{1,0:T(8,128)(2,1)S(1)}, bf16[64,1024]{1,0:T(8,128)(2,1)S(1)}, u32[]{:S(2)}, u32[]{:S(2)}) collective-permute-start(bf16[64,1024]{1,0:T(8,128)(2,1)S(1)} %get-tuple-element.48), channel_id=1, source_target_pairs={{0,1},{1,0},{2,3},{3,2},{4,5},{5,4},{6,7},{7,6},{8,9},{9,8},{10,11... | collective-permute-start | bytes 393224 | tf_op jit(solution)/shard_map/ppermute | solution.py:29
  33.2 1.4 %collective-permute-start.13 = (bf16[64,1024]{1,0:T(8,128)(2,1)S(1)}, bf16[64,1024]{1,0:T(8,128)(2,1)S(1)}, u32[]{:S(2)}, u32[]{:S(2)}) collective-permute-start(bf16[64,1024]{1,0:T(8,128)(2,1)S(1)} %get-tuple-element.57), channel_id=1, source_target_pairs={{0,1},{1,0},{2,3},{3,2},{4,5},{5,4},{6,7},{7,6},{8,9},{9,8},{10,11... | collective-permute-start | bytes 393224 | tf_op jit(solution)/shard_map/ppermute | solution.py:29
  34.6 5.3 %collective-permute-done.5 = bf16[64,1024]{1,0:T(8,128)(2,1)S(1)} collective-permute-done((bf16[64,1024]{1,0:T(8,128)(2,1)S(1)}, bf16[64,1024]{1,0:T(8,128)(2,1)S(1)}, u32[]{:S(2)}, u32[]{:S(2)}) %collective-permute-start.5) | collective-permute-done | bytes 131104 | tf_op jit(solution)/shard_map/ppermute | solution.py:29
  40.5 2.6 %collective-permute-start.11 = (bf16[64,1024]{1,0:T(8,128)(2,1)S(1)}, bf16[64,1024]{1,0:T(8,128)(2,1)S(1)}, u32[]{:S(2)}, u32[]{:S(2)}) collective-permute-start(bf16[64,1024]{1,0:T(8,128)(2,1)S(1)} %add.54), channel_id=1, source_target_pairs={{0,2},{1,3},{2,0},{3,1},{4,6},{5,7},{6,4},{7,5},{8,10},{9,11},{10,... | collective-permute-start | bytes 393224 | tf_op jit(solution)/shard_map/ppermute | solution.py:29
  43.1 4.7 %collective-permute-done.13 = bf16[64,1024]{1,0:T(8,128)(2,1)S(1)} collective-permute-done((bf16[64,1024]{1,0:T(8,128)(2,1)S(1)}, bf16[64,1024]{1,0:T(8,128)(2,1)S(1)}, u32[]{:S(2)}, u32[]{:S(2)}) %collective-permute-start.13) | collective-permute-done | bytes 131104 | tf_op jit(solution)/shard_map/ppermute | solution.py:29
  48.1 2.5 %collective-permute-done.6.theirs_ref = bf16[64,1024]{1,0:T(8,128)(2,1)S(1)} collective-permute-done((bf16[64,1024]{1,0:T(8,128)(2,1)S(1)}, bf16[64,1024]{1,0:T(8,128)(2,1)S(1)}, u32[]{:S(2)}, u32[]{:S(2)}) %collective-permute-start.6) | collective-permute-done | bytes 131104 | tf_op jit(solution)/shard_map/ppermute | solution.py:29
  51.3 3.6 %collective-permute-done.14 = bf16[64,1024]{1,0:T(8,128)(2,1)S(1)} collective-permute-done((bf16[64,1024]{1,0:T(8,128)(2,1)S(1)}, bf16[64,1024]{1,0:T(8,128)(2,1)S(1)}, u32[]{:S(2)}, u32[]{:S(2)}) %collective-permute-start.14) | collective-permute-done | bytes 131104 | tf_op jit(solution)/shard_map/ppermute | solution.py:29
  54.9 1.2 %collective-permute-done.9.theirs_ref = bf16[64,1024]{1,0:T(8,128)(2,1)S(1)} collective-permute-done((bf16[64,1024]{1,0:T(8,128)(2,1)S(1)}, bf16[64,1024]{1,0:T(8,128)(2,1)S(1)}, u32[]{:S(2)}, u32[]{:S(2)}) %collective-permute-start.9) | collective-permute-done | bytes 131104 | tf_op jit(solution)/shard_map/ppermute | solution.py:29
  56.5 1.2 %collective-permute-start.15 = (bf16[64,1024]{1,0:T(8,128)(2,1)S(1)}, bf16[64,1024]{1,0:T(8,128)(2,1)S(1)}, u32[]{:S(2)}, u32[]{:S(2)}) collective-permute-start(bf16[64,1024]{1,0:T(8,128)(2,1)S(1)} %add.57.mine_ref), channel_id=1, source_target_pairs={{0,1},{1,0},{2,3},{3,2},{4,5},{5,4},{6,7},{7,6},{8,9},{9,8},{10,11... | collective-permute-start | bytes 393224 | tf_op jit(solution)/shard_map/ppermute | solution.py:29
  58.7 2.8 %collective-permute-done.15.theirs_ref = bf16[64,1024]{1,0:T(8,128)(2,1)S(1)} collective-permute-done((bf16[64,1024]{1,0:T(8,128)(2,1)S(1)}, bf16[64,1024]{1,0:T(8,128)(2,1)S(1)}, u32[]{:S(2)}, u32[]{:S(2)}) %collective-permute-start.15) | collective-permute-done | bytes 131104 | tf_op jit(solution)/shard_map/ppermute | solution.py:29
  61.5 1.0 %absorb.7 = (bf16[32,1024]{1,0:T(8,128)(2,1)S(1)}, bf16[32,4096]{1,0:T(8,128)(2,1)S(1)}, bf16[32,4096]{1,0:T(8,128)(2,1)S(1)}, bf16[32,4096]{1,0:T(8,128)(2,1)S(1)}, bf16[32,4096]{1,0:T(8,128)(2,1)S(1)}) custom-call(s32[1]{0:T(128)} %bitcast.rank_ref, bf16[64,1024]{1,0:T(8,128)(2,1)S(1)} %add.57.mine_ref, ...), custom_call_target="tpu_custom_call" | custom-call | flops 1024 | bytes 1024 | tf_op jit(solution)/shard_map/absorb/pallas_call | solution.py:294
  62.5 1.2 %collective-permute-start.16 = (bf16[32,4096]{1,0:T(8,128)(2,1)S(1)}, bf16[32,4096]{1,0:T(8,128)(2,1)S(1)}, u32[]{:S(2)}, u32[]{:S(2)}) collective-permute-start(bf16[32,4096]{1,0:T(8,128)(2,1)S(1)} %get-tuple-element.68), channel_id=1, source_target_pairs={{0,1},{1,0},{2,3},{3,2},{4,5},{5,4},{6,7},{7,6},{8,9},{9,8},{10,11... | collective-permute-start | bytes 786440 | tf_op jit(solution)/shard_map/ppermute | solution.py:29
  63.7 1.9 %collective-permute-start.17 = (bf16[32,4096]{1,0:T(8,128)(2,1)S(1)}, bf16[32,4096]{1,0:T(8,128)(2,1)S(1)}, u32[]{:S(2)}, u32[]{:S(2)}) collective-permute-start(bf16[32,4096]{1,0:T(8,128)(2,1)S(1)} %get-tuple-element.69), channel_id=1, source_target_pairs={{0,2},{1,3},{2,0},{3,1},{4,6},{5,7},{6,4},{7,5},{8,10},{9,11},{10,... | collective-permute-start | bytes 786440 | tf_op jit(solution)/shard_map/ppermute | solution.py:29
  65.7 1.3 %collective-permute-start.18 = (bf16[32,4096]{1,0:T(8,128)(2,1)S(1)}, bf16[32,4096]{1,0:T(8,128)(2,1)S(1)}, u32[]{:S(2)}, u32[]{:S(2)}) collective-permute-start(bf16[32,4096]{1,0:T(8,128)(2,1)S(1)} %get-tuple-element.70), channel_id=1, source_target_pairs={{0,3},{1,2},{2,1},{3,0},{4,7},{5,6},{6,5},{7,4},{8,11},{9,10},{10,... | collective-permute-start | bytes 786440 | tf_op jit(solution)/shard_map/ppermute | solution.py:29
  67.7 4.0 %collective-permute-done.16 = bf16[32,4096]{1,0:T(8,128)(2,1)S(1)} collective-permute-done((bf16[32,4096]{1,0:T(8,128)(2,1)S(1)}, bf16[32,4096]{1,0:T(8,128)(2,1)S(1)}, u32[]{:S(2)}, u32[]{:S(2)}) %collective-permute-start.16) | collective-permute-done | bytes 262176 | tf_op jit(solution)/shard_map/ppermute | solution.py:29
  71.7 12.2 %collective-permute-done.17 = bf16[32,4096]{1,0:T(8,128)(2,1)S(1)} collective-permute-done((bf16[32,4096]{1,0:T(8,128)(2,1)S(1)}, bf16[32,4096]{1,0:T(8,128)(2,1)S(1)}, u32[]{:S(2)}, u32[]{:S(2)}) %collective-permute-start.17) | collective-permute-done | bytes 262176 | tf_op jit(solution)/shard_map/ppermute | solution.py:29
  (54 shorter events, 9.8 us)
Async XLA Ops:
  4.1 7.3 %collective-permute-start = (bf16[144,256]{1,0:T(8,128)(2,1)S(1)}, bf16[144,256]{1,0:T(8,128)(2,1)S(1)}, u32[]{:S(2)}, u32[]{:S(2)}) collective-permute-start(bf16[144,256]{1,0:T(8,128)(2,1)S(1)} %fusion.2.refs_0_.refs_1_), channel_id=1, source_target_pairs={{0,8},{4,12},{8,0},{12,4},{16,24},{20,28},{24,16},{28,20},{1,9},{5... | collective-permute-start | bytes 221192 | tf_op jit(solution)/shard_map/ppermute | solution.py:29
  7.1 4.4 %collective-permute-start.1 = (bf16[144,256]{1,0:T(8,128)(2,1)S(1)}, bf16[144,256]{1,0:T(8,128)(2,1)S(1)}, u32[]{:S(2)}, u32[]{:S(2)}) collective-permute-start(bf16[144,256]{1,0:T(8,128)(2,1)S(1)} %fusion.2.refs_0_.refs_1_), channel_id=1, source_target_pairs={{0,16},{4,20},{8,24},{12,28},{16,0},{20,4},{24,8},{28,12},{1,17},{... | collective-permute-start | bytes 221192 | tf_op jit(solution)/shard_map/ppermute | solution.py:29
  8.6 5.3 %collective-permute-start.2 = (bf16[144,256]{1,0:T(8,128)(2,1)S(1)}, bf16[144,256]{1,0:T(8,128)(2,1)S(1)}, u32[]{:S(2)}, u32[]{:S(2)}) collective-permute-start(bf16[144,256]{1,0:T(8,128)(2,1)S(1)} %fusion.2.refs_0_.refs_1_), channel_id=1, source_target_pairs={{0,24},{4,28},{8,16},{12,20},{16,8},{20,12},{24,0},{28,4},{1,25},{... | collective-permute-start | bytes 221192 | tf_op jit(solution)/shard_map/ppermute | solution.py:29
  13.9 1.6 %collective-permute-start.3 = (bf16[576,256]{1,0:T(8,128)(2,1)S(1)}, bf16[576,256]{1,0:T(8,128)(2,1)S(1)}, u32[]{:S(2)}, u32[]{:S(2)}) collective-permute-start(bf16[576,256]{1,0:T(8,128)(2,1)S(1)} %join_after.1.same_ref), channel_id=1, source_target_pairs={{0,4},{4,0},{8,12},{12,8},{16,20},{20,16},{24,28},{28,24},{1,5},{5... | collective-permute-start | bytes 884744 | tf_op jit(solution)/shard_map/ppermute | solution.py:29
  15.5 8.5 %copy-start.5 = (f32[32,8]{0,1:T(8,128)S(1)}, f32[32,8]{0,1:T(8,128)}, u32[]{:S(2)}) copy-start(f32[32,8]{0,1:T(8,128)} %param.21) | copy-start | bytes 3076
  15.5 8.5 %copy-start.6 = (s32[32,8]{0,1:T(8,128)S(1)}, s32[32,8]{0,1:T(8,128)}, u32[]{:S(2)}) copy-start(s32[32,8]{0,1:T(8,128)} %param.20) | copy-start | bytes 3076
  21.9 6.6 %collective-permute-start.4 = (bf16[64,1024]{1,0:T(8,128)(2,1)S(1)}, bf16[64,1024]{1,0:T(8,128)(2,1)S(1)}, u32[]{:S(2)}, u32[]{:S(2)}) collective-permute-start(bf16[64,1024]{1,0:T(8,128)(2,1)S(1)} %get-tuple-element.40), channel_id=1, source_target_pairs={{0,1},{1,0},{2,3},{3,2},{4,5},{5,4},{6,7},{7,6},{8,9},{9,8},{10,11... | collective-permute-start | bytes 393224 | tf_op jit(solution)/shard_map/ppermute | solution.py:29
  23.5 9.2 %collective-permute-start.7 = (bf16[64,1024]{1,0:T(8,128)(2,1)S(1)}, bf16[64,1024]{1,0:T(8,128)(2,1)S(1)}, u32[]{:S(2)}, u32[]{:S(2)}) collective-permute-start(bf16[64,1024]{1,0:T(8,128)(2,1)S(1)} %get-tuple-element.43), channel_id=1, source_target_pairs={{0,1},{1,0},{2,3},{3,2},{4,5},{5,4},{6,7},{7,6},{8,9},{9,8},{10,11... | collective-permute-start | bytes 393224 | tf_op jit(solution)/shard_map/ppermute | solution.py:29
  24.0 26.6 %copy-start = (bf16[1,384,4096]{2,1,0:T(8,128)(2,1)S(1)}, bf16[1,384,4096]{2,1,0:T(8,128)(2,1)}, u32[]{:S(2)}) copy-start(bf16[1,384,4096]{2,1,0:T(8,128)(2,1)} %param.22) | copy-start | bytes 9437188
  24.0 26.6 %copy-start.3 = (f32[4096]{0:T(1024)S(1)}, f32[4096]{0:T(1024)}, u32[]{:S(2)}) copy-start(f32[4096]{0:T(1024)} %param.19) | copy-start | bytes 49156
  28.5 11.4 %collective-permute-start.5 = (bf16[64,1024]{1,0:T(8,128)(2,1)S(1)}, bf16[64,1024]{1,0:T(8,128)(2,1)S(1)}, u32[]{:S(2)}, u32[]{:S(2)}) collective-permute-start(bf16[64,1024]{1,0:T(8,128)(2,1)S(1)} %add.50), channel_id=1, source_target_pairs={{0,2},{1,3},{2,0},{3,1},{4,6},{5,7},{6,4},{7,5},{8,10},{9,11},{10,... | collective-permute-start | bytes 393224 | tf_op jit(solution)/shard_map/ppermute | solution.py:29
  31.1 9.3 %collective-permute-start.10 = (bf16[64,1024]{1,0:T(8,128)(2,1)S(1)}, bf16[64,1024]{1,0:T(8,128)(2,1)S(1)}, u32[]{:S(2)}, u32[]{:S(2)}) collective-permute-start(bf16[64,1024]{1,0:T(8,128)(2,1)S(1)} %get-tuple-element.48), channel_id=1, source_target_pairs={{0,1},{1,0},{2,3},{3,2},{4,5},{5,4},{6,7},{7,6},{8,9},{9,8},{10,11... | collective-permute-start | bytes 393224 | tf_op jit(solution)/shard_map/ppermute | solution.py:29
  32.8 10.3 %collective-permute-start.8 = (bf16[64,1024]{1,0:T(8,128)(2,1)S(1)}, bf16[64,1024]{1,0:T(8,128)(2,1)S(1)}, u32[]{:S(2)}, u32[]{:S(2)}) collective-permute-start(bf16[64,1024]{1,0:T(8,128)(2,1)S(1)} %add.52), channel_id=1, source_target_pairs={{0,2},{1,3},{2,0},{3,1},{4,6},{5,7},{6,4},{7,5},{8,10},{9,11},{10,... | collective-permute-start | bytes 393224 | tf_op jit(solution)/shard_map/ppermute | solution.py:29
  33.2 14.7 %collective-permute-start.13 = (bf16[64,1024]{1,0:T(8,128)(2,1)S(1)}, bf16[64,1024]{1,0:T(8,128)(2,1)S(1)}, u32[]{:S(2)}, u32[]{:S(2)}) collective-permute-start(bf16[64,1024]{1,0:T(8,128)(2,1)S(1)} %get-tuple-element.57), channel_id=1, source_target_pairs={{0,1},{1,0},{2,3},{3,2},{4,5},{5,4},{6,7},{7,6},{8,9},{9,8},{10,11... | collective-permute-start | bytes 393224 | tf_op jit(solution)/shard_map/ppermute | solution.py:29
  39.9 10.7 %collective-permute-start.6 = (bf16[64,1024]{1,0:T(8,128)(2,1)S(1)}, bf16[64,1024]{1,0:T(8,128)(2,1)S(1)}, u32[]{:S(2)}, u32[]{:S(2)}) collective-permute-start(bf16[64,1024]{1,0:T(8,128)(2,1)S(1)} %add.51.mine_ref), channel_id=1, source_target_pairs={{0,1},{1,0},{2,3},{3,2},{4,5},{5,4},{6,7},{7,6},{8,9},{9,8},{10,11... | collective-permute-start | bytes 393224 | tf_op jit(solution)/shard_map/ppermute | solution.py:29
  40.5 10.7 %collective-permute-start.11 = (bf16[64,1024]{1,0:T(8,128)(2,1)S(1)}, bf16[64,1024]{1,0:T(8,128)(2,1)S(1)}, u32[]{:S(2)}, u32[]{:S(2)}) collective-permute-start(bf16[64,1024]{1,0:T(8,128)(2,1)S(1)} %add.54), channel_id=1, source_target_pairs={{0,2},{1,3},{2,0},{3,1},{4,6},{5,7},{6,4},{7,5},{8,10},{9,11},{10,... | collective-permute-start | bytes 393224 | tf_op jit(solution)/shard_map/ppermute | solution.py:29
  47.9 7.0 %collective-permute-start.14 = (bf16[64,1024]{1,0:T(8,128)(2,1)S(1)}, bf16[64,1024]{1,0:T(8,128)(2,1)S(1)}, u32[]{:S(2)}, u32[]{:S(2)}) collective-permute-start(bf16[64,1024]{1,0:T(8,128)(2,1)S(1)} %add.56), channel_id=1, source_target_pairs={{0,2},{1,3},{2,0},{3,1},{4,6},{5,7},{6,4},{7,5},{8,10},{9,11},{10,... | collective-permute-start | bytes 393224 | tf_op jit(solution)/shard_map/ppermute | solution.py:29
  48.0 8.1 %collective-permute-start.9 = (bf16[64,1024]{1,0:T(8,128)(2,1)S(1)}, bf16[64,1024]{1,0:T(8,128)(2,1)S(1)}, u32[]{:S(2)}, u32[]{:S(2)}) collective-permute-start(bf16[64,1024]{1,0:T(8,128)(2,1)S(1)} %add.53.mine_ref), channel_id=1, source_target_pairs={{0,1},{1,0},{2,3},{3,2},{4,5},{5,4},{6,7},{7,6},{8,9},{9,8},{10,11... | collective-permute-start | bytes 393224 | tf_op jit(solution)/shard_map/ppermute | solution.py:29
  51.3 7.1 %collective-permute-start.12 = (bf16[64,1024]{1,0:T(8,128)(2,1)S(1)}, bf16[64,1024]{1,0:T(8,128)(2,1)S(1)}, u32[]{:S(2)}, u32[]{:S(2)}) collective-permute-start(bf16[64,1024]{1,0:T(8,128)(2,1)S(1)} %add.55.mine_ref), channel_id=1, source_target_pairs={{0,1},{1,0},{2,3},{3,2},{4,5},{5,4},{6,7},{7,6},{8,9},{9,8},{10,11... | collective-permute-start | bytes 393224 | tf_op jit(solution)/shard_map/ppermute | solution.py:29
  56.1 5.4 %copy-start.1 = (bf16[1,192,4096]{2,1,0:T(8,128)(2,1)S(1)}, bf16[1,192,4096]{2,1,0:T(8,128)(2,1)}, u32[]{:S(2)}) copy-start(bf16[1,192,4096]{2,1,0:T(8,128)(2,1)} %param.23) | copy-start | bytes 4718596
  56.5 5.0 %collective-permute-start.15 = (bf16[64,1024]{1,0:T(8,128)(2,1)S(1)}, bf16[64,1024]{1,0:T(8,128)(2,1)S(1)}, u32[]{:S(2)}, u32[]{:S(2)}) collective-permute-start(bf16[64,1024]{1,0:T(8,128)(2,1)S(1)} %add.57.mine_ref), channel_id=1, source_target_pairs={{0,1},{1,0},{2,3},{3,2},{4,5},{5,4},{6,7},{7,6},{8,9},{9,8},{10,11... | collective-permute-start | bytes 393224 | tf_op jit(solution)/shard_map/ppermute | solution.py:29
  62.5 9.1 %collective-permute-start.16 = (bf16[32,4096]{1,0:T(8,128)(2,1)S(1)}, bf16[32,4096]{1,0:T(8,128)(2,1)S(1)}, u32[]{:S(2)}, u32[]{:S(2)}) collective-permute-start(bf16[32,4096]{1,0:T(8,128)(2,1)S(1)} %get-tuple-element.68), channel_id=1, source_target_pairs={{0,1},{1,0},{2,3},{3,2},{4,5},{5,4},{6,7},{7,6},{8,9},{9,8},{10,11... | collective-permute-start | bytes 786440 | tf_op jit(solution)/shard_map/ppermute | solution.py:29
  63.7 20.1 %collective-permute-start.17 = (bf16[32,4096]{1,0:T(8,128)(2,1)S(1)}, bf16[32,4096]{1,0:T(8,128)(2,1)S(1)}, u32[]{:S(2)}, u32[]{:S(2)}) collective-permute-start(bf16[32,4096]{1,0:T(8,128)(2,1)S(1)} %get-tuple-element.69), channel_id=1, source_target_pairs={{0,2},{1,3},{2,0},{3,1},{4,6},{5,7},{6,4},{7,5},{8,10},{9,11},{10,... | collective-permute-start | bytes 786440 | tf_op jit(solution)/shard_map/ppermute | solution.py:29
  65.7 18.2 %collective-permute-start.18 = (bf16[32,4096]{1,0:T(8,128)(2,1)S(1)}, bf16[32,4096]{1,0:T(8,128)(2,1)S(1)}, u32[]{:S(2)}, u32[]{:S(2)}) collective-permute-start(bf16[32,4096]{1,0:T(8,128)(2,1)S(1)} %get-tuple-element.70), channel_id=1, source_target_pairs={{0,3},{1,2},{2,1},{3,0},{4,7},{5,6},{6,5},{7,4},{8,11},{9,10},{10,... | collective-permute-start | bytes 786440 | tf_op jit(solution)/shard_map/ppermute | solution.py:29
  (2 other events, 2.0 us)

commit v8 on v7

--- a/solution.py
+++ b/solution.py
@@ -19,6 +19,19 @@
 BASE = 64
 IN_FLIGHT = 2
 EARLY = 2
+XY_START = 0
+XY_NEXT = 3
+XY_LAST = 2
+ADD_ORDER = (
+    ("near", 0),
+    ("near", 1),
+    ("mine", 0),
+    ("near", 2),
+    ("mine", 1),
+    ("near", 3),
+    ("mine", 2),
+    ("mine", 3),
+)
 LOG2E = 1.4426950408889634
 VMEM = pl.BlockSpec(memory_space=pltpu.VMEM)
 ANY = pl.BlockSpec(memory_space=pl.ANY)
@@ -228,78 +241,112 @@
     )(after, *pieces)
 
 
-def absorb_kernel(chunk, rank_ref, mine_ref, theirs_ref, gain_ref, w_ref, *refs):
-    last = chunk == len(WIDTHS) - 1
-    state_count = 0 if chunk == 0 else 2
-    states = refs[:state_count]
-    home_ref = refs[state_count + int(last)]
-    outs = refs[state_count + int(last) + 1 :]
-    first, width = SPANS[chunk]
-    span = slice(first, first + width)
+def shard_kernel(place_ref, in_hbm, back_hbm, out_ref, sems):
+    width = out_ref.shape[1]
+    rows = in_hbm.shape[0]
+    span = pl.ds(pl.multiple_of(place_ref[1] * width, width), width)
+    copies = [
+        pltpu.make_async_copy(in_hbm.at[:, span], out_ref.at[:rows], sems.at[0]),
+        pltpu.make_async_copy(back_hbm.at[:, span], out_ref.at[rows:], sems.at[1]),
+    ]
+    for copy in copies:
+        copy.start()
+    for copy in copies:
+        copy.wait()
+
+
+def make_shard(places, w_in, w_back, width):
+    rows = w_in.shape[0] + w_back.shape[0]
+    return pl.pallas_call(
+        shard_kernel,
+        out_shape=jax.ShapeDtypeStruct((rows, width), jnp.bfloat16),
+        in_specs=[pl.BlockSpec(memory_space=pltpu.SMEM), ANY, ANY],
+        out_specs=VMEM,
+        scratch_shapes=[pltpu.SemaphoreType.DMA((2,))],
+        compiler_params=pltpu.CompilerParams(vmem_limit_bytes=60 * 1024 * 1024),
+        cost_estimate=LIGHT,
+        name="make_shard",
+    )(places, w_in, w_back)
+
+
+def expert_kernel(place_ref, gain_ref, in_ref, back_ref, *refs):
+    count = len(WIDTHS)
+    mine = refs[:count]
+    groups = (refs[count : count + 2], refs[count + 2 : count + 4])
+    home_ref, own_ref, leaving_ref, gained, result = refs[count + 4 :]
     home = home_ref.shape[0]
-    place = rank_ref[0] // 2
-    home_ref[...] = mine_ref[pl.ds(pl.multiple_of(place * home, home), home), :]
-    wide = jnp.concatenate([mine_ref[...], theirs_ref[...]], axis=0).astype(jnp.float32)
-    gained = (wide * gain_ref[:, span]).astype(jnp.bfloat16)
+    index = place_ref[0] // 2
+    near_row = pl.multiple_of(index * home, home)
+    far_row = pl.multiple_of((1 - index) * home, home)
+    rows_in, hidden = in_ref.shape[0], back_ref.shape[0]
+    block_rows = rows_in + hidden
+    square = 0.0
+    for (first, width), part in zip(SPANS, mine):
+        span = slice(first, first + width)
+        home_ref[:, span] = part[pl.ds(near_row, home), :]
+        wide = part[...].astype(jnp.float32)
+        for i in range(width // 128):
+            piece = wide[:, i * 128 : (i + 1) * 128]
+            square = square + piece * piece
+        gained[:, span] = (wide * gain_ref[:, span]).astype(jnp.bfloat16)
+    scale = lax.rsqrt(jnp.sum(square, axis=1, keepdims=True) / D + 1e-06)
+    blocks = []
+    for g, (three, one) in enumerate(groups):
+        shard = three.shape[1]
+        for j in range(4):
+            buf, top = (three, j * block_rows) if j < 3 else (one, 0)
+            cols = pl.multiple_of((place_ref[1] ^ (2 * j + g)) * shard, shard)
+            blocks.append((buf, top, pl.ds(cols, shard)))
+    contract = (((1,), (1,)), ((), ()))
     product = lax.dot_general(
-        gained, w_ref[:, span], (((1,), (1,)), ((), ())), preferred_element_type=jnp.float32
-    )
-    square = sum(
-        wide[:, i * 128 : (i + 1) * 128] * wide[:, i * 128 : (i + 1) * 128]
-        for i in range(width // 128)
-    )
-    if chunk > 0:
-        product += states[0][...]
-        square += states[1][...]
-    if not last:
-        outs[0][...] = product
-        outs[1][...] = square
-        return
-    back_ref = refs[state_count]
-    shares, act_buf = outs[:-1], outs[-1]
-    hidden = product.shape[1] // 2
-    mean_square = jnp.sum(square, axis=1, keepdims=True) / D
-    product = product * lax.rsqrt(mean_square + 1e-06)
-    gate = product[:, :hidden]
-    act_buf[...] = gate / (1.0 + jnp.exp(-gate)) * product[:, hidden:]
-    ordered = []
-    for offset in range(len(shares)):
-        row = (offset % 2) * 2 * home + (place ^ (offset // 2)) * home
-        ordered.append(act_buf[pl.ds(pl.multiple_of(row, home), home), :])
-    ordered = jnp.concatenate(ordered, axis=0).astype(jnp.bfloat16)
-    for part_first, part_width in SPANS:
-        part = slice(part_first, part_first + part_width)
-        result = jnp.dot(ordered, back_ref[:, part], preferred_element_type=jnp.float32)
-        for i, share in enumerate(shares):
-            share[:, part] = result[i * home : (i + 1) * home].astype(jnp.bfloat16)
-
-
-def absorb(chunk, rank, mine, theirs, gain, w_in, states, back):
-    half, width = mine.shape
-    rows = w_in.shape[0]
-    count = lax.axis_size("exp")
-    home = 2 * half // count
-    out_shape = [jax.ShapeDtypeStruct((home, width), jnp.bfloat16)]
-    scratch = []
-    operands = [rank, mine, theirs, gain, w_in, *states]
-    if chunk == len(WIDTHS) - 1:
-        operands.append(back)
-        out_shape += [jax.ShapeDtypeStruct((home, D), jnp.bfloat16)] * count
-        scratch = [pltpu.VMEM((2 * half, rows // 2), jnp.float32)]
-    else:
-        out_shape += [
-            jax.ShapeDtypeStruct((2 * half, rows), jnp.float32),
-            jax.ShapeDtypeStruct((2 * half, 128), jnp.float32),
-        ]
+        gained[...], in_ref[...], contract, preferred_element_type=jnp.float32
+    )
+    other = jnp.zeros_like(product)
+    for buf, top, cols in blocks:
+        other += lax.dot_general(
+            gained[:, cols],
+            buf[top : top + rows_in, :],
+            contract,
+            preferred_element_type=jnp.float32,
+        )
+
+    def activate(value):
+        value = value * scale
+        gate = value[:, :hidden]
+        return (gate / (1.0 + jnp.exp(-gate)) * value[:, hidden:]).astype(jnp.bfloat16)
+
+    act, act_other = activate(product), activate(other)
+    for buf, top, cols in blocks:
+        result[:, cols] = jnp.dot(
+            act, back_ref[:, cols], preferred_element_type=jnp.float32
+        ) + jnp.dot(
+            act_other,
+            buf[top + rows_in : top + block_rows, :],
+            preferred_element_type=jnp.float32,
+        )
+    own_ref[...] = result[pl.ds(near_row, home), :]
+    leaving_ref[...] = result[pl.ds(far_row, home), :].astype(jnp.bfloat16)
+
+
+def experts(places, gain, w_in, w_back, mine, weights):
+    half = mine[0].shape[0]
+    operands = [places, gain, w_in, w_back, *mine, *weights]
     return pl.pallas_call(
-        functools.partial(absorb_kernel, chunk),
-        out_shape=out_shape,
+        expert_kernel,
+        out_shape=[
+            jax.ShapeDtypeStruct((half // 2, D), jnp.bfloat16),
+            jax.ShapeDtypeStruct((half // 2, D), jnp.float32),
+            jax.ShapeDtypeStruct((half // 2, D), jnp.bfloat16),
+        ],
         in_specs=[pl.BlockSpec(memory_space=pltpu.SMEM)] + [VMEM] * (len(operands) - 1),
-        out_specs=[VMEM] * len(out_shape),
-        scratch_shapes=scratch,
+        out_specs=[VMEM] * 3,
+        scratch_shapes=[
+            pltpu.VMEM((half, D), jnp.bfloat16),
+            pltpu.VMEM((half, D), jnp.float32),
+        ],
         compiler_params=pltpu.CompilerParams(vmem_limit_bytes=16 * 1024 * 1024),
         cost_estimate=LIGHT,
-        name="absorb",
+        name="experts",
     )(*operands)
 
 
@@ -351,6 +398,11 @@
     other_keys = exchange(same_keys, "ctx", 1, ctx_count)
 
     ranks = rank.astype(jnp.int32).reshape(1)
+    places = jnp.stack([rank, lax.axis_index("ctx")]).astype(jnp.int32)
+    flat_in = w_in.reshape(2 * hidden, D)
+    flat_back = w_back.reshape(hidden, D)
+    shard = make_shard(places, flat_in, flat_back, D // ctx_count)
+    shard = exchange(shard, "exp", 1, exp_count)
     *parts, attended = attend_project(
         ranks, limits, same_keys, other_keys, staged_queries, staged_residual, w_out
     )
@@ -359,9 +411,6 @@
     coefficient = jnp.sum(jnp.where(routes == 0, shares, 0.0), axis=1, keepdims=True)
     coefficient = coefficient.astype(jnp.bfloat16).astype(jnp.float32)
     gain = norm_gain.reshape(1, D)
-    flat_in = w_in.reshape(2 * hidden, D)
-    flat_back = w_back.reshape(hidden, D)
-    count = len(WIDTHS)
 
     def swap(values, offset):
         results = []
@@ -372,41 +421,37 @@
         return results
 
     arrived = swap(parts[1::2], 1)
-    near = [kept + other for kept, other in zip(parts[::2], arrived)]
-    across = swap(near, 2)
-    mine = [own + other for own, other in zip(near, across)]
-    homes, states, theirs, done = [], [], [], [coefficient]
-    for chunk in range(count):
-        value = mine[chunk]
-        if chunk >= IN_FLIGHT:
-            own, *states = absorb(
-                chunk - IN_FLIGHT,
-                ranks,
-                mine[chunk - IN_FLIGHT],
-                theirs[chunk - IN_FLIGHT],
-                gain,
-                flat_in,
-                states,
-                flat_back,
-            )
-            homes.append(own)
-            done = [states[0]]
-        if chunk >= IN_FLIGHT or chunk == 1:
-            value, *done = lax.optimization_barrier((value, *done))
-            if chunk == 1:
-                coefficient = done[0]
-            else:
-                states[0] = done[0]
-        theirs.append(exchange(value, "exp", 1, exp_count))
-    for chunk in range(count - IN_FLIGHT, count):
-        own, *states = absorb(
-            chunk, ranks, mine[chunk], theirs[chunk], gain, flat_in, states, flat_back
-        )
-        homes.append(own)
-    middle_out = jnp.concatenate(homes, axis=1)
-    expert = states[0].astype(jnp.float32)
-    for offset in range(1, exp_count):
-        expert = expert + exchange(states[offset], "exp", offset, exp_count).astype(jnp.float32)
+    near, across, mine, last = [], [], [], []
+
+    def add_next(left, right):
+        if last:
+            right, _ = lax.optimization_barrier((right, last[-1]))
+        last.append(left + right)
+        return last[-1]
+
+    for kind, chunk in ADD_ORDER:
+        if kind == "near":
+            near.append(add_next(parts[2 * chunk], arrived[chunk]))
+            value = near[chunk]
+            if chunk >= IN_FLIGHT:
+                value, _ = lax.optimization_barrier((value, across[chunk - IN_FLIGHT]))
+            across.append(exchange(value, "exp", 2, exp_count))
+        else:
+            mine.append(add_next(near[chunk], across[chunk]))
+    shard, _ = lax.optimization_barrier((shard, near[XY_START]))
+    from_x = exchange(shard, "ctx", 2, ctx_count)
+    from_y = exchange(shard, "ctx", 4, ctx_count)
+    middle_row = shard.shape[0] // 2
+    same = join_after([shard, from_x, from_y], near[XY_NEXT])
+    upper = exchange(same[shard.shape[0] :][:middle_row], "ctx", 4, ctx_count)
+    lower = exchange(same[2 * shard.shape[0] + middle_row :], "ctx", 2, ctx_count)
+    other = exchange(same, "ctx", 1, ctx_count)
+    corner = join_after([upper, lower], mine[XY_LAST])
+    other_corner = exchange(corner, "ctx", 1, ctx_count)
+    middle_out, own, leaving = experts(
+        places, gain, flat_in, flat_back, mine, [same, corner, other, other_corner]
+    )
+    expert = own + exchange(leaving, "exp", 2, exp_count).astype(jnp.float32)
     return (middle_out, (expert * coefficient).astype(jnp.bfloat16))
 
 

time: 85.4 us -> 89.4 us (1.047)
  Pallas kernels: 13 us -> 18.1 us
  waiting for transfers between devices: 40.9 us -> 43.6 us
  local copies, waits for them, and re-layouts: 2.8 us -> 0.88 us
  other arithmetic: 3.29 us -> 1.81 us
    pallas_call x4 -> x2, Pallas kernels: 2.12 us -> 7.28 us  [the longest x1 4.6 us: experts(): pl.pallas_call(expert_kernel, out_shape=[jax.ShapeDtypeStruct((half // 2,...]
    ppermute x19 -> x20, waiting for transfers between devices: 40.9 us -> 43.6 us  [exchange(): return lax.ppermute(value, axis, [(i, i ^ offset) for i in range(size)])]
    unnamed x14 -> x18, local copies, waits for them, and re-layouts: 2.01 us -> 0.05 us
    ppermute x19 -> x20, starting transfers between devices: 21.3 us -> 21.2 us  [exchange(): return lax.ppermute(value, axis, [(i, i ^ offset) for i in range(size)])]
  transfers between devices with their start and end apart: 19 -> 20, of which waited for: 13 -> 8; matrix products, arithmetic and copies ran while one was open for 3% -> 1% of each run, Pallas kernels for 7% -> 15%
where the time goes in v8:
time: 89.4 us; the launch traced here: 89.2 us
  waiting for transfers between devices  43.6 us (49%)
  starting transfers between devices  21.2 us (24%)
  Pallas kernels  18.1 us (20%)
  between operations  3.57 us (4%)
  other arithmetic  1.81 us (2%)
    ppermute x20, waiting for transfers between devices, exchange(): return lax.ppermute(value, axis, [(i, i ^ offset) for i in range(size)])  43.6 us
    ppermute x20, starting transfers between devices, exchange(): return lax.ppermute(value, axis, [(i, i ^ offset) for i in range(size)])  21.2 us
    pallas_call x1, Pallas kernels, attend_project(): pl.pallas_call(attend_kernel, out_shape=part_shapes(tok, spans) + [jax.Sh...  6.29 us
    pallas_call x1, Pallas kernels, experts(): pl.pallas_call(expert_kernel, out_shape=[jax.ShapeDtypeStruct((half // 2,...  4.6 us
    pallas_call x1, Pallas kernels, project(): pl.pallas_call(project_kernel, out_shape=part_shapes(tok, spans), in_spec...  4.25 us
    pallas_call x1, Pallas kernels, make_shard(): pl.pallas_call(shard_kernel, out_shape=jax.ShapeDtypeStruct((rows, width)...  2.69 us
  transfers between devices with their start and end apart: 20, of which 8 were waited for; matrix products, arithmetic and copies ran while one was open for 1% of the time, Pallas kernels for 15%

profile of v8, /device:TPU:0, one launch (start us, length us, event | category | flops | bytes accessed | tf_op | source)
XLA Modules:
  0.0 89.2 jit_solution(5556410176743863604)
XLA Ops:
  3.3 0.8 constant_dynamic-slice_fusion
  4.1 3.0 %collective-permute-start = (bf16[144,256]{1,0:T(8,128)(2,1)S(1)}, bf16[144,256]{1,0:T(8,128)(2,1)S(1)}, u32[]{:S(2)}, u32[]{:S(2)}) collective-permute-start(bf16[144,256]{1,0:T(8,128)(2,1)S(1)} %fusion.2.refs_0_.refs_1_), channel_id=1, source_target_pairs={{0,8},{4,12},{8,0},{12,4},{16,24},{20,28},{24,16},{28,20},{1,9},{5... | collective-permute-start | bytes 221192 | tf_op jit(solution)/shard_map/ppermute | solution.py:42
  7.1 1.5 %collective-permute-start.1 = (bf16[144,256]{1,0:T(8,128)(2,1)S(1)}, bf16[144,256]{1,0:T(8,128)(2,1)S(1)}, u32[]{:S(2)}, u32[]{:S(2)}) collective-permute-start(bf16[144,256]{1,0:T(8,128)(2,1)S(1)} %fusion.2.refs_0_.refs_1_), channel_id=1, source_target_pairs={{0,16},{4,20},{8,24},{12,28},{16,0},{20,4},{24,8},{28,12},{1,17},{... | collective-permute-start | bytes 221192 | tf_op jit(solution)/shard_map/ppermute | solution.py:42
  9.3 2.7 %make_shard.1 = bf16[576,512]{1,0:T(8,128)(2,1)} custom-call(s32[2]{0:T(128)} %pad_add_fusion.place_ref, bf16[384,4096]{1,0:T(8,128)(2,1)} %bitcast.7, bf16[192,4096]{1,0:T(8,128)(2,1)} %bitcast.9), custom_call_target="tpu_custom_call" | custom-call | flops 1024 | bytes 1024 | tf_op jit(solution)/shard_map/make_shard/pallas_call | solution.py:260
  11.9 2.1 %collective-permute-start.12 = (bf16[576,512]{1,0:T(8,128)(2,1)}, bf16[576,512]{1,0:T(8,128)(2,1)S(1)}, u32[]{:S(2)}, u32[]{:S(2)}) collective-permute-start(bf16[576,512]{1,0:T(8,128)(2,1)} %make_shard.1), channel_id=1, source_target_pairs={{0,1},{1,0},{2,3},{3,2},{4,5},{5,4},{6,7},{7,6},{8,9},{9,8},{10,11... | collective-permute-start | bytes 1769480 | tf_op jit(solution)/shard_map/ppermute | solution.py:42
  14.3 1.5 %collective-permute-done.3.other_ref = bf16[576,256]{1,0:T(8,128)(2,1)S(1)} collective-permute-done((bf16[576,256]{1,0:T(8,128)(2,1)S(1)}, bf16[576,256]{1,0:T(8,128)(2,1)S(1)}, u32[]{:S(2)}, u32[]{:S(2)}) %collective-permute-start.3) | collective-permute-done | bytes 294944 | tf_op jit(solution)/shard_map/ppermute | solution.py:42
  15.8 6.3 %attend_project.1 = (bf16[64,1024]{1,0:T(8,128)(2,1)S(1)}, bf16[64,1024]{1,0:T(8,128)(2,1)S(1)}, bf16[64,1024]{1,0:T(8,128)(2,1)S(1)}, bf16[64,1024]{1,0:T(8,128)(2,1)S(1)}, bf16[128,2048]{1,0:T(8,128)(2,1)S(1)}) custom-call(s32[1]{0:T(128)} %bitcast.rank_ref, bf16[16,256]{1,0:T(8,128)(2,1)S(1)} %broadcast_in_dim.5.limit_ref, ...), custom_call_target="tpu_custom_call" | custom-call | flops 2147483648 | bytes 8388608 | tf_op jit(solution)/shard_map/attend_project/pallas_call | solution.py:141
  22.1 1.3 %collective-permute-start.4 = (bf16[64,1024]{1,0:T(8,128)(2,1)S(1)}, bf16[64,1024]{1,0:T(8,128)(2,1)S(1)}, u32[]{:S(2)}, u32[]{:S(2)}) collective-permute-start(bf16[64,1024]{1,0:T(8,128)(2,1)S(1)} %get-tuple-element.31), channel_id=1, source_target_pairs={{0,1},{1,0},{2,3},{3,2},{4,5},{5,4},{6,7},{7,6},{8,9},{9,8},{10,11... | collective-permute-start | bytes 393224 | tf_op jit(solution)/shard_map/ppermute | solution.py:42
  23.5 6.1 %collective-permute-done.4 = bf16[64,1024]{1,0:T(8,128)(2,1)S(1)} collective-permute-done((bf16[64,1024]{1,0:T(8,128)(2,1)S(1)}, bf16[64,1024]{1,0:T(8,128)(2,1)S(1)}, u32[]{:S(2)}, u32[]{:S(2)}) %collective-permute-start.4) | collective-permute-done | bytes 131104 | tf_op jit(solution)/shard_map/ppermute | solution.py:42
  29.6 1.7 %collective-permute-start.13 = (bf16[576,512]{1,0:T(8,128)(2,1)S(1)}, bf16[576,512]{1,0:T(8,128)(2,1)S(1)}, u32[]{:S(2)}, u32[]{:S(2)}) collective-permute-start(bf16[576,512]{1,0:T(8,128)(2,1)S(1)} %collective-permute-done.12.refs_1_), channel_id=1, source_target_pairs={{0,8},{4,12},{8,0},{12,4},{16,24},{20,28},{24,16},{28,20},{1,9},{5... | collective-permute-start | bytes 1769480 | tf_op jit(solution)/shard_map/ppermute | solution.py:42
  31.3 1.5 %collective-permute-start.14 = (bf16[576,512]{1,0:T(8,128)(2,1)S(1)}, bf16[576,512]{1,0:T(8,128)(2,1)S(1)}, u32[]{:S(2)}, u32[]{:S(2)}) collective-permute-start(bf16[576,512]{1,0:T(8,128)(2,1)S(1)} %collective-permute-done.12.refs_1_), channel_id=1, source_target_pairs={{0,16},{4,20},{8,24},{12,28},{16,0},{20,4},{24,8},{28,12},{1,17},{... | collective-permute-start | bytes 1769480 | tf_op jit(solution)/shard_map/ppermute | solution.py:42
  32.8 1.6 %collective-permute-start.6 = (bf16[64,1024]{1,0:T(8,128)(2,1)S(1)}, bf16[64,1024]{1,0:T(8,128)(2,1)S(1)}, u32[]{:S(2)}, u32[]{:S(2)}) collective-permute-start(bf16[64,1024]{1,0:T(8,128)(2,1)S(1)} %get-tuple-element.33), channel_id=1, source_target_pairs={{0,1},{1,0},{2,3},{3,2},{4,5},{5,4},{6,7},{7,6},{8,9},{9,8},{10,11... | collective-permute-start | bytes 393224 | tf_op jit(solution)/shard_map/ppermute | solution.py:42
  34.4 2.6 %collective-permute-start.5 = (bf16[64,1024]{1,0:T(8,128)(2,1)S(1)}, bf16[64,1024]{1,0:T(8,128)(2,1)S(1)}, u32[]{:S(2)}, u32[]{:S(2)}) collective-permute-start(bf16[64,1024]{1,0:T(8,128)(2,1)S(1)} %add.44), channel_id=1, source_target_pairs={{0,2},{1,3},{2,0},{3,1},{4,6},{5,7},{6,4},{7,5},{8,10},{9,11},{10,... | collective-permute-start | bytes 393224 | tf_op jit(solution)/shard_map/ppermute | solution.py:42
  37.0 4.3 %project.1 = (bf16[64,1024]{1,0:T(8,128)(2,1)S(1)}, bf16[64,1024]{1,0:T(8,128)(2,1)S(1)}, bf16[64,1024]{1,0:T(8,128)(2,1)S(1)}, bf16[64,1024]{1,0:T(8,128)(2,1)S(1)}) custom-call(s32[1]{0:T(128)} %bitcast.rank_ref, bf16[128,2048]{1,0:T(8,128)(2,1)S(1)} %get-tuple-element.36.attended, bf16[32,4096]{1,0:T(8,128)(2,1)S(1)} %get-tuple-element.29.resid_ref, ...), custom_call_target="tpu_custom_call" | custom-call | flops 1073741824 | bytes 8388608 | tf_op jit(solution)/shard_map/project/pallas_call | solution.py:176
  42.2 1.8 %collective-permute-start.10 = (bf16[64,1024]{1,0:T(8,128)(2,1)S(1)}, bf16[64,1024]{1,0:T(8,128)(2,1)S(1)}, u32[]{:S(2)}, u32[]{:S(2)}) collective-permute-start(bf16[64,1024]{1,0:T(8,128)(2,1)S(1)} %get-tuple-element.45), channel_id=1, source_target_pairs={{0,1},{1,0},{2,3},{3,2},{4,5},{5,4},{6,7},{7,6},{8,9},{9,8},{10,11... | collective-permute-start | bytes 393224 | tf_op jit(solution)/shard_map/ppermute | solution.py:42
  44.1 3.8 %collective-permute-done.8 = bf16[64,1024]{1,0:T(8,128)(2,1)S(1)} collective-permute-done((bf16[64,1024]{1,0:T(8,128)(2,1)S(1)}, bf16[64,1024]{1,0:T(8,128)(2,1)S(1)}, u32[]{:S(2)}, u32[]{:S(2)}) %collective-permute-start.8) | collective-permute-done | bytes 131104 | tf_op jit(solution)/shard_map/ppermute | solution.py:42
  47.9 1.4 %collective-permute-done.7 = bf16[64,1024]{1,0:T(8,128)(2,1)S(1)} collective-permute-done((bf16[64,1024]{1,0:T(8,128)(2,1)S(1)}, bf16[64,1024]{1,0:T(8,128)(2,1)S(1)}, u32[]{:S(2)}, u32[]{:S(2)}) %collective-permute-start.7) | collective-permute-done | bytes 131104 | tf_op jit(solution)/shard_map/ppermute | solution.py:42
  51.1 1.1 %collective-permute-start.9 = (bf16[64,1024]{1,0:T(8,128)(2,1)S(1)}, bf16[64,1024]{1,0:T(8,128)(2,1)S(1)}, u32[]{:S(2)}, u32[]{:S(2)}) collective-permute-start(bf16[64,1024]{1,0:T(8,128)(2,1)S(1)} %add.47), channel_id=1, source_target_pairs={{0,2},{1,3},{2,0},{3,1},{4,6},{5,7},{6,4},{7,5},{8,10},{9,11},{10,... | collective-permute-start | bytes 393224 | tf_op jit(solution)/shard_map/ppermute | solution.py:42
  52.3 7.9 %collective-permute-done.9 = bf16[64,1024]{1,0:T(8,128)(2,1)S(1)} collective-permute-done((bf16[64,1024]{1,0:T(8,128)(2,1)S(1)}, bf16[64,1024]{1,0:T(8,128)(2,1)S(1)}, u32[]{:S(2)}, u32[]{:S(2)}) %collective-permute-start.9) | collective-permute-done | bytes 131104 | tf_op jit(solution)/shard_map/ppermute | solution.py:42
  60.4 0.7 collective-permute-start.11
  61.0 8.7 %collective-permute-done.11 = bf16[64,1024]{1,0:T(8,128)(2,1)S(1)} collective-permute-done((bf16[64,1024]{1,0:T(8,128)(2,1)S(1)}, bf16[64,1024]{1,0:T(8,128)(2,1)S(1)}, u32[]{:S(2)}, u32[]{:S(2)}) %collective-permute-start.11) | collective-permute-done | bytes 131104 | tf_op jit(solution)/shard_map/ppermute | solution.py:42
  69.8 4.6 %experts.1 = (bf16[32,4096]{1,0:T(8,128)(2,1)}, f32[32,4096]{1,0:T(8,128)S(1)}, bf16[32,4096]{1,0:T(8,128)(2,1)S(1)}) custom-call(s32[2]{0:T(128)S(1)} %copy-done.5, f32[1,4096]{1,0:T(1,128)S(1)} %bitcast.11, bf16[384,4096]{1,0:T(8,128)(2,1)S(1)} %bitcast.8, bf16[192,4096]{1,0:T(8,128)(2,1)S(1)} %bitcast.10, bf16[64,1024]{1,0:T(8,128)(2,1)S(1)} %add.46.refs_0_, ...), custom_call_target="tpu_custom_call" | custom-call | flops 1024 | bytes 1024 | tf_op jit(solution)/shard_map/experts/pallas_call | solution.py:334
  74.5 13.9 %collective-permute-done.19 = bf16[32,4096]{1,0:T(8,128)(2,1)S(1)} collective-permute-done((bf16[32,4096]{1,0:T(8,128)(2,1)S(1)}, bf16[32,4096]{1,0:T(8,128)(2,1)S(1)}, u32[]{:S(2)}, u32[]{:S(2)}) %collective-permute-start.19) | collective-permute-done | bytes 262176 | tf_op jit(solution)/shard_map/ppermute | solution.py:42
  88.4 0.8 multiply_convert_fusion
  (61 shorter events, 3.9 us)
Async XLA Ops:
  4.1 10.1 %collective-permute-start = (bf16[144,256]{1,0:T(8,128)(2,1)S(1)}, bf16[144,256]{1,0:T(8,128)(2,1)S(1)}, u32[]{:S(2)}, u32[]{:S(2)}) collective-permute-start(bf16[144,256]{1,0:T(8,128)(2,1)S(1)} %fusion.2.refs_0_.refs_1_), channel_id=1, source_target_pairs={{0,8},{4,12},{8,0},{12,4},{16,24},{20,28},{24,16},{28,20},{1,9},{5... | collective-permute-start | bytes 221192 | tf_op jit(solution)/shard_map/ppermute | solution.py:42
  7.1 7.1 %collective-permute-start.1 = (bf16[144,256]{1,0:T(8,128)(2,1)S(1)}, bf16[144,256]{1,0:T(8,128)(2,1)S(1)}, u32[]{:S(2)}, u32[]{:S(2)}) collective-permute-start(bf16[144,256]{1,0:T(8,128)(2,1)S(1)} %fusion.2.refs_0_.refs_1_), channel_id=1, source_target_pairs={{0,16},{4,20},{8,24},{12,28},{16,0},{20,4},{24,8},{28,12},{1,17},{... | collective-permute-start | bytes 221192 | tf_op jit(solution)/shard_map/ppermute | solution.py:42
  8.6 5.6 %collective-permute-start.2 = (bf16[144,256]{1,0:T(8,128)(2,1)S(1)}, bf16[144,256]{1,0:T(8,128)(2,1)S(1)}, u32[]{:S(2)}, u32[]{:S(2)}) collective-permute-start(bf16[144,256]{1,0:T(8,128)(2,1)S(1)} %fusion.2.refs_0_.refs_1_), channel_id=1, source_target_pairs={{0,24},{4,28},{8,16},{12,20},{16,8},{20,12},{24,0},{28,4},{1,25},{... | collective-permute-start | bytes 221192 | tf_op jit(solution)/shard_map/ppermute | solution.py:42
  11.9 17.6 %collective-permute-start.12 = (bf16[576,512]{1,0:T(8,128)(2,1)}, bf16[576,512]{1,0:T(8,128)(2,1)S(1)}, u32[]{:S(2)}, u32[]{:S(2)}) collective-permute-start(bf16[576,512]{1,0:T(8,128)(2,1)} %make_shard.1), channel_id=1, source_target_pairs={{0,1},{1,0},{2,3},{3,2},{4,5},{5,4},{6,7},{7,6},{8,9},{9,8},{10,11... | collective-permute-start | bytes 1769480 | tf_op jit(solution)/shard_map/ppermute | solution.py:42
  14.2 1.6 %collective-permute-start.3 = (bf16[576,256]{1,0:T(8,128)(2,1)S(1)}, bf16[576,256]{1,0:T(8,128)(2,1)S(1)}, u32[]{:S(2)}, u32[]{:S(2)}) collective-permute-start(bf16[576,256]{1,0:T(8,128)(2,1)S(1)} %join_after.3.same_ref), channel_id=1, source_target_pairs={{0,4},{4,0},{8,12},{12,8},{16,20},{20,16},{24,28},{28,24},{1,5},{5... | collective-permute-start | bytes 884744 | tf_op jit(solution)/shard_map/ppermute | solution.py:42
  22.1 7.4 %collective-permute-start.4 = (bf16[64,1024]{1,0:T(8,128)(2,1)S(1)}, bf16[64,1024]{1,0:T(8,128)(2,1)S(1)}, u32[]{:S(2)}, u32[]{:S(2)}) collective-permute-start(bf16[64,1024]{1,0:T(8,128)(2,1)S(1)} %get-tuple-element.31), channel_id=1, source_target_pairs={{0,1},{1,0},{2,3},{3,2},{4,5},{5,4},{6,7},{7,6},{8,9},{9,8},{10,11... | collective-permute-start | bytes 393224 | tf_op jit(solution)/shard_map/ppermute | solution.py:42
  29.6 20.1 %collective-permute-start.13 = (bf16[576,512]{1,0:T(8,128)(2,1)S(1)}, bf16[576,512]{1,0:T(8,128)(2,1)S(1)}, u32[]{:S(2)}, u32[]{:S(2)}) collective-permute-start(bf16[576,512]{1,0:T(8,128)(2,1)S(1)} %collective-permute-done.12.refs_1_), channel_id=1, source_target_pairs={{0,8},{4,12},{8,0},{12,4},{16,24},{20,28},{24,16},{28,20},{1,9},{5... | collective-permute-start | bytes 1769480 | tf_op jit(solution)/shard_map/ppermute | solution.py:42
  31.3 18.4 %collective-permute-start.14 = (bf16[576,512]{1,0:T(8,128)(2,1)S(1)}, bf16[576,512]{1,0:T(8,128)(2,1)S(1)}, u32[]{:S(2)}, u32[]{:S(2)}) collective-permute-start(bf16[576,512]{1,0:T(8,128)(2,1)S(1)} %collective-permute-done.12.refs_1_), channel_id=1, source_target_pairs={{0,16},{4,20},{8,24},{12,28},{16,0},{20,4},{24,8},{28,12},{1,17},{... | collective-permute-start | bytes 1769480 | tf_op jit(solution)/shard_map/ppermute | solution.py:42
  32.8 8.9 %collective-permute-start.6 = (bf16[64,1024]{1,0:T(8,128)(2,1)S(1)}, bf16[64,1024]{1,0:T(8,128)(2,1)S(1)}, u32[]{:S(2)}, u32[]{:S(2)}) collective-permute-start(bf16[64,1024]{1,0:T(8,128)(2,1)S(1)} %get-tuple-element.33), channel_id=1, source_target_pairs={{0,1},{1,0},{2,3},{3,2},{4,5},{5,4},{6,7},{7,6},{8,9},{9,8},{10,11... | collective-permute-start | bytes 393224 | tf_op jit(solution)/shard_map/ppermute | solution.py:42
  34.4 7.8 %collective-permute-start.5 = (bf16[64,1024]{1,0:T(8,128)(2,1)S(1)}, bf16[64,1024]{1,0:T(8,128)(2,1)S(1)}, u32[]{:S(2)}, u32[]{:S(2)}) collective-permute-start(bf16[64,1024]{1,0:T(8,128)(2,1)S(1)} %add.44), channel_id=1, source_target_pairs={{0,2},{1,3},{2,0},{3,1},{4,6},{5,7},{6,4},{7,5},{8,10},{9,11},{10,... | collective-permute-start | bytes 393224 | tf_op jit(solution)/shard_map/ppermute | solution.py:42
  41.3 6.6 %collective-permute-start.8 = (bf16[64,1024]{1,0:T(8,128)(2,1)S(1)}, bf16[64,1024]{1,0:T(8,128)(2,1)S(1)}, u32[]{:S(2)}, u32[]{:S(2)}) collective-permute-start(bf16[64,1024]{1,0:T(8,128)(2,1)S(1)} %get-tuple-element.39), channel_id=1, source_target_pairs={{0,1},{1,0},{2,3},{3,2},{4,5},{5,4},{6,7},{7,6},{8,9},{9,8},{10,11... | collective-permute-start | bytes 393224 | tf_op jit(solution)/shard_map/ppermute | solution.py:42
  41.8 7.5 %collective-permute-start.7 = (bf16[64,1024]{1,0:T(8,128)(2,1)S(1)}, bf16[64,1024]{1,0:T(8,128)(2,1)S(1)}, u32[]{:S(2)}, u32[]{:S(2)}) collective-permute-start(bf16[64,1024]{1,0:T(8,128)(2,1)S(1)} %add.45), channel_id=1, source_target_pairs={{0,2},{1,3},{2,0},{3,1},{4,6},{5,7},{6,4},{7,5},{8,10},{9,11},{10,... | collective-permute-start | bytes 393224 | tf_op jit(solution)/shard_map/ppermute | solution.py:42
  42.2 7.4 %collective-permute-start.10 = (bf16[64,1024]{1,0:T(8,128)(2,1)S(1)}, bf16[64,1024]{1,0:T(8,128)(2,1)S(1)}, u32[]{:S(2)}, u32[]{:S(2)}) collective-permute-start(bf16[64,1024]{1,0:T(8,128)(2,1)S(1)} %get-tuple-element.45), channel_id=1, source_target_pairs={{0,1},{1,0},{2,3},{3,2},{4,5},{5,4},{6,7},{7,6},{8,9},{9,8},{10,11... | collective-permute-start | bytes 393224 | tf_op jit(solution)/shard_map/ppermute | solution.py:42
  49.7 20.0 %copy-start.1 = (bf16[1,192,4096]{2,1,0:T(8,128)(2,1)S(1)}, bf16[1,192,4096]{2,1,0:T(8,128)(2,1)}, u32[]{:S(2)}) copy-start(bf16[1,192,4096]{2,1,0:T(8,128)(2,1)} %param.23) | copy-start | bytes 4718596
  49.9 19.9 %copy-start = (bf16[1,384,4096]{2,1,0:T(8,128)(2,1)S(1)}, bf16[1,384,4096]{2,1,0:T(8,128)(2,1)}, u32[]{:S(2)}) copy-start(bf16[1,384,4096]{2,1,0:T(8,128)(2,1)} %param.22) | copy-start | bytes 9437188
  49.9 19.9 %copy-start.4 = (f32[4096]{0:T(1024)S(1)}, f32[4096]{0:T(1024)}, u32[]{:S(2)}) copy-start(f32[4096]{0:T(1024)} %param.19) | copy-start | bytes 49156
  49.9 19.9 %copy-start.5 = (s32[2]{0:T(128)S(1)}, s32[2]{0:T(128)}, u32[]{:S(2)}) copy-start(s32[2]{0:T(128)} %pad_add_fusion.place_ref) | copy-start | bytes 28
  49.9 19.9 %collective-permute-start.17 = (bf16[1728,512]{1,0:T(8,128)(2,1)S(1)}, bf16[1728,512]{1,0:T(8,128)(2,1)S(1)}, u32[]{:S(2)}, u32[]{:S(2)}) collective-permute-start(bf16[1728,512]{1,0:T(8,128)(2,1)S(1)} %join_after.4.refs_4_), channel_id=1, source_target_pairs={{0,4},{4,0},{8,12},{12,8},{16,20},{20,16},{24,28},{28,24},{1,5},{5... | collective-permute-start | bytes 5308424 | tf_op jit(solution)/shard_map/ppermute | solution.py:42
  50.0 10.2 %collective-permute-start.15 = (bf16[288,512]{1,0:T(8,128)(2,1)S(1)}, bf16[288,512]{1,0:T(8,128)(2,1)S(1)}, u32[]{:S(2)}, u32[]{:S(2)}) collective-permute-start(bf16[288,512]{1,0:T(8,128)(2,1)S(1)} %get-tuple-element.55), channel_id=1, source_target_pairs={{0,16},{4,20},{8,24},{12,28},{16,0},{20,4},{24,8},{28,12},{1,17},{... | collective-permute-start | bytes 884744 | tf_op jit(solution)/shard_map/ppermute | solution.py:42
  50.6 9.6 %collective-permute-start.16 = (bf16[288,512]{1,0:T(8,128)(2,1)S(1)}, bf16[288,512]{1,0:T(8,128)(2,1)S(1)}, u32[]{:S(2)}, u32[]{:S(2)}) collective-permute-start(bf16[288,512]{1,0:T(8,128)(2,1)S(1)} %get-tuple-element.54), channel_id=1, source_target_pairs={{0,8},{4,12},{8,0},{12,4},{16,24},{20,28},{24,16},{28,20},{1,9},{5... | collective-permute-start | bytes 884744 | tf_op jit(solution)/shard_map/ppermute | solution.py:42
  51.1 9.0 %collective-permute-start.9 = (bf16[64,1024]{1,0:T(8,128)(2,1)S(1)}, bf16[64,1024]{1,0:T(8,128)(2,1)S(1)}, u32[]{:S(2)}, u32[]{:S(2)}) collective-permute-start(bf16[64,1024]{1,0:T(8,128)(2,1)S(1)} %add.47), channel_id=1, source_target_pairs={{0,2},{1,3},{2,0},{3,1},{4,6},{5,7},{6,4},{7,5},{8,10},{9,11},{10,... | collective-permute-start | bytes 393224 | tf_op jit(solution)/shard_map/ppermute | solution.py:42
  60.3 9.5 %collective-permute-start.18 = (bf16[576,512]{1,0:T(8,128)(2,1)S(1)}, bf16[576,512]{1,0:T(8,128)(2,1)S(1)}, u32[]{:S(2)}, u32[]{:S(2)}) collective-permute-start(bf16[576,512]{1,0:T(8,128)(2,1)S(1)} %join_after.5.refs_5_), channel_id=1, source_target_pairs={{0,4},{4,0},{8,12},{12,8},{16,20},{20,16},{24,28},{28,24},{1,5},{5... | collective-permute-start | bytes 1769480 | tf_op jit(solution)/shard_map/ppermute | solution.py:42
  60.4 9.3 %collective-permute-start.11 = (bf16[64,1024]{1,0:T(8,128)(2,1)S(1)}, bf16[64,1024]{1,0:T(8,128)(2,1)S(1)}, u32[]{:S(2)}, u32[]{:S(2)}) collective-permute-start(bf16[64,1024]{1,0:T(8,128)(2,1)S(1)} %add.49.refs_0_), channel_id=1, source_target_pairs={{0,2},{1,3},{2,0},{3,1},{4,6},{5,7},{6,4},{7,5},{8,10},{9,11},{10,... | collective-permute-start | bytes 393224 | tf_op jit(solution)/shard_map/ppermute | solution.py:42
  74.4 14.0 %collective-permute-start.19 = (bf16[32,4096]{1,0:T(8,128)(2,1)S(1)}, bf16[32,4096]{1,0:T(8,128)(2,1)S(1)}, u32[]{:S(2)}, u32[]{:S(2)}) collective-permute-start(bf16[32,4096]{1,0:T(8,128)(2,1)S(1)} %get-tuple-element.53), channel_id=1, source_target_pairs={{0,2},{1,3},{2,0},{3,1},{4,6},{5,7},{6,4},{7,5},{8,10},{9,11},{10,... | collective-permute-start | bytes 786440 | tf_op jit(solution)/shard_map/ppermute | solution.py:42
  (5 other events, 23.9 us)

commit v9 on v8

--- a/solution.py
+++ b/solution.py
@@ -19,9 +19,6 @@
 BASE = 64
 IN_FLIGHT = 2
 EARLY = 2
-XY_START = 0
-XY_NEXT = 3
-XY_LAST = 2
 ADD_ORDER = (
     ("near", 0),
     ("near", 1),
@@ -438,15 +435,16 @@
             across.append(exchange(value, "exp", 2, exp_count))
         else:
             mine.append(add_next(near[chunk], across[chunk]))
-    shard, _ = lax.optimization_barrier((shard, near[XY_START]))
+    shard, _ = lax.optimization_barrier((shard, parts[0]))
     from_x = exchange(shard, "ctx", 2, ctx_count)
     from_y = exchange(shard, "ctx", 4, ctx_count)
     middle_row = shard.shape[0] // 2
-    same = join_after([shard, from_x, from_y], near[XY_NEXT])
+    same = join_after([shard, from_x, from_y], mine[1])
     upper = exchange(same[shard.shape[0] :][:middle_row], "ctx", 4, ctx_count)
     lower = exchange(same[2 * shard.shape[0] + middle_row :], "ctx", 2, ctx_count)
-    other = exchange(same, "ctx", 1, ctx_count)
-    corner = join_after([upper, lower], mine[XY_LAST])
+    crossing, _ = lax.optimization_barrier((same, mine[2]))
+    other = exchange(crossing, "ctx", 1, ctx_count)
+    corner = join_after([upper, lower], mine[3])
     other_corner = exchange(corner, "ctx", 1, ctx_count)
     middle_out, own, leaving = experts(
         places, gain, flat_in, flat_back, mine, [same, corner, other, other_corner]

time: 89.4 us -> 88.2 us (0.987)
  starting transfers between devices: 21.2 us -> 19.9 us
    ppermute x20, starting transfers between devices: 21.2 us -> 19.9 us  [exchange(): return lax.ppermute(value, axis, [(i, i ^ offset) for i in range(size)])]
  transfers between devices with their start and end apart: 20 -> 20, of which waited for: 8 -> 11; matrix products, arithmetic and copies ran while one was open for 1% -> 1% of each run, Pallas kernels for 15% -> 15%
where the time goes in v9:
time: 88.2 us; the launch traced here: 88 us
  waiting for transfers between devices  43.8 us (50%)
  starting transfers between devices  19.9 us (23%)
  Pallas kernels  18.1 us (21%)
  between operations  3.53 us (4%)
  other arithmetic  1.82 us (2%)
    ppermute x20, waiting for transfers between devices, exchange(): return lax.ppermute(value, axis, [(i, i ^ offset) for i in range(size)])  43.8 us
    ppermute x20, starting transfers between devices, exchange(): return lax.ppermute(value, axis, [(i, i ^ offset) for i in range(size)])  19.9 us
    pallas_call x1, Pallas kernels, attend_project(): pl.pallas_call(attend_kernel, out_shape=part_shapes(tok, spans) + [jax.Sh...  6.29 us
    pallas_call x1, Pallas kernels, experts(): pl.pallas_call(expert_kernel, out_shape=[jax.ShapeDtypeStruct((half // 2,...  4.6 us
    pallas_call x1, Pallas kernels, project(): pl.pallas_call(project_kernel, out_shape=part_shapes(tok, spans), in_spec...  4.25 us
    pallas_call x1, Pallas kernels, make_shard(): pl.pallas_call(shard_kernel, out_shape=jax.ShapeDtypeStruct((rows, width)...  2.69 us
  transfers between devices with their start and end apart: 20, of which 11 were waited for; matrix products, arithmetic and copies ran while one was open for 1% of the time, Pallas kernels for 15%

profile of v9, /device:TPU:0, one launch (start us, length us, event | category | flops | bytes accessed | tf_op | source)
XLA Modules:
  0.0 88.0 jit_solution(14859126102875462623)
XLA Ops:
  3.3 0.8 constant_dynamic-slice_fusion
  4.1 3.0 %collective-permute-start = (bf16[144,256]{1,0:T(8,128)(2,1)S(1)}, bf16[144,256]{1,0:T(8,128)(2,1)S(1)}, u32[]{:S(2)}, u32[]{:S(2)}) collective-permute-start(bf16[144,256]{1,0:T(8,128)(2,1)S(1)} %fusion.2.refs_0_.refs_1_), channel_id=1, source_target_pairs={{0,8},{4,12},{8,0},{12,4},{16,24},{20,28},{24,16},{28,20},{1,9},{5... | collective-permute-start | bytes 221192 | tf_op jit(solution)/shard_map/ppermute | solution.py:39
  7.1 1.5 %collective-permute-start.1 = (bf16[144,256]{1,0:T(8,128)(2,1)S(1)}, bf16[144,256]{1,0:T(8,128)(2,1)S(1)}, u32[]{:S(2)}, u32[]{:S(2)}) collective-permute-start(bf16[144,256]{1,0:T(8,128)(2,1)S(1)} %fusion.2.refs_0_.refs_1_), channel_id=1, source_target_pairs={{0,16},{4,20},{8,24},{12,28},{16,0},{20,4},{24,8},{28,12},{1,17},{... | collective-permute-start | bytes 221192 | tf_op jit(solution)/shard_map/ppermute | solution.py:39
  9.3 2.7 %make_shard.1 = bf16[576,512]{1,0:T(8,128)(2,1)} custom-call(s32[2]{0:T(128)} %pad_add_fusion.place_ref, bf16[384,4096]{1,0:T(8,128)(2,1)} %bitcast.7, bf16[192,4096]{1,0:T(8,128)(2,1)} %bitcast.9), custom_call_target="tpu_custom_call" | custom-call | flops 1024 | bytes 1024 | tf_op jit(solution)/shard_map/make_shard/pallas_call | solution.py:257
  11.9 2.1 %collective-permute-start.12 = (bf16[576,512]{1,0:T(8,128)(2,1)}, bf16[576,512]{1,0:T(8,128)(2,1)S(1)}, u32[]{:S(2)}, u32[]{:S(2)}) collective-permute-start(bf16[576,512]{1,0:T(8,128)(2,1)} %make_shard.1), channel_id=1, source_target_pairs={{0,1},{1,0},{2,3},{3,2},{4,5},{5,4},{6,7},{7,6},{8,9},{9,8},{10,11... | collective-permute-start | bytes 1769480 | tf_op jit(solution)/shard_map/ppermute | solution.py:39
  14.3 1.5 %collective-permute-done.3.other_ref = bf16[576,256]{1,0:T(8,128)(2,1)S(1)} collective-permute-done((bf16[576,256]{1,0:T(8,128)(2,1)S(1)}, bf16[576,256]{1,0:T(8,128)(2,1)S(1)}, u32[]{:S(2)}, u32[]{:S(2)}) %collective-permute-start.3) | collective-permute-done | bytes 294944 | tf_op jit(solution)/shard_map/ppermute | solution.py:39
  15.8 6.3 %attend_project.1 = (bf16[64,1024]{1,0:T(8,128)(2,1)S(1)}, bf16[64,1024]{1,0:T(8,128)(2,1)S(1)}, bf16[64,1024]{1,0:T(8,128)(2,1)S(1)}, bf16[64,1024]{1,0:T(8,128)(2,1)S(1)}, bf16[128,2048]{1,0:T(8,128)(2,1)S(1)}) custom-call(s32[1]{0:T(128)} %bitcast.rank_ref, bf16[16,256]{1,0:T(8,128)(2,1)S(1)} %broadcast_in_dim.5.limit_ref, ...), custom_call_target="tpu_custom_call" | custom-call | flops 2147483648 | bytes 8388608 | tf_op jit(solution)/shard_map/attend_project/pallas_call | solution.py:138
  22.1 4.6 %collective-permute-done.12.refs_1_ = bf16[576,512]{1,0:T(8,128)(2,1)S(1)} collective-permute-done((bf16[576,512]{1,0:T(8,128)(2,1)}, bf16[576,512]{1,0:T(8,128)(2,1)S(1)}, u32[]{:S(2)}, u32[]{:S(2)}) %collective-permute-start.12) | collective-permute-done | bytes 589856 | tf_op jit(solution)/shard_map/ppermute | solution.py:39
  26.7 1.7 %collective-permute-start.13 = (bf16[576,512]{1,0:T(8,128)(2,1)S(1)}, bf16[576,512]{1,0:T(8,128)(2,1)S(1)}, u32[]{:S(2)}, u32[]{:S(2)}) collective-permute-start(bf16[576,512]{1,0:T(8,128)(2,1)S(1)} %collective-permute-done.12.refs_1_), channel_id=1, source_target_pairs={{0,8},{4,12},{8,0},{12,4},{16,24},{20,28},{24,16},{28,20},{1,9},{5... | collective-permute-start | bytes 1769480 | tf_op jit(solution)/shard_map/ppermute | solution.py:39
  28.4 1.5 %collective-permute-start.14 = (bf16[576,512]{1,0:T(8,128)(2,1)S(1)}, bf16[576,512]{1,0:T(8,128)(2,1)S(1)}, u32[]{:S(2)}, u32[]{:S(2)}) collective-permute-start(bf16[576,512]{1,0:T(8,128)(2,1)S(1)} %collective-permute-done.12.refs_1_), channel_id=1, source_target_pairs={{0,16},{4,20},{8,24},{12,28},{16,0},{20,4},{24,8},{28,12},{1,17},{... | collective-permute-start | bytes 1769480 | tf_op jit(solution)/shard_map/ppermute | solution.py:39
  29.9 1.6 %collective-permute-start.4 = (bf16[64,1024]{1,0:T(8,128)(2,1)S(1)}, bf16[64,1024]{1,0:T(8,128)(2,1)S(1)}, u32[]{:S(2)}, u32[]{:S(2)}) collective-permute-start(bf16[64,1024]{1,0:T(8,128)(2,1)S(1)} %get-tuple-element.32), channel_id=1, source_target_pairs={{0,1},{1,0},{2,3},{3,2},{4,5},{5,4},{6,7},{7,6},{8,9},{9,8},{10,11... | collective-permute-start | bytes 393224 | tf_op jit(solution)/shard_map/ppermute | solution.py:39
  31.9 2.9 %collective-permute-done.4 = bf16[64,1024]{1,0:T(8,128)(2,1)S(1)} collective-permute-done((bf16[64,1024]{1,0:T(8,128)(2,1)S(1)}, bf16[64,1024]{1,0:T(8,128)(2,1)S(1)}, u32[]{:S(2)}, u32[]{:S(2)}) %collective-permute-start.4) | collective-permute-done | bytes 131104 | tf_op jit(solution)/shard_map/ppermute | solution.py:39
  34.9 3.5 %collective-permute-start.5 = (bf16[64,1024]{1,0:T(8,128)(2,1)S(1)}, bf16[64,1024]{1,0:T(8,128)(2,1)S(1)}, u32[]{:S(2)}, u32[]{:S(2)}) collective-permute-start(bf16[64,1024]{1,0:T(8,128)(2,1)S(1)} %add.44), channel_id=1, source_target_pairs={{0,2},{1,3},{2,0},{3,1},{4,6},{5,7},{6,4},{7,5},{8,10},{9,11},{10,... | collective-permute-start | bytes 393224 | tf_op jit(solution)/shard_map/ppermute | solution.py:39
  38.4 4.3 %project.1 = (bf16[64,1024]{1,0:T(8,128)(2,1)S(1)}, bf16[64,1024]{1,0:T(8,128)(2,1)S(1)}, bf16[64,1024]{1,0:T(8,128)(2,1)S(1)}, bf16[64,1024]{1,0:T(8,128)(2,1)S(1)}) custom-call(s32[1]{0:T(128)} %bitcast.rank_ref, bf16[128,2048]{1,0:T(8,128)(2,1)S(1)} %get-tuple-element.37.attended, bf16[32,4096]{1,0:T(8,128)(2,1)S(1)} %get-tuple-element.30.resid_ref, ...), custom_call_target="tpu_custom_call" | custom-call | flops 1073741824 | bytes 8388608 | tf_op jit(solution)/shard_map/project/pallas_call | solution.py:173
  42.7 0.8 collective-permute-start.8
  43.9 1.5 %collective-permute-start.10 = (bf16[64,1024]{1,0:T(8,128)(2,1)S(1)}, bf16[64,1024]{1,0:T(8,128)(2,1)S(1)}, u32[]{:S(2)}, u32[]{:S(2)}) collective-permute-start(bf16[64,1024]{1,0:T(8,128)(2,1)S(1)} %get-tuple-element.46), channel_id=1, source_target_pairs={{0,1},{1,0},{2,3},{3,2},{4,5},{5,4},{6,7},{7,6},{8,9},{9,8},{10,11... | collective-permute-start | bytes 393224 | tf_op jit(solution)/shard_map/ppermute | solution.py:39
  45.5 3.4 %collective-permute-done.8 = bf16[64,1024]{1,0:T(8,128)(2,1)S(1)} collective-permute-done((bf16[64,1024]{1,0:T(8,128)(2,1)S(1)}, bf16[64,1024]{1,0:T(8,128)(2,1)S(1)}, u32[]{:S(2)}, u32[]{:S(2)}) %collective-permute-start.8) | collective-permute-done | bytes 131104 | tf_op jit(solution)/shard_map/ppermute | solution.py:39
  49.3 2.8 %collective-permute-done.7 = bf16[64,1024]{1,0:T(8,128)(2,1)S(1)} collective-permute-done((bf16[64,1024]{1,0:T(8,128)(2,1)S(1)}, bf16[64,1024]{1,0:T(8,128)(2,1)S(1)}, u32[]{:S(2)}, u32[]{:S(2)}) %collective-permute-start.7) | collective-permute-done | bytes 131104 | tf_op jit(solution)/shard_map/ppermute | solution.py:39
  52.2 4.1 %collective-permute-done.9 = bf16[64,1024]{1,0:T(8,128)(2,1)S(1)} collective-permute-done((bf16[64,1024]{1,0:T(8,128)(2,1)S(1)}, bf16[64,1024]{1,0:T(8,128)(2,1)S(1)}, u32[]{:S(2)}, u32[]{:S(2)}) %collective-permute-start.9) | collective-permute-done | bytes 131104 | tf_op jit(solution)/shard_map/ppermute | solution.py:39
  57.9 8.1 %collective-permute-done.11 = bf16[64,1024]{1,0:T(8,128)(2,1)S(1)} collective-permute-done((bf16[64,1024]{1,0:T(8,128)(2,1)S(1)}, bf16[64,1024]{1,0:T(8,128)(2,1)S(1)}, u32[]{:S(2)}, u32[]{:S(2)}) %collective-permute-start.11) | collective-permute-done | bytes 131104 | tf_op jit(solution)/shard_map/ppermute | solution.py:39
  66.6 2.0 %collective-permute-done.18.refs_7_ = bf16[576,512]{1,0:T(8,128)(2,1)S(1)} collective-permute-done((bf16[576,512]{1,0:T(8,128)(2,1)S(1)}, bf16[576,512]{1,0:T(8,128)(2,1)S(1)}, u32[]{:S(2)}, u32[]{:S(2)}) %collective-permute-start.18) | collective-permute-done | bytes 589856 | tf_op jit(solution)/shard_map/ppermute | solution.py:39
  68.7 4.6 %experts.1 = (bf16[32,4096]{1,0:T(8,128)(2,1)}, f32[32,4096]{1,0:T(8,128)S(1)}, bf16[32,4096]{1,0:T(8,128)(2,1)S(1)}) custom-call(s32[2]{0:T(128)S(1)} %copy-done.5, f32[1,4096]{1,0:T(1,128)S(1)} %bitcast.11, bf16[384,4096]{1,0:T(8,128)(2,1)S(1)} %bitcast.8, bf16[192,4096]{1,0:T(8,128)(2,1)S(1)} %bitcast.10, bf16[64,1024]{1,0:T(8,128)(2,1)S(1)} %add.46.refs_0_, ...), custom_call_target="tpu_custom_call" | custom-call | flops 1024 | bytes 1024 | tf_op jit(solution)/shard_map/experts/pallas_call | solution.py:331
  73.3 13.8 %collective-permute-done.19 = bf16[32,4096]{1,0:T(8,128)(2,1)S(1)} collective-permute-done((bf16[32,4096]{1,0:T(8,128)(2,1)S(1)}, bf16[32,4096]{1,0:T(8,128)(2,1)S(1)}, u32[]{:S(2)}, u32[]{:S(2)}) %collective-permute-start.19) | collective-permute-done | bytes 262176 | tf_op jit(solution)/shard_map/ppermute | solution.py:39
  87.2 0.8 multiply_convert_fusion
  (61 shorter events, 4.6 us)
Async XLA Ops:
  4.1 10.1 %collective-permute-start = (bf16[144,256]{1,0:T(8,128)(2,1)S(1)}, bf16[144,256]{1,0:T(8,128)(2,1)S(1)}, u32[]{:S(2)}, u32[]{:S(2)}) collective-permute-start(bf16[144,256]{1,0:T(8,128)(2,1)S(1)} %fusion.2.refs_0_.refs_1_), channel_id=1, source_target_pairs={{0,8},{4,12},{8,0},{12,4},{16,24},{20,28},{24,16},{28,20},{1,9},{5... | collective-permute-start | bytes 221192 | tf_op jit(solution)/shard_map/ppermute | solution.py:39
  7.1 7.1 %collective-permute-start.1 = (bf16[144,256]{1,0:T(8,128)(2,1)S(1)}, bf16[144,256]{1,0:T(8,128)(2,1)S(1)}, u32[]{:S(2)}, u32[]{:S(2)}) collective-permute-start(bf16[144,256]{1,0:T(8,128)(2,1)S(1)} %fusion.2.refs_0_.refs_1_), channel_id=1, source_target_pairs={{0,16},{4,20},{8,24},{12,28},{16,0},{20,4},{24,8},{28,12},{1,17},{... | collective-permute-start | bytes 221192 | tf_op jit(solution)/shard_map/ppermute | solution.py:39
  8.6 5.6 %collective-permute-start.2 = (bf16[144,256]{1,0:T(8,128)(2,1)S(1)}, bf16[144,256]{1,0:T(8,128)(2,1)S(1)}, u32[]{:S(2)}, u32[]{:S(2)}) collective-permute-start(bf16[144,256]{1,0:T(8,128)(2,1)S(1)} %fusion.2.refs_0_.refs_1_), channel_id=1, source_target_pairs={{0,24},{4,28},{8,16},{12,20},{16,8},{20,12},{24,0},{28,4},{1,25},{... | collective-permute-start | bytes 221192 | tf_op jit(solution)/shard_map/ppermute | solution.py:39
  11.9 14.8 %collective-permute-start.12 = (bf16[576,512]{1,0:T(8,128)(2,1)}, bf16[576,512]{1,0:T(8,128)(2,1)S(1)}, u32[]{:S(2)}, u32[]{:S(2)}) collective-permute-start(bf16[576,512]{1,0:T(8,128)(2,1)} %make_shard.1), channel_id=1, source_target_pairs={{0,1},{1,0},{2,3},{3,2},{4,5},{5,4},{6,7},{7,6},{8,9},{9,8},{10,11... | collective-permute-start | bytes 1769480 | tf_op jit(solution)/shard_map/ppermute | solution.py:39
  14.2 1.6 %collective-permute-start.3 = (bf16[576,256]{1,0:T(8,128)(2,1)S(1)}, bf16[576,256]{1,0:T(8,128)(2,1)S(1)}, u32[]{:S(2)}, u32[]{:S(2)}) collective-permute-start(bf16[576,256]{1,0:T(8,128)(2,1)S(1)} %join_after.3.same_ref), channel_id=1, source_target_pairs={{0,4},{4,0},{8,12},{12,8},{16,20},{20,16},{24,28},{28,24},{1,5},{5... | collective-permute-start | bytes 884744 | tf_op jit(solution)/shard_map/ppermute | solution.py:39
  26.7 29.6 %collective-permute-start.13 = (bf16[576,512]{1,0:T(8,128)(2,1)S(1)}, bf16[576,512]{1,0:T(8,128)(2,1)S(1)}, u32[]{:S(2)}, u32[]{:S(2)}) collective-permute-start(bf16[576,512]{1,0:T(8,128)(2,1)S(1)} %collective-permute-done.12.refs_1_), channel_id=1, source_target_pairs={{0,8},{4,12},{8,0},{12,4},{16,24},{20,28},{24,16},{28,20},{1,9},{5... | collective-permute-start | bytes 1769480 | tf_op jit(solution)/shard_map/ppermute | solution.py:39
  28.4 27.9 %collective-permute-start.14 = (bf16[576,512]{1,0:T(8,128)(2,1)S(1)}, bf16[576,512]{1,0:T(8,128)(2,1)S(1)}, u32[]{:S(2)}, u32[]{:S(2)}) collective-permute-start(bf16[576,512]{1,0:T(8,128)(2,1)S(1)} %collective-permute-done.12.refs_1_), channel_id=1, source_target_pairs={{0,16},{4,20},{8,24},{12,28},{16,0},{20,4},{24,8},{28,12},{1,17},{... | collective-permute-start | bytes 1769480 | tf_op jit(solution)/shard_map/ppermute | solution.py:39
  29.9 5.0 %collective-permute-start.4 = (bf16[64,1024]{1,0:T(8,128)(2,1)S(1)}, bf16[64,1024]{1,0:T(8,128)(2,1)S(1)}, u32[]{:S(2)}, u32[]{:S(2)}) collective-permute-start(bf16[64,1024]{1,0:T(8,128)(2,1)S(1)} %get-tuple-element.32), channel_id=1, source_target_pairs={{0,1},{1,0},{2,3},{3,2},{4,5},{5,4},{6,7},{7,6},{8,9},{9,8},{10,11... | collective-permute-start | bytes 393224 | tf_op jit(solution)/shard_map/ppermute | solution.py:39
  31.5 12.0 %collective-permute-start.6 = (bf16[64,1024]{1,0:T(8,128)(2,1)S(1)}, bf16[64,1024]{1,0:T(8,128)(2,1)S(1)}, u32[]{:S(2)}, u32[]{:S(2)}) collective-permute-start(bf16[64,1024]{1,0:T(8,128)(2,1)S(1)} %get-tuple-element.34), channel_id=1, source_target_pairs={{0,1},{1,0},{2,3},{3,2},{4,5},{5,4},{6,7},{7,6},{8,9},{9,8},{10,11... | collective-permute-start | bytes 393224 | tf_op jit(solution)/shard_map/ppermute | solution.py:39
  34.9 9.0 %collective-permute-start.5 = (bf16[64,1024]{1,0:T(8,128)(2,1)S(1)}, bf16[64,1024]{1,0:T(8,128)(2,1)S(1)}, u32[]{:S(2)}, u32[]{:S(2)}) collective-permute-start(bf16[64,1024]{1,0:T(8,128)(2,1)S(1)} %add.44), channel_id=1, source_target_pairs={{0,2},{1,3},{2,0},{3,1},{4,6},{5,7},{6,4},{7,5},{8,10},{9,11},{10,... | collective-permute-start | bytes 393224 | tf_op jit(solution)/shard_map/ppermute | solution.py:39
  42.7 6.3 %collective-permute-start.8 = (bf16[64,1024]{1,0:T(8,128)(2,1)S(1)}, bf16[64,1024]{1,0:T(8,128)(2,1)S(1)}, u32[]{:S(2)}, u32[]{:S(2)}) collective-permute-start(bf16[64,1024]{1,0:T(8,128)(2,1)S(1)} %get-tuple-element.40), channel_id=1, source_target_pairs={{0,1},{1,0},{2,3},{3,2},{4,5},{5,4},{6,7},{7,6},{8,9},{9,8},{10,11... | collective-permute-start | bytes 393224 | tf_op jit(solution)/shard_map/ppermute | solution.py:39
  43.5 8.6 %collective-permute-start.7 = (bf16[64,1024]{1,0:T(8,128)(2,1)S(1)}, bf16[64,1024]{1,0:T(8,128)(2,1)S(1)}, u32[]{:S(2)}, u32[]{:S(2)}) collective-permute-start(bf16[64,1024]{1,0:T(8,128)(2,1)S(1)} %add.45), channel_id=1, source_target_pairs={{0,2},{1,3},{2,0},{3,1},{4,6},{5,7},{6,4},{7,5},{8,10},{9,11},{10,... | collective-permute-start | bytes 393224 | tf_op jit(solution)/shard_map/ppermute | solution.py:39
  43.9 8.2 %collective-permute-start.10 = (bf16[64,1024]{1,0:T(8,128)(2,1)S(1)}, bf16[64,1024]{1,0:T(8,128)(2,1)S(1)}, u32[]{:S(2)}, u32[]{:S(2)}) collective-permute-start(bf16[64,1024]{1,0:T(8,128)(2,1)S(1)} %get-tuple-element.46), channel_id=1, source_target_pairs={{0,1},{1,0},{2,3},{3,2},{4,5},{5,4},{6,7},{7,6},{8,9},{9,8},{10,11... | collective-permute-start | bytes 393224 | tf_op jit(solution)/shard_map/ppermute | solution.py:39
  48.9 7.3 %collective-permute-start.9 = (bf16[64,1024]{1,0:T(8,128)(2,1)S(1)}, bf16[64,1024]{1,0:T(8,128)(2,1)S(1)}, u32[]{:S(2)}, u32[]{:S(2)}) collective-permute-start(bf16[64,1024]{1,0:T(8,128)(2,1)S(1)} %add.47), channel_id=1, source_target_pairs={{0,2},{1,3},{2,0},{3,1},{4,6},{5,7},{6,4},{7,5},{8,10},{9,11},{10,... | collective-permute-start | bytes 393224 | tf_op jit(solution)/shard_map/ppermute | solution.py:39
  56.3 12.3 %copy-start = (bf16[1,384,4096]{2,1,0:T(8,128)(2,1)S(1)}, bf16[1,384,4096]{2,1,0:T(8,128)(2,1)}, u32[]{:S(2)}) copy-start(bf16[1,384,4096]{2,1,0:T(8,128)(2,1)} %param.22) | copy-start | bytes 9437188
  56.5 12.2 %copy-start.1 = (bf16[1,192,4096]{2,1,0:T(8,128)(2,1)S(1)}, bf16[1,192,4096]{2,1,0:T(8,128)(2,1)}, u32[]{:S(2)}) copy-start(bf16[1,192,4096]{2,1,0:T(8,128)(2,1)} %param.23) | copy-start | bytes 4718596
  56.5 12.2 %copy-start.4 = (f32[4096]{0:T(1024)S(1)}, f32[4096]{0:T(1024)}, u32[]{:S(2)}) copy-start(f32[4096]{0:T(1024)} %param.19) | copy-start | bytes 49156
  56.5 12.2 %copy-start.5 = (s32[2]{0:T(128)S(1)}, s32[2]{0:T(128)}, u32[]{:S(2)}) copy-start(s32[2]{0:T(128)} %pad_add_fusion.place_ref) | copy-start | bytes 28
  56.5 12.1 %collective-permute-start.17 = (bf16[1728,512]{1,0:T(8,128)(2,1)S(1)}, bf16[1728,512]{1,0:T(8,128)(2,1)S(1)}, u32[]{:S(2)}, u32[]{:S(2)}) collective-permute-start(bf16[1728,512]{1,0:T(8,128)(2,1)S(1)} %join_after.4.refs_4_), channel_id=1, source_target_pairs={{0,4},{4,0},{8,12},{12,8},{16,20},{20,16},{24,28},{28,24},{1,5},{5... | collective-permute-start | bytes 5308424 | tf_op jit(solution)/shard_map/ppermute | solution.py:39
  56.6 9.5 %collective-permute-start.15 = (bf16[288,512]{1,0:T(8,128)(2,1)S(1)}, bf16[288,512]{1,0:T(8,128)(2,1)S(1)}, u32[]{:S(2)}, u32[]{:S(2)}) collective-permute-start(bf16[288,512]{1,0:T(8,128)(2,1)S(1)} %get-tuple-element.57), channel_id=1, source_target_pairs={{0,16},{4,20},{8,24},{12,28},{16,0},{20,4},{24,8},{28,12},{1,17},{... | collective-permute-start | bytes 884744 | tf_op jit(solution)/shard_map/ppermute | solution.py:39
  57.4 9.1 %collective-permute-start.16 = (bf16[288,512]{1,0:T(8,128)(2,1)S(1)}, bf16[288,512]{1,0:T(8,128)(2,1)S(1)}, u32[]{:S(2)}, u32[]{:S(2)}) collective-permute-start(bf16[288,512]{1,0:T(8,128)(2,1)S(1)} %get-tuple-element.56), channel_id=1, source_target_pairs={{0,8},{4,12},{8,0},{12,4},{16,24},{20,28},{24,16},{28,20},{1,9},{5... | collective-permute-start | bytes 884744 | tf_op jit(solution)/shard_map/ppermute | solution.py:39
  57.9 8.1 %collective-permute-start.11 = (bf16[64,1024]{1,0:T(8,128)(2,1)S(1)}, bf16[64,1024]{1,0:T(8,128)(2,1)S(1)}, u32[]{:S(2)}, u32[]{:S(2)}) collective-permute-start(bf16[64,1024]{1,0:T(8,128)(2,1)S(1)} %add.49), channel_id=1, source_target_pairs={{0,2},{1,3},{2,0},{3,1},{4,6},{5,7},{6,4},{7,5},{8,10},{9,11},{10,... | collective-permute-start | bytes 393224 | tf_op jit(solution)/shard_map/ppermute | solution.py:39
  66.6 2.1 %collective-permute-start.18 = (bf16[576,512]{1,0:T(8,128)(2,1)S(1)}, bf16[576,512]{1,0:T(8,128)(2,1)S(1)}, u32[]{:S(2)}, u32[]{:S(2)}) collective-permute-start(bf16[576,512]{1,0:T(8,128)(2,1)S(1)} %join_after.5.refs_5_), channel_id=1, source_target_pairs={{0,4},{4,0},{8,12},{12,8},{16,20},{20,16},{24,28},{28,24},{1,5},{5... | collective-permute-start | bytes 1769480 | tf_op jit(solution)/shard_map/ppermute | solution.py:39
  73.3 13.9 %collective-permute-start.19 = (bf16[32,4096]{1,0:T(8,128)(2,1)S(1)}, bf16[32,4096]{1,0:T(8,128)(2,1)S(1)}, u32[]{:S(2)}, u32[]{:S(2)}) collective-permute-start(bf16[32,4096]{1,0:T(8,128)(2,1)S(1)} %get-tuple-element.55), channel_id=1, source_target_pairs={{0,2},{1,3},{2,0},{3,1},{4,6},{5,7},{6,4},{7,5},{8,10},{9,11},{10,... | collective-permute-start | bytes 786440 | tf_op jit(solution)/shard_map/ppermute | solution.py:39
  (5 other events, 23.9 us)

commit v10 on v7

--- a/solution.py
+++ b/solution.py
@@ -345,7 +345,7 @@
     limits = jnp.concatenate([bounds // BASE, bounds % BASE]).astype(jnp.bfloat16)
     limits = jnp.broadcast_to(limits.reshape(1, width), (PAD_ROWS, width))
     same_keys = join_after(
-        [payload] + [exchange(payload, "ctx", r, ctx_count) for r in range(2, ctx_count, 2)],
+        [payload] + [exchange(payload, "ctx", r, ctx_count) for r in range(ctx_count - 2, 0, -2)],
         payload,
     )
     other_keys = exchange(same_keys, "ctx", 1, ctx_count)
@@ -378,7 +378,7 @@
     homes, states, theirs, done = [], [], [], [coefficient]
     for chunk in range(count):
         value = mine[chunk]
-        if chunk >= IN_FLIGHT:
+        if chunk == IN_FLIGHT:
             own, *states = absorb(
                 chunk - IN_FLIGHT,
                 ranks,
@@ -391,14 +391,14 @@
             )
             homes.append(own)
             done = [states[0]]
-        if chunk >= IN_FLIGHT or chunk == 1:
+        if chunk == IN_FLIGHT or chunk == 1:
             value, *done = lax.optimization_barrier((value, *done))
             if chunk == 1:
                 coefficient = done[0]
             else:
                 states[0] = done[0]
         theirs.append(exchange(value, "exp", 1, exp_count))
-    for chunk in range(count - IN_FLIGHT, count):
+    for chunk in range(1, count):
         own, *states = absorb(
             chunk, ranks, mine[chunk], theirs[chunk], gain, flat_in, states, flat_back
         )

time: 85.4 us -> 86.2 us (level)
  other arithmetic: 3.29 us -> 9.59 us
  waiting for transfers between devices: 40.9 us -> 36.3 us
  starting transfers between devices: 21.3 us -> 20.2 us
    ppermute x19, waiting for transfers between devices: 40.9 us -> 36.3 us  [exchange(): return lax.ppermute(value, axis, [(i, i ^ offset) for i in range(size)])]
    add x4, other arithmetic: 0.15 us -> 3.24 us  [line_device(): near = [kept + other for kept, other in zip(parts[::2], arrived)]]
    add x4, other arithmetic: 0.15 us -> 2.07 us  [line_device(): mine = [own + other for own, other in zip(near, across)]]
    ppermute x19, starting transfers between devices: 21.3 us -> 20.2 us  [exchange(): return lax.ppermute(value, axis, [(i, i ^ offset) for i in range(size)])]
    unnamed x14 -> x10, local copies, waits for them, and re-layouts: 2.01 us -> 2 us
  transfers between devices with their start and end apart: 19 -> 19, of which waited for: 13 -> 12; matrix products, arithmetic and copies ran while one was open for 3% -> 10% of each run, Pallas kernels for 7% -> 7%
where the time goes in v10:
time: 86.2 us; the launch traced here: 85.4 us
  waiting for transfers between devices  36.3 us (42%)
  starting transfers between devices  20.2 us (23%)
  Pallas kernels  13.1 us (15%)
  other arithmetic  9.59 us (11%)
  between operations  3.4 us (4%)
  local copies, waits for them, and re-layouts  2.79 us (3%)
    ppermute x19, waiting for transfers between devices, exchange(): return lax.ppermute(value, axis, [(i, i ^ offset) for i in range(size)])  36.3 us
    ppermute x19, starting transfers between devices, exchange(): return lax.ppermute(value, axis, [(i, i ^ offset) for i in range(size)])  20.2 us
    pallas_call x1, Pallas kernels, attend_project(): pl.pallas_call(attend_kernel, out_shape=part_shapes(tok, spans) + [jax.Sh...  6.3 us
    pallas_call x1, Pallas kernels, project(): pl.pallas_call(project_kernel, out_shape=part_shapes(tok, spans), in_spec...  4.61 us
    add x4, other arithmetic, line_device(): near = [kept + other for kept, other in zip(parts[::2], arrived)]  3.24 us
    pallas_call x4, Pallas kernels, absorb(): pl.pallas_call(functools.partial(absorb_kernel, chunk), out_shape=out_sha...  2.12 us
    add x4, other arithmetic, line_device(): mine = [own + other for own, other in zip(near, across)]  2.07 us
    unnamed x10, local copies, waits for them, and re-layouts  2 us
  transfers between devices with their start and end apart: 19, of which 12 were waited for; matrix products, arithmetic and copies ran while one was open for 10% of the time, Pallas kernels for 7%

profile of v10, /device:TPU:0, one launch (start us, length us, event | category | flops | bytes accessed | tf_op | source)
XLA Modules:
  0.0 85.4 jit_solution(8836177250335728654)
XLA Ops:
  4.1 4.0 %collective-permute-start = (bf16[144,256]{1,0:T(8,128)(2,1)S(1)}, bf16[144,256]{1,0:T(8,128)(2,1)S(1)}, u32[]{:S(2)}, u32[]{:S(2)}) collective-permute-start(bf16[144,256]{1,0:T(8,128)(2,1)S(1)} %fusion.2.refs_0_.refs_1_), channel_id=1, source_target_pairs={{0,24},{4,28},{8,16},{12,20},{16,8},{20,12},{24,0},{28,4},{1,25},{... | collective-permute-start | bytes 221192 | tf_op jit(solution)/shard_map/ppermute | solution.py:29
  8.7 1.0 %copy-done.2 = bf16[128,2048]{1,0:T(8,128)(2,1)S(1)} copy-done((bf16[128,2048]{1,0:T(8,128)(2,1)S(1)}, bf16[128,2048]{1,0:T(8,128)(2,1)}, u32[]{:S(2)}) %copy-start.2) | copy-done | bytes 524312
  10.7 1.6 %collective-permute-done.1.refs_3_ = bf16[144,256]{1,0:T(8,128)(2,1)S(1)} collective-permute-done((bf16[144,256]{1,0:T(8,128)(2,1)S(1)}, bf16[144,256]{1,0:T(8,128)(2,1)S(1)}, u32[]{:S(2)}, u32[]{:S(2)}) %collective-permute-start.1) | collective-permute-done | bytes 73760 | tf_op jit(solution)/shard_map/ppermute | solution.py:29
  14.5 6.3 %attend_project.1 = (bf16[64,1024]{1,0:T(8,128)(2,1)S(1)}, bf16[64,1024]{1,0:T(8,128)(2,1)S(1)}, bf16[64,1024]{1,0:T(8,128)(2,1)S(1)}, bf16[64,1024]{1,0:T(8,128)(2,1)S(1)}, bf16[128,2048]{1,0:T(8,128)(2,1)S(1)}) custom-call(s32[1]{0:T(128)} %bitcast.rank_ref, bf16[16,256]{1,0:T(8,128)(2,1)S(1)} %broadcast_in_dim.5.limit_ref, ...), custom_call_target="tpu_custom_call" | custom-call | flops 2147483648 | bytes 8388608 | tf_op jit(solution)/shard_map/attend_project/pallas_call | solution.py:128
  20.9 1.6 %collective-permute-start.4 = (bf16[64,1024]{1,0:T(8,128)(2,1)S(1)}, bf16[64,1024]{1,0:T(8,128)(2,1)S(1)}, u32[]{:S(2)}, u32[]{:S(2)}) collective-permute-start(bf16[64,1024]{1,0:T(8,128)(2,1)S(1)} %get-tuple-element.38), channel_id=1, source_target_pairs={{0,1},{1,0},{2,3},{3,2},{4,5},{5,4},{6,7},{7,6},{8,9},{9,8},{10,11... | collective-permute-start | bytes 393224 | tf_op jit(solution)/shard_map/ppermute | solution.py:29
  23.0 4.6 %project.1 = (bf16[64,1024]{1,0:T(8,128)(2,1)S(1)}, bf16[64,1024]{1,0:T(8,128)(2,1)}, bf16[64,1024]{1,0:T(8,128)(2,1)S(1)}, bf16[64,1024]{1,0:T(8,128)(2,1)S(1)}) custom-call(s32[1]{0:T(128)} %bitcast.rank_ref, bf16[128,2048]{1,0:T(8,128)(2,1)S(1)} %get-tuple-element.43.attended, bf16[32,4096]{1,0:T(8,128)(2,1)S(1)} %get-tuple-element.36.resid_ref, ...), custom_call_target="tpu_custom_call" | custom-call | flops 1073741824 | bytes 8388608 | tf_op jit(solution)/shard_map/project/pallas_call | solution.py:163
  28.3 2.6 %collective-permute-start.5 = (bf16[64,1024]{1,0:T(8,128)(2,1)}, bf16[64,1024]{1,0:T(8,128)(2,1)}, u32[]{:S(2)}, u32[]{:S(2)}) collective-permute-start(bf16[64,1024]{1,0:T(8,128)(2,1)} %add.50), channel_id=1, source_target_pairs={{0,2},{1,3},{2,0},{3,1},{4,6},{5,7},{6,4},{7,5},{8,10},{9,11},{10,... | collective-permute-start | bytes 393224 | tf_op jit(solution)/shard_map/ppermute | solution.py:29
  30.9 1.6 %collective-permute-start.10 = (bf16[64,1024]{1,0:T(8,128)(2,1)}, bf16[64,1024]{1,0:T(8,128)(2,1)}, u32[]{:S(2)}, u32[]{:S(2)}) collective-permute-start(bf16[64,1024]{1,0:T(8,128)(2,1)} %get-tuple-element.46), channel_id=1, source_target_pairs={{0,1},{1,0},{2,3},{3,2},{4,5},{5,4},{6,7},{7,6},{8,9},{9,8},{10,11... | collective-permute-start | bytes 393224 | tf_op jit(solution)/shard_map/ppermute | solution.py:29
  34.1 1.3 %reduce_sum.18 = f32[32]{0:T(128)} reduce(f32[32,8]{0,1:T(8,128)} %param.21, f32[]{:T(128)} %constant.63.clone.1), dimensions={1}, to_apply=%region_0.1 | reduce | flops 224 | bytes 1156 | tf_op jit(solution)/shard_map/reduce_sum | solution.py:358
  36.1 1.9 %collective-permute-done.5 = bf16[64,1024]{1,0:T(8,128)(2,1)} collective-permute-done((bf16[64,1024]{1,0:T(8,128)(2,1)}, bf16[64,1024]{1,0:T(8,128)(2,1)}, u32[]{:S(2)}, u32[]{:S(2)}) %collective-permute-start.5) | collective-permute-done | bytes 131104 | tf_op jit(solution)/shard_map/ppermute | solution.py:29
  38.1 1.0 %add.51.mine_ref = bf16[64,1024]{1,0:T(8,128)(2,1)S(1)} add(bf16[64,1024]{1,0:T(8,128)(2,1)} %add.50, bf16[64,1024]{1,0:T(8,128)(2,1)} %collective-permute-done.5) | non-fusion elementwise | flops 65536 | bytes 393216 | tf_op jit(solution)/shard_map/add | solution.py:377
  39.1 2.7 %collective-permute-done.10 = bf16[64,1024]{1,0:T(8,128)(2,1)} collective-permute-done((bf16[64,1024]{1,0:T(8,128)(2,1)}, bf16[64,1024]{1,0:T(8,128)(2,1)}, u32[]{:S(2)}, u32[]{:S(2)}) %collective-permute-start.10) | collective-permute-done | bytes 131104 | tf_op jit(solution)/shard_map/ppermute | solution.py:29
  43.6 1.4 %collective-permute-done.13 = bf16[64,1024]{1,0:T(8,128)(2,1)} collective-permute-done((bf16[64,1024]{1,0:T(8,128)(2,1)S(1)}, bf16[64,1024]{1,0:T(8,128)(2,1)}, u32[]{:S(2)}, u32[]{:S(2)}) %collective-permute-start.13) | collective-permute-done | bytes 131104 | tf_op jit(solution)/shard_map/ppermute | solution.py:29
  45.9 1.1 %collective-permute-start.14 = (bf16[64,1024]{1,0:T(8,128)(2,1)S(1)}, bf16[64,1024]{1,0:T(8,128)(2,1)S(1)}, u32[]{:S(2)}, u32[]{:S(2)}) collective-permute-start(bf16[64,1024]{1,0:T(8,128)(2,1)S(1)} %add.56), channel_id=1, source_target_pairs={{0,2},{1,3},{2,0},{3,1},{4,6},{5,7},{6,4},{7,5},{8,10},{9,11},{10,... | collective-permute-start | bytes 393224 | tf_op jit(solution)/shard_map/ppermute | solution.py:29
  48.0 1.0 %collective-permute-start.9 = (bf16[64,1024]{1,0:T(8,128)(2,1)S(1)}, bf16[64,1024]{1,0:T(8,128)(2,1)S(1)}, u32[]{:S(2)}, u32[]{:S(2)}) collective-permute-start(bf16[64,1024]{1,0:T(8,128)(2,1)S(1)} %add.53.mine_ref), channel_id=1, source_target_pairs={{0,1},{1,0},{2,3},{3,2},{4,5},{5,4},{6,7},{7,6},{8,9},{9,8},{10,11... | collective-permute-start | bytes 393224 | tf_op jit(solution)/shard_map/ppermute | solution.py:29
  49.5 5.5 %collective-permute-done.11 = bf16[64,1024]{1,0:T(8,128)(2,1)S(1)} collective-permute-done((bf16[64,1024]{1,0:T(8,128)(2,1)S(1)}, bf16[64,1024]{1,0:T(8,128)(2,1)S(1)}, u32[]{:S(2)}, u32[]{:S(2)}) %collective-permute-start.11) | collective-permute-done | bytes 131104 | tf_op jit(solution)/shard_map/ppermute | solution.py:29
  55.1 1.3 %collective-permute-done.14 = bf16[64,1024]{1,0:T(8,128)(2,1)S(1)} collective-permute-done((bf16[64,1024]{1,0:T(8,128)(2,1)S(1)}, bf16[64,1024]{1,0:T(8,128)(2,1)S(1)}, u32[]{:S(2)}, u32[]{:S(2)}) %collective-permute-start.14) | collective-permute-done | bytes 131104 | tf_op jit(solution)/shard_map/ppermute | solution.py:29
  57.6 3.0 %collective-permute-done.12.theirs_ref = bf16[64,1024]{1,0:T(8,128)(2,1)S(1)} collective-permute-done((bf16[64,1024]{1,0:T(8,128)(2,1)S(1)}, bf16[64,1024]{1,0:T(8,128)(2,1)S(1)}, u32[]{:S(2)}, u32[]{:S(2)}) %collective-permute-start.12) | collective-permute-done | bytes 131104 | tf_op jit(solution)/shard_map/ppermute | solution.py:29
  61.0 1.0 %collective-permute-done.15.theirs_ref = bf16[64,1024]{1,0:T(8,128)(2,1)S(1)} collective-permute-done((bf16[64,1024]{1,0:T(8,128)(2,1)S(1)}, bf16[64,1024]{1,0:T(8,128)(2,1)S(1)}, u32[]{:S(2)}, u32[]{:S(2)}) %collective-permute-start.15) | collective-permute-done | bytes 131104 | tf_op jit(solution)/shard_map/ppermute | solution.py:29
  62.0 1.0 %absorb.7 = (bf16[32,1024]{1,0:T(8,128)(2,1)S(1)}, bf16[32,4096]{1,0:T(8,128)(2,1)S(1)}, bf16[32,4096]{1,0:T(8,128)(2,1)S(1)}, bf16[32,4096]{1,0:T(8,128)(2,1)S(1)}, bf16[32,4096]{1,0:T(8,128)(2,1)S(1)}) custom-call(s32[1]{0:T(128)} %bitcast.rank_ref, bf16[64,1024]{1,0:T(8,128)(2,1)S(1)} %add.57.mine_ref, ...), custom_call_target="tpu_custom_call" | custom-call | flops 1024 | bytes 1024 | tf_op jit(solution)/shard_map/absorb/pallas_call | solution.py:294
  63.4 2.3 %collective-permute-start.17 = (bf16[32,4096]{1,0:T(8,128)(2,1)S(1)}, bf16[32,4096]{1,0:T(8,128)(2,1)S(1)}, u32[]{:S(2)}, u32[]{:S(2)}) collective-permute-start(bf16[32,4096]{1,0:T(8,128)(2,1)S(1)} %get-tuple-element.65), channel_id=1, source_target_pairs={{0,2},{1,3},{2,0},{3,1},{4,6},{5,7},{6,4},{7,5},{8,10},{9,11},{10,... | collective-permute-start | bytes 786440 | tf_op jit(solution)/shard_map/ppermute | solution.py:29
  65.7 1.8 %collective-permute-start.18 = (bf16[32,4096]{1,0:T(8,128)(2,1)S(1)}, bf16[32,4096]{1,0:T(8,128)(2,1)S(1)}, u32[]{:S(2)}, u32[]{:S(2)}) collective-permute-start(bf16[32,4096]{1,0:T(8,128)(2,1)S(1)} %get-tuple-element.66), channel_id=1, source_target_pairs={{0,3},{1,2},{2,1},{3,0},{4,7},{5,6},{6,5},{7,4},{8,11},{9,10},{10,... | collective-permute-start | bytes 786440 | tf_op jit(solution)/shard_map/ppermute | solution.py:29
  68.2 5.1 %collective-permute-done.16 = bf16[32,4096]{1,0:T(8,128)(2,1)S(1)} collective-permute-done((bf16[32,4096]{1,0:T(8,128)(2,1)S(1)}, bf16[32,4096]{1,0:T(8,128)(2,1)S(1)}, u32[]{:S(2)}, u32[]{:S(2)}) %collective-permute-start.16) | collective-permute-done | bytes 262176 | tf_op jit(solution)/shard_map/ppermute | solution.py:29
  73.3 11.2 %collective-permute-done.17 = bf16[32,4096]{1,0:T(8,128)(2,1)S(1)} collective-permute-done((bf16[32,4096]{1,0:T(8,128)(2,1)S(1)}, bf16[32,4096]{1,0:T(8,128)(2,1)S(1)}, u32[]{:S(2)}, u32[]{:S(2)}) %collective-permute-start.17) | collective-permute-done | bytes 262176 | tf_op jit(solution)/shard_map/ppermute | solution.py:29
  (50 shorter events, 15.9 us)
Async XLA Ops:
  4.1 6.7 %collective-permute-start = (bf16[144,256]{1,0:T(8,128)(2,1)S(1)}, bf16[144,256]{1,0:T(8,128)(2,1)S(1)}, u32[]{:S(2)}, u32[]{:S(2)}) collective-permute-start(bf16[144,256]{1,0:T(8,128)(2,1)S(1)} %fusion.2.refs_0_.refs_1_), channel_id=1, source_target_pairs={{0,24},{4,28},{8,16},{12,20},{16,8},{20,12},{24,0},{28,4},{1,25},{... | collective-permute-start | bytes 221192 | tf_op jit(solution)/shard_map/ppermute | solution.py:29
  8.0 4.4 %collective-permute-start.1 = (bf16[144,256]{1,0:T(8,128)(2,1)S(1)}, bf16[144,256]{1,0:T(8,128)(2,1)S(1)}, u32[]{:S(2)}, u32[]{:S(2)}) collective-permute-start(bf16[144,256]{1,0:T(8,128)(2,1)S(1)} %fusion.2.refs_0_.refs_1_), channel_id=1, source_target_pairs={{0,16},{4,20},{8,24},{12,28},{16,0},{20,4},{24,8},{28,12},{1,17},{... | collective-permute-start | bytes 221192 | tf_op jit(solution)/shard_map/ppermute | solution.py:29
  8.5 4.4 %collective-permute-start.2 = (bf16[144,256]{1,0:T(8,128)(2,1)S(1)}, bf16[144,256]{1,0:T(8,128)(2,1)S(1)}, u32[]{:S(2)}, u32[]{:S(2)}) collective-permute-start(bf16[144,256]{1,0:T(8,128)(2,1)S(1)} %fusion.2.refs_0_.refs_1_), channel_id=1, source_target_pairs={{0,8},{4,12},{8,0},{12,4},{16,24},{20,28},{24,16},{28,20},{1,9},{5... | collective-permute-start | bytes 221192 | tf_op jit(solution)/shard_map/ppermute | solution.py:29
  8.7 1.0 %copy-start.2 = (bf16[128,2048]{1,0:T(8,128)(2,1)S(1)}, bf16[128,2048]{1,0:T(8,128)(2,1)}, u32[]{:S(2)}) copy-start(bf16[128,2048]{1,0:T(8,128)(2,1)} %q_hbm.1) | copy-start | bytes 1572868
  9.7 0.9 %copy-start.4 = (bf16[32,4096]{1,0:T(8,128)(2,1)S(1)}, bf16[32,4096]{1,0:T(8,128)(2,1)}, u32[]{:S(2)}) copy-start(bf16[32,4096]{1,0:T(8,128)(2,1)} %resid_hbm.1) | copy-start | bytes 786436
  12.9 1.6 %collective-permute-start.3 = (bf16[576,256]{1,0:T(8,128)(2,1)S(1)}, bf16[576,256]{1,0:T(8,128)(2,1)S(1)}, u32[]{:S(2)}, u32[]{:S(2)}) collective-permute-start(bf16[576,256]{1,0:T(8,128)(2,1)S(1)} %join_after.1.same_ref), channel_id=1, source_target_pairs={{0,4},{4,0},{8,12},{12,8},{16,20},{20,16},{24,28},{28,24},{1,5},{5... | collective-permute-start | bytes 884744 | tf_op jit(solution)/shard_map/ppermute | solution.py:29
  20.9 6.7 %collective-permute-start.4 = (bf16[64,1024]{1,0:T(8,128)(2,1)S(1)}, bf16[64,1024]{1,0:T(8,128)(2,1)S(1)}, u32[]{:S(2)}, u32[]{:S(2)}) collective-permute-start(bf16[64,1024]{1,0:T(8,128)(2,1)S(1)} %get-tuple-element.38), channel_id=1, source_target_pairs={{0,1},{1,0},{2,3},{3,2},{4,5},{5,4},{6,7},{7,6},{8,9},{9,8},{10,11... | collective-permute-start | bytes 393224 | tf_op jit(solution)/shard_map/ppermute | solution.py:29
  22.5 10.0 %collective-permute-start.7 = (bf16[64,1024]{1,0:T(8,128)(2,1)S(1)}, bf16[64,1024]{1,0:T(8,128)(2,1)S(1)}, u32[]{:S(2)}, u32[]{:S(2)}) collective-permute-start(bf16[64,1024]{1,0:T(8,128)(2,1)S(1)} %get-tuple-element.41), channel_id=1, source_target_pairs={{0,1},{1,0},{2,3},{3,2},{4,5},{5,4},{6,7},{7,6},{8,9},{9,8},{10,11... | collective-permute-start | bytes 393224 | tf_op jit(solution)/shard_map/ppermute | solution.py:29
  22.9 26.1 %copy-start = (bf16[1,384,4096]{2,1,0:T(8,128)(2,1)S(1)}, bf16[1,384,4096]{2,1,0:T(8,128)(2,1)}, u32[]{:S(2)}) copy-start(bf16[1,384,4096]{2,1,0:T(8,128)(2,1)} %param.22) | copy-start | bytes 9437188
  22.9 26.1 %copy-start.3 = (f32[4096]{0:T(1024)S(1)}, f32[4096]{0:T(1024)}, u32[]{:S(2)}) copy-start(f32[4096]{0:T(1024)} %param.19) | copy-start | bytes 49156
  28.3 9.8 %collective-permute-start.5 = (bf16[64,1024]{1,0:T(8,128)(2,1)}, bf16[64,1024]{1,0:T(8,128)(2,1)}, u32[]{:S(2)}, u32[]{:S(2)}) collective-permute-start(bf16[64,1024]{1,0:T(8,128)(2,1)} %add.50), channel_id=1, source_target_pairs={{0,2},{1,3},{2,0},{3,1},{4,6},{5,7},{6,4},{7,5},{8,10},{9,11},{10,... | collective-permute-start | bytes 393224 | tf_op jit(solution)/shard_map/ppermute | solution.py:29
  30.9 11.0 %collective-permute-start.10 = (bf16[64,1024]{1,0:T(8,128)(2,1)}, bf16[64,1024]{1,0:T(8,128)(2,1)}, u32[]{:S(2)}, u32[]{:S(2)}) collective-permute-start(bf16[64,1024]{1,0:T(8,128)(2,1)} %get-tuple-element.46), channel_id=1, source_target_pairs={{0,1},{1,0},{2,3},{3,2},{4,5},{5,4},{6,7},{7,6},{8,9},{9,8},{10,11... | collective-permute-start | bytes 393224 | tf_op jit(solution)/shard_map/ppermute | solution.py:29
  32.5 12.5 %collective-permute-start.13 = (bf16[64,1024]{1,0:T(8,128)(2,1)S(1)}, bf16[64,1024]{1,0:T(8,128)(2,1)}, u32[]{:S(2)}, u32[]{:S(2)}) collective-permute-start(bf16[64,1024]{1,0:T(8,128)(2,1)S(1)} %get-tuple-element.58), channel_id=1, source_target_pairs={{0,1},{1,0},{2,3},{3,2},{4,5},{5,4},{6,7},{7,6},{8,9},{9,8},{10,11... | collective-permute-start | bytes 393224 | tf_op jit(solution)/shard_map/ppermute | solution.py:29
  33.6 12.4 %collective-permute-start.8 = (bf16[64,1024]{1,0:T(8,128)(2,1)}, bf16[64,1024]{1,0:T(8,128)(2,1)}, u32[]{:S(2)}, u32[]{:S(2)}) collective-permute-start(bf16[64,1024]{1,0:T(8,128)(2,1)} %add.52), channel_id=1, source_target_pairs={{0,2},{1,3},{2,0},{3,1},{4,6},{5,7},{6,4},{7,5},{8,10},{9,11},{10,... | collective-permute-start | bytes 393224 | tf_op jit(solution)/shard_map/ppermute | solution.py:29
  39.1 10.0 %collective-permute-start.6 = (bf16[64,1024]{1,0:T(8,128)(2,1)S(1)}, bf16[64,1024]{1,0:T(8,128)(2,1)S(1)}, u32[]{:S(2)}, u32[]{:S(2)}) collective-permute-start(bf16[64,1024]{1,0:T(8,128)(2,1)S(1)} %add.51.mine_ref), channel_id=1, source_target_pairs={{0,1},{1,0},{2,3},{3,2},{4,5},{5,4},{6,7},{7,6},{8,9},{9,8},{10,11... | collective-permute-start | bytes 393224 | tf_op jit(solution)/shard_map/ppermute | solution.py:29
  42.8 12.2 %collective-permute-start.11 = (bf16[64,1024]{1,0:T(8,128)(2,1)S(1)}, bf16[64,1024]{1,0:T(8,128)(2,1)S(1)}, u32[]{:S(2)}, u32[]{:S(2)}) collective-permute-start(bf16[64,1024]{1,0:T(8,128)(2,1)S(1)} %add.54), channel_id=1, source_target_pairs={{0,2},{1,3},{2,0},{3,1},{4,6},{5,7},{6,4},{7,5},{8,10},{9,11},{10,... | collective-permute-start | bytes 393224 | tf_op jit(solution)/shard_map/ppermute | solution.py:29
  45.9 10.5 %collective-permute-start.14 = (bf16[64,1024]{1,0:T(8,128)(2,1)S(1)}, bf16[64,1024]{1,0:T(8,128)(2,1)S(1)}, u32[]{:S(2)}, u32[]{:S(2)}) collective-permute-start(bf16[64,1024]{1,0:T(8,128)(2,1)S(1)} %add.56), channel_id=1, source_target_pairs={{0,2},{1,3},{2,0},{3,1},{4,6},{5,7},{6,4},{7,5},{8,10},{9,11},{10,... | collective-permute-start | bytes 393224 | tf_op jit(solution)/shard_map/ppermute | solution.py:29
  48.0 9.2 %collective-permute-start.9 = (bf16[64,1024]{1,0:T(8,128)(2,1)S(1)}, bf16[64,1024]{1,0:T(8,128)(2,1)S(1)}, u32[]{:S(2)}, u32[]{:S(2)}) collective-permute-start(bf16[64,1024]{1,0:T(8,128)(2,1)S(1)} %add.53.mine_ref), channel_id=1, source_target_pairs={{0,1},{1,0},{2,3},{3,2},{4,5},{5,4},{6,7},{7,6},{8,9},{9,8},{10,11... | collective-permute-start | bytes 393224 | tf_op jit(solution)/shard_map/ppermute | solution.py:29
  55.0 5.6 %collective-permute-start.12 = (bf16[64,1024]{1,0:T(8,128)(2,1)S(1)}, bf16[64,1024]{1,0:T(8,128)(2,1)S(1)}, u32[]{:S(2)}, u32[]{:S(2)}) collective-permute-start(bf16[64,1024]{1,0:T(8,128)(2,1)S(1)} %add.55.mine_ref), channel_id=1, source_target_pairs={{0,1},{1,0},{2,3},{3,2},{4,5},{5,4},{6,7},{7,6},{8,9},{9,8},{10,11... | collective-permute-start | bytes 393224 | tf_op jit(solution)/shard_map/ppermute | solution.py:29
  56.4 5.6 %collective-permute-start.15 = (bf16[64,1024]{1,0:T(8,128)(2,1)S(1)}, bf16[64,1024]{1,0:T(8,128)(2,1)S(1)}, u32[]{:S(2)}, u32[]{:S(2)}) collective-permute-start(bf16[64,1024]{1,0:T(8,128)(2,1)S(1)} %add.57.mine_ref), channel_id=1, source_target_pairs={{0,1},{1,0},{2,3},{3,2},{4,5},{5,4},{6,7},{7,6},{8,9},{9,8},{10,11... | collective-permute-start | bytes 393224 | tf_op jit(solution)/shard_map/ppermute | solution.py:29
  57.2 4.8 %copy-start.1 = (bf16[1,192,4096]{2,1,0:T(8,128)(2,1)S(1)}, bf16[1,192,4096]{2,1,0:T(8,128)(2,1)}, u32[]{:S(2)}) copy-start(bf16[1,192,4096]{2,1,0:T(8,128)(2,1)} %param.23) | copy-start | bytes 4718596
  63.0 10.3 %collective-permute-start.16 = (bf16[32,4096]{1,0:T(8,128)(2,1)S(1)}, bf16[32,4096]{1,0:T(8,128)(2,1)S(1)}, u32[]{:S(2)}, u32[]{:S(2)}) collective-permute-start(bf16[32,4096]{1,0:T(8,128)(2,1)S(1)} %get-tuple-element.64), channel_id=1, source_target_pairs={{0,1},{1,0},{2,3},{3,2},{4,5},{5,4},{6,7},{7,6},{8,9},{9,8},{10,11... | collective-permute-start | bytes 786440 | tf_op jit(solution)/shard_map/ppermute | solution.py:29
  63.4 21.1 %collective-permute-start.17 = (bf16[32,4096]{1,0:T(8,128)(2,1)S(1)}, bf16[32,4096]{1,0:T(8,128)(2,1)S(1)}, u32[]{:S(2)}, u32[]{:S(2)}) collective-permute-start(bf16[32,4096]{1,0:T(8,128)(2,1)S(1)} %get-tuple-element.65), channel_id=1, source_target_pairs={{0,2},{1,3},{2,0},{3,1},{4,6},{5,7},{6,4},{7,5},{8,10},{9,11},{10,... | collective-permute-start | bytes 786440 | tf_op jit(solution)/shard_map/ppermute | solution.py:29
  65.7 18.8 %collective-permute-start.18 = (bf16[32,4096]{1,0:T(8,128)(2,1)S(1)}, bf16[32,4096]{1,0:T(8,128)(2,1)S(1)}, u32[]{:S(2)}, u32[]{:S(2)}) collective-permute-start(bf16[32,4096]{1,0:T(8,128)(2,1)S(1)} %get-tuple-element.66), channel_id=1, source_target_pairs={{0,3},{1,2},{2,1},{3,0},{4,7},{5,6},{6,5},{7,4},{8,11},{9,10},{10,... | collective-permute-start | bytes 786440 | tf_op jit(solution)/shard_map/ppermute | solution.py:29

commit v11 on v10

--- a/solution.py
+++ b/solution.py
@@ -345,7 +345,7 @@
     limits = jnp.concatenate([bounds // BASE, bounds % BASE]).astype(jnp.bfloat16)
     limits = jnp.broadcast_to(limits.reshape(1, width), (PAD_ROWS, width))
     same_keys = join_after(
-        [payload] + [exchange(payload, "ctx", r, ctx_count) for r in range(ctx_count - 2, 0, -2)],
+        [payload] + [exchange(payload, "ctx", r, ctx_count) for r in range(2, ctx_count, 2)],
         payload,
     )
     other_keys = exchange(same_keys, "ctx", 1, ctx_count)

time: 86.2 us -> 87.1 us (1.010)
  waiting for transfers between devices: 36.3 us -> 37.3 us
    ppermute x19, waiting for transfers between devices: 36.3 us -> 37.3 us  [exchange(): return lax.ppermute(value, axis, [(i, i ^ offset) for i in range(size)])]
where the time goes in v11:
time: 87.1 us; the launch traced here: 86.3 us
  waiting for transfers between devices  37.3 us (43%)
  starting transfers between devices  20.1 us (23%)
  Pallas kernels  13.1 us (15%)
  other arithmetic  9.59 us (11%)
  between operations  3.4 us (4%)
  local copies, waits for them, and re-layouts  2.79 us (3%)
    ppermute x19, waiting for transfers between devices, exchange(): return lax.ppermute(value, axis, [(i, i ^ offset) for i in range(size)])  37.3 us
    ppermute x19, starting transfers between devices, exchange(): return lax.ppermute(value, axis, [(i, i ^ offset) for i in range(size)])  20.1 us
    pallas_call x1, Pallas kernels, attend_project(): pl.pallas_call(attend_kernel, out_shape=part_shapes(tok, spans) + [jax.Sh...  6.3 us
    pallas_call x1, Pallas kernels, project(): pl.pallas_call(project_kernel, out_shape=part_shapes(tok, spans), in_spec...  4.61 us
    add x4, other arithmetic, line_device(): near = [kept + other for kept, other in zip(parts[::2], arrived)]  3.24 us
    pallas_call x4, Pallas kernels, absorb(): pl.pallas_call(functools.partial(absorb_kernel, chunk), out_shape=out_sha...  2.12 us
    add x4, other arithmetic, line_device(): mine = [own + other for own, other in zip(near, across)]  2.07 us
    unnamed x10, local copies, waits for them, and re-layouts  2 us
  transfers between devices with their start and end apart: 19, of which 12 were waited for; matrix products, arithmetic and copies ran while one was open for 10% of the time, Pallas kernels for 7%

profile of v11, /device:TPU:0, one launch (start us, length us, event | category | flops | bytes accessed | tf_op | source)
XLA Modules:
  0.0 86.3 jit_solution(11548493933953840625)
XLA Ops:
  4.1 3.0 %collective-permute-start = (bf16[144,256]{1,0:T(8,128)(2,1)S(1)}, bf16[144,256]{1,0:T(8,128)(2,1)S(1)}, u32[]{:S(2)}, u32[]{:S(2)}) collective-permute-start(bf16[144,256]{1,0:T(8,128)(2,1)S(1)} %fusion.2.refs_0_.refs_1_), channel_id=1, source_target_pairs={{0,8},{4,12},{8,0},{12,4},{16,24},{20,28},{24,16},{28,20},{1,9},{5... | collective-permute-start | bytes 221192 | tf_op jit(solution)/shard_map/ppermute | solution.py:29
  7.1 1.5 %collective-permute-start.1 = (bf16[144,256]{1,0:T(8,128)(2,1)S(1)}, bf16[144,256]{1,0:T(8,128)(2,1)S(1)}, u32[]{:S(2)}, u32[]{:S(2)}) collective-permute-start(bf16[144,256]{1,0:T(8,128)(2,1)S(1)} %fusion.2.refs_0_.refs_1_), channel_id=1, source_target_pairs={{0,16},{4,20},{8,24},{12,28},{16,0},{20,4},{24,8},{28,12},{1,17},{... | collective-permute-start | bytes 221192 | tf_op jit(solution)/shard_map/ppermute | solution.py:29
  8.6 1.0 %copy-done.2 = bf16[128,2048]{1,0:T(8,128)(2,1)S(1)} copy-done((bf16[128,2048]{1,0:T(8,128)(2,1)S(1)}, bf16[128,2048]{1,0:T(8,128)(2,1)}, u32[]{:S(2)}) %copy-start.2) | copy-done | bytes 524312
  11.4 2.4 %collective-permute-done.2.refs_4_ = bf16[144,256]{1,0:T(8,128)(2,1)S(1)} collective-permute-done((bf16[144,256]{1,0:T(8,128)(2,1)S(1)}, bf16[144,256]{1,0:T(8,128)(2,1)S(1)}, u32[]{:S(2)}, u32[]{:S(2)}) %collective-permute-start.2) | collective-permute-done | bytes 73760 | tf_op jit(solution)/shard_map/ppermute | solution.py:29
  15.5 6.3 %attend_project.1 = (bf16[64,1024]{1,0:T(8,128)(2,1)S(1)}, bf16[64,1024]{1,0:T(8,128)(2,1)S(1)}, bf16[64,1024]{1,0:T(8,128)(2,1)S(1)}, bf16[64,1024]{1,0:T(8,128)(2,1)S(1)}, bf16[128,2048]{1,0:T(8,128)(2,1)S(1)}) custom-call(s32[1]{0:T(128)} %bitcast.rank_ref, bf16[16,256]{1,0:T(8,128)(2,1)S(1)} %broadcast_in_dim.5.limit_ref, ...), custom_call_target="tpu_custom_call" | custom-call | flops 2147483648 | bytes 8388608 | tf_op jit(solution)/shard_map/attend_project/pallas_call | solution.py:128
  21.8 1.6 %collective-permute-start.4 = (bf16[64,1024]{1,0:T(8,128)(2,1)S(1)}, bf16[64,1024]{1,0:T(8,128)(2,1)S(1)}, u32[]{:S(2)}, u32[]{:S(2)}) collective-permute-start(bf16[64,1024]{1,0:T(8,128)(2,1)S(1)} %get-tuple-element.38), channel_id=1, source_target_pairs={{0,1},{1,0},{2,3},{3,2},{4,5},{5,4},{6,7},{7,6},{8,9},{9,8},{10,11... | collective-permute-start | bytes 393224 | tf_op jit(solution)/shard_map/ppermute | solution.py:29
  23.9 4.6 %project.1 = (bf16[64,1024]{1,0:T(8,128)(2,1)S(1)}, bf16[64,1024]{1,0:T(8,128)(2,1)}, bf16[64,1024]{1,0:T(8,128)(2,1)S(1)}, bf16[64,1024]{1,0:T(8,128)(2,1)S(1)}) custom-call(s32[1]{0:T(128)} %bitcast.rank_ref, bf16[128,2048]{1,0:T(8,128)(2,1)S(1)} %get-tuple-element.43.attended, bf16[32,4096]{1,0:T(8,128)(2,1)S(1)} %get-tuple-element.36.resid_ref, ...), custom_call_target="tpu_custom_call" | custom-call | flops 1073741824 | bytes 8388608 | tf_op jit(solution)/shard_map/project/pallas_call | solution.py:163
  29.2 2.6 %collective-permute-start.5 = (bf16[64,1024]{1,0:T(8,128)(2,1)}, bf16[64,1024]{1,0:T(8,128)(2,1)}, u32[]{:S(2)}, u32[]{:S(2)}) collective-permute-start(bf16[64,1024]{1,0:T(8,128)(2,1)} %add.50), channel_id=1, source_target_pairs={{0,2},{1,3},{2,0},{3,1},{4,6},{5,7},{6,4},{7,5},{8,10},{9,11},{10,... | collective-permute-start | bytes 393224 | tf_op jit(solution)/shard_map/ppermute | solution.py:29
  31.8 1.6 %collective-permute-start.10 = (bf16[64,1024]{1,0:T(8,128)(2,1)}, bf16[64,1024]{1,0:T(8,128)(2,1)}, u32[]{:S(2)}, u32[]{:S(2)}) collective-permute-start(bf16[64,1024]{1,0:T(8,128)(2,1)} %get-tuple-element.46), channel_id=1, source_target_pairs={{0,1},{1,0},{2,3},{3,2},{4,5},{5,4},{6,7},{7,6},{8,9},{9,8},{10,11... | collective-permute-start | bytes 393224 | tf_op jit(solution)/shard_map/ppermute | solution.py:29
  35.1 1.3 %reduce_sum.18 = f32[32]{0:T(128)} reduce(f32[32,8]{0,1:T(8,128)} %param.21, f32[]{:T(128)} %constant.63.clone.1), dimensions={1}, to_apply=%region_0.1 | reduce | flops 224 | bytes 1156 | tf_op jit(solution)/shard_map/reduce_sum | solution.py:358
  37.1 1.9 %collective-permute-done.5 = bf16[64,1024]{1,0:T(8,128)(2,1)} collective-permute-done((bf16[64,1024]{1,0:T(8,128)(2,1)}, bf16[64,1024]{1,0:T(8,128)(2,1)}, u32[]{:S(2)}, u32[]{:S(2)}) %collective-permute-start.5) | collective-permute-done | bytes 131104 | tf_op jit(solution)/shard_map/ppermute | solution.py:29
  39.0 1.0 %add.51.mine_ref = bf16[64,1024]{1,0:T(8,128)(2,1)S(1)} add(bf16[64,1024]{1,0:T(8,128)(2,1)} %add.50, bf16[64,1024]{1,0:T(8,128)(2,1)} %collective-permute-done.5) | non-fusion elementwise | flops 65536 | bytes 393216 | tf_op jit(solution)/shard_map/add | solution.py:377
  40.1 2.7 %collective-permute-done.10 = bf16[64,1024]{1,0:T(8,128)(2,1)} collective-permute-done((bf16[64,1024]{1,0:T(8,128)(2,1)}, bf16[64,1024]{1,0:T(8,128)(2,1)}, u32[]{:S(2)}, u32[]{:S(2)}) %collective-permute-start.10) | collective-permute-done | bytes 131104 | tf_op jit(solution)/shard_map/ppermute | solution.py:29
  44.5 1.4 %collective-permute-done.13 = bf16[64,1024]{1,0:T(8,128)(2,1)} collective-permute-done((bf16[64,1024]{1,0:T(8,128)(2,1)S(1)}, bf16[64,1024]{1,0:T(8,128)(2,1)}, u32[]{:S(2)}, u32[]{:S(2)}) %collective-permute-start.13) | collective-permute-done | bytes 131104 | tf_op jit(solution)/shard_map/ppermute | solution.py:29
  46.9 1.1 %collective-permute-start.14 = (bf16[64,1024]{1,0:T(8,128)(2,1)S(1)}, bf16[64,1024]{1,0:T(8,128)(2,1)S(1)}, u32[]{:S(2)}, u32[]{:S(2)}) collective-permute-start(bf16[64,1024]{1,0:T(8,128)(2,1)S(1)} %add.56), channel_id=1, source_target_pairs={{0,2},{1,3},{2,0},{3,1},{4,6},{5,7},{6,4},{7,5},{8,10},{9,11},{10,... | collective-permute-start | bytes 393224 | tf_op jit(solution)/shard_map/ppermute | solution.py:29
  50.4 5.5 %collective-permute-done.11 = bf16[64,1024]{1,0:T(8,128)(2,1)S(1)} collective-permute-done((bf16[64,1024]{1,0:T(8,128)(2,1)S(1)}, bf16[64,1024]{1,0:T(8,128)(2,1)S(1)}, u32[]{:S(2)}, u32[]{:S(2)}) %collective-permute-start.11) | collective-permute-done | bytes 131104 | tf_op jit(solution)/shard_map/ppermute | solution.py:29
  56.0 1.3 %collective-permute-done.14 = bf16[64,1024]{1,0:T(8,128)(2,1)S(1)} collective-permute-done((bf16[64,1024]{1,0:T(8,128)(2,1)S(1)}, bf16[64,1024]{1,0:T(8,128)(2,1)S(1)}, u32[]{:S(2)}, u32[]{:S(2)}) %collective-permute-start.14) | collective-permute-done | bytes 131104 | tf_op jit(solution)/shard_map/ppermute | solution.py:29
  58.5 3.0 %collective-permute-done.12.theirs_ref = bf16[64,1024]{1,0:T(8,128)(2,1)S(1)} collective-permute-done((bf16[64,1024]{1,0:T(8,128)(2,1)S(1)}, bf16[64,1024]{1,0:T(8,128)(2,1)S(1)}, u32[]{:S(2)}, u32[]{:S(2)}) %collective-permute-start.12) | collective-permute-done | bytes 131104 | tf_op jit(solution)/shard_map/ppermute | solution.py:29
  61.9 1.0 %collective-permute-done.15.theirs_ref = bf16[64,1024]{1,0:T(8,128)(2,1)S(1)} collective-permute-done((bf16[64,1024]{1,0:T(8,128)(2,1)S(1)}, bf16[64,1024]{1,0:T(8,128)(2,1)S(1)}, u32[]{:S(2)}, u32[]{:S(2)}) %collective-permute-start.15) | collective-permute-done | bytes 131104 | tf_op jit(solution)/shard_map/ppermute | solution.py:29
  63.0 1.0 %absorb.7 = (bf16[32,1024]{1,0:T(8,128)(2,1)S(1)}, bf16[32,4096]{1,0:T(8,128)(2,1)S(1)}, bf16[32,4096]{1,0:T(8,128)(2,1)S(1)}, bf16[32,4096]{1,0:T(8,128)(2,1)S(1)}, bf16[32,4096]{1,0:T(8,128)(2,1)S(1)}) custom-call(s32[1]{0:T(128)} %bitcast.rank_ref, bf16[64,1024]{1,0:T(8,128)(2,1)S(1)} %add.57.mine_ref, ...), custom_call_target="tpu_custom_call" | custom-call | flops 1024 | bytes 1024 | tf_op jit(solution)/shard_map/absorb/pallas_call | solution.py:294
  64.3 2.4 %collective-permute-start.17 = (bf16[32,4096]{1,0:T(8,128)(2,1)S(1)}, bf16[32,4096]{1,0:T(8,128)(2,1)S(1)}, u32[]{:S(2)}, u32[]{:S(2)}) collective-permute-start(bf16[32,4096]{1,0:T(8,128)(2,1)S(1)} %get-tuple-element.65), channel_id=1, source_target_pairs={{0,2},{1,3},{2,0},{3,1},{4,6},{5,7},{6,4},{7,5},{8,10},{9,11},{10,... | collective-permute-start | bytes 786440 | tf_op jit(solution)/shard_map/ppermute | solution.py:29
  66.7 1.7 %collective-permute-start.18 = (bf16[32,4096]{1,0:T(8,128)(2,1)S(1)}, bf16[32,4096]{1,0:T(8,128)(2,1)S(1)}, u32[]{:S(2)}, u32[]{:S(2)}) collective-permute-start(bf16[32,4096]{1,0:T(8,128)(2,1)S(1)} %get-tuple-element.66), channel_id=1, source_target_pairs={{0,3},{1,2},{2,1},{3,0},{4,7},{5,6},{6,5},{7,4},{8,11},{9,10},{10,... | collective-permute-start | bytes 786440 | tf_op jit(solution)/shard_map/ppermute | solution.py:29
  69.1 5.2 %collective-permute-done.16 = bf16[32,4096]{1,0:T(8,128)(2,1)S(1)} collective-permute-done((bf16[32,4096]{1,0:T(8,128)(2,1)S(1)}, bf16[32,4096]{1,0:T(8,128)(2,1)S(1)}, u32[]{:S(2)}, u32[]{:S(2)}) %collective-permute-start.16) | collective-permute-done | bytes 262176 | tf_op jit(solution)/shard_map/ppermute | solution.py:29
  74.3 11.1 %collective-permute-done.17 = bf16[32,4096]{1,0:T(8,128)(2,1)S(1)} collective-permute-done((bf16[32,4096]{1,0:T(8,128)(2,1)S(1)}, bf16[32,4096]{1,0:T(8,128)(2,1)S(1)}, u32[]{:S(2)}, u32[]{:S(2)}) %collective-permute-start.17) | collective-permute-done | bytes 262176 | tf_op jit(solution)/shard_map/ppermute | solution.py:29
  (50 shorter events, 16.5 us)
Async XLA Ops:
  4.1 6.6 %collective-permute-start = (bf16[144,256]{1,0:T(8,128)(2,1)S(1)}, bf16[144,256]{1,0:T(8,128)(2,1)S(1)}, u32[]{:S(2)}, u32[]{:S(2)}) collective-permute-start(bf16[144,256]{1,0:T(8,128)(2,1)S(1)} %fusion.2.refs_0_.refs_1_), channel_id=1, source_target_pairs={{0,8},{4,12},{8,0},{12,4},{16,24},{20,28},{24,16},{28,20},{1,9},{5... | collective-permute-start | bytes 221192 | tf_op jit(solution)/shard_map/ppermute | solution.py:29
  7.1 4.4 %collective-permute-start.1 = (bf16[144,256]{1,0:T(8,128)(2,1)S(1)}, bf16[144,256]{1,0:T(8,128)(2,1)S(1)}, u32[]{:S(2)}, u32[]{:S(2)}) collective-permute-start(bf16[144,256]{1,0:T(8,128)(2,1)S(1)} %fusion.2.refs_0_.refs_1_), channel_id=1, source_target_pairs={{0,16},{4,20},{8,24},{12,28},{16,0},{20,4},{24,8},{28,12},{1,17},{... | collective-permute-start | bytes 221192 | tf_op jit(solution)/shard_map/ppermute | solution.py:29
  8.6 5.3 %collective-permute-start.2 = (bf16[144,256]{1,0:T(8,128)(2,1)S(1)}, bf16[144,256]{1,0:T(8,128)(2,1)S(1)}, u32[]{:S(2)}, u32[]{:S(2)}) collective-permute-start(bf16[144,256]{1,0:T(8,128)(2,1)S(1)} %fusion.2.refs_0_.refs_1_), channel_id=1, source_target_pairs={{0,24},{4,28},{8,16},{12,20},{16,8},{20,12},{24,0},{28,4},{1,25},{... | collective-permute-start | bytes 221192 | tf_op jit(solution)/shard_map/ppermute | solution.py:29
  8.6 1.0 %copy-start.2 = (bf16[128,2048]{1,0:T(8,128)(2,1)S(1)}, bf16[128,2048]{1,0:T(8,128)(2,1)}, u32[]{:S(2)}) copy-start(bf16[128,2048]{1,0:T(8,128)(2,1)} %q_hbm.1) | copy-start | bytes 1572868
  9.6 0.9 %copy-start.4 = (bf16[32,4096]{1,0:T(8,128)(2,1)S(1)}, bf16[32,4096]{1,0:T(8,128)(2,1)}, u32[]{:S(2)}) copy-start(bf16[32,4096]{1,0:T(8,128)(2,1)} %resid_hbm.1) | copy-start | bytes 786436
  13.9 1.6 %collective-permute-start.3 = (bf16[576,256]{1,0:T(8,128)(2,1)S(1)}, bf16[576,256]{1,0:T(8,128)(2,1)S(1)}, u32[]{:S(2)}, u32[]{:S(2)}) collective-permute-start(bf16[576,256]{1,0:T(8,128)(2,1)S(1)} %join_after.1.same_ref), channel_id=1, source_target_pairs={{0,4},{4,0},{8,12},{12,8},{16,20},{20,16},{24,28},{28,24},{1,5},{5... | collective-permute-start | bytes 884744 | tf_op jit(solution)/shard_map/ppermute | solution.py:29
  21.8 6.7 %collective-permute-start.4 = (bf16[64,1024]{1,0:T(8,128)(2,1)S(1)}, bf16[64,1024]{1,0:T(8,128)(2,1)S(1)}, u32[]{:S(2)}, u32[]{:S(2)}) collective-permute-start(bf16[64,1024]{1,0:T(8,128)(2,1)S(1)} %get-tuple-element.38), channel_id=1, source_target_pairs={{0,1},{1,0},{2,3},{3,2},{4,5},{5,4},{6,7},{7,6},{8,9},{9,8},{10,11... | collective-permute-start | bytes 393224 | tf_op jit(solution)/shard_map/ppermute | solution.py:29
  23.5 9.9 %collective-permute-start.7 = (bf16[64,1024]{1,0:T(8,128)(2,1)S(1)}, bf16[64,1024]{1,0:T(8,128)(2,1)S(1)}, u32[]{:S(2)}, u32[]{:S(2)}) collective-permute-start(bf16[64,1024]{1,0:T(8,128)(2,1)S(1)} %get-tuple-element.41), channel_id=1, source_target_pairs={{0,1},{1,0},{2,3},{3,2},{4,5},{5,4},{6,7},{7,6},{8,9},{9,8},{10,11... | collective-permute-start | bytes 393224 | tf_op jit(solution)/shard_map/ppermute | solution.py:29
  23.9 26.1 %copy-start = (bf16[1,384,4096]{2,1,0:T(8,128)(2,1)S(1)}, bf16[1,384,4096]{2,1,0:T(8,128)(2,1)}, u32[]{:S(2)}) copy-start(bf16[1,384,4096]{2,1,0:T(8,128)(2,1)} %param.22) | copy-start | bytes 9437188
  23.9 26.1 %copy-start.3 = (f32[4096]{0:T(1024)S(1)}, f32[4096]{0:T(1024)}, u32[]{:S(2)}) copy-start(f32[4096]{0:T(1024)} %param.19) | copy-start | bytes 49156
  29.2 9.8 %collective-permute-start.5 = (bf16[64,1024]{1,0:T(8,128)(2,1)}, bf16[64,1024]{1,0:T(8,128)(2,1)}, u32[]{:S(2)}, u32[]{:S(2)}) collective-permute-start(bf16[64,1024]{1,0:T(8,128)(2,1)} %add.50), channel_id=1, source_target_pairs={{0,2},{1,3},{2,0},{3,1},{4,6},{5,7},{6,4},{7,5},{8,10},{9,11},{10,... | collective-permute-start | bytes 393224 | tf_op jit(solution)/shard_map/ppermute | solution.py:29
  31.8 11.0 %collective-permute-start.10 = (bf16[64,1024]{1,0:T(8,128)(2,1)}, bf16[64,1024]{1,0:T(8,128)(2,1)}, u32[]{:S(2)}, u32[]{:S(2)}) collective-permute-start(bf16[64,1024]{1,0:T(8,128)(2,1)} %get-tuple-element.46), channel_id=1, source_target_pairs={{0,1},{1,0},{2,3},{3,2},{4,5},{5,4},{6,7},{7,6},{8,9},{9,8},{10,11... | collective-permute-start | bytes 393224 | tf_op jit(solution)/shard_map/ppermute | solution.py:29
  33.4 12.6 %collective-permute-start.13 = (bf16[64,1024]{1,0:T(8,128)(2,1)S(1)}, bf16[64,1024]{1,0:T(8,128)(2,1)}, u32[]{:S(2)}, u32[]{:S(2)}) collective-permute-start(bf16[64,1024]{1,0:T(8,128)(2,1)S(1)} %get-tuple-element.58), channel_id=1, source_target_pairs={{0,1},{1,0},{2,3},{3,2},{4,5},{5,4},{6,7},{7,6},{8,9},{9,8},{10,11... | collective-permute-start | bytes 393224 | tf_op jit(solution)/shard_map/ppermute | solution.py:29
  34.5 12.4 %collective-permute-start.8 = (bf16[64,1024]{1,0:T(8,128)(2,1)}, bf16[64,1024]{1,0:T(8,128)(2,1)}, u32[]{:S(2)}, u32[]{:S(2)}) collective-permute-start(bf16[64,1024]{1,0:T(8,128)(2,1)} %add.52), channel_id=1, source_target_pairs={{0,2},{1,3},{2,0},{3,1},{4,6},{5,7},{6,4},{7,5},{8,10},{9,11},{10,... | collective-permute-start | bytes 393224 | tf_op jit(solution)/shard_map/ppermute | solution.py:29
  40.0 10.0 %collective-permute-start.6 = (bf16[64,1024]{1,0:T(8,128)(2,1)S(1)}, bf16[64,1024]{1,0:T(8,128)(2,1)S(1)}, u32[]{:S(2)}, u32[]{:S(2)}) collective-permute-start(bf16[64,1024]{1,0:T(8,128)(2,1)S(1)} %add.51.mine_ref), channel_id=1, source_target_pairs={{0,1},{1,0},{2,3},{3,2},{4,5},{5,4},{6,7},{7,6},{8,9},{9,8},{10,11... | collective-permute-start | bytes 393224 | tf_op jit(solution)/shard_map/ppermute | solution.py:29
  43.7 12.2 %collective-permute-start.11 = (bf16[64,1024]{1,0:T(8,128)(2,1)S(1)}, bf16[64,1024]{1,0:T(8,128)(2,1)S(1)}, u32[]{:S(2)}, u32[]{:S(2)}) collective-permute-start(bf16[64,1024]{1,0:T(8,128)(2,1)S(1)} %add.54), channel_id=1, source_target_pairs={{0,2},{1,3},{2,0},{3,1},{4,6},{5,7},{6,4},{7,5},{8,10},{9,11},{10,... | collective-permute-start | bytes 393224 | tf_op jit(solution)/shard_map/ppermute | solution.py:29
  46.9 10.4 %collective-permute-start.14 = (bf16[64,1024]{1,0:T(8,128)(2,1)S(1)}, bf16[64,1024]{1,0:T(8,128)(2,1)S(1)}, u32[]{:S(2)}, u32[]{:S(2)}) collective-permute-start(bf16[64,1024]{1,0:T(8,128)(2,1)S(1)} %add.56), channel_id=1, source_target_pairs={{0,2},{1,3},{2,0},{3,1},{4,6},{5,7},{6,4},{7,5},{8,10},{9,11},{10,... | collective-permute-start | bytes 393224 | tf_op jit(solution)/shard_map/ppermute | solution.py:29
  49.0 9.2 %collective-permute-start.9 = (bf16[64,1024]{1,0:T(8,128)(2,1)S(1)}, bf16[64,1024]{1,0:T(8,128)(2,1)S(1)}, u32[]{:S(2)}, u32[]{:S(2)}) collective-permute-start(bf16[64,1024]{1,0:T(8,128)(2,1)S(1)} %add.53.mine_ref), channel_id=1, source_target_pairs={{0,1},{1,0},{2,3},{3,2},{4,5},{5,4},{6,7},{7,6},{8,9},{9,8},{10,11... | collective-permute-start | bytes 393224 | tf_op jit(solution)/shard_map/ppermute | solution.py:29
  55.9 5.6 %collective-permute-start.12 = (bf16[64,1024]{1,0:T(8,128)(2,1)S(1)}, bf16[64,1024]{1,0:T(8,128)(2,1)S(1)}, u32[]{:S(2)}, u32[]{:S(2)}) collective-permute-start(bf16[64,1024]{1,0:T(8,128)(2,1)S(1)} %add.55.mine_ref), channel_id=1, source_target_pairs={{0,1},{1,0},{2,3},{3,2},{4,5},{5,4},{6,7},{7,6},{8,9},{9,8},{10,11... | collective-permute-start | bytes 393224 | tf_op jit(solution)/shard_map/ppermute | solution.py:29
  57.4 5.6 %collective-permute-start.15 = (bf16[64,1024]{1,0:T(8,128)(2,1)S(1)}, bf16[64,1024]{1,0:T(8,128)(2,1)S(1)}, u32[]{:S(2)}, u32[]{:S(2)}) collective-permute-start(bf16[64,1024]{1,0:T(8,128)(2,1)S(1)} %add.57.mine_ref), channel_id=1, source_target_pairs={{0,1},{1,0},{2,3},{3,2},{4,5},{5,4},{6,7},{7,6},{8,9},{9,8},{10,11... | collective-permute-start | bytes 393224 | tf_op jit(solution)/shard_map/ppermute | solution.py:29
  58.1 4.8 %copy-start.1 = (bf16[1,192,4096]{2,1,0:T(8,128)(2,1)S(1)}, bf16[1,192,4096]{2,1,0:T(8,128)(2,1)}, u32[]{:S(2)}) copy-start(bf16[1,192,4096]{2,1,0:T(8,128)(2,1)} %param.23) | copy-start | bytes 4718596
  64.0 10.4 %collective-permute-start.16 = (bf16[32,4096]{1,0:T(8,128)(2,1)S(1)}, bf16[32,4096]{1,0:T(8,128)(2,1)S(1)}, u32[]{:S(2)}, u32[]{:S(2)}) collective-permute-start(bf16[32,4096]{1,0:T(8,128)(2,1)S(1)} %get-tuple-element.64), channel_id=1, source_target_pairs={{0,1},{1,0},{2,3},{3,2},{4,5},{5,4},{6,7},{7,6},{8,9},{9,8},{10,11... | collective-permute-start | bytes 786440 | tf_op jit(solution)/shard_map/ppermute | solution.py:29
  64.3 21.1 %collective-permute-start.17 = (bf16[32,4096]{1,0:T(8,128)(2,1)S(1)}, bf16[32,4096]{1,0:T(8,128)(2,1)S(1)}, u32[]{:S(2)}, u32[]{:S(2)}) collective-permute-start(bf16[32,4096]{1,0:T(8,128)(2,1)S(1)} %get-tuple-element.65), channel_id=1, source_target_pairs={{0,2},{1,3},{2,0},{3,1},{4,6},{5,7},{6,4},{7,5},{8,10},{9,11},{10,... | collective-permute-start | bytes 786440 | tf_op jit(solution)/shard_map/ppermute | solution.py:29
  66.7 18.8 %collective-permute-start.18 = (bf16[32,4096]{1,0:T(8,128)(2,1)S(1)}, bf16[32,4096]{1,0:T(8,128)(2,1)S(1)}, u32[]{:S(2)}, u32[]{:S(2)}) collective-permute-start(bf16[32,4096]{1,0:T(8,128)(2,1)S(1)} %get-tuple-element.66), channel_id=1, source_target_pairs={{0,3},{1,2},{2,1},{3,0},{4,7},{5,6},{6,5},{7,4},{8,11},{9,10},{10,... | collective-permute-start | bytes 786440 | tf_op jit(solution)/shard_map/ppermute | solution.py:29

commit v12 on v7

--- a/solution.py
+++ b/solution.py
@@ -405,7 +405,7 @@
         homes.append(own)
     middle_out = jnp.concatenate(homes, axis=1)
     expert = states[0].astype(jnp.float32)
-    for offset in range(1, exp_count):
+    for offset in (2, 3, 1):
         expert = expert + exchange(states[offset], "exp", offset, exp_count).astype(jnp.float32)
     return (middle_out, (expert * coefficient).astype(jnp.bfloat16))
 

time: 85.4 us -> 85.1 us (level)
  the two profiles are of different devices: /device:TPU:0 before, /device:TPU:17 now
where the time goes in v12:
time: 85.1 us; the launch traced here: 84.7 us
  waiting for transfers between devices  31.7 us (37%)
  starting transfers between devices  30.5 us (36%)
  Pallas kernels  13 us (15%)
  between operations  3.42 us (4%)
  other arithmetic  3.29 us (4%)
  local copies, waits for them, and re-layouts  2.8 us (3%)
    ppermute x19, waiting for transfers between devices, exchange(): return lax.ppermute(value, axis, [(i, i ^ offset) for i in range(size)])  31.7 us
    ppermute x19, starting transfers between devices, exchange(): return lax.ppermute(value, axis, [(i, i ^ offset) for i in range(size)])  30.5 us
    pallas_call x1, Pallas kernels, attend_project(): pl.pallas_call(attend_kernel, out_shape=part_shapes(tok, spans) + [jax.Sh...  6.36 us
    pallas_call x1, Pallas kernels, project(): pl.pallas_call(project_kernel, out_shape=part_shapes(tok, spans), in_spec...  4.41 us
    pallas_call x4, Pallas kernels, absorb(): pl.pallas_call(functools.partial(absorb_kernel, chunk), out_shape=out_sha...  2.13 us
    unnamed x14, local copies, waits for them, and re-layouts  2.01 us
  transfers between devices with their start and end apart: 19, of which 10 were waited for; matrix products, arithmetic and copies ran while one was open for 3% of the time, Pallas kernels for 7%

profile of v12, /device:TPU:17, one launch (start us, length us, event | category | flops | bytes accessed | tf_op | source)
XLA Modules:
  0.0 84.7 jit_solution(17392210397948217359)
XLA Ops:
  4.1 1.3 %collective-permute-start = (bf16[144,256]{1,0:T(8,128)(2,1)S(1)}, bf16[144,256]{1,0:T(8,128)(2,1)S(1)}, u32[]{:S(2)}, u32[]{:S(2)}) collective-permute-start(bf16[144,256]{1,0:T(8,128)(2,1)S(1)} %fusion.2.refs_0_.refs_1_), channel_id=1, source_target_pairs={{0,8},{4,12},{8,0},{12,4},{16,24},{20,28},{24,16},{28,20},{1,9},{5... | collective-permute-start | bytes 221192 | tf_op jit(solution)/shard_map/ppermute | solution.py:29
  5.3 1.2 %collective-permute-start.1 = (bf16[144,256]{1,0:T(8,128)(2,1)S(1)}, bf16[144,256]{1,0:T(8,128)(2,1)S(1)}, u32[]{:S(2)}, u32[]{:S(2)}) collective-permute-start(bf16[144,256]{1,0:T(8,128)(2,1)S(1)} %fusion.2.refs_0_.refs_1_), channel_id=1, source_target_pairs={{0,16},{4,20},{8,24},{12,28},{16,0},{20,4},{24,8},{28,12},{1,17},{... | collective-permute-start | bytes 221192 | tf_op jit(solution)/shard_map/ppermute | solution.py:29
  6.8 1.0 %copy-done.2 = bf16[128,2048]{1,0:T(8,128)(2,1)S(1)} copy-done((bf16[128,2048]{1,0:T(8,128)(2,1)S(1)}, bf16[128,2048]{1,0:T(8,128)(2,1)}, u32[]{:S(2)}) %copy-start.2) | copy-done | bytes 524312
  7.8 0.9 %copy-done.4 = bf16[32,4096]{1,0:T(8,128)(2,1)S(1)} copy-done((bf16[32,4096]{1,0:T(8,128)(2,1)S(1)}, bf16[32,4096]{1,0:T(8,128)(2,1)}, u32[]{:S(2)}) %copy-start.4) | copy-done | bytes 262168
  9.6 1.2 %collective-permute-done.2.refs_4_ = bf16[144,256]{1,0:T(8,128)(2,1)S(1)} collective-permute-done((bf16[144,256]{1,0:T(8,128)(2,1)S(1)}, bf16[144,256]{1,0:T(8,128)(2,1)S(1)}, u32[]{:S(2)}, u32[]{:S(2)}) %collective-permute-start.2) | collective-permute-done | bytes 73760 | tf_op jit(solution)/shard_map/ppermute | solution.py:29
  10.8 2.4 %collective-permute-start.3 = (bf16[576,256]{1,0:T(8,128)(2,1)S(1)}, bf16[576,256]{1,0:T(8,128)(2,1)S(1)}, u32[]{:S(2)}, u32[]{:S(2)}) collective-permute-start(bf16[576,256]{1,0:T(8,128)(2,1)S(1)} %join_after.1.same_ref), channel_id=1, source_target_pairs={{0,4},{4,0},{8,12},{12,8},{16,20},{20,16},{24,28},{28,24},{1,5},{5... | collective-permute-start | bytes 884744 | tf_op jit(solution)/shard_map/ppermute | solution.py:29
  14.4 6.4 %attend_project.1 = (bf16[64,1024]{1,0:T(8,128)(2,1)S(1)}, bf16[64,1024]{1,0:T(8,128)(2,1)S(1)}, bf16[64,1024]{1,0:T(8,128)(2,1)S(1)}, bf16[64,1024]{1,0:T(8,128)(2,1)S(1)}, bf16[128,2048]{1,0:T(8,128)(2,1)S(1)}) custom-call(s32[1]{0:T(128)} %bitcast.rank_ref, bf16[16,256]{1,0:T(8,128)(2,1)S(1)} %broadcast_in_dim.5.limit_ref, ...), custom_call_target="tpu_custom_call" | custom-call | flops 2147483648 | bytes 8388608 | tf_op jit(solution)/shard_map/attend_project/pallas_call | solution.py:128
  20.7 1.4 %collective-permute-start.4 = (bf16[64,1024]{1,0:T(8,128)(2,1)S(1)}, bf16[64,1024]{1,0:T(8,128)(2,1)S(1)}, u32[]{:S(2)}, u32[]{:S(2)}) collective-permute-start(bf16[64,1024]{1,0:T(8,128)(2,1)S(1)} %get-tuple-element.40), channel_id=1, source_target_pairs={{0,1},{1,0},{2,3},{3,2},{4,5},{5,4},{6,7},{7,6},{8,9},{9,8},{10,11... | collective-permute-start | bytes 393224 | tf_op jit(solution)/shard_map/ppermute | solution.py:29
  22.3 4.4 %project.1 = (bf16[64,1024]{1,0:T(8,128)(2,1)S(1)}, bf16[64,1024]{1,0:T(8,128)(2,1)S(1)}, bf16[64,1024]{1,0:T(8,128)(2,1)S(1)}, bf16[64,1024]{1,0:T(8,128)(2,1)S(1)}) custom-call(s32[1]{0:T(128)} %bitcast.rank_ref, bf16[128,2048]{1,0:T(8,128)(2,1)S(1)} %get-tuple-element.45.attended, bf16[32,4096]{1,0:T(8,128)(2,1)S(1)} %get-tuple-element.38.resid_ref, ...), custom_call_target="tpu_custom_call" | custom-call | flops 1073741824 | bytes 8388608 | tf_op jit(solution)/shard_map/project/pallas_call | solution.py:163
  26.9 1.3 %collective-permute-start.10 = (bf16[64,1024]{1,0:T(8,128)(2,1)S(1)}, bf16[64,1024]{1,0:T(8,128)(2,1)S(1)}, u32[]{:S(2)}, u32[]{:S(2)}) collective-permute-start(bf16[64,1024]{1,0:T(8,128)(2,1)S(1)} %get-tuple-element.48), channel_id=1, source_target_pairs={{0,1},{1,0},{2,3},{3,2},{4,5},{5,4},{6,7},{7,6},{8,9},{9,8},{10,11... | collective-permute-start | bytes 393224 | tf_op jit(solution)/shard_map/ppermute | solution.py:29
  28.4 2.3 %collective-permute-start.8 = (bf16[64,1024]{1,0:T(8,128)(2,1)S(1)}, bf16[64,1024]{1,0:T(8,128)(2,1)S(1)}, u32[]{:S(2)}, u32[]{:S(2)}) collective-permute-start(bf16[64,1024]{1,0:T(8,128)(2,1)S(1)} %add.52), channel_id=1, source_target_pairs={{0,2},{1,3},{2,0},{3,1},{4,6},{5,7},{6,4},{7,5},{8,10},{9,11},{10,... | collective-permute-start | bytes 393224 | tf_op jit(solution)/shard_map/ppermute | solution.py:29
  31.7 6.9 %collective-permute-start.6 = (bf16[64,1024]{1,0:T(8,128)(2,1)S(1)}, bf16[64,1024]{1,0:T(8,128)(2,1)S(1)}, u32[]{:S(2)}, u32[]{:S(2)}) collective-permute-start(bf16[64,1024]{1,0:T(8,128)(2,1)S(1)} %add.51.mine_ref), channel_id=1, source_target_pairs={{0,1},{1,0},{2,3},{3,2},{4,5},{5,4},{6,7},{7,6},{8,9},{9,8},{10,11... | collective-permute-start | bytes 393224 | tf_op jit(solution)/shard_map/ppermute | solution.py:29
  39.4 1.9 %collective-permute-start.14 = (bf16[64,1024]{1,0:T(8,128)(2,1)S(1)}, bf16[64,1024]{1,0:T(8,128)(2,1)S(1)}, u32[]{:S(2)}, u32[]{:S(2)}) collective-permute-start(bf16[64,1024]{1,0:T(8,128)(2,1)S(1)} %add.56), channel_id=1, source_target_pairs={{0,2},{1,3},{2,0},{3,1},{4,6},{5,7},{6,4},{7,5},{8,10},{9,11},{10,... | collective-permute-start | bytes 393224 | tf_op jit(solution)/shard_map/ppermute | solution.py:29
  41.2 1.8 %collective-permute-start.9 = (bf16[64,1024]{1,0:T(8,128)(2,1)S(1)}, bf16[64,1024]{1,0:T(8,128)(2,1)S(1)}, u32[]{:S(2)}, u32[]{:S(2)}) collective-permute-start(bf16[64,1024]{1,0:T(8,128)(2,1)S(1)} %add.53.mine_ref), channel_id=1, source_target_pairs={{0,1},{1,0},{2,3},{3,2},{4,5},{5,4},{6,7},{7,6},{8,9},{9,8},{10,11... | collective-permute-start | bytes 393224 | tf_op jit(solution)/shard_map/ppermute | solution.py:29
  43.0 3.1 %collective-permute-done.6.theirs_ref = bf16[64,1024]{1,0:T(8,128)(2,1)S(1)} collective-permute-done((bf16[64,1024]{1,0:T(8,128)(2,1)S(1)}, bf16[64,1024]{1,0:T(8,128)(2,1)S(1)}, u32[]{:S(2)}, u32[]{:S(2)}) %collective-permute-start.6) | collective-permute-done | bytes 131104 | tf_op jit(solution)/shard_map/ppermute | solution.py:29
  46.6 2.3 %collective-permute-start.12 = (bf16[64,1024]{1,0:T(8,128)(2,1)S(1)}, bf16[64,1024]{1,0:T(8,128)(2,1)S(1)}, u32[]{:S(2)}, u32[]{:S(2)}) collective-permute-start(bf16[64,1024]{1,0:T(8,128)(2,1)S(1)} %add.55.mine_ref), channel_id=1, source_target_pairs={{0,1},{1,0},{2,3},{3,2},{4,5},{5,4},{6,7},{7,6},{8,9},{9,8},{10,11... | collective-permute-start | bytes 393224 | tf_op jit(solution)/shard_map/ppermute | solution.py:29
  48.9 1.6 %collective-permute-done.9.theirs_ref = bf16[64,1024]{1,0:T(8,128)(2,1)S(1)} collective-permute-done((bf16[64,1024]{1,0:T(8,128)(2,1)S(1)}, bf16[64,1024]{1,0:T(8,128)(2,1)S(1)}, u32[]{:S(2)}, u32[]{:S(2)}) %collective-permute-start.9) | collective-permute-done | bytes 131104 | tf_op jit(solution)/shard_map/ppermute | solution.py:29
  50.9 3.5 %collective-permute-start.15 = (bf16[64,1024]{1,0:T(8,128)(2,1)S(1)}, bf16[64,1024]{1,0:T(8,128)(2,1)S(1)}, u32[]{:S(2)}, u32[]{:S(2)}) collective-permute-start(bf16[64,1024]{1,0:T(8,128)(2,1)S(1)} %add.57.mine_ref), channel_id=1, source_target_pairs={{0,1},{1,0},{2,3},{3,2},{4,5},{5,4},{6,7},{7,6},{8,9},{9,8},{10,11... | collective-permute-start | bytes 393224 | tf_op jit(solution)/shard_map/ppermute | solution.py:29
  54.8 2.0 %collective-permute-done.15.theirs_ref = bf16[64,1024]{1,0:T(8,128)(2,1)S(1)} collective-permute-done((bf16[64,1024]{1,0:T(8,128)(2,1)S(1)}, bf16[64,1024]{1,0:T(8,128)(2,1)S(1)}, u32[]{:S(2)}, u32[]{:S(2)}) %collective-permute-start.15) | collective-permute-done | bytes 131104 | tf_op jit(solution)/shard_map/ppermute | solution.py:29
  56.8 1.0 %absorb.7 = (bf16[32,1024]{1,0:T(8,128)(2,1)S(1)}, bf16[32,4096]{1,0:T(8,128)(2,1)S(1)}, bf16[32,4096]{1,0:T(8,128)(2,1)S(1)}, bf16[32,4096]{1,0:T(8,128)(2,1)S(1)}, bf16[32,4096]{1,0:T(8,128)(2,1)S(1)}) custom-call(s32[1]{0:T(128)} %bitcast.rank_ref, bf16[64,1024]{1,0:T(8,128)(2,1)S(1)} %add.57.mine_ref, ...), custom_call_target="tpu_custom_call" | custom-call | flops 1024 | bytes 1024 | tf_op jit(solution)/shard_map/absorb/pallas_call | solution.py:294
  58.6 1.9 %collective-permute-start.17 = (bf16[32,4096]{1,0:T(8,128)(2,1)S(1)}, bf16[32,4096]{1,0:T(8,128)(2,1)S(1)}, u32[]{:S(2)}, u32[]{:S(2)}) collective-permute-start(bf16[32,4096]{1,0:T(8,128)(2,1)S(1)} %get-tuple-element.69), channel_id=1, source_target_pairs={{0,3},{1,2},{2,1},{3,0},{4,7},{5,6},{6,5},{7,4},{8,11},{9,10},{10,... | collective-permute-start | bytes 786440 | tf_op jit(solution)/shard_map/ppermute | solution.py:29
  60.5 0.9 %collective-permute-start.18 = (bf16[32,4096]{1,0:T(8,128)(2,1)S(1)}, bf16[32,4096]{1,0:T(8,128)(2,1)S(1)}, u32[]{:S(2)}, u32[]{:S(2)}) collective-permute-start(bf16[32,4096]{1,0:T(8,128)(2,1)S(1)} %get-tuple-element.70), channel_id=1, source_target_pairs={{0,1},{1,0},{2,3},{3,2},{4,5},{5,4},{6,7},{7,6},{8,9},{9,8},{10,11... | collective-permute-start | bytes 786440 | tf_op jit(solution)/shard_map/ppermute | solution.py:29
  62.1 13.1 %collective-permute-done.16 = bf16[32,4096]{1,0:T(8,128)(2,1)S(1)} collective-permute-done((bf16[32,4096]{1,0:T(8,128)(2,1)S(1)}, bf16[32,4096]{1,0:T(8,128)(2,1)S(1)}, u32[]{:S(2)}, u32[]{:S(2)}) %collective-permute-start.16) | collective-permute-done | bytes 262176 | tf_op jit(solution)/shard_map/ppermute | solution.py:29
  75.3 8.6 %collective-permute-done.17 = bf16[32,4096]{1,0:T(8,128)(2,1)S(1)} collective-permute-done((bf16[32,4096]{1,0:T(8,128)(2,1)S(1)}, bf16[32,4096]{1,0:T(8,128)(2,1)S(1)}, u32[]{:S(2)}, u32[]{:S(2)}) %collective-permute-start.17) | collective-permute-done | bytes 262176 | tf_op jit(solution)/shard_map/ppermute | solution.py:29
  (54 shorter events, 8.9 us)
Async XLA Ops:
  4.1 5.5 %collective-permute-start = (bf16[144,256]{1,0:T(8,128)(2,1)S(1)}, bf16[144,256]{1,0:T(8,128)(2,1)S(1)}, u32[]{:S(2)}, u32[]{:S(2)}) collective-permute-start(bf16[144,256]{1,0:T(8,128)(2,1)S(1)} %fusion.2.refs_0_.refs_1_), channel_id=1, source_target_pairs={{0,8},{4,12},{8,0},{12,4},{16,24},{20,28},{24,16},{28,20},{1,9},{5... | collective-permute-start | bytes 221192 | tf_op jit(solution)/shard_map/ppermute | solution.py:29
  5.3 4.2 %collective-permute-start.1 = (bf16[144,256]{1,0:T(8,128)(2,1)S(1)}, bf16[144,256]{1,0:T(8,128)(2,1)S(1)}, u32[]{:S(2)}, u32[]{:S(2)}) collective-permute-start(bf16[144,256]{1,0:T(8,128)(2,1)S(1)} %fusion.2.refs_0_.refs_1_), channel_id=1, source_target_pairs={{0,16},{4,20},{8,24},{12,28},{16,0},{20,4},{24,8},{28,12},{1,17},{... | collective-permute-start | bytes 221192 | tf_op jit(solution)/shard_map/ppermute | solution.py:29
  6.6 4.2 %collective-permute-start.2 = (bf16[144,256]{1,0:T(8,128)(2,1)S(1)}, bf16[144,256]{1,0:T(8,128)(2,1)S(1)}, u32[]{:S(2)}, u32[]{:S(2)}) collective-permute-start(bf16[144,256]{1,0:T(8,128)(2,1)S(1)} %fusion.2.refs_0_.refs_1_), channel_id=1, source_target_pairs={{0,24},{4,28},{8,16},{12,20},{16,8},{20,12},{24,0},{28,4},{1,25},{... | collective-permute-start | bytes 221192 | tf_op jit(solution)/shard_map/ppermute | solution.py:29
  10.8 3.6 %collective-permute-start.3 = (bf16[576,256]{1,0:T(8,128)(2,1)S(1)}, bf16[576,256]{1,0:T(8,128)(2,1)S(1)}, u32[]{:S(2)}, u32[]{:S(2)}) collective-permute-start(bf16[576,256]{1,0:T(8,128)(2,1)S(1)} %join_after.1.same_ref), channel_id=1, source_target_pairs={{0,4},{4,0},{8,12},{12,8},{16,20},{20,16},{24,28},{28,24},{1,5},{5... | collective-permute-start | bytes 884744 | tf_op jit(solution)/shard_map/ppermute | solution.py:29
  14.4 7.9 %copy-start.5 = (f32[32,8]{0,1:T(8,128)S(1)}, f32[32,8]{0,1:T(8,128)}, u32[]{:S(2)}) copy-start(f32[32,8]{0,1:T(8,128)} %param.21) | copy-start | bytes 3076
  14.4 7.9 %copy-start.6 = (s32[32,8]{0,1:T(8,128)S(1)}, s32[32,8]{0,1:T(8,128)}, u32[]{:S(2)}) copy-start(s32[32,8]{0,1:T(8,128)} %param.20) | copy-start | bytes 3076
  20.7 6.0 %collective-permute-start.4 = (bf16[64,1024]{1,0:T(8,128)(2,1)S(1)}, bf16[64,1024]{1,0:T(8,128)(2,1)S(1)}, u32[]{:S(2)}, u32[]{:S(2)}) collective-permute-start(bf16[64,1024]{1,0:T(8,128)(2,1)S(1)} %get-tuple-element.40), channel_id=1, source_target_pairs={{0,1},{1,0},{2,3},{3,2},{4,5},{5,4},{6,7},{7,6},{8,9},{9,8},{10,11... | collective-permute-start | bytes 393224 | tf_op jit(solution)/shard_map/ppermute | solution.py:29
  22.1 6.2 %collective-permute-start.7 = (bf16[64,1024]{1,0:T(8,128)(2,1)S(1)}, bf16[64,1024]{1,0:T(8,128)(2,1)S(1)}, u32[]{:S(2)}, u32[]{:S(2)}) collective-permute-start(bf16[64,1024]{1,0:T(8,128)(2,1)S(1)} %get-tuple-element.43), channel_id=1, source_target_pairs={{0,1},{1,0},{2,3},{3,2},{4,5},{5,4},{6,7},{7,6},{8,9},{9,8},{10,11... | collective-permute-start | bytes 393224 | tf_op jit(solution)/shard_map/ppermute | solution.py:29
  22.3 23.9 %copy-start = (bf16[1,384,4096]{2,1,0:T(8,128)(2,1)S(1)}, bf16[1,384,4096]{2,1,0:T(8,128)(2,1)}, u32[]{:S(2)}) copy-start(bf16[1,384,4096]{2,1,0:T(8,128)(2,1)} %param.22) | copy-start | bytes 9437188
  22.3 23.9 %copy-start.3 = (f32[4096]{0:T(1024)S(1)}, f32[4096]{0:T(1024)}, u32[]{:S(2)}) copy-start(f32[4096]{0:T(1024)} %param.19) | copy-start | bytes 49156
  26.8 4.9 %collective-permute-start.5 = (bf16[64,1024]{1,0:T(8,128)(2,1)S(1)}, bf16[64,1024]{1,0:T(8,128)(2,1)S(1)}, u32[]{:S(2)}, u32[]{:S(2)}) collective-permute-start(bf16[64,1024]{1,0:T(8,128)(2,1)S(1)} %add.50), channel_id=1, source_target_pairs={{0,2},{1,3},{2,0},{3,1},{4,6},{5,7},{6,4},{7,5},{8,10},{9,11},{10,... | collective-permute-start | bytes 393224 | tf_op jit(solution)/shard_map/ppermute | solution.py:29
  26.9 11.7 %collective-permute-start.10 = (bf16[64,1024]{1,0:T(8,128)(2,1)S(1)}, bf16[64,1024]{1,0:T(8,128)(2,1)S(1)}, u32[]{:S(2)}, u32[]{:S(2)}) collective-permute-start(bf16[64,1024]{1,0:T(8,128)(2,1)S(1)} %get-tuple-element.48), channel_id=1, source_target_pairs={{0,1},{1,0},{2,3},{3,2},{4,5},{5,4},{6,7},{7,6},{8,9},{9,8},{10,11... | collective-permute-start | bytes 393224 | tf_op jit(solution)/shard_map/ppermute | solution.py:29
  28.4 10.4 %collective-permute-start.8 = (bf16[64,1024]{1,0:T(8,128)(2,1)S(1)}, bf16[64,1024]{1,0:T(8,128)(2,1)S(1)}, u32[]{:S(2)}, u32[]{:S(2)}) collective-permute-start(bf16[64,1024]{1,0:T(8,128)(2,1)S(1)} %add.52), channel_id=1, source_target_pairs={{0,2},{1,3},{2,0},{3,1},{4,6},{5,7},{6,4},{7,5},{8,10},{9,11},{10,... | collective-permute-start | bytes 393224 | tf_op jit(solution)/shard_map/ppermute | solution.py:29
  30.6 8.7 %collective-permute-start.13 = (bf16[64,1024]{1,0:T(8,128)(2,1)S(1)}, bf16[64,1024]{1,0:T(8,128)(2,1)S(1)}, u32[]{:S(2)}, u32[]{:S(2)}) collective-permute-start(bf16[64,1024]{1,0:T(8,128)(2,1)S(1)} %get-tuple-element.57), channel_id=1, source_target_pairs={{0,1},{1,0},{2,3},{3,2},{4,5},{5,4},{6,7},{7,6},{8,9},{9,8},{10,11... | collective-permute-start | bytes 393224 | tf_op jit(solution)/shard_map/ppermute | solution.py:29
  31.7 14.4 %collective-permute-start.6 = (bf16[64,1024]{1,0:T(8,128)(2,1)S(1)}, bf16[64,1024]{1,0:T(8,128)(2,1)S(1)}, u32[]{:S(2)}, u32[]{:S(2)}) collective-permute-start(bf16[64,1024]{1,0:T(8,128)(2,1)S(1)} %add.51.mine_ref), channel_id=1, source_target_pairs={{0,1},{1,0},{2,3},{3,2},{4,5},{5,4},{6,7},{7,6},{8,9},{9,8},{10,11... | collective-permute-start | bytes 393224 | tf_op jit(solution)/shard_map/ppermute | solution.py:29
  38.7 7.9 %collective-permute-start.11 = (bf16[64,1024]{1,0:T(8,128)(2,1)S(1)}, bf16[64,1024]{1,0:T(8,128)(2,1)S(1)}, u32[]{:S(2)}, u32[]{:S(2)}) collective-permute-start(bf16[64,1024]{1,0:T(8,128)(2,1)S(1)} %add.54), channel_id=1, source_target_pairs={{0,2},{1,3},{2,0},{3,1},{4,6},{5,7},{6,4},{7,5},{8,10},{9,11},{10,... | collective-permute-start | bytes 393224 | tf_op jit(solution)/shard_map/ppermute | solution.py:29
  39.4 9.5 %collective-permute-start.14 = (bf16[64,1024]{1,0:T(8,128)(2,1)S(1)}, bf16[64,1024]{1,0:T(8,128)(2,1)S(1)}, u32[]{:S(2)}, u32[]{:S(2)}) collective-permute-start(bf16[64,1024]{1,0:T(8,128)(2,1)S(1)} %add.56), channel_id=1, source_target_pairs={{0,2},{1,3},{2,0},{3,1},{4,6},{5,7},{6,4},{7,5},{8,10},{9,11},{10,... | collective-permute-start | bytes 393224 | tf_op jit(solution)/shard_map/ppermute | solution.py:29
  41.2 9.3 %collective-permute-start.9 = (bf16[64,1024]{1,0:T(8,128)(2,1)S(1)}, bf16[64,1024]{1,0:T(8,128)(2,1)S(1)}, u32[]{:S(2)}, u32[]{:S(2)}) collective-permute-start(bf16[64,1024]{1,0:T(8,128)(2,1)S(1)} %add.53.mine_ref), channel_id=1, source_target_pairs={{0,1},{1,0},{2,3},{3,2},{4,5},{5,4},{6,7},{7,6},{8,9},{9,8},{10,11... | collective-permute-start | bytes 393224 | tf_op jit(solution)/shard_map/ppermute | solution.py:29
  46.6 7.8 %collective-permute-start.12 = (bf16[64,1024]{1,0:T(8,128)(2,1)S(1)}, bf16[64,1024]{1,0:T(8,128)(2,1)S(1)}, u32[]{:S(2)}, u32[]{:S(2)}) collective-permute-start(bf16[64,1024]{1,0:T(8,128)(2,1)S(1)} %add.55.mine_ref), channel_id=1, source_target_pairs={{0,1},{1,0},{2,3},{3,2},{4,5},{5,4},{6,7},{7,6},{8,9},{9,8},{10,11... | collective-permute-start | bytes 393224 | tf_op jit(solution)/shard_map/ppermute | solution.py:29
  50.5 6.3 %copy-start.1 = (bf16[1,192,4096]{2,1,0:T(8,128)(2,1)S(1)}, bf16[1,192,4096]{2,1,0:T(8,128)(2,1)}, u32[]{:S(2)}) copy-start(bf16[1,192,4096]{2,1,0:T(8,128)(2,1)} %param.23) | copy-start | bytes 4718596
  50.9 5.9 %collective-permute-start.15 = (bf16[64,1024]{1,0:T(8,128)(2,1)S(1)}, bf16[64,1024]{1,0:T(8,128)(2,1)S(1)}, u32[]{:S(2)}, u32[]{:S(2)}) collective-permute-start(bf16[64,1024]{1,0:T(8,128)(2,1)S(1)} %add.57.mine_ref), channel_id=1, source_target_pairs={{0,1},{1,0},{2,3},{3,2},{4,5},{5,4},{6,7},{7,6},{8,9},{9,8},{10,11... | collective-permute-start | bytes 393224 | tf_op jit(solution)/shard_map/ppermute | solution.py:29
  57.8 17.5 %collective-permute-start.16 = (bf16[32,4096]{1,0:T(8,128)(2,1)S(1)}, bf16[32,4096]{1,0:T(8,128)(2,1)S(1)}, u32[]{:S(2)}, u32[]{:S(2)}) collective-permute-start(bf16[32,4096]{1,0:T(8,128)(2,1)S(1)} %get-tuple-element.68), channel_id=1, source_target_pairs={{0,2},{1,3},{2,0},{3,1},{4,6},{5,7},{6,4},{7,5},{8,10},{9,11},{10,... | collective-permute-start | bytes 786440 | tf_op jit(solution)/shard_map/ppermute | solution.py:29
  58.6 25.3 %collective-permute-start.17 = (bf16[32,4096]{1,0:T(8,128)(2,1)S(1)}, bf16[32,4096]{1,0:T(8,128)(2,1)S(1)}, u32[]{:S(2)}, u32[]{:S(2)}) collective-permute-start(bf16[32,4096]{1,0:T(8,128)(2,1)S(1)} %get-tuple-element.69), channel_id=1, source_target_pairs={{0,3},{1,2},{2,1},{3,0},{4,7},{5,6},{6,5},{7,4},{8,11},{9,10},{10,... | collective-permute-start | bytes 786440 | tf_op jit(solution)/shard_map/ppermute | solution.py:29
  60.5 23.3 %collective-permute-start.18 = (bf16[32,4096]{1,0:T(8,128)(2,1)S(1)}, bf16[32,4096]{1,0:T(8,128)(2,1)S(1)}, u32[]{:S(2)}, u32[]{:S(2)}) collective-permute-start(bf16[32,4096]{1,0:T(8,128)(2,1)S(1)} %get-tuple-element.70), channel_id=1, source_target_pairs={{0,1},{1,0},{2,3},{3,2},{4,5},{5,4},{6,7},{7,6},{8,9},{9,8},{10,11... | collective-permute-start | bytes 786440 | tf_op jit(solution)/shard_map/ppermute | solution.py:29
  (2 other events, 2.0 us)
